TPU v7x, 32 devices: a whole 2x2x4 slice. The times are simulated.
32 devices in a mesh: grp: 1, date: 4 (over y, x), shard: 8 (over z, core).
Axes of the slice: x: 2, y: 2, z: 4, core: 2. Of those that a mesh axis runs over, the one named last changes fastest.
Arguments:
- echo_spectra: bfloat16 [4, 2, 128, 8192], P(('grp', 'date'), None, 'shard'), may hold values from -6 to 6
- range_reference: float32 [2, 8192], replicated, may hold values from -5 to 5
- azimuth_reference: bfloat16 [2, 128, 8192], P(None, None, 'shard'), may hold values from -5 to 5
- block_owner: int32 [4, 64], P(('grp', 'date')), may hold values from 0 to 7, as said below
- block_slot: int32 [4, 64], P(('grp', 'date')), may hold values from 0 to 15, as said below
- kernel_index: int32 [4, 64], P(('grp', 'date')), may hold values from 0 to 7
Outputs:
- filtered: bfloat16 [4, 128, 2, 2, 128, 128], P(('grp', 'date'), 'shard')
Inputs may be any that keep to these rules, and one draw needn't show every extreme that they name: `block_owner`: every date carries the same owners (the stack is coregistered onto one map grid). Within a date, the 8 blocks of one range-column group name any one owner at most 2 times, and some group names some owner exactly 2 times; every owner is named by at most 16 blocks, and some owner by exactly 16. `block_slot`: every date carries the same slots. Within a date, blocks that name the same owner have distinct slots.
All inputs are finite; a program needn't handle non-finite values.
Results may differ from a plain program's by a relative error of at most 0.017.
Values may be sent and summed in bfloat16 or wider, within the bound.
No kernel may reach another device: no remote copies, remote signals or barrier semaphores. Data moves between devices by JAX's collectives and lax.ppermute only.
A program may use at most 128 MiB of HBM per device.

v0:
```python
import math

import jax
import jax.numpy as jnp
from jax import lax
from jax.sharding import PartitionSpec as P

RNG = 8192
RSPLIT = 64
BLK = 128
NSUB = 8
BLK_DEV = 8


def passed_along(value, axis, steps):
    count = lax.axis_size(axis)
    pairs = [(source, (source + steps) % count) for source in range(count)]
    return lax.ppermute(value, axis, pairs)


def dft_block(size, sign):
    index = jnp.arange(size, dtype=jnp.int32)
    phase = index[:, None] * index[None, :] % size
    angle = 2.0 * math.pi / size * phase.astype(jnp.float32)
    scale = 1.0 / math.sqrt(size)
    cosine = jnp.cos(angle) * scale
    sine = sign * jnp.sin(angle) * scale
    table = jnp.stack([jnp.stack([cosine, -sine]), jnp.stack([sine, cosine])])
    return jnp.transpose(table, (0, 2, 1, 3)).astype(jnp.bfloat16)


def twiddle(first_len, second_len, total):
    left = jnp.arange(first_len, dtype=jnp.int32)
    right = jnp.arange(second_len, dtype=jnp.int32)
    phase = left[:, None] * right[None, :] % total
    angle = 2.0 * math.pi / total * phase.astype(jnp.float32)
    return (jnp.cos(angle), jnp.sin(angle))


def kernel_table():
    offset = (jnp.arange(NSUB, dtype=jnp.float32) + 0.5) / NSUB
    cells = jnp.arange(BLK, dtype=jnp.float32)
    dist = cells[None, None, :] - cells[None, :, None] - offset[:, None, None]
    window = jnp.where(jnp.abs(dist) < 4.0, 0.5 + 0.5 * jnp.cos(math.pi * dist / 4.0), 0.0)
    return (jnp.sinc(dist) * window).astype(jnp.bfloat16)


def bdot(form, left, right):
    return jnp.einsum(form, left, right, preferred_element_type=jnp.float32)


def range_compress(spectra, reference):
    real_in = spectra[0].astype(jnp.float32)
    imag_in = spectra[1].astype(jnp.float32)
    matched = jnp.stack(
        [
            real_in * reference[0] + imag_in * reference[1],
            imag_in * reference[0] - real_in * reference[1],
        ]
    ).astype(jnp.bfloat16)
    count = spectra.shape[1]
    outer_len = RSPLIT
    inner_len = RNG // RSPLIT
    shaped = matched.reshape(2, count, outer_len, inner_len)
    section = bdot("cnek,epkb->cpnb", dft_block(outer_len, 1), shaped)
    twc, tws = twiddle(outer_len, inner_len, RNG)
    first = jnp.stack(
        [section[0] * twc - section[1] * tws, section[0] * tws + section[1] * twc]
    ).astype(jnp.bfloat16)
    second = bdot("cmek,epnk->cpmn", dft_block(inner_len, 1), first)
    return second.reshape(2, count, RNG).astype(jnp.bfloat16)


def azimuth_focus(columns, reference):
    count = columns.shape[1]
    doppler = bdot("cuep,epk->cuk", dft_block(count, -1), columns)
    ref_re = reference[0].astype(jnp.float32)
    ref_im = reference[1].astype(jnp.float32)
    shaped = jnp.stack(
        [doppler[0] * ref_re - doppler[1] * ref_im, doppler[0] * ref_im + doppler[1] * ref_re]
    ).astype(jnp.bfloat16)
    return bdot("cuep,epk->cuk", dft_block(count, 1), shaped).astype(jnp.bfloat16)


def resample(blocks, kinds):
    count = blocks.shape[0]
    picker = (kinds[:, None] == jnp.arange(NSUB, dtype=jnp.int32)[None, :]).astype(jnp.bfloat16)
    table = kernel_table().reshape(NSUB, BLK * BLK)
    kernels = (
        jnp.dot(picker, table, preferred_element_type=jnp.float32)
        .astype(jnp.bfloat16)
        .reshape(count, BLK, BLK)
    )
    return bdot("nij,ncjk->ncik", kernels, blocks).astype(jnp.bfloat16)


def cross(first, second):
    fre = first[:, 0].astype(jnp.float32)
    fim = first[:, 1].astype(jnp.float32)
    sre = second[:, 0].astype(jnp.float32)
    sim = second[:, 1].astype(jnp.float32)
    return jnp.stack([fre * sre + fim * sim, fim * sre - fre * sim], axis=1)


def goldstein(patches):
    forward = dft_block(BLK, -1)
    backward = dft_block(BLK, 1)
    rows = bdot("cuei,npeij->npcuj", forward, patches).astype(jnp.bfloat16)
    spectrum = bdot("npeuj,cvej->npcuv", rows, forward)
    power = spectrum[:, :, 0] ** 2 + spectrum[:, :, 1] ** 2
    smooth = jnp.zeros_like(power)
    for down in (-1, 0, 1):
        for across in (-1, 0, 1):
            smooth = smooth + jnp.roll(power, (down, across), axis=(-2, -1))
    smooth = smooth / 9.0
    level = jnp.mean(smooth, axis=(-2, -1), keepdims=True)
    weight = jnp.sqrt(jnp.sqrt(smooth / (level + 1e-06)))
    weighted = (spectrum * weight[:, :, None]).astype(jnp.bfloat16)
    back = bdot("cuei,npeij->npcuj", backward, weighted).astype(jnp.bfloat16)
    return bdot("npeuj,cvej->npcuv", back, backward).astype(jnp.bfloat16)


def body(echo_spectra, range_reference, azimuth_reference, block_owner, block_slot, kernel_index):
    shards = lax.axis_size("shard")
    most = max(2, 2 * BLK_DEV // shards)
    capacity = min(2 * BLK_DEV, shards * most)
    outgoing = shards * most
    compressed = range_compress(echo_spectra[0], range_reference)
    columns = lax.all_to_all(compressed, "shard", split_axis=2, concat_axis=1, tiled=True)
    image = azimuth_focus(columns, azimuth_reference)
    row_blocks = image.shape[1] // BLK
    col_blocks = image.shape[2] // BLK
    blocks = image.reshape(2, row_blocks, BLK, col_blocks, BLK)
    blocks = jnp.transpose(blocks, (1, 3, 0, 2, 4)).reshape(BLK_DEV, 2, BLK, BLK)
    owners = block_owner[0]
    slots = block_slot[0]
    kinds = kernel_index[0]
    total = owners.shape[0]
    me_index = lax.axis_index("shard")
    numbers = jnp.arange(total, dtype=jnp.int32)
    sender = numbers // BLK_DEV
    earlier = (
        (sender[:, None] == sender[None, :])
        & (owners[:, None] == owners[None, :])
        & (numbers[None, :] < numbers[:, None])
    )
    rank = jnp.sum(earlier.astype(jnp.int32), axis=1)
    target = owners * most + rank
    my_target = lax.dynamic_slice_in_dim(target, me_index * BLK_DEV, BLK_DEV)
    chooser = (my_target[None, :] == jnp.arange(outgoing, dtype=jnp.int32)[:, None]).astype(
        jnp.bfloat16
    )
    outbox = bdot("en,nxyz->exyz", chooser, blocks).astype(jnp.bfloat16)
    outbox = outbox.reshape(shards, most, 2, BLK, BLK)
    inbox = lax.all_to_all(outbox, "shard", split_axis=0, concat_axis=0, tiled=True).reshape(
        outgoing, 2, BLK, BLK
    )
    entry = sender * most + rank
    hits = owners == me_index
    slot_hit = (slots[None, :] == jnp.arange(capacity, dtype=jnp.int32)[:, None]) & hits[None, :]
    entry_hit = entry[:, None] == jnp.arange(outgoing, dtype=jnp.int32)[None, :]
    placing = jnp.dot(slot_hit.astype(jnp.float32), entry_hit.astype(jnp.float32)).astype(
        jnp.bfloat16
    )
    tile = bdot("qe,exyz->qxyz", placing, inbox).astype(jnp.bfloat16)
    slot_kinds = jnp.sum(slot_hit.astype(jnp.int32) * kinds[None, :], axis=1)
    tile = resample(tile, slot_kinds)
    following = passed_along(tile, "date", -1)
    second = passed_along(tile, "date", -2)
    pairs = jnp.stack([cross(tile, following), cross(tile, second)], axis=1).astype(jnp.bfloat16)
    return goldstein(pairs)[None]


def solution(mesh):
    in_specs = (
        P(("grp", "date"), None, "shard", None),
        P(),
        P(None, None, "shard"),
        P(("grp", "date"), None),
        P(("grp", "date"), None),
        P(("grp", "date"), None),
    )
    out_specs = P(("grp", "date"), "shard", None, None, None, None)
    return jax.shard_map(body, mesh=mesh, in_specs=in_specs, out_specs=out_specs, check_vma=False)
```

profile of v0, /device:TPU:2, one launch (start us, length us, event | category | flops | bytes accessed | tf_op | source)
XLA Modules:
  0.0 187.9 jit_solution(73576553824263236)
XLA Ops:
  0.0 0.2 negate_convert_fusion.2
  0.5 0.3 negate_convert_fusion
  0.7 0.3 multiply_convert_fusion.1
  1.0 0.3 multiply_convert_fusion.3
  1.3 1.1 convert_bitcast_fusion.1
  2.7 0.2 fusion.84
  2.9 0.3 convolution_bitcast_fusion.1
  3.2 0.2 subtract_convert_fusion
  3.4 0.3 fusion.38
  3.8 5.6 %copy.128 = bf16[2,16,128,64]{1,0,3,2:T(2,128)(2,1)} copy(bf16[2,16,128,64]{2,3,0,1:T(8,128)(2,1)S(1)} %fusion.38) | data formatting | bytes 1048576 | tf_op jit(solution)/shard_map/convert_element_type | solution.py:71
  9.3 6.5 %reshape.594 = bf16[8,2,16384]{2,1,0:T(2,128)(2,1)} reshape(bf16[8192,2,16]{2,1,0:T(2,128)(2,1)} %bitcast.278) | data formatting | bytes 1048576
  15.8 4.9 %all-to-all-start = ((bf16[8,2,16384]{2,1,0:T(2,128)(2,1)}), bf16[8,2,16384]{2,1,0:T(2,128)(2,1)S(1)}, u32[]{:S(2)}, u32[]{:S(2)}) async-start(bf16[8,2,16384]{2,1,0:T(2,128)(2,1)} %reshape.594), calls=%async_computation | async-start | bytes 1048576 | tf_op jit(solution)/shard_map/all_to_all | solution.py:129
  20.7 0.2 convert_reduce_fusion
  21.0 15.1 %all-to-all-done = bf16[8,2,16384]{2,1,0:T(2,128)(2,1)S(1)} async-done(((bf16[8,2,16384]{2,1,0:T(2,128)(2,1)}), bf16[8,2,16384]{2,1,0:T(2,128)(2,1)S(1)}, u32[]{:S(2)}, u32[]{:S(2)}) %all-to-all-start) | async-done | bytes 524320 | tf_op jit(solution)/shard_map/all_to_all | solution.py:129
  36.0 4.1 %reshape.595 = bf16[8192,2,16]{2,1,0:T(2,128)(2,1)} reshape(bf16[8,2,16384]{2,1,0:T(2,128)(2,1)S(1)} %all-to-all-done) | data formatting | bytes 1048576
  40.1 9.0 %copy.130 = bf16[2,16,8,1024]{3,1,2,0:T(8,128)(2,1)S(1)} copy(bf16[2,16,8,1024]{1,0,3,2:T(2,128)(2,1)} %bitcast.279) | data formatting | bytes 1048576 | tf_op jit(solution)/shard_map/all_to_all | solution.py:129
  49.1 0.3 convolution_bitcast_fusion.3
  49.4 0.2 fusion.56
  49.6 0.3 fusion.37
  50.0 0.5 convolution_convert_fusion.2
  50.6 2.0 %copy.79 = bf16[8,2,2,128,128]{4,1,3,2,0:T(2,128)(2,1)} copy(bf16[8,2,2,128,128]{4,1,0,3,2:T(2,128)(2,1)S(1)} %bitcast.281) | data formatting | bytes 2097152 | tf_op jit(solution)/shard_map/reshape | solution.py:154
  52.6 3.6 %all-to-all-start.1 = ((bf16[8,2,2,128,128]{4,1,3,2,0:T(2,128)(2,1)}), bf16[8,2,2,128,128]{4,1,3,2,0:T(2,128)(2,1)S(1)}, u32[]{:S(2)}, u32[]{:S(2)}) async-start(bf16[8,2,2,128,128]{4,1,3,2,0:T(2,128)(2,1)} %copy.79), calls=%async_computation.1 | async-start | bytes 2097152 | tf_op jit(solution)/shard_map/all_to_all | solution.py:155
  56.3 2.8 %fusion.39 = bf16[2,8,128,128]{3,1,2,0:T(8,128)(2,1)S(1)} fusion(f32[8]{0:T(128)S(1)} %add_multiply_fusion, f32[16384]{0:T(1024)S(1)} %subtract_bitcast_fusion, s32[16]{0:T(128)S(1)} %select_reduce_fusion), kind=kOutput, calls=%fused_computation.74 | convolution fusion | flops 9830528 | bytes 589920 | tf_op jit(solution)/shard_map/dot_general | solution.py:90
  59.2 23.4 %all-to-all-done.1 = bf16[8,2,2,128,128]{4,1,3,2,0:T(2,128)(2,1)S(1)} async-done(((bf16[8,2,2,128,128]{4,1,3,2,0:T(2,128)(2,1)}), bf16[8,2,2,128,128]{4,1,3,2,0:T(2,128)(2,1)S(1)}, u32[]{:S(2)}, u32[]{:S(2)}) %all-to-all-start.1) | async-done | bytes 1048608 | tf_op jit(solution)/shard_map/all_to_all | solution.py:155
  82.6 0.7 copy.80
  83.4 0.6 convolution_convert_fusion.1
  84.0 0.5 fusion.35
  84.5 0.8 collective-permute-start
  85.2 1.5 collective-permute-start.1
  86.8 23.6 %collective-permute-done = bf16[16,2,128,128]{2,3,1,0:T(8,128)(2,1)S(1)} collective-permute-done((bf16[16,2,128,128]{2,3,1,0:T(8,128)(2,1)S(1)}, bf16[16,2,128,128]{2,3,1,0:T(8,128)(2,1)S(1)}, u32[]{:S(2)}, u32[]{:S(2)}) %collective-permute-start) | collective-permute-done | bytes 1048608 | tf_op jit(solution)/shard_map/ppermute | solution.py:18
  110.4 21.7 %collective-permute-done.1 = bf16[16,2,128,128]{2,3,1,0:T(8,128)(2,1)S(1)} collective-permute-done((bf16[16,2,128,128]{2,3,1,0:T(8,128)(2,1)S(1)}, bf16[16,2,128,128]{2,3,1,0:T(8,128)(2,1)S(1)}, u32[]{:S(2)}, u32[]{:S(2)}) %collective-permute-start.1) | collective-permute-done | bytes 1048608 | tf_op jit(solution)/shard_map/ppermute | solution.py:18
  132.1 1.0 fusion.45
  133.4 3.4 %convolution_bitcast_fusion = f32[16,2,2,128,128]{3,4,1,0,2:T(8,128)} fusion(bf16[1,2,128,128]{3,2,1,0:T(8,128)(2,1)S(1)} %get-tuple-element.44, bf16[1,2,128,128]{3,2,1,0:T(8,128)(2,1)S(1)} %get-tuple-element.43, bf16[16,1,2,128,128]{3,4,2,0,1:T(8,128)(2,1)S(1)} %maximum_bitcast_fusion.2, bf16[16,1,2,128,128]{3,4,2,0,1:T(8,128)(2,1)S(1)} %maximum_bitcast_fusion.1), kind=kOutput, calls=%fused_computation.5 | convolution fusion | flops 1076363264 | bytes 6422528 | tf_op jit(solution)/shard_map/npeuj,cvej->npcuv/dot_general | solution.py:49
  136.8 2.5 %fusion.96 = f32[16,2,128,128]{2,3,1,0:T(8,128)S(1)} fusion(f32[16,2,2,128,128]{3,4,1,0,2:T(8,128)} %convolution_bitcast_fusion), kind=kLoop, calls=%fused_computation.151 | loop fusion | flops 1572864 | bytes 6291456 | tf_op jit(solution)/shard_map/add | solution.py:110
  139.4 3.0 %slice_bitcast_fusion.5 = (f32[16,2,1,127,128]{3,4,1,0,2:T(8,128)}, f32[16,2,1,127,128]{3,4,1,0,2:T(8,128)}, f32[16,2,127,128]{2,3,1,0:T(8,128)S(1)}, f32[16,2,127,128]{2,3,1,0:T(8,128)S(1)}) fusion(f32[16,2,128,128]{2,3,1,0:T(8,128)S(1)} %fusion.96), kind=kLoop, calls=%fused_computation.281 | loop fusion | bytes 12484608 | tf_op jit(solution)/shard_map/jit(_roll_static)/concatenate | solution.py:114
  142.4 0.7 fusion.191
  143.3 0.5 copy-done.2
  143.7 3.2 %slice_maximum_fusion.3 = (f32[16,2,128,127]{2,3,1,0:T(8,128)}, f32[16,2,128,127]{2,3,1,0:T(8,128)}) fusion(f32[16,2,1,128]{2,3,1,0:T(8,128)S(1)} %get-tuple-element.25, f32[16,2,127,128]{2,3,1,0:T(8,128)S(1)} %get-tuple-element.24), kind=kLoop, calls=%fused_computation.10 | loop fusion | flops 1040384 | bytes 6258688 | tf_op jit(solution)/shard_map/jit(_roll_static)/concatenate | solution.py:114
  147.1 3.3 %slice_maximum_fusion.1 = (f32[16,2,128,127]{2,3,1,0:T(8,128)}, f32[16,2,128,127]{2,3,1,0:T(8,128)}) fusion(f32[16,2,127,128]{2,3,1,0:T(8,128)S(1)} %get-tuple-element.23, f32[16,2,1,128]{2,3,1,0:T(8,128)S(1)} %get-tuple-element.26), kind=kLoop, calls=%fused_computation.8 | loop fusion | flops 1040384 | bytes 6258688 | tf_op jit(solution)/shard_map/jit(_roll_static)/concatenate | solution.py:114
  150.4 4.0 %fusion.189 = (f32[16,2,128,127]{2,3,1,0:T(8,128)}, f32[16,2,1,128,127]{3,4,1,0,2:T(8,128)}, f32[16,2,1,128,127]{3,4,1,0,2:T(8,128)}, f32[16,2,128,127]{2,3,1,0:T(8,128)}) fusion(f32[16,2,128,128]{2,3,1,0:T(8,128)S(1)} %fusion.96), kind=kLoop, calls=%fused_computation.282 | loop fusion | bytes 12484608 | tf_op jit(solution)/shard_map/jit(_roll_static)/slice | solution.py:114
  154.4 2.2 %copy.99 = f32[16,2,1,128]{3,0,2,1:T(8,128)S(1)} copy(f32[16,2,1,128]{2,3,1,0:T(8,128)} %copy-done) | data formatting | bytes 32768 | tf_op jit(solution)/shard_map/jit(_roll_static)/slice | solution.py:114
  156.6 0.6 copy.88
  157.3 9.2 %fusion.23 = f32[16,2]{1,0:T(8,128)S(1)} fusion(f32[16,2,128,127]{2,3,1,0:T(8,128)} %get-tuple-element.10, f32[16,2,128,1]{2,3,1,0:T(1,128)S(1)} %get-tuple-element.12, f32[16,2,128,1]{2,3,1,0:T(1,128)S(1)} %get-tuple-element.11, f32[16,2,128,127]{2,3,1,0:T(8,128)} %get-tuple-element.9, f32[16,2,128,127]{2,3,1,0:T(8,128)} %get-tuple-element.16, ...), kind=kLoop, calls=%fused_computation.39 | loop fusion | flops 11010016 | bytes 20971648 | tf_op jit(solution)/shard_map/reduce_sum | solution.py:116
  166.5 1.9 %copy.100 = f32[16,2,1,1,128]{3,4,1,0,2:T(8,128)} copy(f32[16,2,1,1,128]{4,0,3,2,1:T(8,128)S(1)} %bitcast.293) | data formatting | bytes 32768 | tf_op jit(solution)/shard_map/jit(_roll_static)/concatenate | solution.py:114
  168.4 2.0 %copy.89 = f32[16,2,1,1,128]{3,4,1,0,2:T(8,128)} copy(f32[16,2,1,1,128]{4,0,3,2,1:T(8,128)S(1)} %bitcast.292) | data formatting | bytes 32768 | tf_op jit(solution)/shard_map/jit(_roll_static)/concatenate | solution.py:114
  170.4 10.6 %sqrt_bitcast_fusion = f32[16,2,128,128]{2,3,1,0:T(8,128)} fusion(f32[16,2,1,128,127]{3,4,1,0,2:T(8,128)} %bitcast.277, f32[16,2,1,128,1]{3,4,1,0,2:T(1,128)S(1)} %bitcast.289, f32[16,2,1,127,128]{3,4,1,0,2:T(8,128)} %get-tuple-element.22, f32[16,2,1,1,128]{3,4,1,0,2:T(8,128)} %copy.100, f32[16,2,1,128,1]{3,4,1,0,2:T(1,128)S(1)} %bitcast.288, ...), kind=kLoop, calls=%fused_computation.38 | loop fusion | flops 11010048 | bytes 23068800 | tf_op jit(solution)/shard_map/mul | solution.py:118
  181.0 4.3 %fusion.24 = bf16[1,16,2,2,128,128]{4,5,2,1,3,0:T(8,128)(2,1)S(1)} fusion(bf16[1,2,128,128]{3,2,1,0:T(8,128)(2,1)S(1)} %get-tuple-element.45, bf16[1,2,128,128]{3,2,1,0:T(8,128)(2,1)S(1)} %get-tuple-element.46, f32[16,2,2,128,128]{3,4,1,0,2:T(8,128)} %convolution_bitcast_fusion, f32[16,2,128,128]{2,3,1,0:T(8,128)} %sqrt_bitcast_fusion), kind=kOutput, calls=%fused_computation.54 | convolution fusion | flops 1078460416 | bytes 8519680 | tf_op jit(solution)/shard_map/npeuj,cvej->npcuv/dot_general | solution.py:49
  185.3 2.6 %copy.106 = bf16[1,16,2,2,128,128]{5,4,3,2,1,0:T(8,128)(2,1)} copy(bf16[1,16,2,2,128,128]{4,5,2,1,3,0:T(8,128)(2,1)S(1)} %fusion.24) | data formatting | bytes 4194304 | tf_op jit(solution)/shard_map/broadcast_in_dim | solution.py:171
  (39 shorter events, 1.6 us)
Async XLA Ops:
  0.0 2.6 %copy-start.5 = (f32[2,8192]{1,0:T(2,128)S(1)}, f32[2,8192]{1,0:T(2,128)}, u32[]{:S(2)}) copy-start(f32[2,8192]{1,0:T(2,128)} %param.7) | copy-start | bytes 196612
  9.3 11.3 %copy-start.6 = (s32[1,64]{1,0:T(1,128)S(1)}, s32[1,64]{1,0:T(1,128)}, u32[]{:S(2)}) copy-start(s32[1,64]{1,0:T(1,128)} %param.9) | copy-start | bytes 772
  15.8 20.2 %all-to-all-start = ((bf16[8,2,16384]{2,1,0:T(2,128)(2,1)}), bf16[8,2,16384]{2,1,0:T(2,128)(2,1)S(1)}, u32[]{:S(2)}, u32[]{:S(2)}) async-start(bf16[8,2,16384]{2,1,0:T(2,128)(2,1)} %reshape.594), calls=%async_computation | async-start | bytes 1048576 | tf_op jit(solution)/shard_map/all_to_all | solution.py:129
  40.1 9.3 %copy-start.4 = (bf16[2,128,1024]{2,1,0:T(8,128)(2,1)S(1)}, bf16[2,128,1024]{2,1,0:T(8,128)(2,1)}, u32[]{:S(2)}) copy-start(bf16[2,128,1024]{2,1,0:T(8,128)(2,1)} %param.8) | copy-start | bytes 1572868
  50.5 5.6 %copy-start.7 = (s32[1,64]{1,0:T(1,128)S(1)}, s32[1,64]{1,0:T(1,128)}, u32[]{:S(2)}) copy-start(s32[1,64]{1,0:T(1,128)} %param.10) | copy-start | bytes 772
  50.6 5.6 %copy-start.8 = (s32[1,64]{1,0:T(1,128)S(1)}, s32[1,64]{1,0:T(1,128)}, u32[]{:S(2)}) copy-start(s32[1,64]{1,0:T(1,128)} %param.11) | copy-start | bytes 772
  52.6 30.1 %all-to-all-start.1 = ((bf16[8,2,2,128,128]{4,1,3,2,0:T(2,128)(2,1)}), bf16[8,2,2,128,128]{4,1,3,2,0:T(2,128)(2,1)S(1)}, u32[]{:S(2)}, u32[]{:S(2)}) async-start(bf16[8,2,2,128,128]{4,1,3,2,0:T(2,128)(2,1)} %copy.79), calls=%async_computation.1 | async-start | bytes 2097152 | tf_op jit(solution)/shard_map/all_to_all | solution.py:155
  84.5 25.9 %collective-permute-start = (bf16[16,2,128,128]{2,3,1,0:T(8,128)(2,1)S(1)}, bf16[16,2,128,128]{2,3,1,0:T(8,128)(2,1)S(1)}, u32[]{:S(2)}, u32[]{:S(2)}) collective-permute-start(bf16[16,2,128,128]{2,3,1,0:T(8,128)(2,1)S(1)} %fusion.35), channel_id=1, source_target_pairs={{0,24},{8,0},{16,8},{24,16},{1,25},{9,1},{17,9},{25,17},{2,26},{10... | collective-permute-start | bytes 3145736 | tf_op jit(solution)/shard_map/ppermute | solution.py:18
  85.2 46.9 %collective-permute-start.1 = (bf16[16,2,128,128]{2,3,1,0:T(8,128)(2,1)S(1)}, bf16[16,2,128,128]{2,3,1,0:T(8,128)(2,1)S(1)}, u32[]{:S(2)}, u32[]{:S(2)}) collective-permute-start(bf16[16,2,128,128]{2,3,1,0:T(8,128)(2,1)S(1)} %fusion.35), channel_id=1, source_target_pairs={{0,16},{8,24},{16,0},{24,8},{1,17},{9,25},{17,1},{25,9},{2,18},{10... | collective-permute-start | bytes 3145736 | tf_op jit(solution)/shard_map/ppermute | solution.py:18
  142.4 1.4 copy-start.2
  142.4 4.7 %copy-start.1 = (f32[16,2,127,128]{2,3,1,0:T(8,128)}, f32[16,2,127,128]{2,3,1,0:T(8,128)S(1)}, u32[]{:S(2)}) copy-start(f32[16,2,127,128]{2,3,1,0:T(8,128)S(1)} %get-tuple-element.23) | copy-start | bytes 6242308
  143.1 4.0 %copy-start = (f32[16,2,1,128]{2,3,1,0:T(8,128)}, f32[16,2,1,128]{2,3,1,0:T(8,128)S(1)}, u32[]{:S(2)}) copy-start(f32[16,2,1,128]{2,3,1,0:T(8,128)S(1)} %get-tuple-element.26) | copy-start | bytes 49156
  166.4 4.0 %copy-start.3 = (f32[16,2,128,127]{2,3,1,0:T(8,128)S(1)}, f32[16,2,128,127]{2,3,1,0:T(8,128)}, u32[]{:S(2)}) copy-start(f32[16,2,128,127]{2,3,1,0:T(8,128)} %get-tuple-element.5) | copy-start | bytes 6242308
where the time goes:
time: 188 us
  waiting for transfers between devices  83.8 us (45%)
  local copies, waits for them, and re-layouts  46 us (24%)
  other arithmetic  33.5 us (18%)
  matrix products  13.5 us (7%)
  starting transfers between devices  10.7 us (6%)
    ppermute x2, waiting for transfers between devices, passed_along(): return lax.ppermute(value, axis, pairs)  45.4 us
    all_to_all x1, waiting for transfers between devices, body(): lax.all_to_all(outbox, 'shard', split_axis=0, concat_axis=0, tiled=True)  23.4 us
    all_to_all x1, waiting for transfers between devices, body(): lax.all_to_all(compressed, 'shard', split_axis=2, concat_axis=1, tiled=True)  15.1 us
    unnamed x24, local copies, waits for them, and re-layouts  11.4 us
    dot_general x9, matrix products, bdot(): return jnp.einsum(form, left, right, preferred_element_type=jnp.float32)  10.7 us
    mul x1, other arithmetic, goldstein(): weighted = (spectrum * weight[:, :, None]).astype(jnp.bfloat16)  10.6 us
    reduce_sum x1, other arithmetic, goldstein(): level = jnp.mean(smooth, axis=(-2, -1), keepdims=True)  9.16 us
    all_to_all x1, local copies, waits for them, and re-layouts, body(): lax.all_to_all(compressed, 'shard', split_axis=2, concat_axis=1, tiled=True)  8.96 us
  transfers between devices with their start and end apart: 4, of which 4 were waited for; matrix products, arithmetic and copies ran while one was open for 2% of the time, Pallas kernels for 0%

commit v1 on v0

v1 whole, which is shorter than its diff:
```python
import math

import jax
import jax.numpy as jnp
import numpy as np
from jax import lax
from jax.experimental import pallas as pl
from jax.experimental.pallas import tpu as pltpu
from jax.sharding import PartitionSpec as P

BLK = 128
NSUB = 8
BF = jnp.bfloat16
F32 = jnp.float32
VMEM_BYTES = 32 * 1024 * 1024


def dft(rows, cols, size, sign, scale):
    phase = np.outer(np.arange(rows), np.arange(cols)) % size
    angle = 2.0 * np.pi / size * phase
    cosine = np.cos(angle) * scale
    sine = sign * np.sin(angle) * scale
    return np.block([[cosine, -sine], [sine, cosine]])


def kernel_table():
    offset = (np.arange(NSUB) + 0.5) / NSUB
    cells = np.arange(BLK)
    dist = cells[None, None, :] - cells[None, :, None] - offset[:, None, None]
    window = np.where(np.abs(dist) < 4.0, 0.5 + 0.5 * np.cos(np.pi * dist / 4.0), 0.0)
    return np.sinc(dist) * window


def resample_table(pulses):
    inverse = dft(pulses, pulses, pulses, 1, 1.0 / math.sqrt(pulses))
    rows = pulses // BLK
    table = np.zeros((NSUB, rows, 2 * BLK, 2 * pulses))
    kernels = kernel_table()
    for kind in range(NSUB):
        for row in range(rows):
            for part in range(2):
                start = part * pulses + row * BLK
                table[kind, row, part * BLK : (part + 1) * BLK] = (
                    kernels[kind] @ inverse[start : start + BLK]
                )
    return table.reshape(NSUB * rows, 2 * BLK, 2 * pulses)


def const(table):
    return jnp.asarray(table.astype(np.float32)).astype(BF)


def mm(left, right):
    return jnp.dot(left, right, preferred_element_type=F32)


def whole(count):
    return [pl.BlockSpec(memory_space=pltpu.VMEM)] * count


def params():
    return pltpu.CompilerParams(vmem_limit_bytes=VMEM_BYTES)


def is_pow2(count):
    return count & (count - 1) == 0


def target_of(index, step, count):
    if is_pow2(count):
        return index ^ step
    return (index + step) % count


def source_of(index, step, count):
    if is_pow2(count):
        return index ^ step
    return (index + count - step) % count


def hop(value, axis, step):
    count = lax.axis_size(axis)
    return lax.ppermute(value, axis, [(i, target_of(i, step, count)) for i in range(count)])


def shift(value, axis, steps):
    count = lax.axis_size(axis)
    return lax.ppermute(value, axis, [(i, (i + steps) % count) for i in range(count)])


def range_compress(echo, reference, table, me, chunks):
    _, pulses, samples = echo.shape
    shards, capacity = table.shape
    outer = samples // BLK
    each = capacity // chunks
    first = const(dft(outer, outer, outer, 1, 1.0 / math.sqrt(outer)))
    second = const(dft(outer, BLK, outer, 1, 1.0 / math.sqrt(BLK)))
    phase = np.outer(np.arange(BLK), np.arange(BLK)) % samples
    angle = 2.0 * np.pi / samples * phase
    turn = jnp.asarray(np.stack([np.cos(angle), np.sin(angle)]).astype(np.float32))
    spread = BLK // outer

    def kernel(table_ref, me_ref, echo_ref, ref_ref, first_ref, second_ref, turn_ref, *rest):
        outs = rest[: chunks * shards]
        x_re, x_im, y_re, y_im = rest[chunks * shards :]
        for j in range(outer):
            lanes = slice(j * BLK, (j + 1) * BLK)
            a = echo_ref[0, :, lanes].astype(F32)
            b = echo_ref[1, :, lanes].astype(F32)
            c = ref_ref[0:1, lanes]
            d = ref_ref[1:2, lanes]
            x_re[pl.ds(j, pulses, stride=outer), :] = a * c + b * d
            x_im[pl.ds(j, pulses, stride=outer), :] = b * c - a * d
        turn_c = turn_ref[0]
        turn_s = turn_ref[1]
        for q in range(pulses // 2):
            pair = []
            for p in (2 * q, 2 * q + 1):
                rows = slice(p * outer, (p + 1) * outer)
                pair.append(jnp.concatenate([x_re[rows, :], x_im[rows, :]], axis=0))
            section = mm(first_ref[...], jnp.concatenate(pair, axis=1).astype(BF))
            turned = []
            for p in range(2):
                lanes = slice(p * BLK, (p + 1) * BLK)
                re = jnp.concatenate([section[:outer, lanes]] * spread, axis=0)
                im = jnp.concatenate([section[outer:, lanes]] * spread, axis=0)
                turned.append(
                    jnp.concatenate(
                        [re * turn_c - im * turn_s, re * turn_s + im * turn_c], axis=1
                    )
                )
            turned = jnp.concatenate(turned, axis=0).astype(BF)
            done = lax.dot_general(
                second_ref[...], turned, (((1,), (1,)), ((), ())), preferred_element_type=F32
            )
            for p in range(2):
                lanes = slice(p * BLK, (p + 1) * BLK)
                rows = slice((2 * q + p) * outer, (2 * q + p + 1) * outer)
                y_re[rows, :] = done[:outer, lanes]
                y_im[rows, :] = done[outer:, lanes]
        for chunk in range(chunks):
            for k in range(shards):
                owner = target_of(me_ref[0], k, shards)
                out = outs[chunk * shards + k]
                for s in range(each):
                    column = table_ref[owner, chunk * each + s]
                    rows = pl.ds(column, pulses, stride=outer)
                    out[s, 0] = y_re[rows, :].astype(BF)
                    out[s, 1] = y_im[rows, :].astype(BF)

    piece = jax.ShapeDtypeStruct((each, 2, pulses, BLK), BF)
    smem = pl.BlockSpec(memory_space=pltpu.SMEM)
    outs = pl.pallas_call(
        kernel,
        out_shape=[piece] * (chunks * shards),
        in_specs=[smem, smem] + whole(5),
        out_specs=whole(chunks * shards),
        scratch_shapes=[pltpu.VMEM((pulses * outer, BLK), F32)] * 4,
        compiler_params=params(),
        name="range_compress",
    )(table, me, echo, reference, first, second, turn)
    return [outs[chunk * shards : (chunk + 1) * shards] for chunk in range(chunks)]


def filter_columns(reference, table, place, chunks, dates):
    _, doppler, columns = reference.shape
    shards, most = table.shape
    rows = doppler // dates
    each = most // chunks

    def kernel(table_ref, place_ref, ref_ref, *outs):
        start = pl.multiple_of(place_ref[1] * rows, rows)
        for chunk in range(chunks):
            for owner in range(shards):
                for e in range(each):
                    column = table_ref[owner, chunk * each + e]
                    lanes = pl.ds(pl.multiple_of(column * BLK, BLK), BLK)
                    for part in range(2):
                        outs[chunk][owner, e, part] = ref_ref[part, pl.ds(start, rows), lanes]

    smem = pl.BlockSpec(memory_space=pltpu.SMEM)
    piece = jax.ShapeDtypeStruct((shards, each, 2, rows, BLK), BF)
    return pl.pallas_call(
        kernel,
        out_shape=[piece] * chunks,
        in_specs=[smem, smem] + whole(1),
        out_specs=whole(chunks),
        compiler_params=params(),
        name="filter_columns",
    )(table, place, reference)


def focus(pieces, filters, place, entry, kernel_row, valid, subs):
    each, _, share, _ = pieces[0].shape
    shards = len(pieces)
    dates = len(filters)
    pulses = share * shards
    rows = filters[0].shape[-2]
    forward = const(dft(pulses, pulses, pulses, -1, 1.0 / math.sqrt(pulses)))
    back = const(resample_table(pulses))
    per = each // subs

    def kernel(place_ref, entry_ref, row_ref, valid_ref, forward_ref, back_ref, *rest):
        piece_refs = rest[:shards]
        filter_refs = rest[shards : shards + dates]
        outs = rest[shards + dates : shards + dates + subs]
        col, fil = rest[shards + dates + subs :]
        for k in range(shards):
            source = source_of(place_ref[0], k, shards)
            at = pl.multiple_of(source * share, share)
            for s in range(each):
                for part in range(2):
                    col[s, part, pl.ds(at, share), :] = piece_refs[k][s, part]
        for e in range(dates):
            at = pl.multiple_of(source_of(place_ref[1], e, dates) * rows, rows)
            for s in range(each):
                for part in range(2):
                    fil[s, part, pl.ds(at, rows), :] = filter_refs[e][entry_ref[s], part]
        for s in range(0, each, 2):
            both = [col[t].reshape(2 * pulses, BLK) for t in (s, s + 1)]
            doppler = mm(forward_ref[...], jnp.concatenate(both, axis=1))
            for t in (0, 1):
                lanes = slice(t * BLK, (t + 1) * BLK)
                re = doppler[:pulses, lanes]
                im = doppler[pulses:, lanes]
                a = fil[s + t, 0].astype(F32)
                b = fil[s + t, 1].astype(F32)
                shaped = jnp.concatenate([re * a - im * b, re * b + im * a], axis=0).astype(BF)
                image = mm(back_ref[row_ref[s + t]], shaped)
                image = jnp.where(valid_ref[s + t] > 0, image, 0.0).astype(BF)
                out = outs[(s + t) // per]
                out[(s + t) % per, 0] = image[:BLK]
                out[(s + t) % per, 1] = image[BLK:]

    smem = pl.BlockSpec(memory_space=pltpu.SMEM)
    return pl.pallas_call(
        kernel,
        out_shape=[jax.ShapeDtypeStruct((per, 2, BLK, BLK), BF)] * subs,
        in_specs=[smem] * 4 + whole(2 + shards + dates),
        out_specs=whole(subs),
        scratch_shapes=[
            pltpu.VMEM((each, 2, pulses, BLK), BF),
            pltpu.VMEM((each, 2, pulses, BLK), BF),
        ],
        compiler_params=params(),
        name="focus",
    )(place, entry, kernel_row, valid, forward, back, *pieces, *filters)


def goldstein(tile, follows, second, slots, result, capacity):
    count = tile.shape[0]
    scale = 1.0 / math.sqrt(BLK)
    ahead = dft(BLK, BLK, BLK, -1, scale)
    behind = dft(BLK, BLK, BLK, 1, scale)
    tables = [const(ahead), const(ahead.T), const(behind), const(behind.T)]
    have = 0 if result is None else 1

    def sides(left):
        low, high = slice(0, BLK), slice(BLK, 2 * BLK)
        return jnp.concatenate(
            [
                jnp.concatenate([left[low, low], left[high, low]], axis=1),
                jnp.concatenate([left[low, high], left[high, high]], axis=1),
            ],
            axis=0,
        )

    def around(power):
        power = power + (pltpu.roll(power, 1, 0) + pltpu.roll(power, BLK - 1, 0))
        return power + (pltpu.roll(power, 1, 1) + pltpu.roll(power, BLK - 1, 1))

    def kernel(slot_ref, *rest):
        tile_ref, second_ref = rest[:2]
        follow_refs = rest[2 : 2 + len(follows)]
        al_ref, ar_ref, bl_ref, br_ref = rest[2 + len(follows) : 6 + len(follows)]
        out_ref, buffer, sems = rest[6 + len(follows) + have :]
        for s in range(count):
            t_re = tile_ref[s, 0].astype(F32)
            t_im = tile_ref[s, 1].astype(F32)
            f = follow_refs[0][s]
            for other in follow_refs[1:]:
                f = f + other[s]
            pairs = []
            for o in (f, second_ref[s]):
                o_re = o[0].astype(F32)
                o_im = o[1].astype(F32)
                pairs.append((t_re * o_re + t_im * o_im, t_im * o_re - t_re * o_im))
            x = jnp.concatenate(
                [
                    jnp.concatenate([pairs[0][0], pairs[1][0]], axis=1),
                    jnp.concatenate([pairs[0][1], pairs[1][1]], axis=1),
                ],
                axis=0,
            ).astype(BF)
            rows = sides(mm(al_ref[...], x).astype(BF))
            spectrum = mm(rows, ar_ref[...])
            s_re = spectrum[:, :BLK]
            s_im = spectrum[:, BLK:]
            power = s_re * s_re + s_im * s_im
            weights = []
            for p in range(2):
                one = power[p * BLK : (p + 1) * BLK]
                level = jnp.sum(jnp.sum(one, axis=0, keepdims=True), axis=1, keepdims=True)
                inverse = 1.0 / (9.0 * (level * (1.0 / (BLK * BLK)) + 1e-06))
                weights.append(lax.rsqrt(lax.rsqrt(around(one) * inverse)))
            weight = jnp.concatenate(weights, axis=0)
            weighted = jnp.concatenate([s_re * weight, s_im * weight], axis=1).astype(BF)
            back = sides(mm(bl_ref[...], sides(weighted)).astype(BF))
            filtered = mm(back, br_ref[...]).astype(BF)
            for p in range(2):
                for part in range(2):
                    buffer[s, p, part] = filtered[
                        p * BLK : (p + 1) * BLK, part * BLK : (part + 1) * BLK
                    ]
            pltpu.make_async_copy(buffer.at[s], out_ref.at[slot_ref[s]], sems.at[s]).start()
        for s in range(count):
            pltpu.make_async_copy(buffer.at[s], out_ref.at[slot_ref[s]], sems.at[s]).wait()

    anywhere = pl.BlockSpec(memory_space=pl.ANY)
    smem = pl.BlockSpec(memory_space=pltpu.SMEM)
    operands = [slots, tile, second, *follows, *tables] + ([result] if have else [])
    return pl.pallas_call(
        kernel,
        out_shape=jax.ShapeDtypeStruct((capacity, 2, 2, BLK, BLK), BF),
        in_specs=[smem] + whole(6 + len(follows)) + [anywhere] * have,
        out_specs=anywhere,
        scratch_shapes=[
            pltpu.VMEM((count, 2, 2, BLK, BLK), BF),
            pltpu.SemaphoreType.DMA((count,)),
        ],
        input_output_aliases={len(operands) - 1: 0} if have else {},
        compiler_params=params(),
        name="goldstein",
    )(*operands)


def body(echo_spectra, range_reference, azimuth_reference, block_owner, block_slot, kernel_index):
    shards = lax.axis_size("shard")
    dates = lax.axis_size("date")
    me = lax.axis_index("shard")
    date = lax.axis_index("date")
    place = jnp.stack([me, date]).astype(jnp.int32)
    owners, slots, kinds = block_owner[0], block_slot[0], kernel_index[0]
    total = owners.shape[0]
    group = total // shards
    capacity = 2 * group
    most = max(2, capacity // shards)
    pulses = echo_spectra.shape[2] * shards
    group_columns = azimuth_reference.shape[2] // BLK
    row_blocks = pulses // BLK

    numbers = jnp.arange(total, dtype=jnp.int32)
    sender = numbers // group
    column = numbers % group % group_columns
    row = numbers % group // group_columns
    earlier = (
        (sender[:, None] == sender[None, :])
        & (owners[:, None] == owners[None, :])
        & (numbers[None, :] < numbers[:, None])
    )
    rank = jnp.sum(earlier.astype(jnp.int32), axis=1)
    by_rank = shards * most == capacity
    chunks = most if by_rank else 1
    each = capacity // chunks
    where = rank * shards + sender if by_rank else slots
    at = owners * capacity + where
    cells = jnp.arange(shards * capacity, dtype=jnp.int32)
    found = at[None, :] == cells[:, None]
    columns = jnp.sum(jnp.where(found, (sender * group_columns + column)[None, :], 0), axis=1)
    columns = columns.reshape(shards, capacity)
    mine = (owners[None, :] == me) & (where[None, :] == jnp.arange(capacity)[:, None])

    def of_mine(values):
        return jnp.sum(jnp.where(mine, values[None, :], 0), axis=1)

    valid = of_mine(jnp.ones_like(numbers))
    kernel_row = of_mine(kinds * row_blocks + row)
    entry = of_mine(sender * (most // chunks) + rank % (most // chunks))
    named = of_mine(slots)
    used = jnp.sum(
        ((named[None, :] == jnp.arange(capacity)[:, None]) & (valid > 0)[None, :]).astype(jnp.int32),
        axis=1,
    )
    lower = jnp.arange(capacity)[None, :] < jnp.arange(capacity)[:, None]
    empty_rank = jnp.sum(jnp.where(lower, 1 - valid[None, :], 0), axis=1)
    free_rank = jnp.sum(jnp.where(lower, 1 - used[None, :], 0), axis=1)
    free = (free_rank[None, :] == empty_rank[:, None]) & (used == 0)[None, :]
    spare = jnp.sum(jnp.where(free, jnp.arange(capacity)[None, :], 0), axis=1)
    slot_of = jnp.where(valid > 0, named, spare)

    hits = (
        (sender == me)[None, :]
        & ((owners * most + rank)[None, :] == jnp.arange(shards * most)[:, None])
    )
    filter_table = jnp.sum(jnp.where(hits, column[None, :], 0), axis=1).reshape(shards, most)

    shares = filter_columns(azimuth_reference, filter_table, place, chunks, dates)
    filters = []
    for share in shares:
        got = lax.all_to_all(share, "shard", split_axis=0, concat_axis=0, tiled=True)
        got = got.reshape((shards * (most // chunks),) + got.shape[2:])
        filters.append([got] + [hop(got, "date", e) for e in range(1, dates)])

    outbox = range_compress(echo_spectra[0], range_reference, columns, place, chunks)
    subs = 2
    per = each // subs
    result = None
    for chunk in range(chunks):
        pieces = [outbox[chunk][0]] + [
            hop(outbox[chunk][k], "shard", k) for k in range(1, shards)
        ]
        span = slice(chunk * each, (chunk + 1) * each)
        tiles = focus(
            pieces, filters[chunk], place, entry[span], kernel_row[span], valid[span], subs
        )
        for sub, tile in enumerate(tiles):
            if dates == 4:
                second = hop(tile, "date", 2)
                follows = [
                    lax.ppermute(tile, "date", [(1, 0), (3, 2)]),
                    lax.ppermute(second, "date", [(0, 1), (2, 3)]),
                ]
            else:
                second = shift(tile, "date", -2)
                follows = [shift(tile, "date", -1)]
            start = chunk * each + sub * per
            result = goldstein(
                tile, follows, second, slot_of[start : start + per], result, capacity
            )
    return result[None]


def solution(mesh):
    in_specs = (
        P(("grp", "date"), None, "shard", None),
        P(),
        P(None, None, "shard"),
        P(("grp", "date"), None),
        P(("grp", "date"), None),
        P(("grp", "date"), None),
    )
    out_specs = P(("grp", "date"), "shard", None, None, None, None)
    return jax.shard_map(body, mesh=mesh, in_specs=in_specs, out_specs=out_specs, check_vma=False)
```

time: 188 us -> 109 us (0.58)
  the two profiles are of different devices: /device:TPU:2 before, /device:TPU:0 now
where the time goes in v1:
time: 109 us; the launch traced here: 108 us
  starting transfers between devices  57.5 us (53%)
  Pallas kernels  24.8 us (23%)
  waiting for transfers between devices  14.3 us (13%)
  local copies, waits for them, and re-layouts  6.73 us (6%)
  other arithmetic  4.49 us (4%)
    ppermute x24, starting transfers between devices, hop(): lax.ppermute(value, axis, [(i, target_of(i, step, count)) for i in range(...  33.1 us
    pallas_call x4, Pallas kernels, goldstein(): pl.pallas_call(kernel, out_shape=jax.ShapeDtypeStruct((capacity, 2, 2, BL...  15.3 us
    ppermute x24, waiting for transfers between devices, hop(): lax.ppermute(value, axis, [(i, target_of(i, step, count)) for i in range(...  13.6 us
    ppermute x4, starting transfers between devices, body(): lax.ppermute(second, 'date', [(0, 1), (2, 3)])  10.2 us
    all_to_all x2, starting transfers between devices, body(): lax.all_to_all(share, 'shard', split_axis=0, concat_axis=0, tiled=True)  9.05 us
    unnamed x20, local copies, waits for them, and re-layouts  6.35 us
    ppermute x4, starting transfers between devices, body(): lax.ppermute(tile, 'date', [(1, 0), (3, 2)])  5.15 us
    pallas_call x1, Pallas kernels, range_compress(): pl.pallas_call(kernel, out_shape=[piece] * (chunks * shards), in_specs=[s...  4.69 us
  transfers between devices with their start and end apart: 34, of which 5 were waited for; matrix products, arithmetic and copies ran while one was open for 3% of the time, Pallas kernels for 15%

profile of v1, /device:TPU:0, one launch (start us, length us, event | category | flops | bytes accessed | tf_op | source)
XLA Modules:
  0.0 108.3 jit_solution(3027868635540185573)
XLA Ops:
  0.0 0.9 convert_reduce_fusion
  1.0 0.7 fusion.7
  1.9 1.0 copy-done.5
  2.9 0.9 copy-done.6
  3.8 0.8 copy-done.7
  4.7 0.8 copy-done.8
  5.5 0.8 copy-done.9
  6.3 4.7 %range_compress.1 = (bf16[8,2,16,128]{3,2,1,0:T(8,128)(2,1)S(1)}, bf16[8,2,16,128]{3,2,1,0:T(8,128)(2,1)S(1)}, bf16[8,2,16,128]{3,2,1,0:T(8,128)(2,1)S(1)}, bf16...) custom-call(s32[8,16]{1,0:T(8,128)S(1)} %reshape.178.table_ref, ...), custom_call_target="tpu_custom_call" | custom-call | tf_op jit(solution)/shard_map/range_compress/pallas_call | solution.py:153
  11.5 2.6 %collective-permute-start.17 = (bf16[8,2,16,128]{3,2,1,0:T(8,128)(2,1)S(1)}, bf16[8,2,16,128]{3,2,1,0:T(8,128)(2,1)S(1)}, u32[]{:S(2)}, u32[]{:S(2)}) collective-permute-start(bf16[8,2,16,128]{3,2,1,0:T(8,128)(2,1)S(1)} %get-tuple-element.40), channel_id=1, source_target_pairs={{0,2},{1,3},{2,0},{3,1},{4,6},{5,7},{6,4},{7,5},{8,10},{9,11},{10,... | collective-permute-start | bytes 196616 | tf_op jit(solution)/shard_map/ppermute | solution.py:83
  14.2 2.8 %collective-permute-start.19 = (bf16[8,2,16,128]{3,2,1,0:T(8,128)(2,1)S(1)}, bf16[8,2,16,128]{3,2,1,0:T(8,128)(2,1)S(1)}, u32[]{:S(2)}, u32[]{:S(2)}) collective-permute-start(bf16[8,2,16,128]{3,2,1,0:T(8,128)(2,1)S(1)} %get-tuple-element.42), channel_id=1, source_target_pairs={{0,4},{1,5},{2,6},{3,7},{4,0},{5,1},{6,2},{7,3},{8,12},{9,13},{10,... | collective-permute-start | bytes 196616 | tf_op jit(solution)/shard_map/ppermute | solution.py:83
  17.2 1.0 copy-done.4
  18.3 1.4 %filter_columns.1 = (bf16[8,1,2,32,128]{4,3,2,1,0:T(8,128)(2,1)}, bf16[8,1,2,32,128]{4,3,2,1,0:T(8,128)(2,1)}) custom-call(s32[8,2]{1,0:T(8,128)S(1)} %reshape.179.table_ref, s32[2]{0:T(128)S(1)} %pad_add_fusion.me_ref.place_ref, bf16[2,128,1024]{2,1,0:T(8,128)(2,1)S(1)} %copy-done.4), custom_call_target="tpu_custom_call" | custom-call | tf_op jit(solution)/shard_map/filter_columns/pallas_call | solution.py:183
  19.6 4.9 %all-to-all-start.1 = ((bf16[8,1,2,32,128]{4,3,2,1,0:T(8,128)(2,1)}), bf16[8,1,2,32,128]{4,3,2,1,0:T(8,128)(2,1)S(1)}, u32[]{:S(2)}, u32[]{:S(2)}) async-start(bf16[8,1,2,32,128]{4,3,2,1,0:T(8,128)(2,1)} %get-tuple-element.46), calls=%async_computation.1 | async-start | bytes 262144 | tf_op jit(solution)/shard_map/all_to_all | solution.py:400
  24.5 0.7 compare_bitcast_fusion
  25.2 0.7 add_bitcast_fusion
  25.9 0.8 select_reduce_fusion.2
  26.8 3.8 %collective-permute-start.21 = (bf16[8,2,16,128]{3,2,1,0:T(8,128)(2,1)S(1)}, bf16[8,2,16,128]{3,2,1,0:T(8,128)(2,1)S(1)}, u32[]{:S(2)}, u32[]{:S(2)}) collective-permute-start(bf16[8,2,16,128]{3,2,1,0:T(8,128)(2,1)S(1)} %get-tuple-element.44), channel_id=1, source_target_pairs={{0,6},{1,7},{2,4},{3,5},{4,2},{5,3},{6,0},{7,1},{8,14},{9,15},{10,... | collective-permute-start | bytes 196616 | tf_op jit(solution)/shard_map/ppermute | solution.py:83
  30.7 0.7 all-to-all-done.1
  31.3 4.1 %all-to-all-start = ((bf16[8,1,2,32,128]{4,3,2,1,0:T(8,128)(2,1)}), bf16[8,1,2,32,128]{4,3,2,1,0:T(8,128)(2,1)S(1)}, u32[]{:S(2)}, u32[]{:S(2)}) async-start(bf16[8,1,2,32,128]{4,3,2,1,0:T(8,128)(2,1)} %get-tuple-element.35), calls=%async_computation | async-start | bytes 262144 | tf_op jit(solution)/shard_map/all_to_all | solution.py:400
  35.5 1.6 %collective-permute-start.23 = (bf16[8,2,32,128]{3,2,1,0:T(8,128)(2,1)S(1)}, bf16[8,2,32,128]{3,2,1,0:T(8,128)(2,1)S(1)}, u32[]{:S(2)}, u32[]{:S(2)}) collective-permute-start(bf16[8,2,32,128]{3,2,1,0:T(8,128)(2,1)S(1)} %bitcast.29), channel_id=1, source_target_pairs={{0,8},{8,0},{16,24},{24,16},{1,9},{9,1},{17,25},{25,17},{2,10},{10... | collective-permute-start | bytes 393224 | tf_op jit(solution)/shard_map/ppermute | solution.py:83
  37.0 1.5 %collective-permute-start.24 = (bf16[8,2,32,128]{3,2,1,0:T(8,128)(2,1)S(1)}, bf16[8,2,32,128]{3,2,1,0:T(8,128)(2,1)S(1)}, u32[]{:S(2)}, u32[]{:S(2)}) collective-permute-start(bf16[8,2,32,128]{3,2,1,0:T(8,128)(2,1)S(1)} %bitcast.30), channel_id=1, source_target_pairs={{0,16},{8,24},{16,0},{24,8},{1,17},{9,25},{17,1},{25,9},{2,18},{10... | collective-permute-start | bytes 393224 | tf_op jit(solution)/shard_map/ppermute | solution.py:83
  38.7 2.0 %collective-permute-start.1 = (bf16[8,2,16,128]{3,2,1,0:T(8,128)(2,1)S(1)}, bf16[8,2,16,128]{3,2,1,0:T(8,128)(2,1)S(1)}, u32[]{:S(2)}, u32[]{:S(2)}) collective-permute-start(bf16[8,2,16,128]{3,2,1,0:T(8,128)(2,1)S(1)} %get-tuple-element.29), channel_id=1, source_target_pairs={{0,2},{1,3},{2,0},{3,1},{4,6},{5,7},{6,4},{7,5},{8,10},{9,11},{10,... | collective-permute-start | bytes 196616 | tf_op jit(solution)/shard_map/ppermute | solution.py:83
  41.4 2.6 %collective-permute-start.3 = (bf16[8,2,16,128]{3,2,1,0:T(8,128)(2,1)S(1)}, bf16[8,2,16,128]{3,2,1,0:T(8,128)(2,1)S(1)}, u32[]{:S(2)}, u32[]{:S(2)}) collective-permute-start(bf16[8,2,16,128]{3,2,1,0:T(8,128)(2,1)S(1)} %get-tuple-element.31), channel_id=1, source_target_pairs={{0,4},{1,5},{2,6},{3,7},{4,0},{5,1},{6,2},{7,3},{8,12},{9,13},{10,... | collective-permute-start | bytes 196616 | tf_op jit(solution)/shard_map/ppermute | solution.py:83
  44.0 2.4 %collective-permute-start.25 = (bf16[8,2,32,128]{3,2,1,0:T(8,128)(2,1)S(1)}, bf16[8,2,32,128]{3,2,1,0:T(8,128)(2,1)S(1)}, u32[]{:S(2)}, u32[]{:S(2)}) collective-permute-start(bf16[8,2,32,128]{3,2,1,0:T(8,128)(2,1)S(1)} %bitcast.31), channel_id=1, source_target_pairs={{0,24},{8,16},{16,8},{24,0},{1,25},{9,17},{17,9},{25,1},{2,26},{10... | collective-permute-start | bytes 393224 | tf_op jit(solution)/shard_map/ppermute | solution.py:83
  46.4 3.4 %collective-permute-done.25.rest_11_ = bf16[8,2,32,128]{3,2,1,0:T(8,128)(2,1)S(1)} collective-permute-done((bf16[8,2,32,128]{3,2,1,0:T(8,128)(2,1)S(1)}, bf16[8,2,32,128]{3,2,1,0:T(8,128)(2,1)S(1)}, u32[]{:S(2)}, u32[]{:S(2)}) %collective-permute-start.25) | collective-permute-done | bytes 131104 | tf_op jit(solution)/shard_map/ppermute | solution.py:83
  49.8 0.9 copy-done
  50.7 1.7 %focus.3 = (bf16[4,2,128,128]{3,2,1,0:T(8,128)(2,1)S(1)}, bf16[4,2,128,128]{3,2,1,0:T(8,128)(2,1)S(1)}) custom-call(s32[2]{0:T(128)S(1)} %pad_add_fusion.me_ref.place_ref, s32[8]{0:T(128)S(1)} %get-tuple-element.63.entry_ref, s32[8]{0:T(128)S(1)} %get-tuple-element.66.row_ref, s32[8]{0:T(128)S(1)} %get-tuple-element.59.valid_ref, ...), custom_call_target="tpu_custom_call" | custom-call | tf_op jit(solution)/shard_map/focus/pallas_call | solution.py:236
  52.5 2.2 %collective-permute-start.5 = (bf16[8,2,16,128]{3,2,1,0:T(8,128)(2,1)S(1)}, bf16[8,2,16,128]{3,2,1,0:T(8,128)(2,1)S(1)}, u32[]{:S(2)}, u32[]{:S(2)}) collective-permute-start(bf16[8,2,16,128]{3,2,1,0:T(8,128)(2,1)S(1)} %get-tuple-element.33), channel_id=1, source_target_pairs={{0,6},{1,7},{2,4},{3,5},{4,2},{5,3},{6,0},{7,1},{8,14},{9,15},{10,... | collective-permute-start | bytes 196616 | tf_op jit(solution)/shard_map/ppermute | solution.py:83
  54.6 2.4 %collective-permute-start.6 = (bf16[8,2,16,128]{3,2,1,0:T(8,128)(2,1)S(1)}, bf16[8,2,16,128]{3,2,1,0:T(8,128)(2,1)S(1)}, u32[]{:S(2)}, u32[]{:S(2)}) collective-permute-start(bf16[8,2,16,128]{3,2,1,0:T(8,128)(2,1)S(1)} %get-tuple-element.34), channel_id=1, source_target_pairs={{0,7},{1,6},{2,5},{3,4},{4,3},{5,2},{6,1},{7,0},{8,15},{9,14},{10,... | collective-permute-start | bytes 196616 | tf_op jit(solution)/shard_map/ppermute | solution.py:83
  57.0 1.5 %collective-permute-start.29 = (bf16[4,2,128,128]{3,2,1,0:T(8,128)(2,1)S(1)}, bf16[4,2,128,128]{3,2,1,0:T(8,128)(2,1)S(1)}, u32[]{:S(2)}, u32[]{:S(2)}) collective-permute-start(bf16[4,2,128,128]{3,2,1,0:T(8,128)(2,1)S(1)} %get-tuple-element.48.rest_0_), channel_id=1, source_target_pairs={{0,16},{8,24},{16,0},{24,8},{1,17},{9,25},{17,1},{25,9},{2,18},{10... | collective-permute-start | bytes 786440 | tf_op jit(solution)/shard_map/ppermute | solution.py:83
  58.5 1.3 %collective-permute-start.30 = (bf16[4,2,128,128]{3,2,1,0:T(8,128)(2,1)S(1)}, bf16[4,2,128,128]{3,2,1,0:T(8,128)(2,1)S(1)}, u32[]{:S(2)}, u32[]{:S(2)}) collective-permute-start(bf16[4,2,128,128]{3,2,1,0:T(8,128)(2,1)S(1)} %get-tuple-element.48.rest_0_), channel_id=1, source_target_pairs={{8,0},{24,16},{9,1},{25,17},{10,2},{26,18},{11,3},{27,19},{12,4},{... | collective-permute-start | bytes 786440 | tf_op jit(solution)/shard_map/ppermute | solution.py:420
  59.9 2.7 %collective-permute-start.7 = (bf16[8,2,32,128]{3,2,1,0:T(8,128)(2,1)S(1)}, bf16[8,2,32,128]{3,2,1,0:T(8,128)(2,1)S(1)}, u32[]{:S(2)}, u32[]{:S(2)}) collective-permute-start(bf16[8,2,32,128]{3,2,1,0:T(8,128)(2,1)S(1)} %bitcast.25), channel_id=1, source_target_pairs={{0,8},{8,0},{16,24},{24,16},{1,9},{9,1},{17,25},{25,17},{2,10},{10... | collective-permute-start | bytes 393224 | tf_op jit(solution)/shard_map/ppermute | solution.py:83
  63.2 1.0 collective-permute-start.9
  64.2 7.8 %collective-permute-done.7.rest_9_ = bf16[8,2,32,128]{3,2,1,0:T(8,128)(2,1)S(1)} collective-permute-done((bf16[8,2,32,128]{3,2,1,0:T(8,128)(2,1)S(1)}, bf16[8,2,32,128]{3,2,1,0:T(8,128)(2,1)S(1)}, u32[]{:S(2)}, u32[]{:S(2)}) %collective-permute-start.7) | collective-permute-done | bytes 131104 | tf_op jit(solution)/shard_map/ppermute | solution.py:83
  72.5 1.3 %collective-permute-start.27 = (bf16[4,2,128,128]{3,2,1,0:T(8,128)(2,1)S(1)}, bf16[4,2,128,128]{3,2,1,0:T(8,128)(2,1)S(1)}, u32[]{:S(2)}, u32[]{:S(2)}) collective-permute-start(bf16[4,2,128,128]{3,2,1,0:T(8,128)(2,1)S(1)} %get-tuple-element.47.rest_0_), channel_id=1, source_target_pairs={{8,0},{24,16},{9,1},{25,17},{10,2},{26,18},{11,3},{27,19},{12,4},{... | collective-permute-start | bytes 786440 | tf_op jit(solution)/shard_map/ppermute | solution.py:420
  73.8 1.7 %focus.2 = (bf16[4,2,128,128]{3,2,1,0:T(8,128)(2,1)S(1)}, bf16[4,2,128,128]{3,2,1,0:T(8,128)(2,1)S(1)}) custom-call(s32[2]{0:T(128)S(1)} %pad_add_fusion.me_ref.place_ref, s32[8]{0:T(128)S(1)} %get-tuple-element.64.entry_ref, s32[8]{0:T(128)S(1)} %get-tuple-element.65.row_ref, s32[8]{0:T(128)S(1)} %get-tuple-element.60.valid_ref, ...), custom_call_target="tpu_custom_call" | custom-call | tf_op jit(solution)/shard_map/focus/pallas_call | solution.py:236
  75.6 1.6 %collective-permute-start.13 = (bf16[4,2,128,128]{3,2,1,0:T(8,128)(2,1)S(1)}, bf16[4,2,128,128]{3,2,1,0:T(8,128)(2,1)S(1)}, u32[]{:S(2)}, u32[]{:S(2)}) collective-permute-start(bf16[4,2,128,128]{3,2,1,0:T(8,128)(2,1)S(1)} %get-tuple-element.37.rest_0_), channel_id=1, source_target_pairs={{0,16},{8,24},{16,0},{24,8},{1,17},{9,25},{17,1},{25,9},{2,18},{10... | collective-permute-start | bytes 786440 | tf_op jit(solution)/shard_map/ppermute | solution.py:83
  77.7 4.6 %collective-permute-start.31 = (bf16[4,2,128,128]{3,2,1,0:T(8,128)(2,1)S(1)}, bf16[4,2,128,128]{3,2,1,0:T(8,128)(2,1)S(1)}, u32[]{:S(2)}, u32[]{:S(2)}) collective-permute-start(bf16[4,2,128,128]{3,2,1,0:T(8,128)(2,1)S(1)} %collective-permute-done.29.rest_1_), channel_id=1, source_target_pairs={{0,8},{16,24},{1,9},{17,25},{2,10},{18,26},{3,11},{19,27},{4,12},{... | collective-permute-start | bytes 786440 | tf_op jit(solution)/shard_map/ppermute | solution.py:421
  82.5 1.3 %collective-permute-start.14 = (bf16[4,2,128,128]{3,2,1,0:T(8,128)(2,1)S(1)}, bf16[4,2,128,128]{3,2,1,0:T(8,128)(2,1)S(1)}, u32[]{:S(2)}, u32[]{:S(2)}) collective-permute-start(bf16[4,2,128,128]{3,2,1,0:T(8,128)(2,1)S(1)} %get-tuple-element.37.rest_0_), channel_id=1, source_target_pairs={{8,0},{24,16},{9,1},{25,17},{10,2},{26,18},{11,3},{27,19},{12,4},{... | collective-permute-start | bytes 786440 | tf_op jit(solution)/shard_map/ppermute | solution.py:420
  83.9 1.3 %collective-permute-start.11 = (bf16[4,2,128,128]{3,2,1,0:T(8,128)(2,1)S(1)}, bf16[4,2,128,128]{3,2,1,0:T(8,128)(2,1)S(1)}, u32[]{:S(2)}, u32[]{:S(2)}) collective-permute-start(bf16[4,2,128,128]{3,2,1,0:T(8,128)(2,1)S(1)} %get-tuple-element.36.rest_0_), channel_id=1, source_target_pairs={{8,0},{24,16},{9,1},{25,17},{10,2},{26,18},{11,3},{27,19},{12,4},{... | collective-permute-start | bytes 786440 | tf_op jit(solution)/shard_map/ppermute | solution.py:420
  85.2 1.7 %collective-permute-done.13.rest_1_ = bf16[4,2,128,128]{3,2,1,0:T(8,128)(2,1)S(1)} collective-permute-done((bf16[4,2,128,128]{3,2,1,0:T(8,128)(2,1)S(1)}, bf16[4,2,128,128]{3,2,1,0:T(8,128)(2,1)S(1)}, u32[]{:S(2)}, u32[]{:S(2)}) %collective-permute-start.13) | collective-permute-done | bytes 262176 | tf_op jit(solution)/shard_map/ppermute | solution.py:83
  86.9 2.9 %collective-permute-start.28 = (bf16[4,2,128,128]{3,2,1,0:T(8,128)(2,1)S(1)}, bf16[4,2,128,128]{3,2,1,0:T(8,128)(2,1)S(1)}, u32[]{:S(2)}, u32[]{:S(2)}) collective-permute-start(bf16[4,2,128,128]{3,2,1,0:T(8,128)(2,1)S(1)} %collective-permute-done.26.rest_1_), channel_id=1, source_target_pairs={{0,8},{16,24},{1,9},{17,25},{2,10},{18,26},{3,11},{19,27},{4,12},{... | collective-permute-start | bytes 786440 | tf_op jit(solution)/shard_map/ppermute | solution.py:421
  89.8 1.3 %collective-permute-start.15 = (bf16[4,2,128,128]{3,2,1,0:T(8,128)(2,1)S(1)}, bf16[4,2,128,128]{3,2,1,0:T(8,128)(2,1)S(1)}, u32[]{:S(2)}, u32[]{:S(2)}) collective-permute-start(bf16[4,2,128,128]{3,2,1,0:T(8,128)(2,1)S(1)} %collective-permute-done.13.rest_1_), channel_id=1, source_target_pairs={{0,8},{16,24},{1,9},{17,25},{2,10},{18,26},{3,11},{19,27},{4,12},{... | collective-permute-start | bytes 786440 | tf_op jit(solution)/shard_map/ppermute | solution.py:421
  91.1 1.5 %collective-permute-start.12 = (bf16[4,2,128,128]{3,2,1,0:T(8,128)(2,1)S(1)}, bf16[4,2,128,128]{3,2,1,0:T(8,128)(2,1)S(1)}, u32[]{:S(2)}, u32[]{:S(2)}) collective-permute-start(bf16[4,2,128,128]{3,2,1,0:T(8,128)(2,1)S(1)} %collective-permute-done.10.rest_1_), channel_id=1, source_target_pairs={{0,8},{16,24},{1,9},{17,25},{2,10},{18,26},{3,11},{19,27},{4,12},{... | collective-permute-start | bytes 786440 | tf_op jit(solution)/shard_map/ppermute | solution.py:421
  92.7 3.8 %goldstein.4.rest_8_ = bf16[16,2,2,128,128]{4,3,2,1,0:T(8,128)(2,1)} custom-call(s32[4]{0:T(128)S(1)} %get-tuple-element.55.slot_ref, bf16[4,2,128,128]{3,2,1,0:T(8,128)(2,1)S(1)} %get-tuple-element.48.rest_0_, bf16[4,2,128,128]{3,2,1,0:T(8,128)(2,1)S(1)} %collective-permute-done.29.rest_1_, bf16[4,2,128,128]{3,2,1,0:T(8,128)(2,1)S(1)} %collective-permute-done.30.rest_2_, ...), custom_call_target="tpu_custom_call" | custom-call | tf_op jit(solution)/shard_map/goldstein/pallas_call | solution.py:322
  96.5 3.8 %goldstein.5.rest_8_ = bf16[16,2,2,128,128]{4,3,2,1,0:T(8,128)(2,1)} custom-call(s32[4]{0:T(128)S(1)} %get-tuple-element.56.slot_ref, bf16[4,2,128,128]{3,2,1,0:T(8,128)(2,1)S(1)} %get-tuple-element.47.rest_0_, bf16[4,2,128,128]{3,2,1,0:T(8,128)(2,1)S(1)} %collective-permute-done.26.rest_1_, ...), custom_call_target="tpu_custom_call", output_to_operand_aliasing={{}: (9, {})} | custom-call | tf_op jit(solution)/shard_map/goldstein/pallas_call | solution.py:322
  100.4 3.8 %goldstein.6.rest_8_ = bf16[16,2,2,128,128]{4,3,2,1,0:T(8,128)(2,1)} custom-call(s32[4]{0:T(128)S(1)} %get-tuple-element.57.slot_ref, bf16[4,2,128,128]{3,2,1,0:T(8,128)(2,1)S(1)} %get-tuple-element.37.rest_0_, bf16[4,2,128,128]{3,2,1,0:T(8,128)(2,1)S(1)} %collective-permute-done.13.rest_1_, ...), custom_call_target="tpu_custom_call", output_to_operand_aliasing={{}: (9, {})} | custom-call | tf_op jit(solution)/shard_map/goldstein/pallas_call | solution.py:322
  104.3 3.8 %goldstein.7 = bf16[16,2,2,128,128]{4,3,2,1,0:T(8,128)(2,1)} custom-call(s32[4]{0:T(128)S(1)} %get-tuple-element.58.slot_ref, bf16[4,2,128,128]{3,2,1,0:T(8,128)(2,1)S(1)} %get-tuple-element.36.rest_0_, bf16[4,2,128,128]{3,2,1,0:T(8,128)(2,1)S(1)} %collective-permute-done.10.rest_1_, ...), custom_call_target="tpu_custom_call", output_to_operand_aliasing={{}: (9, {})} | custom-call | tf_op jit(solution)/shard_map/goldstein/pallas_call | solution.py:322
  (74 shorter events, 4.1 us)
Async XLA Ops:
  0.0 49.8 %copy-start.3 = (bf16[8,256,256]{2,1,0:T(8,128)(2,1)S(1)}, bf16[8,256,256]{2,1,0:T(8,128)(2,1)}, u32[]{:S(2)}) copy-start(bf16[8,256,256]{2,1,0:T(8,128)(2,1)} %constant.108.back_ref) | copy-start | bytes 3145732
  1.9 1.1 copy-start.5
  2.9 0.9 copy-start.6
  3.8 0.8 copy-start.7
  4.7 0.8 copy-start.8
  5.5 0.8 copy-start.9
  6.3 67.5 %copy-start.1 = (bf16[256,256]{1,0:T(8,128)(2,1)S(1)}, bf16[256,256]{1,0:T(8,128)(2,1)}, u32[]{:S(2)}) copy-start(bf16[256,256]{1,0:T(8,128)(2,1)} %constant.107.forward_ref.rest_4_.rest_7_) | copy-start | bytes 393220
  11.0 15.8 %collective-permute-start.16 = (bf16[8,2,16,128]{3,2,1,0:T(8,128)(2,1)S(1)}, bf16[8,2,16,128]{3,2,1,0:T(8,128)(2,1)S(1)}, u32[]{:S(2)}, u32[]{:S(2)}) collective-permute-start(bf16[8,2,16,128]{3,2,1,0:T(8,128)(2,1)S(1)} %get-tuple-element.39), channel_id=1, source_target_pairs={{0,1},{1,0},{2,3},{3,2},{4,5},{5,4},{6,7},{7,6},{8,9},{9,8},{10,11... | collective-permute-start | bytes 196616 | tf_op jit(solution)/shard_map/ppermute | solution.py:83
  11.5 19.1 %collective-permute-start.17 = (bf16[8,2,16,128]{3,2,1,0:T(8,128)(2,1)S(1)}, bf16[8,2,16,128]{3,2,1,0:T(8,128)(2,1)S(1)}, u32[]{:S(2)}, u32[]{:S(2)}) collective-permute-start(bf16[8,2,16,128]{3,2,1,0:T(8,128)(2,1)S(1)} %get-tuple-element.40), channel_id=1, source_target_pairs={{0,2},{1,3},{2,0},{3,1},{4,6},{5,7},{6,4},{7,5},{8,10},{9,11},{10,... | collective-permute-start | bytes 196616 | tf_op jit(solution)/shard_map/ppermute | solution.py:83
  14.2 21.3 %collective-permute-start.18 = (bf16[8,2,16,128]{3,2,1,0:T(8,128)(2,1)S(1)}, bf16[8,2,16,128]{3,2,1,0:T(8,128)(2,1)S(1)}, u32[]{:S(2)}, u32[]{:S(2)}) collective-permute-start(bf16[8,2,16,128]{3,2,1,0:T(8,128)(2,1)S(1)} %get-tuple-element.41), channel_id=1, source_target_pairs={{0,3},{1,2},{2,1},{3,0},{4,7},{5,6},{6,5},{7,4},{8,11},{9,10},{10,... | collective-permute-start | bytes 196616 | tf_op jit(solution)/shard_map/ppermute | solution.py:83
  14.2 22.8 %collective-permute-start.19 = (bf16[8,2,16,128]{3,2,1,0:T(8,128)(2,1)S(1)}, bf16[8,2,16,128]{3,2,1,0:T(8,128)(2,1)S(1)}, u32[]{:S(2)}, u32[]{:S(2)}) collective-permute-start(bf16[8,2,16,128]{3,2,1,0:T(8,128)(2,1)S(1)} %get-tuple-element.42), channel_id=1, source_target_pairs={{0,4},{1,5},{2,6},{3,7},{4,0},{5,1},{6,2},{7,3},{8,12},{9,13},{10,... | collective-permute-start | bytes 196616 | tf_op jit(solution)/shard_map/ppermute | solution.py:83
  17.0 21.6 %collective-permute-start.20 = (bf16[8,2,16,128]{3,2,1,0:T(8,128)(2,1)S(1)}, bf16[8,2,16,128]{3,2,1,0:T(8,128)(2,1)S(1)}, u32[]{:S(2)}, u32[]{:S(2)}) collective-permute-start(bf16[8,2,16,128]{3,2,1,0:T(8,128)(2,1)S(1)} %get-tuple-element.43), channel_id=1, source_target_pairs={{0,5},{1,4},{2,7},{3,6},{4,1},{5,0},{6,3},{7,2},{8,13},{9,12},{10,... | collective-permute-start | bytes 196616 | tf_op jit(solution)/shard_map/ppermute | solution.py:83
  17.2 1.1 copy-start.4
  19.6 11.7 %all-to-all-start.1 = ((bf16[8,1,2,32,128]{4,3,2,1,0:T(8,128)(2,1)}), bf16[8,1,2,32,128]{4,3,2,1,0:T(8,128)(2,1)S(1)}, u32[]{:S(2)}, u32[]{:S(2)}) async-start(bf16[8,1,2,32,128]{4,3,2,1,0:T(8,128)(2,1)} %get-tuple-element.46), calls=%async_computation.1 | async-start | bytes 262144 | tf_op jit(solution)/shard_map/all_to_all | solution.py:400
  26.8 11.8 %collective-permute-start.21 = (bf16[8,2,16,128]{3,2,1,0:T(8,128)(2,1)S(1)}, bf16[8,2,16,128]{3,2,1,0:T(8,128)(2,1)S(1)}, u32[]{:S(2)}, u32[]{:S(2)}) collective-permute-start(bf16[8,2,16,128]{3,2,1,0:T(8,128)(2,1)S(1)} %get-tuple-element.44), channel_id=1, source_target_pairs={{0,6},{1,7},{2,4},{3,5},{4,2},{5,3},{6,0},{7,1},{8,14},{9,15},{10,... | collective-permute-start | bytes 196616 | tf_op jit(solution)/shard_map/ppermute | solution.py:83
  30.7 10.0 %collective-permute-start.22 = (bf16[8,2,16,128]{3,2,1,0:T(8,128)(2,1)S(1)}, bf16[8,2,16,128]{3,2,1,0:T(8,128)(2,1)S(1)}, u32[]{:S(2)}, u32[]{:S(2)}) collective-permute-start(bf16[8,2,16,128]{3,2,1,0:T(8,128)(2,1)S(1)} %get-tuple-element.45), channel_id=1, source_target_pairs={{0,7},{1,6},{2,5},{3,4},{4,3},{5,2},{6,1},{7,0},{8,15},{9,14},{10,... | collective-permute-start | bytes 196616 | tf_op jit(solution)/shard_map/ppermute | solution.py:83
  31.3 28.6 %all-to-all-start = ((bf16[8,1,2,32,128]{4,3,2,1,0:T(8,128)(2,1)}), bf16[8,1,2,32,128]{4,3,2,1,0:T(8,128)(2,1)S(1)}, u32[]{:S(2)}, u32[]{:S(2)}) async-start(bf16[8,1,2,32,128]{4,3,2,1,0:T(8,128)(2,1)} %get-tuple-element.35), calls=%async_computation | async-start | bytes 262144 | tf_op jit(solution)/shard_map/all_to_all | solution.py:400
  35.5 5.9 %collective-permute-start.23 = (bf16[8,2,32,128]{3,2,1,0:T(8,128)(2,1)S(1)}, bf16[8,2,32,128]{3,2,1,0:T(8,128)(2,1)S(1)}, u32[]{:S(2)}, u32[]{:S(2)}) collective-permute-start(bf16[8,2,32,128]{3,2,1,0:T(8,128)(2,1)S(1)} %bitcast.29), channel_id=1, source_target_pairs={{0,8},{8,0},{16,24},{24,16},{1,9},{9,1},{17,25},{25,17},{2,10},{10... | collective-permute-start | bytes 393224 | tf_op jit(solution)/shard_map/ppermute | solution.py:83
  37.0 6.9 %collective-permute-start.24 = (bf16[8,2,32,128]{3,2,1,0:T(8,128)(2,1)S(1)}, bf16[8,2,32,128]{3,2,1,0:T(8,128)(2,1)S(1)}, u32[]{:S(2)}, u32[]{:S(2)}) collective-permute-start(bf16[8,2,32,128]{3,2,1,0:T(8,128)(2,1)S(1)} %bitcast.30), channel_id=1, source_target_pairs={{0,16},{8,24},{16,0},{24,8},{1,17},{9,25},{17,1},{25,9},{2,18},{10... | collective-permute-start | bytes 393224 | tf_op jit(solution)/shard_map/ppermute | solution.py:83
  38.6 13.9 %collective-permute-start = (bf16[8,2,16,128]{3,2,1,0:T(8,128)(2,1)S(1)}, bf16[8,2,16,128]{3,2,1,0:T(8,128)(2,1)S(1)}, u32[]{:S(2)}, u32[]{:S(2)}) collective-permute-start(bf16[8,2,16,128]{3,2,1,0:T(8,128)(2,1)S(1)} %get-tuple-element.28), channel_id=1, source_target_pairs={{0,1},{1,0},{2,3},{3,2},{4,5},{5,4},{6,7},{7,6},{8,9},{9,8},{10,11... | collective-permute-start | bytes 196616 | tf_op jit(solution)/shard_map/ppermute | solution.py:83
  38.7 16.0 %collective-permute-start.1 = (bf16[8,2,16,128]{3,2,1,0:T(8,128)(2,1)S(1)}, bf16[8,2,16,128]{3,2,1,0:T(8,128)(2,1)S(1)}, u32[]{:S(2)}, u32[]{:S(2)}) collective-permute-start(bf16[8,2,16,128]{3,2,1,0:T(8,128)(2,1)S(1)} %get-tuple-element.29), channel_id=1, source_target_pairs={{0,2},{1,3},{2,0},{3,1},{4,6},{5,7},{6,4},{7,5},{8,10},{9,11},{10,... | collective-permute-start | bytes 196616 | tf_op jit(solution)/shard_map/ppermute | solution.py:83
  40.7 16.3 %collective-permute-start.2 = (bf16[8,2,16,128]{3,2,1,0:T(8,128)(2,1)S(1)}, bf16[8,2,16,128]{3,2,1,0:T(8,128)(2,1)S(1)}, u32[]{:S(2)}, u32[]{:S(2)}) collective-permute-start(bf16[8,2,16,128]{3,2,1,0:T(8,128)(2,1)S(1)} %get-tuple-element.30), channel_id=1, source_target_pairs={{0,3},{1,2},{2,1},{3,0},{4,7},{5,6},{6,5},{7,4},{8,11},{9,10},{10,... | collective-permute-start | bytes 196616 | tf_op jit(solution)/shard_map/ppermute | solution.py:83
  41.4 17.1 %collective-permute-start.3 = (bf16[8,2,16,128]{3,2,1,0:T(8,128)(2,1)S(1)}, bf16[8,2,16,128]{3,2,1,0:T(8,128)(2,1)S(1)}, u32[]{:S(2)}, u32[]{:S(2)}) collective-permute-start(bf16[8,2,16,128]{3,2,1,0:T(8,128)(2,1)S(1)} %get-tuple-element.31), channel_id=1, source_target_pairs={{0,4},{1,5},{2,6},{3,7},{4,0},{5,1},{6,2},{7,3},{8,12},{9,13},{10,... | collective-permute-start | bytes 196616 | tf_op jit(solution)/shard_map/ppermute | solution.py:83
  44.0 5.9 %collective-permute-start.25 = (bf16[8,2,32,128]{3,2,1,0:T(8,128)(2,1)S(1)}, bf16[8,2,32,128]{3,2,1,0:T(8,128)(2,1)S(1)}, u32[]{:S(2)}, u32[]{:S(2)}) collective-permute-start(bf16[8,2,32,128]{3,2,1,0:T(8,128)(2,1)S(1)} %bitcast.31), channel_id=1, source_target_pairs={{0,24},{8,16},{16,8},{24,0},{1,25},{9,17},{17,9},{25,1},{2,26},{10... | collective-permute-start | bytes 393224 | tf_op jit(solution)/shard_map/ppermute | solution.py:83
  49.8 10.1 %collective-permute-start.4 = (bf16[8,2,16,128]{3,2,1,0:T(8,128)(2,1)S(1)}, bf16[8,2,16,128]{3,2,1,0:T(8,128)(2,1)S(1)}, u32[]{:S(2)}, u32[]{:S(2)}) collective-permute-start(bf16[8,2,16,128]{3,2,1,0:T(8,128)(2,1)S(1)} %get-tuple-element.32), channel_id=1, source_target_pairs={{0,5},{1,4},{2,7},{3,6},{4,1},{5,0},{6,3},{7,2},{8,13},{9,12},{10,... | collective-permute-start | bytes 196616 | tf_op jit(solution)/shard_map/ppermute | solution.py:83
  49.8 0.9 copy-start
  50.7 41.9 %copy-start.2 = (bf16[256,256]{1,0:T(8,128)(2,1)S(1)}, bf16[256,256]{1,0:T(8,128)(2,1)}, u32[]{:S(2)}) copy-start(bf16[256,256]{1,0:T(8,128)(2,1)} %constant.111.rest_5_.rest_6_) | copy-start | bytes 393220
  52.5 10.2 %collective-permute-start.5 = (bf16[8,2,16,128]{3,2,1,0:T(8,128)(2,1)S(1)}, bf16[8,2,16,128]{3,2,1,0:T(8,128)(2,1)S(1)}, u32[]{:S(2)}, u32[]{:S(2)}) collective-permute-start(bf16[8,2,16,128]{3,2,1,0:T(8,128)(2,1)S(1)} %get-tuple-element.33), channel_id=1, source_target_pairs={{0,6},{1,7},{2,4},{3,5},{4,2},{5,3},{6,0},{7,1},{8,14},{9,15},{10,... | collective-permute-start | bytes 196616 | tf_op jit(solution)/shard_map/ppermute | solution.py:83
  54.6 8.5 %collective-permute-start.6 = (bf16[8,2,16,128]{3,2,1,0:T(8,128)(2,1)S(1)}, bf16[8,2,16,128]{3,2,1,0:T(8,128)(2,1)S(1)}, u32[]{:S(2)}, u32[]{:S(2)}) collective-permute-start(bf16[8,2,16,128]{3,2,1,0:T(8,128)(2,1)S(1)} %get-tuple-element.34), channel_id=1, source_target_pairs={{0,7},{1,6},{2,5},{3,4},{4,3},{5,2},{6,1},{7,0},{8,15},{9,14},{10,... | collective-permute-start | bytes 196616 | tf_op jit(solution)/shard_map/ppermute | solution.py:83
  57.0 20.1 %collective-permute-start.29 = (bf16[4,2,128,128]{3,2,1,0:T(8,128)(2,1)S(1)}, bf16[4,2,128,128]{3,2,1,0:T(8,128)(2,1)S(1)}, u32[]{:S(2)}, u32[]{:S(2)}) collective-permute-start(bf16[4,2,128,128]{3,2,1,0:T(8,128)(2,1)S(1)} %get-tuple-element.48.rest_0_), channel_id=1, source_target_pairs={{0,16},{8,24},{16,0},{24,8},{1,17},{9,25},{17,1},{25,9},{2,18},{10... | collective-permute-start | bytes 786440 | tf_op jit(solution)/shard_map/ppermute | solution.py:83
  58.5 19.1 %collective-permute-start.30 = (bf16[4,2,128,128]{3,2,1,0:T(8,128)(2,1)S(1)}, bf16[4,2,128,128]{3,2,1,0:T(8,128)(2,1)S(1)}, u32[]{:S(2)}, u32[]{:S(2)}) collective-permute-start(bf16[4,2,128,128]{3,2,1,0:T(8,128)(2,1)S(1)} %get-tuple-element.48.rest_0_), channel_id=1, source_target_pairs={{8,0},{24,16},{9,1},{25,17},{10,2},{26,18},{11,3},{27,19},{12,4},{... | collective-permute-start | bytes 786440 | tf_op jit(solution)/shard_map/ppermute | solution.py:420
  59.9 12.1 %collective-permute-start.7 = (bf16[8,2,32,128]{3,2,1,0:T(8,128)(2,1)S(1)}, bf16[8,2,32,128]{3,2,1,0:T(8,128)(2,1)S(1)}, u32[]{:S(2)}, u32[]{:S(2)}) collective-permute-start(bf16[8,2,32,128]{3,2,1,0:T(8,128)(2,1)S(1)} %bitcast.25), channel_id=1, source_target_pairs={{0,8},{8,0},{16,24},{24,16},{1,9},{9,1},{17,25},{25,17},{2,10},{10... | collective-permute-start | bytes 393224 | tf_op jit(solution)/shard_map/ppermute | solution.py:83
  62.7 9.9 %collective-permute-start.8 = (bf16[8,2,32,128]{3,2,1,0:T(8,128)(2,1)S(1)}, bf16[8,2,32,128]{3,2,1,0:T(8,128)(2,1)S(1)}, u32[]{:S(2)}, u32[]{:S(2)}) collective-permute-start(bf16[8,2,32,128]{3,2,1,0:T(8,128)(2,1)S(1)} %bitcast.26), channel_id=1, source_target_pairs={{0,16},{8,24},{16,0},{24,8},{1,17},{9,25},{17,1},{25,9},{2,18},{10... | collective-permute-start | bytes 393224 | tf_op jit(solution)/shard_map/ppermute | solution.py:83
  63.2 10.6 %collective-permute-start.9 = (bf16[8,2,32,128]{3,2,1,0:T(8,128)(2,1)S(1)}, bf16[8,2,32,128]{3,2,1,0:T(8,128)(2,1)S(1)}, u32[]{:S(2)}, u32[]{:S(2)}) collective-permute-start(bf16[8,2,32,128]{3,2,1,0:T(8,128)(2,1)S(1)} %bitcast.27), channel_id=1, source_target_pairs={{0,24},{8,16},{16,8},{24,0},{1,25},{9,17},{17,9},{25,1},{2,26},{10... | collective-permute-start | bytes 393224 | tf_op jit(solution)/shard_map/ppermute | solution.py:83
  72.0 10.5 %collective-permute-start.26 = (bf16[4,2,128,128]{3,2,1,0:T(8,128)(2,1)S(1)}, bf16[4,2,128,128]{3,2,1,0:T(8,128)(2,1)S(1)}, u32[]{:S(2)}, u32[]{:S(2)}) collective-permute-start(bf16[4,2,128,128]{3,2,1,0:T(8,128)(2,1)S(1)} %get-tuple-element.47.rest_0_), channel_id=1, source_target_pairs={{0,16},{8,24},{16,0},{24,8},{1,17},{9,25},{17,1},{25,9},{2,18},{10... | collective-permute-start | bytes 786440 | tf_op jit(solution)/shard_map/ppermute | solution.py:83
  72.5 11.3 %collective-permute-start.27 = (bf16[4,2,128,128]{3,2,1,0:T(8,128)(2,1)S(1)}, bf16[4,2,128,128]{3,2,1,0:T(8,128)(2,1)S(1)}, u32[]{:S(2)}, u32[]{:S(2)}) collective-permute-start(bf16[4,2,128,128]{3,2,1,0:T(8,128)(2,1)S(1)} %get-tuple-element.47.rest_0_), channel_id=1, source_target_pairs={{8,0},{24,16},{9,1},{25,17},{10,2},{26,18},{11,3},{27,19},{12,4},{... | collective-permute-start | bytes 786440 | tf_op jit(solution)/shard_map/ppermute | solution.py:420
  75.6 11.3 %collective-permute-start.13 = (bf16[4,2,128,128]{3,2,1,0:T(8,128)(2,1)S(1)}, bf16[4,2,128,128]{3,2,1,0:T(8,128)(2,1)S(1)}, u32[]{:S(2)}, u32[]{:S(2)}) collective-permute-start(bf16[4,2,128,128]{3,2,1,0:T(8,128)(2,1)S(1)} %get-tuple-element.37.rest_0_), channel_id=1, source_target_pairs={{0,16},{8,24},{16,0},{24,8},{1,17},{9,25},{17,1},{25,9},{2,18},{10... | collective-permute-start | bytes 786440 | tf_op jit(solution)/shard_map/ppermute | solution.py:83
  77.1 12.6 %collective-permute-start.10 = (bf16[4,2,128,128]{3,2,1,0:T(8,128)(2,1)S(1)}, bf16[4,2,128,128]{3,2,1,0:T(8,128)(2,1)S(1)}, u32[]{:S(2)}, u32[]{:S(2)}) collective-permute-start(bf16[4,2,128,128]{3,2,1,0:T(8,128)(2,1)S(1)} %get-tuple-element.36.rest_0_), channel_id=1, source_target_pairs={{0,16},{8,24},{16,0},{24,8},{1,17},{9,25},{17,1},{25,9},{2,18},{10... | collective-permute-start | bytes 786440 | tf_op jit(solution)/shard_map/ppermute | solution.py:83
  77.7 13.4 %collective-permute-start.31 = (bf16[4,2,128,128]{3,2,1,0:T(8,128)(2,1)S(1)}, bf16[4,2,128,128]{3,2,1,0:T(8,128)(2,1)S(1)}, u32[]{:S(2)}, u32[]{:S(2)}) collective-permute-start(bf16[4,2,128,128]{3,2,1,0:T(8,128)(2,1)S(1)} %collective-permute-done.29.rest_1_), channel_id=1, source_target_pairs={{0,8},{16,24},{1,9},{17,25},{2,10},{18,26},{3,11},{19,27},{4,12},{... | collective-permute-start | bytes 786440 | tf_op jit(solution)/shard_map/ppermute | solution.py:421
  82.5 17.8 %collective-permute-start.14 = (bf16[4,2,128,128]{3,2,1,0:T(8,128)(2,1)S(1)}, bf16[4,2,128,128]{3,2,1,0:T(8,128)(2,1)S(1)}, u32[]{:S(2)}, u32[]{:S(2)}) collective-permute-start(bf16[4,2,128,128]{3,2,1,0:T(8,128)(2,1)S(1)} %get-tuple-element.37.rest_0_), channel_id=1, source_target_pairs={{8,0},{24,16},{9,1},{25,17},{10,2},{26,18},{11,3},{27,19},{12,4},{... | collective-permute-start | bytes 786440 | tf_op jit(solution)/shard_map/ppermute | solution.py:420
  83.9 20.4 %collective-permute-start.11 = (bf16[4,2,128,128]{3,2,1,0:T(8,128)(2,1)S(1)}, bf16[4,2,128,128]{3,2,1,0:T(8,128)(2,1)S(1)}, u32[]{:S(2)}, u32[]{:S(2)}) collective-permute-start(bf16[4,2,128,128]{3,2,1,0:T(8,128)(2,1)S(1)} %get-tuple-element.36.rest_0_), channel_id=1, source_target_pairs={{8,0},{24,16},{9,1},{25,17},{10,2},{26,18},{11,3},{27,19},{12,4},{... | collective-permute-start | bytes 786440 | tf_op jit(solution)/shard_map/ppermute | solution.py:420
  86.9 9.6 %collective-permute-start.28 = (bf16[4,2,128,128]{3,2,1,0:T(8,128)(2,1)S(1)}, bf16[4,2,128,128]{3,2,1,0:T(8,128)(2,1)S(1)}, u32[]{:S(2)}, u32[]{:S(2)}) collective-permute-start(bf16[4,2,128,128]{3,2,1,0:T(8,128)(2,1)S(1)} %collective-permute-done.26.rest_1_), channel_id=1, source_target_pairs={{0,8},{16,24},{1,9},{17,25},{2,10},{18,26},{3,11},{19,27},{4,12},{... | collective-permute-start | bytes 786440 | tf_op jit(solution)/shard_map/ppermute | solution.py:421
  89.8 10.6 %collective-permute-start.15 = (bf16[4,2,128,128]{3,2,1,0:T(8,128)(2,1)S(1)}, bf16[4,2,128,128]{3,2,1,0:T(8,128)(2,1)S(1)}, u32[]{:S(2)}, u32[]{:S(2)}) collective-permute-start(bf16[4,2,128,128]{3,2,1,0:T(8,128)(2,1)S(1)} %collective-permute-done.13.rest_1_), channel_id=1, source_target_pairs={{0,8},{16,24},{1,9},{17,25},{2,10},{18,26},{3,11},{19,27},{4,12},{... | collective-permute-start | bytes 786440 | tf_op jit(solution)/shard_map/ppermute | solution.py:421
  91.1 13.1 %collective-permute-start.12 = (bf16[4,2,128,128]{3,2,1,0:T(8,128)(2,1)S(1)}, bf16[4,2,128,128]{3,2,1,0:T(8,128)(2,1)S(1)}, u32[]{:S(2)}, u32[]{:S(2)}) collective-permute-start(bf16[4,2,128,128]{3,2,1,0:T(8,128)(2,1)S(1)} %collective-permute-done.10.rest_1_), channel_id=1, source_target_pairs={{0,8},{16,24},{1,9},{17,25},{2,10},{18,26},{3,11},{19,27},{4,12},{... | collective-permute-start | bytes 786440 | tf_op jit(solution)/shard_map/ppermute | solution.py:421

commit v2 on v1

v2 whole, which is shorter than its diff:
```python
import math

import jax
import jax.numpy as jnp
import numpy as np
from jax import lax
from jax.experimental import pallas as pl
from jax.experimental.pallas import tpu as pltpu
from jax.sharding import PartitionSpec as P

BLK = 128
NSUB = 8
BF = jnp.bfloat16
F32 = jnp.float32
MIB = 1024 * 1024
K1_MIB = 56


def dft(rows, cols, size, sign, scale):
    phase = np.outer(np.arange(rows), np.arange(cols)) % size
    angle = 2.0 * np.pi / size * phase
    cosine = np.cos(angle) * scale
    sine = sign * np.sin(angle) * scale
    return np.block([[cosine, -sine], [sine, cosine]])


def kernel_table():
    offset = (np.arange(NSUB) + 0.5) / NSUB
    cells = np.arange(BLK)
    dist = cells[None, None, :] - cells[None, :, None] - offset[:, None, None]
    window = np.where(np.abs(dist) < 4.0, 0.5 + 0.5 * np.cos(np.pi * dist / 4.0), 0.0)
    return np.sinc(dist) * window


def resample_table(pulses):
    inverse = dft(pulses, pulses, pulses, 1, 1.0 / math.sqrt(pulses))
    rows = pulses // BLK
    table = np.zeros((NSUB, rows, 2 * BLK, 2 * pulses))
    kernels = kernel_table()
    for kind in range(NSUB):
        for row in range(rows):
            for part in range(2):
                start = part * pulses + row * BLK
                table[kind, row, part * BLK : (part + 1) * BLK] = (
                    kernels[kind] @ inverse[start : start + BLK]
                )
    return table.reshape(NSUB * rows, 2 * BLK, 2 * pulses)


def const(table):
    return jnp.asarray(table.astype(np.float32)).astype(BF)


def mm(left, right):
    return jnp.dot(left, right, preferred_element_type=F32)


def whole(count):
    return [pl.BlockSpec(memory_space=pltpu.VMEM)] * count


def loaded(arrays):
    def spec(shape):
        return pl.BlockSpec(shape, lambda *_: (0,) * len(shape))

    return [spec(a.shape) for a in arrays]


def params(mib):
    return pltpu.CompilerParams(vmem_limit_bytes=mib * MIB)


def cost(macs, arrays):
    size = sum(math.prod(a.shape) * a.dtype.itemsize for a in arrays)
    return pl.CostEstimate(flops=2 * macs, bytes_accessed=size, transcendentals=0)


def is_pow2(count):
    return count & (count - 1) == 0


def target_of(index, step, count):
    if is_pow2(count):
        return index ^ step
    return (index + step) % count


def source_of(index, step, count):
    if is_pow2(count):
        return index ^ step
    return (index + count - step) % count


def step_from(index, source, count):
    if is_pow2(count):
        return index ^ source
    return (index + count - source) % count


def hop(value, axis, step, within=None):
    count = lax.axis_size(axis)
    if within is None and axis == "shard" and count % 2 == 0:
        pairs = [(i, target_of(i // 2, step // 2, count // 2) * 2 + i % 2) for i in range(count)]
    else:
        size = within or count
        pairs = [(i, i // size * size + target_of(i % size, step, size)) for i in range(count)]
    return lax.ppermute(value, axis, pairs)


def shift(value, axis, steps):
    count = lax.axis_size(axis)
    return lax.ppermute(value, axis, [(i, (i + steps) % count) for i in range(count)])


def position(rank, sender, slot, shards, most, capacity):
    if shards * most == capacity:
        return rank * shards + sender
    return slot


def range_compress(echo, reference, owners, slots, place, plan):
    _, pulses, samples = echo.shape
    shards, capacity, most, group, group_columns = plan
    total = owners.shape[0]
    outer = samples // BLK
    first = const(dft(outer, outer, outer, 1, 1.0 / math.sqrt(outer)))
    second = const(dft(outer, BLK, outer, 1, 1.0 / math.sqrt(BLK)))
    phase = np.outer(np.arange(BLK), np.arange(BLK)) % samples
    angle = 2.0 * np.pi / samples * phase
    turn = jnp.asarray(np.stack([np.cos(angle), np.sin(angle)]).astype(np.float32))
    spread = BLK // outer
    operands = [echo, reference, first, second, turn]
    smem = pl.BlockSpec(memory_space=pltpu.SMEM)

    def arrange(owner_ref, slot_ref, place_ref, block_ref, out_slot_ref, count_ref, free_ref):
        for o in range(shards):
            for w in range(capacity):
                block_ref[o, w] = 0
            for g in range(shards):
                count_ref[g, o] = 0
        for b in range(total):
            g = b // group
            owner = owner_ref[b]
            rank = count_ref[g, owner]
            count_ref[g, owner] = rank + 1
            where = position(rank, g, slot_ref[b], shards, most, capacity)
            block_ref[owner, where] = (b + 1) * most + rank
        me = place_ref[0]
        for w in range(capacity):
            free_ref[w] = 0
        for w in range(capacity):
            code = block_ref[me, w] // most
            slot = slot_ref[jnp.maximum(code - 1, 0)]
            out_slot_ref[w] = jnp.where(code > 0, slot, -1)
            free_ref[jnp.where(code > 0, slot, capacity)] = 1
        spare = 0
        for w in range(capacity):
            taken = free_ref[w]
            free_ref[capacity + 1 + spare] = w
            spare = spare + 1 - taken
        spare = 0
        for w in range(capacity):
            slot = out_slot_ref[w]
            out_slot_ref[w] = jnp.where(slot < 0, free_ref[capacity + 1 + spare], slot)
            spare = spare + jnp.where(slot < 0, 1, 0)

    def kernel(owner_ref, slot_ref, place_ref, *refs):
        count = len(operands)
        out_ref, block_ref, out_slot_ref = refs[count : count + 3]
        local = refs[count + 3 : 2 * count + 3]
        x_re, x_im, y_re, y_im, sems, count_ref, free_ref = refs[2 * count + 3 :]
        copies = [
            pltpu.make_async_copy(refs[i], local[i], sems.at[i]) for i in range(count)
        ]
        for copy in copies:
            copy.start()
        arrange(owner_ref, slot_ref, place_ref, block_ref, out_slot_ref, count_ref, free_ref)
        for copy in copies:
            copy.wait()
        echo_ref, ref_ref, first_ref, second_ref, turn_ref = local
        for j in range(outer):
            lanes = slice(j * BLK, (j + 1) * BLK)
            a = echo_ref[0, :, lanes].astype(F32)
            b = echo_ref[1, :, lanes].astype(F32)
            c = ref_ref[0:1, lanes]
            d = ref_ref[1:2, lanes]
            x_re[pl.ds(j, pulses, stride=outer), :] = a * c + b * d
            x_im[pl.ds(j, pulses, stride=outer), :] = b * c - a * d
        turn_c = turn_ref[0]
        turn_s = turn_ref[1]
        for q in range(pulses // 2):
            pair = []
            for p in (2 * q, 2 * q + 1):
                rows = slice(p * outer, (p + 1) * outer)
                pair.append(jnp.concatenate([x_re[rows, :], x_im[rows, :]], axis=0))
            section = mm(first_ref[...], jnp.concatenate(pair, axis=1).astype(BF))
            turned = []
            for p in range(2):
                lanes = slice(p * BLK, (p + 1) * BLK)
                re = jnp.concatenate([section[:outer, lanes]] * spread, axis=0)
                im = jnp.concatenate([section[outer:, lanes]] * spread, axis=0)
                turned.append(
                    jnp.concatenate(
                        [re * turn_c - im * turn_s, re * turn_s + im * turn_c], axis=1
                    )
                )
            turned = jnp.concatenate(turned, axis=0).astype(BF)
            done = lax.dot_general(
                second_ref[...], turned, (((1,), (1,)), ((), ())), preferred_element_type=F32
            )
            for p in range(2):
                lanes = slice(p * BLK, (p + 1) * BLK)
                rows = slice((2 * q + p) * outer, (2 * q + p + 1) * outer)
                y_re[rows, :] = done[:outer, lanes]
                y_im[rows, :] = done[outer:, lanes]
        for j in range(outer):
            rows = pl.ds(j, pulses, stride=outer)
            out_ref[0, j] = y_re[rows, :].astype(BF)
            out_ref[1, j] = y_im[rows, :].astype(BF)

    return pl.pallas_call(
        kernel,
        out_shape=[
            jax.ShapeDtypeStruct((2, outer, pulses, BLK), BF),
            jax.ShapeDtypeStruct((shards, capacity), jnp.int32),
            jax.ShapeDtypeStruct((capacity,), jnp.int32),
        ],
        in_specs=[smem] * 3 + [pl.BlockSpec(memory_space=pl.ANY)] * len(operands),
        out_specs=[pl.BlockSpec(memory_space=pltpu.VMEM)] + [smem] * 2,
        scratch_shapes=[pltpu.VMEM(a.shape, a.dtype) for a in operands]
        + [pltpu.VMEM((pulses * outer, BLK), F32)] * 4
        + [
            pltpu.SemaphoreType.DMA((len(operands),)),
            pltpu.SMEM((shards, shards), jnp.int32),
            pltpu.SMEM((2 * capacity + 2,), jnp.int32),
        ],
        compiler_params=params(K1_MIB),
        cost_estimate=cost(
            pulses * 4 * BLK * outer * (outer + BLK), [echo, echo, echo, reference, turn]
        ),
        name="range_compress",
    )(owners, slots, place, *operands)


def spread_columns(parts, table, place, chunks, plan):
    _, _, pulses, _ = parts[0].shape
    cores = len(parts)
    shards, capacity, most, group, group_columns = plan
    chips = shards // cores
    each = capacity // chunks

    def kernel(table_ref, place_ref, *rest):
        part_refs = rest[:cores]
        outs = rest[cores:]
        chip = place_ref[0] // cores
        core = place_ref[0] % cores
        for chunk in range(chunks):
            for k in range(chips):
                owner = target_of(chip, k, chips) * cores + core
                out = outs[chunk * chips + k]
                for s in range(each):
                    block = jnp.maximum(table_ref[owner, chunk * each + s] // most - 1, 0)
                    column = block // group * group_columns + block % group % group_columns
                    for c in range(cores):
                        at = source_of(core, c, cores) * pulses
                        rows = pl.ds(pl.multiple_of(at, pulses), pulses)
                        out[s, 0, rows, :] = part_refs[c][0, column]
                        out[s, 1, rows, :] = part_refs[c][1, column]

    piece = jax.ShapeDtypeStruct((each, 2, cores * pulses, BLK), BF)
    smem = pl.BlockSpec(memory_space=pltpu.SMEM)
    outs = pl.pallas_call(
        kernel,
        out_shape=[piece] * (chunks * chips),
        in_specs=[smem, smem] + whole(cores),
        out_specs=whole(chunks * chips),
        compiler_params=params(16),
        cost_estimate=cost(0, [*parts] * 2),
        name="spread_columns",
    )(table, place, *parts)
    return [outs[chunk * chips : (chunk + 1) * chips] for chunk in range(chunks)]


def filter_columns(parts, owners, place, plan):
    _, rows, columns = parts[0].shape
    cores = len(parts)
    shards, _, most, group, group_columns = plan
    chips = shards // cores

    def kernel(owner_ref, place_ref, *rest):
        part_refs = rest[:cores]
        outs = rest[cores : cores + chips]
        column_ref, count_ref = rest[cores + chips :]
        chip = place_ref[0] // cores
        core = place_ref[0] % cores
        for c in range(cores):
            for o in range(shards):
                count_ref[c, o] = 0
                for r in range(most):
                    column_ref[c, o * most + r] = 0
            for b in range(group):
                owner = owner_ref[(chip * cores + c) * group + b]
                rank = count_ref[c, owner]
                count_ref[c, owner] = rank + 1
                column_ref[c, owner * most + rank] = b % group_columns
        for k in range(chips):
            owner = target_of(chip, k, chips) * cores + core
            for c in range(cores):
                at = source_of(core, c, cores)
                for e in range(most):
                    column = column_ref[at, owner * most + e]
                    lanes = pl.ds(pl.multiple_of(column * BLK, BLK), BLK)
                    for part in range(2):
                        outs[k][at * most + e, part] = part_refs[c][part, :, lanes]

    piece = jax.ShapeDtypeStruct((cores * most, 2, rows, BLK), BF)
    smem = pl.BlockSpec(memory_space=pltpu.SMEM)
    return pl.pallas_call(
        kernel,
        out_shape=[piece] * chips,
        in_specs=[smem, smem] + whole(cores),
        out_specs=whole(chips),
        scratch_shapes=[
            pltpu.SMEM((cores, shards * most), jnp.int32),
            pltpu.SMEM((cores, shards), jnp.int32),
        ],
        compiler_params=params(16),
        cost_estimate=cost(0, [*parts] * 2),
        name="filter_columns",
    )(owners, place, *parts)


def focus(pieces, filters, place, table, kinds, start, cores, subs, plan):
    each, _, share, _ = pieces[0].shape
    chips = len(pieces)
    dates = len(filters)
    pulses = share * chips
    rows = filters[0].shape[-2]
    forward = const(dft(pulses, pulses, pulses, -1, 1.0 / math.sqrt(pulses)))
    back = const(resample_table(pulses))
    per = each // subs

    _, _, most, group, group_columns = plan

    def kernel(place_ref, table_ref, kind_ref, forward_ref, back_ref, *rest):
        piece_refs = rest[:chips]
        filter_refs = rest[chips : chips + dates]
        outs = rest[chips + dates : chips + dates + subs]
        col, fil = rest[chips + dates + subs :]
        chip = place_ref[0] // cores
        entries, table_rows, valid = [], [], []
        for s in range(each):
            code = table_ref[place_ref[0], start + s]
            block = code // most - 1
            valid.append(block >= 0)
            block = jnp.maximum(block, 0)
            sender = block // group
            step = step_from(chip, sender // cores, chips)
            entries.append((step * cores + sender % cores) * most + code % most)
            table_rows.append(kind_ref[block] * (pulses // BLK) + block % group // group_columns)
        for k in range(chips):
            source = source_of(chip, k, chips)
            at = pl.multiple_of(source * share, share)
            for s in range(each):
                for part in range(2):
                    col[s, part, pl.ds(at, share), :] = piece_refs[k][s, part]
        for e in range(dates):
            at = pl.multiple_of(source_of(place_ref[1], e, dates) * rows, rows)
            for s in range(each):
                for part in range(2):
                    fil[s, part, pl.ds(at, rows), :] = filter_refs[e][entries[s], part]
        for s in range(0, each, 2):
            both = [col[t].reshape(2 * pulses, BLK) for t in (s, s + 1)]
            doppler = mm(forward_ref[...], jnp.concatenate(both, axis=1))
            for t in (0, 1):
                lanes = slice(t * BLK, (t + 1) * BLK)
                re = doppler[:pulses, lanes]
                im = doppler[pulses:, lanes]
                a = fil[s + t, 0].astype(F32)
                b = fil[s + t, 1].astype(F32)
                shaped = jnp.concatenate([re * a - im * b, re * b + im * a], axis=0).astype(BF)
                image = mm(back_ref[table_rows[s + t]], shaped)
                image = jnp.where(valid[s + t], image, 0.0).astype(BF)
                out = outs[(s + t) // per]
                out[(s + t) % per, 0] = image[:BLK]
                out[(s + t) % per, 1] = image[BLK:]

    smem = pl.BlockSpec(memory_space=pltpu.SMEM)
    return pl.pallas_call(
        kernel,
        out_shape=[jax.ShapeDtypeStruct((per, 2, BLK, BLK), BF)] * subs,
        in_specs=[smem] * 3 + whole(2 + chips + dates),
        out_specs=whole(subs),
        scratch_shapes=[
            pltpu.VMEM((each, 2, pulses, BLK), BF),
            pltpu.VMEM((each, 2, pulses, BLK), BF),
        ],
        compiler_params=params(16),
        cost_estimate=cost(
            each * 4 * pulses * (pulses + BLK) * BLK, [*pieces, *filters, forward, back]
        ),
        name="focus",
    )(place, table, kinds, forward, back, *pieces, *filters)


def goldstein(tiles, follows, seconds, slots, start, result):
    sizes = [tile.shape[0] for tile in tiles]
    count = sum(sizes)
    homes = [(i, s) for i, size in enumerate(sizes) for s in range(size)]
    capacity = slots.shape[0]
    scale = 1.0 / math.sqrt(BLK)
    ahead = dft(BLK, BLK, BLK, -1, scale)
    behind = dft(BLK, BLK, BLK, 1, scale)
    tables = [const(ahead), const(ahead.T), const(behind), const(behind.T)]
    have = 0 if result is None else 1
    batch = 4

    def aside(left):
        pairs = left.shape[1] // BLK
        return jnp.concatenate(
            [
                jnp.concatenate(
                    [left[:BLK, p * BLK : (p + 1) * BLK], left[BLK:, p * BLK : (p + 1) * BLK]],
                    axis=1,
                )
                for p in range(pairs)
            ],
            axis=0,
        )

    def around(power):
        power = power + (pltpu.roll(power, 1, 0) + pltpu.roll(power, BLK - 1, 0))
        return power + (pltpu.roll(power, 1, 1) + pltpu.roll(power, BLK - 1, 1))

    def kernel(slot_ref, *rest):
        many = len(tiles)
        tile_refs, follow_refs, second_refs = (rest[i * many : (i + 1) * many] for i in range(3))
        al_ref, ar_ref, bl_ref, br_ref = rest[3 * many : 3 * many + 4]
        out_ref, buffer, sems = rest[3 * many + 4 + have :]
        for base in range(0, count, batch):
            batched = range(base, min(base + batch, count))
            pairs = []
            for s in batched:
                i, at = homes[s]
                t_re = tile_refs[i][at, 0].astype(F32)
                t_im = tile_refs[i][at, 1].astype(F32)
                for o in (follow_refs[i][at], second_refs[i][at]):
                    o_re = o[0].astype(F32)
                    o_im = o[1].astype(F32)
                    re = (t_re * o_re + t_im * o_im).astype(BF)
                    im = (t_im * o_re - t_re * o_im).astype(BF)
                    pairs.append(jnp.concatenate([re, im], axis=0))
            rows = aside(mm(al_ref[...], jnp.concatenate(pairs, axis=1)).astype(BF))
            spectrum = mm(rows, ar_ref[...])
            weighted = []
            for p in range(len(pairs)):
                s_re = spectrum[p * BLK : (p + 1) * BLK, :BLK]
                s_im = spectrum[p * BLK : (p + 1) * BLK, BLK:]
                power = s_re * s_re + s_im * s_im
                level = jnp.sum(jnp.sum(power, axis=0, keepdims=True), axis=1, keepdims=True)
                inverse = 1.0 / (9.0 * (level * (1.0 / (BLK * BLK)) + 1e-06))
                weight = lax.rsqrt(lax.rsqrt(around(power) * inverse))
                weighted.append(
                    jnp.concatenate([(s_re * weight).astype(BF), (s_im * weight).astype(BF)], axis=0)
                )
            back = aside(mm(bl_ref[...], jnp.concatenate(weighted, axis=1)).astype(BF))
            filtered = mm(back, br_ref[...]).astype(BF)
            for p in range(len(pairs)):
                for part in range(2):
                    buffer[base + p // 2, p % 2, part] = filtered[
                        p * BLK : (p + 1) * BLK, part * BLK : (part + 1) * BLK
                    ]
            for s in batched:
                pltpu.make_async_copy(buffer.at[s], out_ref.at[slot_ref[start + s]], sems.at[s]).start()
        for s in range(count):
            pltpu.make_async_copy(buffer.at[s], out_ref.at[slot_ref[start + s]], sems.at[s]).wait()

    anywhere = pl.BlockSpec(memory_space=pl.ANY)
    smem = pl.BlockSpec(memory_space=pltpu.SMEM)
    operands = [slots, *tiles, *follows, *seconds, *tables] + ([result] if have else [])
    return pl.pallas_call(
        kernel,
        out_shape=jax.ShapeDtypeStruct((capacity, 2, 2, BLK, BLK), BF),
        in_specs=[smem] + whole(3 * len(tiles) + 4) + [anywhere] * have,
        out_specs=anywhere,
        scratch_shapes=[
            pltpu.VMEM((count, 2, 2, BLK, BLK), BF),
            pltpu.SemaphoreType.DMA((count,)),
        ],
        input_output_aliases={len(operands) - 1: 0} if have else {},
        compiler_params=params(16),
        cost_estimate=cost(count * 2 * 4 * 4 * BLK**3, operands + [*seconds] * 2),
        name="goldstein",
    )(*operands)


def body(echo_spectra, range_reference, azimuth_reference, block_owner, block_slot, kernel_index):
    shards = lax.axis_size("shard")
    dates = lax.axis_size("date")
    me = lax.axis_index("shard")
    date = lax.axis_index("date")
    place = jnp.stack([me, date]).astype(jnp.int32)
    owners, slots, kinds = block_owner[0], block_slot[0], kernel_index[0]
    cores = 2 if shards % 2 == 0 else 1
    chips = shards // cores
    total = owners.shape[0]
    group = total // shards
    capacity = 2 * group
    most = max(2, capacity // shards)
    group_columns = azimuth_reference.shape[2] // BLK
    plan = (shards, capacity, most, group, group_columns)
    chunks = most if shards * most == capacity else 1
    each = capacity // chunks

    rows = azimuth_reference.shape[1] // dates
    share = lax.dynamic_slice_in_dim(azimuth_reference, date * rows, rows, axis=1)
    shares = [share] + [hop(share, "shard", c, cores) for c in range(1, cores)]
    sent = filter_columns(shares, owners, place, plan)
    echo = echo_spectra[0]
    echo, sent = lax.optimization_barrier((echo, sent))
    got = [sent[0]] + [hop(sent[k], "shard", k * cores) for k in range(1, chips)]
    got = jnp.concatenate(got, axis=0)
    filters = [got] + [hop(got, "date", e) for e in range(1, dates)]
    compressed, blocks, slot_of = range_compress(
        echo, range_reference, owners, slots, place, plan
    )
    parts = [compressed] + [hop(compressed, "shard", c, cores) for c in range(1, cores)]
    outbox = spread_columns(parts, blocks, place, chunks, plan)
    splits = (4, 2)
    tiles, follows, seconds = [], [], []
    for chunk in range(chunks):
        pieces = [outbox[chunk][0]] + [
            hop(outbox[chunk][k], "shard", k * cores) for k in range(1, chips)
        ]
        if chunk > 0 and 1 > 0:
            pieces, kept = lax.optimization_barrier((pieces, follows[0][:1]))
            follows[0][:1] = kept
        subs = splits[chunk] if each % (2 * splits[chunk]) == 0 else 1
        mine = focus(pieces, filters, place, blocks, kinds, chunk * each, cores, subs, plan)
        tiles.append(mine)
        follows.append([])
        seconds.append([])
        for tile in mine:
            if dates == 4:
                second = hop(tile, "date", 2)
                follow = hop(jnp.where(date % 2 == 0, second, tile), "date", 1)
            else:
                second = shift(tile, "date", -2)
                follow = shift(tile, "date", -1)
            follows[-1].append(follow)
            seconds[-1].append(second)
    result = None
    start = 0
    for chunk in range(chunks):
        last = chunk == chunks - 1
        parts = [slice(i, i + 1) for i in range(len(tiles[chunk]))] if last else [slice(None)]
        for part in parts:
            mine = tiles[chunk][part]
            result = goldstein(
                mine, follows[chunk][part], seconds[chunk][part], slot_of, start, result
            )
            start += sum(tile.shape[0] for tile in mine)
    return result[None]


def solution(mesh):
    in_specs = (
        P(("grp", "date"), None, "shard", None),
        P(),
        P(None, None, "shard"),
        P(("grp", "date"), None),
        P(("grp", "date"), None),
        P(("grp", "date"), None),
    )
    out_specs = P(("grp", "date"), "shard", None, None, None, None)
    return jax.shard_map(body, mesh=mesh, in_specs=in_specs, out_specs=out_specs, check_vma=False)
```

time: 109 us -> 79.5 us (0.73)
  starting transfers between devices: 57.5 us -> 31.7 us
  waiting for transfers between devices: 14.3 us -> 22.2 us
  Pallas kernels: 24.8 us -> 19.5 us
  other arithmetic: 4.49 us -> 0.2 us
  local copies, waits for them, and re-layouts: 6.73 us -> 4.77 us
    ppermute x32 -> x26, starting transfers between devices: 48.4 us -> 31.7 us  [hop(): return lax.ppermute(value, axis, pairs)]
    all_to_all x2 -> x0, starting transfers between devices: 9.05 us -> none  [body(): lax.all_to_all(share, 'shard', split_axis=0, concat_axis=0, tiled=True)]
    ppermute x32 -> x26, waiting for transfers between devices: 13.6 us -> 22.2 us  [hop(): return lax.ppermute(value, axis, pairs)]
    pallas_call x4 -> x3, Pallas kernels: 15.3 us -> 8.76 us  [goldstein(): pl.pallas_call(kernel, out_shape=jax.ShapeDtypeStruct((capacity, 2, 2, BL...]
    reduce_sum x7 -> x0, other arithmetic: 2.38 us -> none  [the longest x1 0.94 us: body(): rank = jnp.sum(earlier.astype(jnp.int32), axis=1)]
    unnamed x20 -> x37, local copies, waits for them, and re-layouts: 6.35 us -> 4.75 us
    pallas_call x2 -> x3, Pallas kernels: 6.06 us -> 7.18 us  [the longest x1 5.1 us: range_compress(): pl.pallas_call(kernel, out_shape=[jax.ShapeDtypeStruct((2, outer, pulses,...]
  transfers between devices with their start and end apart: 34 -> 26, of which waited for: 5 -> 10; matrix products, arithmetic and copies ran while one was open for 3% -> 0% of each run, Pallas kernels for 15% -> 18%
where the time goes in v2:
time: 79.5 us; the launch traced here: 78.7 us
  starting transfers between devices  31.7 us (40%)
  waiting for transfers between devices  22.2 us (28%)
  Pallas kernels  19.5 us (25%)
  local copies, waits for them, and re-layouts  4.77 us (6%)
    ppermute x26, starting transfers between devices, hop(): return lax.ppermute(value, axis, pairs)  31.7 us
    ppermute x26, waiting for transfers between devices, hop(): return lax.ppermute(value, axis, pairs)  22.2 us
    pallas_call x3, Pallas kernels, goldstein(): pl.pallas_call(kernel, out_shape=jax.ShapeDtypeStruct((capacity, 2, 2, BL...  8.76 us
    pallas_call x1, Pallas kernels, range_compress(): pl.pallas_call(kernel, out_shape=[jax.ShapeDtypeStruct((2, outer, pulses,...  5.1 us
    unnamed x37, local copies, waits for them, and re-layouts  4.75 us
    pallas_call x2, Pallas kernels, focus(): pl.pallas_call(kernel, out_shape=[jax.ShapeDtypeStruct((per, 2, BLK, BLK)...  3.56 us
  transfers between devices with their start and end apart: 26, of which 10 were waited for; matrix products, arithmetic and copies ran while one was open for 0% of the time, Pallas kernels for 18%

profile of v2, /device:TPU:0, one launch (start us, length us, event | category | flops | bytes accessed | tf_op | source)
XLA Modules:
  0.0 78.7 jit_solution(6394623926251032288)
XLA Ops:
  0.0 1.0 %copy-done = bf16[2,128,1024]{2,1,0:T(8,128)(2,1)S(1)} copy-done((bf16[2,128,1024]{2,1,0:T(8,128)(2,1)S(1)}, bf16[2,128,1024]{2,1,0:T(8,128)(2,1)}, u32[]{:S(2)}) %copy-start) | copy-done | bytes 524312
  1.1 0.5 collective-permute-start
  1.7 0.9 %collective-permute-done.rest_1_ = bf16[2,32,1024]{2,1,0:T(8,128)(2,1)S(1)} collective-permute-done((bf16[2,32,1024]{2,1,0:T(8,128)(2,1)S(1)}, bf16[2,32,1024]{2,1,0:T(8,128)(2,1)S(1)}, u32[]{:S(2)}, u32[]{:S(2)}) %collective-permute-start) | collective-permute-done | bytes 131104 | tf_op jit(solution)/shard_map/ppermute | solution.py:107
  2.6 0.7 copy-done.13
  3.2 0.7 filter_columns.1
  4.0 3.0 %collective-permute-start.8 = (bf16[4,2,32,128]{3,2,1,0:T(8,128)(2,1)S(1)}, bf16[4,2,32,128]{3,2,1,0:T(8,128)(2,1)S(1)}, u32[]{:S(2)}, u32[]{:S(2)}) collective-permute-start(bf16[4,2,32,128]{3,2,1,0:T(8,128)(2,1)S(1)} %get-tuple-element.53), channel_id=1, source_target_pairs={{0,2},{1,3},{2,0},{3,1},{4,6},{5,7},{6,4},{7,5},{8,10},{9,11},{10,... | collective-permute-start | bytes 196616 | tf_op jit(solution)/shard_map/ppermute | solution.py:107
  7.0 2.6 %collective-permute-start.9 = (bf16[4,2,32,128]{3,2,1,0:T(8,128)(2,1)S(1)}, bf16[4,2,32,128]{3,2,1,0:T(8,128)(2,1)S(1)}, u32[]{:S(2)}, u32[]{:S(2)}) collective-permute-start(bf16[4,2,32,128]{3,2,1,0:T(8,128)(2,1)S(1)} %get-tuple-element.54), channel_id=1, source_target_pairs={{0,4},{1,5},{2,6},{3,7},{4,0},{5,1},{6,2},{7,3},{8,12},{9,13},{10,... | collective-permute-start | bytes 196616 | tf_op jit(solution)/shard_map/ppermute | solution.py:107
  9.6 5.1 %range_compress.1 = (bf16[2,64,16,128]{3,2,1,0:T(8,128)(2,1)}, s32[8,16]{1,0:T(8,128)}, s32[16]{0:T(128)}) custom-call(s32[64]{0:T(128)} %bitcast.9, s32[64]{0:T(128)} %bitcast.12, s32[2]{0:T(128)} %copy-done.8, bf16[2,16,8192]{2,1,0:T(8,128)(2,1)} %bitcast.11, f32[2,8192]{1,0:T(2,128)} %refs_1_.1, bf16[128,128]{1,0:T(8,128)(2,1)} %constant.58.refs_2_, ...), custom_call_target="tpu_custom_call" | custom-call | flops 201326592 | bytes 1769472 | tf_op jit(solution)/shard_map/range_compress/pallas_call | solution.py:221
  14.8 0.9 %collective-permute-done.10 = bf16[4,2,32,128]{3,2,1,0:T(8,128)(2,1)S(1)} collective-permute-done((bf16[4,2,32,128]{3,2,1,0:T(8,128)(2,1)S(1)}, bf16[4,2,32,128]{3,2,1,0:T(8,128)(2,1)S(1)}, u32[]{:S(2)}, u32[]{:S(2)}) %collective-permute-start.10) | collective-permute-done | bytes 65568 | tf_op jit(solution)/shard_map/ppermute | solution.py:107
  15.7 1.6 %collective-permute-start.11 = (bf16[16,2,32,128]{3,2,1,0:T(8,128)(2,1)S(1)}, bf16[16,2,32,128]{3,2,1,0:T(8,128)(2,1)S(1)}, u32[]{:S(2)}, u32[]{:S(2)}) collective-permute-start(bf16[16,2,32,128]{3,2,1,0:T(8,128)(2,1)S(1)} %constant_dynamic-update-slice_fusion.rest_4_), channel_id=1, source_target_pairs={{0,8},{8,0},{16,24},{24,16},{1,9},{9,1},{17,25},{25,17},{2,10},{10... | collective-permute-start | bytes 786440 | tf_op jit(solution)/shard_map/ppermute | solution.py:107
  17.3 1.5 %collective-permute-start.12 = (bf16[16,2,32,128]{3,2,1,0:T(8,128)(2,1)S(1)}, bf16[16,2,32,128]{3,2,1,0:T(8,128)(2,1)S(1)}, u32[]{:S(2)}, u32[]{:S(2)}) collective-permute-start(bf16[16,2,32,128]{3,2,1,0:T(8,128)(2,1)S(1)} %constant_dynamic-update-slice_fusion.rest_4_), channel_id=1, source_target_pairs={{0,16},{8,24},{16,0},{24,8},{1,17},{9,25},{17,1},{25,9},{2,18},{10... | collective-permute-start | bytes 786440 | tf_op jit(solution)/shard_map/ppermute | solution.py:107
  18.8 0.5 collective-permute-start.13
  19.3 1.0 %copy-done.4 = bf16[2,64,16,128]{3,2,1,0:T(8,128)(2,1)S(1)} copy-done((bf16[2,64,16,128]{3,2,1,0:T(8,128)(2,1)S(1)}, bf16[2,64,16,128]{3,2,1,0:T(8,128)(2,1)}, u32[]{:S(2)}) %copy-start.4) | copy-done | bytes 524312
  20.3 0.7 copy-done.5
  21.0 0.6 copy-done.9
  21.6 1.3 %spread_columns.1 = (bf16[8,2,32,128]{3,2,1,0:T(8,128)(2,1)S(1)}, bf16[8,2,32,128]{3,2,1,0:T(8,128)(2,1)S(1)}, bf16[8,2,32,128]{3,2,1,0:T(8,128)(2,1)S(1)}, bf16...) custom-call(s32[8,16]{1,0:T(8,128)S(1)} %copy-done.5, ...), custom_call_target="tpu_custom_call" | custom-call | bytes 2097152 | tf_op jit(solution)/shard_map/spread_columns/pallas_call | solution.py:272
  23.0 0.9 %collective-permute-start.5 = (bf16[8,2,32,128]{3,2,1,0:T(8,128)(2,1)S(1)}, bf16[8,2,32,128]{3,2,1,0:T(8,128)(2,1)S(1)}, u32[]{:S(2)}, u32[]{:S(2)}) collective-permute-start(bf16[8,2,32,128]{3,2,1,0:T(8,128)(2,1)S(1)} %get-tuple-element.49), channel_id=1, source_target_pairs={{0,2},{1,3},{2,0},{3,1},{4,6},{5,7},{6,4},{7,5},{8,10},{9,11},{10,... | collective-permute-start | bytes 393224 | tf_op jit(solution)/shard_map/ppermute | solution.py:107
  23.9 2.6 %collective-permute-start.6 = (bf16[8,2,32,128]{3,2,1,0:T(8,128)(2,1)S(1)}, bf16[8,2,32,128]{3,2,1,0:T(8,128)(2,1)S(1)}, u32[]{:S(2)}, u32[]{:S(2)}) collective-permute-start(bf16[8,2,32,128]{3,2,1,0:T(8,128)(2,1)S(1)} %get-tuple-element.50), channel_id=1, source_target_pairs={{0,4},{1,5},{2,6},{3,7},{4,0},{5,1},{6,2},{7,3},{8,12},{9,13},{10,... | collective-permute-start | bytes 393224 | tf_op jit(solution)/shard_map/ppermute | solution.py:107
  26.6 1.3 %collective-permute-start.7 = (bf16[8,2,32,128]{3,2,1,0:T(8,128)(2,1)S(1)}, bf16[8,2,32,128]{3,2,1,0:T(8,128)(2,1)S(1)}, u32[]{:S(2)}, u32[]{:S(2)}) collective-permute-start(bf16[8,2,32,128]{3,2,1,0:T(8,128)(2,1)S(1)} %get-tuple-element.51), channel_id=1, source_target_pairs={{0,6},{1,7},{2,4},{3,5},{4,2},{5,3},{6,0},{7,1},{8,14},{9,15},{10,... | collective-permute-start | bytes 393224 | tf_op jit(solution)/shard_map/ppermute | solution.py:107
  27.8 2.8 %collective-permute-done.12.rest_6_ = bf16[16,2,32,128]{3,2,1,0:T(8,128)(2,1)S(1)} collective-permute-done((bf16[16,2,32,128]{3,2,1,0:T(8,128)(2,1)S(1)}, bf16[16,2,32,128]{3,2,1,0:T(8,128)(2,1)S(1)}, u32[]{:S(2)}, u32[]{:S(2)}) %collective-permute-start.12) | collective-permute-done | bytes 262176 | tf_op jit(solution)/shard_map/ppermute | solution.py:107
  30.7 6.0 %collective-permute-done.6.rest_2_ = bf16[8,2,32,128]{3,2,1,0:T(8,128)(2,1)S(1)} collective-permute-done((bf16[8,2,32,128]{3,2,1,0:T(8,128)(2,1)S(1)}, bf16[8,2,32,128]{3,2,1,0:T(8,128)(2,1)S(1)}, u32[]{:S(2)}, u32[]{:S(2)}) %collective-permute-start.6) | collective-permute-done | bytes 131104 | tf_op jit(solution)/shard_map/ppermute | solution.py:107
  36.7 0.7 copy-done.6
  37.3 1.8 %focus.2 = (bf16[2,2,128,128]{3,2,1,0:T(8,128)(2,1)S(1)}, bf16[2,2,128,128]{3,2,1,0:T(8,128)(2,1)S(1)}, bf16[2,2,128,128]{3,2,1,0:T(8,128)(2,1)S(1)}, bf16[2,2,128,128]{3,2,1,0:T(8,128)(2,1)S(1)}) custom-call(s32[2]{0:T(128)S(1)} %copy-done.9, s32[8,16]{1,0:T(8,128)S(1)} %copy-done.6, s32[64]{0:T(128)S(1)} %bitcast.7, bf16[256,256]{1,0:T(8,128)(2,1)S(1)} %copy-done.1, ...), custom_call_target="tpu_custom_call" | custom-call | flops 268435456 | bytes 2752512 | tf_op jit(solution)/shard_map/focus/pallas_call | solution.py:389
  39.1 1.6 %collective-permute-start.14 = (bf16[2,2,128,128]{3,2,1,0:T(8,128)(2,1)S(1)}, bf16[2,2,128,128]{3,2,1,0:T(8,128)(2,1)S(1)}, u32[]{:S(2)}, u32[]{:S(2)}) collective-permute-start(bf16[2,2,128,128]{3,2,1,0:T(8,128)(2,1)S(1)} %get-tuple-element.56.rest_0_), channel_id=1, source_target_pairs={{0,16},{8,24},{16,0},{24,8},{1,17},{9,25},{17,1},{25,9},{2,18},{10... | collective-permute-start | bytes 393224 | tf_op jit(solution)/shard_map/ppermute | solution.py:107
  40.7 2.0 %collective-permute-start.2 = (bf16[8,2,32,128]{3,2,1,0:T(8,128)(2,1)}, bf16[8,2,32,128]{3,2,1,0:T(8,128)(2,1)S(1)}, u32[]{:S(2)}, u32[]{:S(2)}) collective-permute-start(bf16[8,2,32,128]{3,2,1,0:T(8,128)(2,1)} %copy-done.16), channel_id=1, source_target_pairs={{0,2},{1,3},{2,0},{3,1},{4,6},{5,7},{6,4},{7,5},{8,10},{9,11},{10,... | collective-permute-start | bytes 393224 | tf_op jit(solution)/shard_map/ppermute | solution.py:107
  42.7 1.0 %collective-permute-start.3 = (bf16[8,2,32,128]{3,2,1,0:T(8,128)(2,1)}, bf16[8,2,32,128]{3,2,1,0:T(8,128)(2,1)S(1)}, u32[]{:S(2)}, u32[]{:S(2)}) collective-permute-start(bf16[8,2,32,128]{3,2,1,0:T(8,128)(2,1)} %copy-done.15), channel_id=1, source_target_pairs={{0,4},{1,5},{2,6},{3,7},{4,0},{5,1},{6,2},{7,3},{8,12},{9,13},{10,... | collective-permute-start | bytes 393224 | tf_op jit(solution)/shard_map/ppermute | solution.py:107
  43.7 1.4 %collective-permute-start.4 = (bf16[8,2,32,128]{3,2,1,0:T(8,128)(2,1)}, bf16[8,2,32,128]{3,2,1,0:T(8,128)(2,1)S(1)}, u32[]{:S(2)}, u32[]{:S(2)}) collective-permute-start(bf16[8,2,32,128]{3,2,1,0:T(8,128)(2,1)} %copy-done.14), channel_id=1, source_target_pairs={{0,6},{1,7},{2,4},{3,5},{4,2},{5,3},{6,0},{7,1},{8,14},{9,15},{10,... | collective-permute-start | bytes 393224 | tf_op jit(solution)/shard_map/ppermute | solution.py:107
  45.1 0.5 collective-permute-start.24
  45.6 1.5 %collective-permute-start.22 = (bf16[2,2,128,128]{3,2,1,0:T(8,128)(2,1)S(1)}, bf16[2,2,128,128]{3,2,1,0:T(8,128)(2,1)S(1)}, u32[]{:S(2)}, u32[]{:S(2)}) collective-permute-start(bf16[2,2,128,128]{3,2,1,0:T(8,128)(2,1)S(1)} %get-tuple-element.64.rest_2_), channel_id=1, source_target_pairs={{0,16},{8,24},{16,0},{24,8},{1,17},{9,25},{17,1},{25,9},{2,18},{10... | collective-permute-start | bytes 393224 | tf_op jit(solution)/shard_map/ppermute | solution.py:107
  47.2 2.9 %collective-permute-done.24.rest_11_ = bf16[2,2,128,128]{3,2,1,0:T(8,128)(2,1)S(1)} collective-permute-done((bf16[2,2,128,128]{3,2,1,0:T(8,128)(2,1)S(1)}, bf16[2,2,128,128]{3,2,1,0:T(8,128)(2,1)S(1)}, u32[]{:S(2)}, u32[]{:S(2)}) %collective-permute-start.24) | collective-permute-done | bytes 131104 | tf_op jit(solution)/shard_map/ppermute | solution.py:107
  50.1 1.5 %collective-permute-start.15 = (bf16[2,2,128,128]{3,2,1,0:T(8,128)(2,1)S(1)}, bf16[2,2,128,128]{3,2,1,0:T(8,128)(2,1)S(1)}, u32[]{:S(2)}, u32[]{:S(2)}) collective-permute-start(bf16[2,2,128,128]{3,2,1,0:T(8,128)(2,1)S(1)} %broadcast_select_fusion.5), channel_id=1, source_target_pairs={{0,8},{8,0},{16,24},{24,16},{1,9},{9,1},{17,25},{25,17},{2,10},{10... | collective-permute-start | bytes 393224 | tf_op jit(solution)/shard_map/ppermute | solution.py:107
  51.6 0.6 collective-permute-start.20
  52.2 2.2 %collective-permute-done.3.rest_2_ = bf16[8,2,32,128]{3,2,1,0:T(8,128)(2,1)S(1)} collective-permute-done((bf16[8,2,32,128]{3,2,1,0:T(8,128)(2,1)}, bf16[8,2,32,128]{3,2,1,0:T(8,128)(2,1)S(1)}, u32[]{:S(2)}, u32[]{:S(2)}) %collective-permute-start.3) | collective-permute-done | bytes 131104 | tf_op jit(solution)/shard_map/ppermute | solution.py:107
  54.5 1.5 %collective-permute-start.25 = (bf16[2,2,128,128]{3,2,1,0:T(8,128)(2,1)S(1)}, bf16[2,2,128,128]{3,2,1,0:T(8,128)(2,1)S(1)}, u32[]{:S(2)}, u32[]{:S(2)}) collective-permute-start(bf16[2,2,128,128]{3,2,1,0:T(8,128)(2,1)S(1)} %broadcast_select_fusion.2), channel_id=1, source_target_pairs={{0,8},{8,0},{16,24},{24,16},{1,9},{9,1},{17,25},{25,17},{2,10},{10... | collective-permute-start | bytes 393224 | tf_op jit(solution)/shard_map/ppermute | solution.py:107
  56.0 1.8 %focus.3 = (bf16[4,2,128,128]{3,2,1,0:T(8,128)(2,1)S(1)}, bf16[4,2,128,128]{3,2,1,0:T(8,128)(2,1)S(1)}) custom-call(s32[2]{0:T(128)S(1)} %copy-done.10, s32[8,16]{1,0:T(8,128)S(1)} %copy-done.7, s32[64]{0:T(128)S(1)} %bitcast.8, bf16[256,256]{1,0:T(8,128)(2,1)S(1)} %copy-done.1, bf16[8,256,256]{2,1,0:T(8,128)(2,1)S(1)} %copy-done.3, ...), custom_call_target="tpu_custom_call" | custom-call | flops 268435456 | bytes 2752512 | tf_op jit(solution)/shard_map/focus/pallas_call | solution.py:389
  57.8 0.6 collective-permute-start.18
  58.4 0.7 collective-permute-start.23
  59.0 1.5 %collective-permute-start.16 = (bf16[4,2,128,128]{3,2,1,0:T(8,128)(2,1)S(1)}, bf16[4,2,128,128]{3,2,1,0:T(8,128)(2,1)S(1)}, u32[]{:S(2)}, u32[]{:S(2)}) collective-permute-start(bf16[4,2,128,128]{3,2,1,0:T(8,128)(2,1)S(1)} %get-tuple-element.61.rest_0_), channel_id=1, source_target_pairs={{0,16},{8,24},{16,0},{24,8},{1,17},{9,25},{17,1},{25,9},{2,18},{10... | collective-permute-start | bytes 786440 | tf_op jit(solution)/shard_map/ppermute | solution.py:107
  60.6 1.5 %collective-permute-start.21 = (bf16[2,2,128,128]{3,2,1,0:T(8,128)(2,1)S(1)}, bf16[2,2,128,128]{3,2,1,0:T(8,128)(2,1)S(1)}, u32[]{:S(2)}, u32[]{:S(2)}) collective-permute-start(bf16[2,2,128,128]{3,2,1,0:T(8,128)(2,1)S(1)} %broadcast_select_fusion.4), channel_id=1, source_target_pairs={{0,8},{8,0},{16,24},{24,16},{1,9},{9,1},{17,25},{25,17},{2,10},{10... | collective-permute-start | bytes 393224 | tf_op jit(solution)/shard_map/ppermute | solution.py:107
  62.1 3.0 %collective-permute-done.18.rest_2_ = bf16[4,2,128,128]{3,2,1,0:T(8,128)(2,1)S(1)} collective-permute-done((bf16[4,2,128,128]{3,2,1,0:T(8,128)(2,1)S(1)}, bf16[4,2,128,128]{3,2,1,0:T(8,128)(2,1)S(1)}, u32[]{:S(2)}, u32[]{:S(2)}) %collective-permute-start.18) | collective-permute-done | bytes 262176 | tf_op jit(solution)/shard_map/ppermute | solution.py:107
  65.1 0.6 collective-permute-start.19
  65.8 2.1 %collective-permute-done.16.rest_2_ = bf16[4,2,128,128]{3,2,1,0:T(8,128)(2,1)S(1)} collective-permute-done((bf16[4,2,128,128]{3,2,1,0:T(8,128)(2,1)S(1)}, bf16[4,2,128,128]{3,2,1,0:T(8,128)(2,1)S(1)}, u32[]{:S(2)}, u32[]{:S(2)}) %collective-permute-start.16) | collective-permute-done | bytes 262176 | tf_op jit(solution)/shard_map/ppermute | solution.py:107
  67.9 0.6 collective-permute-start.17
  68.6 3.5 %goldstein.3.rest_7_ = bf16[16,2,2,128,128]{4,3,2,1,0:T(8,128)(2,1)} custom-call(s32[16]{0:T(128)S(1)} %copy-done.11, bf16[2,2,128,128]{3,2,1,0:T(8,128)(2,1)S(1)} %get-tuple-element.56.rest_0_, bf16[2,2,128,128]{3,2,1,0:T(8,128)(2,1)S(1)} %get-tuple-element.63.rest_1_, bf16[2,2,128,128]{3,2,1,0:T(8,128)(2,1)S(1)} %get-tuple-element.64.rest_2_, ...), custom_call_target="tpu_custom_call" | custom-call | flops 1073741824 | bytes 3145792 | tf_op jit(solution)/shard_map/goldstein/pallas_call | solution.py:481
  72.2 1.1 %collective-permute-done.19.rest_1_ = bf16[4,2,128,128]{3,2,1,0:T(8,128)(2,1)S(1)} collective-permute-done((bf16[4,2,128,128]{3,2,1,0:T(8,128)(2,1)S(1)}, bf16[4,2,128,128]{3,2,1,0:T(8,128)(2,1)S(1)}, u32[]{:S(2)}, u32[]{:S(2)}) %collective-permute-start.19) | collective-permute-done | bytes 262176 | tf_op jit(solution)/shard_map/ppermute | solution.py:107
  73.2 2.6 %goldstein.4.rest_7_ = bf16[16,2,2,128,128]{4,3,2,1,0:T(8,128)(2,1)} custom-call(s32[16]{0:T(128)S(1)} %copy-done.11, bf16[4,2,128,128]{3,2,1,0:T(8,128)(2,1)S(1)} %get-tuple-element.62.rest_0_, bf16[4,2,128,128]{3,2,1,0:T(8,128)(2,1)S(1)} %collective-permute-done.19.rest_1_, ...), custom_call_target="tpu_custom_call", output_to_operand_aliasing={{}: (8, {})} | custom-call | flops 536870912 | bytes 3932224 | tf_op jit(solution)/shard_map/goldstein/pallas_call | solution.py:481
  75.8 0.2 collective-permute-done.17.rest_1_
  76.0 2.6 %goldstein.5 = bf16[16,2,2,128,128]{4,3,2,1,0:T(8,128)(2,1)} custom-call(s32[16]{0:T(128)S(1)} %copy-done.11, bf16[4,2,128,128]{3,2,1,0:T(8,128)(2,1)S(1)} %get-tuple-element.61.rest_0_, bf16[4,2,128,128]{3,2,1,0:T(8,128)(2,1)S(1)} %collective-permute-done.17.rest_1_, ...), custom_call_target="tpu_custom_call", output_to_operand_aliasing={{}: (8, {})} | custom-call | flops 536870912 | bytes 3932224 | tf_op jit(solution)/shard_map/goldstein/pallas_call | solution.py:481
  (58 shorter events, 0.4 us)
Async XLA Ops:
  0.0 1.0 %copy-start = (bf16[2,128,1024]{2,1,0:T(8,128)(2,1)S(1)}, bf16[2,128,1024]{2,1,0:T(8,128)(2,1)}, u32[]{:S(2)}) copy-start(bf16[2,128,1024]{2,1,0:T(8,128)(2,1)} %param.27) | copy-start | bytes 1572868
  0.0 36.6 %copy-start.1 = (bf16[256,256]{1,0:T(8,128)(2,1)S(1)}, bf16[256,256]{1,0:T(8,128)(2,1)}, u32[]{:S(2)}) copy-start(bf16[256,256]{1,0:T(8,128)(2,1)} %constant.60.forward_ref.rest_12_.rest_15_.rest_3_.rest_6_) | copy-start | bytes 393220
  0.0 36.6 %copy-start.3 = (bf16[8,256,256]{2,1,0:T(8,128)(2,1)S(1)}, bf16[8,256,256]{2,1,0:T(8,128)(2,1)}, u32[]{:S(2)}) copy-start(bf16[8,256,256]{2,1,0:T(8,128)(2,1)} %constant.61.back_ref) | copy-start | bytes 3145732
  0.0 36.6 %copy-start.12 = (s32[1,64]{1,0:T(1,128)S(1)}, s32[1,64]{1,0:T(1,128)}, u32[]{:S(2)}) copy-start(s32[1,64]{1,0:T(1,128)} %param.30) | copy-start | bytes 772
  1.1 1.5 %collective-permute-start = (bf16[2,32,1024]{2,1,0:T(8,128)(2,1)S(1)}, bf16[2,32,1024]{2,1,0:T(8,128)(2,1)S(1)}, u32[]{:S(2)}, u32[]{:S(2)}) collective-permute-start(bf16[2,32,1024]{2,1,0:T(8,128)(2,1)S(1)} %constant_dynamic-slice_fusion.rest_0_), channel_id=1, source_target_pairs={{0,1},{1,0},{2,3},{3,2},{4,5},{5,4},{6,7},{7,6},{8,9},{9,8},{10,11... | collective-permute-start | bytes 393224 | tf_op jit(solution)/shard_map/ppermute | solution.py:107
  1.6 7.9 %copy-start.8 = (s32[2]{0:T(128)}, s32[2]{0:T(128)S(1)}, u32[]{:S(2)}) copy-start(s32[2]{0:T(128)S(1)} %pad_add_fusion.place_ref) | copy-start | bytes 28
  2.6 0.7 copy-start.13
  4.0 10.8 %collective-permute-start.8 = (bf16[4,2,32,128]{3,2,1,0:T(8,128)(2,1)S(1)}, bf16[4,2,32,128]{3,2,1,0:T(8,128)(2,1)S(1)}, u32[]{:S(2)}, u32[]{:S(2)}) collective-permute-start(bf16[4,2,32,128]{3,2,1,0:T(8,128)(2,1)S(1)} %get-tuple-element.53), channel_id=1, source_target_pairs={{0,2},{1,3},{2,0},{3,1},{4,6},{5,7},{6,4},{7,5},{8,10},{9,11},{10,... | collective-permute-start | bytes 196616 | tf_op jit(solution)/shard_map/ppermute | solution.py:107
  7.0 7.8 %collective-permute-start.9 = (bf16[4,2,32,128]{3,2,1,0:T(8,128)(2,1)S(1)}, bf16[4,2,32,128]{3,2,1,0:T(8,128)(2,1)S(1)}, u32[]{:S(2)}, u32[]{:S(2)}) collective-permute-start(bf16[4,2,32,128]{3,2,1,0:T(8,128)(2,1)S(1)} %get-tuple-element.54), channel_id=1, source_target_pairs={{0,4},{1,5},{2,6},{3,7},{4,0},{5,1},{6,2},{7,3},{8,12},{9,13},{10,... | collective-permute-start | bytes 196616 | tf_op jit(solution)/shard_map/ppermute | solution.py:107
  9.6 6.2 %collective-permute-start.10 = (bf16[4,2,32,128]{3,2,1,0:T(8,128)(2,1)S(1)}, bf16[4,2,32,128]{3,2,1,0:T(8,128)(2,1)S(1)}, u32[]{:S(2)}, u32[]{:S(2)}) collective-permute-start(bf16[4,2,32,128]{3,2,1,0:T(8,128)(2,1)S(1)} %get-tuple-element.55), channel_id=1, source_target_pairs={{0,6},{1,7},{2,4},{3,5},{4,2},{5,3},{6,0},{7,1},{8,14},{9,15},{10,... | collective-permute-start | bytes 196616 | tf_op jit(solution)/shard_map/ppermute | solution.py:107
  14.7 4.6 %collective-permute-start.1 = (bf16[2,64,16,128]{3,2,1,0:T(8,128)(2,1)}, bf16[2,64,16,128]{3,2,1,0:T(8,128)(2,1)S(1)}, u32[]{:S(2)}, u32[]{:S(2)}) collective-permute-start(bf16[2,64,16,128]{3,2,1,0:T(8,128)(2,1)} %get-tuple-element.43.rest_0_), channel_id=1, source_target_pairs={{0,1},{1,0},{2,3},{3,2},{4,5},{5,4},{6,7},{7,6},{8,9},{9,8},{10,11... | collective-permute-start | bytes 1572872 | tf_op jit(solution)/shard_map/ppermute | solution.py:107
  15.7 10.8 %collective-permute-start.11 = (bf16[16,2,32,128]{3,2,1,0:T(8,128)(2,1)S(1)}, bf16[16,2,32,128]{3,2,1,0:T(8,128)(2,1)S(1)}, u32[]{:S(2)}, u32[]{:S(2)}) collective-permute-start(bf16[16,2,32,128]{3,2,1,0:T(8,128)(2,1)S(1)} %constant_dynamic-update-slice_fusion.rest_4_), channel_id=1, source_target_pairs={{0,8},{8,0},{16,24},{24,16},{1,9},{9,1},{17,25},{25,17},{2,10},{10... | collective-permute-start | bytes 786440 | tf_op jit(solution)/shard_map/ppermute | solution.py:107
  17.3 13.4 %collective-permute-start.12 = (bf16[16,2,32,128]{3,2,1,0:T(8,128)(2,1)S(1)}, bf16[16,2,32,128]{3,2,1,0:T(8,128)(2,1)S(1)}, u32[]{:S(2)}, u32[]{:S(2)}) collective-permute-start(bf16[16,2,32,128]{3,2,1,0:T(8,128)(2,1)S(1)} %constant_dynamic-update-slice_fusion.rest_4_), channel_id=1, source_target_pairs={{0,16},{8,24},{16,0},{24,8},{1,17},{9,25},{17,1},{25,9},{2,18},{10... | collective-permute-start | bytes 786440 | tf_op jit(solution)/shard_map/ppermute | solution.py:107
  18.8 11.8 %collective-permute-start.13 = (bf16[16,2,32,128]{3,2,1,0:T(8,128)(2,1)S(1)}, bf16[16,2,32,128]{3,2,1,0:T(8,128)(2,1)S(1)}, u32[]{:S(2)}, u32[]{:S(2)}) collective-permute-start(bf16[16,2,32,128]{3,2,1,0:T(8,128)(2,1)S(1)} %constant_dynamic-update-slice_fusion.rest_4_), channel_id=1, source_target_pairs={{0,24},{8,16},{16,8},{24,0},{1,25},{9,17},{17,9},{25,1},{2,26},{10... | collective-permute-start | bytes 786440 | tf_op jit(solution)/shard_map/ppermute | solution.py:107
  19.3 1.0 %copy-start.4 = (bf16[2,64,16,128]{3,2,1,0:T(8,128)(2,1)S(1)}, bf16[2,64,16,128]{3,2,1,0:T(8,128)(2,1)}, u32[]{:S(2)}) copy-start(bf16[2,64,16,128]{3,2,1,0:T(8,128)(2,1)} %get-tuple-element.43.rest_0_) | copy-start | bytes 1572868
  20.3 0.7 copy-start.5
  21.0 0.6 copy-start.9
  21.6 34.3 %copy-start.7 = (s32[8,16]{1,0:T(8,128)S(1)}, s32[8,16]{1,0:T(8,128)}, u32[]{:S(2)}) copy-start(s32[8,16]{1,0:T(8,128)} %get-tuple-element.42.table_ref) | copy-start | bytes 1540
  21.6 34.3 %copy-start.10 = (s32[2]{0:T(128)S(1)}, s32[2]{0:T(128)}, u32[]{:S(2)}) copy-start(s32[2]{0:T(128)} %copy-done.8) | copy-start | bytes 28
  23.0 16.1 %copy-start.14 = (bf16[8,2,32,128]{3,2,1,0:T(8,128)(2,1)}, bf16[8,2,32,128]{3,2,1,0:T(8,128)(2,1)S(1)}, u32[]{:S(2)}) copy-start(bf16[8,2,32,128]{3,2,1,0:T(8,128)(2,1)S(1)} %get-tuple-element.47) | copy-start | bytes 393220
  23.0 16.1 %copy-start.15 = (bf16[8,2,32,128]{3,2,1,0:T(8,128)(2,1)}, bf16[8,2,32,128]{3,2,1,0:T(8,128)(2,1)S(1)}, u32[]{:S(2)}) copy-start(bf16[8,2,32,128]{3,2,1,0:T(8,128)(2,1)S(1)} %get-tuple-element.46) | copy-start | bytes 393220
  23.0 16.1 %copy-start.16 = (bf16[8,2,32,128]{3,2,1,0:T(8,128)(2,1)}, bf16[8,2,32,128]{3,2,1,0:T(8,128)(2,1)S(1)}, u32[]{:S(2)}) copy-start(bf16[8,2,32,128]{3,2,1,0:T(8,128)(2,1)S(1)} %get-tuple-element.45) | copy-start | bytes 393220
  23.0 7.7 %collective-permute-start.5 = (bf16[8,2,32,128]{3,2,1,0:T(8,128)(2,1)S(1)}, bf16[8,2,32,128]{3,2,1,0:T(8,128)(2,1)S(1)}, u32[]{:S(2)}, u32[]{:S(2)}) collective-permute-start(bf16[8,2,32,128]{3,2,1,0:T(8,128)(2,1)S(1)} %get-tuple-element.49), channel_id=1, source_target_pairs={{0,2},{1,3},{2,0},{3,1},{4,6},{5,7},{6,4},{7,5},{8,10},{9,11},{10,... | collective-permute-start | bytes 393224 | tf_op jit(solution)/shard_map/ppermute | solution.py:107
  23.9 12.7 %collective-permute-start.6 = (bf16[8,2,32,128]{3,2,1,0:T(8,128)(2,1)S(1)}, bf16[8,2,32,128]{3,2,1,0:T(8,128)(2,1)S(1)}, u32[]{:S(2)}, u32[]{:S(2)}) collective-permute-start(bf16[8,2,32,128]{3,2,1,0:T(8,128)(2,1)S(1)} %get-tuple-element.50), channel_id=1, source_target_pairs={{0,4},{1,5},{2,6},{3,7},{4,0},{5,1},{6,2},{7,3},{8,12},{9,13},{10,... | collective-permute-start | bytes 393224 | tf_op jit(solution)/shard_map/ppermute | solution.py:107
  26.6 10.1 %collective-permute-start.7 = (bf16[8,2,32,128]{3,2,1,0:T(8,128)(2,1)S(1)}, bf16[8,2,32,128]{3,2,1,0:T(8,128)(2,1)S(1)}, u32[]{:S(2)}, u32[]{:S(2)}) collective-permute-start(bf16[8,2,32,128]{3,2,1,0:T(8,128)(2,1)S(1)} %get-tuple-element.51), channel_id=1, source_target_pairs={{0,6},{1,7},{2,4},{3,5},{4,2},{5,3},{6,0},{7,1},{8,14},{9,15},{10,... | collective-permute-start | bytes 393224 | tf_op jit(solution)/shard_map/ppermute | solution.py:107
  36.6 0.7 copy-start.6
  39.1 6.5 %collective-permute-start.14 = (bf16[2,2,128,128]{3,2,1,0:T(8,128)(2,1)S(1)}, bf16[2,2,128,128]{3,2,1,0:T(8,128)(2,1)S(1)}, u32[]{:S(2)}, u32[]{:S(2)}) collective-permute-start(bf16[2,2,128,128]{3,2,1,0:T(8,128)(2,1)S(1)} %get-tuple-element.56.rest_0_), channel_id=1, source_target_pairs={{0,16},{8,24},{16,0},{24,8},{1,17},{9,25},{17,1},{25,9},{2,18},{10... | collective-permute-start | bytes 393224 | tf_op jit(solution)/shard_map/ppermute | solution.py:107
  40.7 10.9 %collective-permute-start.2 = (bf16[8,2,32,128]{3,2,1,0:T(8,128)(2,1)}, bf16[8,2,32,128]{3,2,1,0:T(8,128)(2,1)S(1)}, u32[]{:S(2)}, u32[]{:S(2)}) collective-permute-start(bf16[8,2,32,128]{3,2,1,0:T(8,128)(2,1)} %copy-done.16), channel_id=1, source_target_pairs={{0,2},{1,3},{2,0},{3,1},{4,6},{5,7},{6,4},{7,5},{8,10},{9,11},{10,... | collective-permute-start | bytes 393224 | tf_op jit(solution)/shard_map/ppermute | solution.py:107
  42.7 11.8 %collective-permute-start.3 = (bf16[8,2,32,128]{3,2,1,0:T(8,128)(2,1)}, bf16[8,2,32,128]{3,2,1,0:T(8,128)(2,1)S(1)}, u32[]{:S(2)}, u32[]{:S(2)}) collective-permute-start(bf16[8,2,32,128]{3,2,1,0:T(8,128)(2,1)} %copy-done.15), channel_id=1, source_target_pairs={{0,4},{1,5},{2,6},{3,7},{4,0},{5,1},{6,2},{7,3},{8,12},{9,13},{10,... | collective-permute-start | bytes 393224 | tf_op jit(solution)/shard_map/ppermute | solution.py:107
  43.7 12.3 %collective-permute-start.4 = (bf16[8,2,32,128]{3,2,1,0:T(8,128)(2,1)}, bf16[8,2,32,128]{3,2,1,0:T(8,128)(2,1)S(1)}, u32[]{:S(2)}, u32[]{:S(2)}) collective-permute-start(bf16[8,2,32,128]{3,2,1,0:T(8,128)(2,1)} %copy-done.14), channel_id=1, source_target_pairs={{0,6},{1,7},{2,4},{3,5},{4,2},{5,3},{6,0},{7,1},{8,14},{9,15},{10,... | collective-permute-start | bytes 393224 | tf_op jit(solution)/shard_map/ppermute | solution.py:107
  45.1 5.0 %collective-permute-start.24 = (bf16[2,2,128,128]{3,2,1,0:T(8,128)(2,1)S(1)}, bf16[2,2,128,128]{3,2,1,0:T(8,128)(2,1)S(1)}, u32[]{:S(2)}, u32[]{:S(2)}) collective-permute-start(bf16[2,2,128,128]{3,2,1,0:T(8,128)(2,1)S(1)} %get-tuple-element.65.rest_3_), channel_id=1, source_target_pairs={{0,16},{8,24},{16,0},{24,8},{1,17},{9,25},{17,1},{25,9},{2,18},{10... | collective-permute-start | bytes 393224 | tf_op jit(solution)/shard_map/ppermute | solution.py:107
  45.6 12.7 %collective-permute-start.22 = (bf16[2,2,128,128]{3,2,1,0:T(8,128)(2,1)S(1)}, bf16[2,2,128,128]{3,2,1,0:T(8,128)(2,1)S(1)}, u32[]{:S(2)}, u32[]{:S(2)}) collective-permute-start(bf16[2,2,128,128]{3,2,1,0:T(8,128)(2,1)S(1)} %get-tuple-element.64.rest_2_), channel_id=1, source_target_pairs={{0,16},{8,24},{16,0},{24,8},{1,17},{9,25},{17,1},{25,9},{2,18},{10... | collective-permute-start | bytes 393224 | tf_op jit(solution)/shard_map/ppermute | solution.py:107
  50.1 5.8 %collective-permute-start.15 = (bf16[2,2,128,128]{3,2,1,0:T(8,128)(2,1)S(1)}, bf16[2,2,128,128]{3,2,1,0:T(8,128)(2,1)S(1)}, u32[]{:S(2)}, u32[]{:S(2)}) collective-permute-start(bf16[2,2,128,128]{3,2,1,0:T(8,128)(2,1)S(1)} %broadcast_select_fusion.5), channel_id=1, source_target_pairs={{0,8},{8,0},{16,24},{24,16},{1,9},{9,1},{17,25},{25,17},{2,10},{10... | collective-permute-start | bytes 393224 | tf_op jit(solution)/shard_map/ppermute | solution.py:107
  51.6 8.9 %collective-permute-start.20 = (bf16[2,2,128,128]{3,2,1,0:T(8,128)(2,1)S(1)}, bf16[2,2,128,128]{3,2,1,0:T(8,128)(2,1)S(1)}, u32[]{:S(2)}, u32[]{:S(2)}) collective-permute-start(bf16[2,2,128,128]{3,2,1,0:T(8,128)(2,1)S(1)} %get-tuple-element.63.rest_1_), channel_id=1, source_target_pairs={{0,16},{8,24},{16,0},{24,8},{1,17},{9,25},{17,1},{25,9},{2,18},{10... | collective-permute-start | bytes 393224 | tf_op jit(solution)/shard_map/ppermute | solution.py:107
  54.5 14.1 %collective-permute-start.25 = (bf16[2,2,128,128]{3,2,1,0:T(8,128)(2,1)S(1)}, bf16[2,2,128,128]{3,2,1,0:T(8,128)(2,1)S(1)}, u32[]{:S(2)}, u32[]{:S(2)}) collective-permute-start(bf16[2,2,128,128]{3,2,1,0:T(8,128)(2,1)S(1)} %broadcast_select_fusion.2), channel_id=1, source_target_pairs={{0,8},{8,0},{16,24},{24,16},{1,9},{9,1},{17,25},{25,17},{2,10},{10... | collective-permute-start | bytes 393224 | tf_op jit(solution)/shard_map/ppermute | solution.py:107
  56.0 12.6 %copy-start.2 = (bf16[256,256]{1,0:T(8,128)(2,1)S(1)}, bf16[256,256]{1,0:T(8,128)(2,1)}, u32[]{:S(2)}) copy-start(bf16[256,256]{1,0:T(8,128)(2,1)} %constant.62.rest_13_.rest_14_.rest_4_.rest_5_) | copy-start | bytes 393220
  56.0 12.6 %copy-start.11 = (s32[16]{0:T(128)S(1)}, s32[16]{0:T(128)}, u32[]{:S(2)}) copy-start(s32[16]{0:T(128)} %get-tuple-element.41.slot_ref) | copy-start | bytes 196
  57.8 7.3 %collective-permute-start.18 = (bf16[4,2,128,128]{3,2,1,0:T(8,128)(2,1)S(1)}, bf16[4,2,128,128]{3,2,1,0:T(8,128)(2,1)S(1)}, u32[]{:S(2)}, u32[]{:S(2)}) collective-permute-start(bf16[4,2,128,128]{3,2,1,0:T(8,128)(2,1)S(1)} %get-tuple-element.62.rest_0_), channel_id=1, source_target_pairs={{0,16},{8,24},{16,0},{24,8},{1,17},{9,25},{17,1},{25,9},{2,18},{10... | collective-permute-start | bytes 786440 | tf_op jit(solution)/shard_map/ppermute | solution.py:107
  58.4 10.2 %collective-permute-start.23 = (bf16[2,2,128,128]{3,2,1,0:T(8,128)(2,1)S(1)}, bf16[2,2,128,128]{3,2,1,0:T(8,128)(2,1)S(1)}, u32[]{:S(2)}, u32[]{:S(2)}) collective-permute-start(bf16[2,2,128,128]{3,2,1,0:T(8,128)(2,1)S(1)} %broadcast_select_fusion.3), channel_id=1, source_target_pairs={{0,8},{8,0},{16,24},{24,16},{1,9},{9,1},{17,25},{25,17},{2,10},{10... | collective-permute-start | bytes 393224 | tf_op jit(solution)/shard_map/ppermute | solution.py:107
  59.0 8.9 %collective-permute-start.16 = (bf16[4,2,128,128]{3,2,1,0:T(8,128)(2,1)S(1)}, bf16[4,2,128,128]{3,2,1,0:T(8,128)(2,1)S(1)}, u32[]{:S(2)}, u32[]{:S(2)}) collective-permute-start(bf16[4,2,128,128]{3,2,1,0:T(8,128)(2,1)S(1)} %get-tuple-element.61.rest_0_), channel_id=1, source_target_pairs={{0,16},{8,24},{16,0},{24,8},{1,17},{9,25},{17,1},{25,9},{2,18},{10... | collective-permute-start | bytes 786440 | tf_op jit(solution)/shard_map/ppermute | solution.py:107
  60.6 8.0 %collective-permute-start.21 = (bf16[2,2,128,128]{3,2,1,0:T(8,128)(2,1)S(1)}, bf16[2,2,128,128]{3,2,1,0:T(8,128)(2,1)S(1)}, u32[]{:S(2)}, u32[]{:S(2)}) collective-permute-start(bf16[2,2,128,128]{3,2,1,0:T(8,128)(2,1)S(1)} %broadcast_select_fusion.4), channel_id=1, source_target_pairs={{0,8},{8,0},{16,24},{24,16},{1,9},{9,1},{17,25},{25,17},{2,10},{10... | collective-permute-start | bytes 393224 | tf_op jit(solution)/shard_map/ppermute | solution.py:107
  65.1 8.1 %collective-permute-start.19 = (bf16[4,2,128,128]{3,2,1,0:T(8,128)(2,1)S(1)}, bf16[4,2,128,128]{3,2,1,0:T(8,128)(2,1)S(1)}, u32[]{:S(2)}, u32[]{:S(2)}) collective-permute-start(bf16[4,2,128,128]{3,2,1,0:T(8,128)(2,1)S(1)} %broadcast_select_fusion), channel_id=1, source_target_pairs={{0,8},{8,0},{16,24},{24,16},{1,9},{9,1},{17,25},{25,17},{2,10},{10... | collective-permute-start | bytes 786440 | tf_op jit(solution)/shard_map/ppermute | solution.py:107
  67.9 8.1 %collective-permute-start.17 = (bf16[4,2,128,128]{3,2,1,0:T(8,128)(2,1)S(1)}, bf16[4,2,128,128]{3,2,1,0:T(8,128)(2,1)S(1)}, u32[]{:S(2)}, u32[]{:S(2)}) collective-permute-start(bf16[4,2,128,128]{3,2,1,0:T(8,128)(2,1)S(1)} %broadcast_select_fusion.1), channel_id=1, source_target_pairs={{0,8},{8,0},{16,24},{24,16},{1,9},{9,1},{17,25},{25,17},{2,10},{10... | collective-permute-start | bytes 786440 | tf_op jit(solution)/shard_map/ppermute | solution.py:107

commit v3 on v2

--- a/solution.py
+++ b/solution.py
@@ -72,7 +72,7 @@
 
 def cost(macs, arrays):
     size = sum(math.prod(a.shape) * a.dtype.itemsize for a in arrays)
-    return pl.CostEstimate(flops=2 * macs, bytes_accessed=size, transcendentals=0)
+    return pl.CostEstimate(flops=int(2 * macs), bytes_accessed=size, transcendentals=0)
 
 
 def is_pow2(count):
@@ -112,13 +112,7 @@
     return lax.ppermute(value, axis, [(i, (i + steps) % count) for i in range(count)])
 
 
-def position(rank, sender, slot, shards, most, capacity):
-    if shards * most == capacity:
-        return rank * shards + sender
-    return slot
-
-
-def range_compress(echo, reference, owners, slots, place, plan):
+def range_compress(echo, reference, owners, slots, plan):
     _, pulses, samples = echo.shape
     shards, capacity, most, group, group_columns = plan
     total = owners.shape[0]
@@ -132,49 +126,32 @@
     operands = [echo, reference, first, second, turn]
     smem = pl.BlockSpec(memory_space=pltpu.SMEM)
 
-    def arrange(owner_ref, slot_ref, place_ref, block_ref, out_slot_ref, count_ref, free_ref):
+    def arrange(owner_ref, slot_ref, block_ref, place_ref, count_ref):
         for o in range(shards):
             for w in range(capacity):
                 block_ref[o, w] = 0
+                place_ref[o, w] = 0
             for g in range(shards):
                 count_ref[g, o] = 0
         for b in range(total):
-            g = b // group
             owner = owner_ref[b]
-            rank = count_ref[g, owner]
-            count_ref[g, owner] = rank + 1
-            where = position(rank, g, slot_ref[b], shards, most, capacity)
-            block_ref[owner, where] = (b + 1) * most + rank
-        me = place_ref[0]
-        for w in range(capacity):
-            free_ref[w] = 0
-        for w in range(capacity):
-            code = block_ref[me, w] // most
-            slot = slot_ref[jnp.maximum(code - 1, 0)]
-            out_slot_ref[w] = jnp.where(code > 0, slot, -1)
-            free_ref[jnp.where(code > 0, slot, capacity)] = 1
-        spare = 0
-        for w in range(capacity):
-            taken = free_ref[w]
-            free_ref[capacity + 1 + spare] = w
-            spare = spare + 1 - taken
-        spare = 0
-        for w in range(capacity):
-            slot = out_slot_ref[w]
-            out_slot_ref[w] = jnp.where(slot < 0, free_ref[capacity + 1 + spare], slot)
-            spare = spare + jnp.where(slot < 0, 1, 0)
-
-    def kernel(owner_ref, slot_ref, place_ref, *refs):
+            rank = count_ref[b // group, owner]
+            count_ref[b // group, owner] = rank + 1
+            slot = slot_ref[b]
+            block_ref[owner, slot] = (b + 1) * most + rank
+            place_ref[owner, slot] = b // group * group_columns + b % group % group_columns
+
+    def kernel(owner_ref, slot_ref, *refs):
         count = len(operands)
-        out_ref, block_ref, out_slot_ref = refs[count : count + 3]
+        out_ref, block_ref, place_ref = refs[count : count + 3]
         local = refs[count + 3 : 2 * count + 3]
-        x_re, x_im, y_re, y_im, sems, count_ref, free_ref = refs[2 * count + 3 :]
+        x_re, x_im, y_re, y_im, sems, count_ref = refs[2 * count + 3 :]
         copies = [
             pltpu.make_async_copy(refs[i], local[i], sems.at[i]) for i in range(count)
         ]
         for copy in copies:
             copy.start()
-        arrange(owner_ref, slot_ref, place_ref, block_ref, out_slot_ref, count_ref, free_ref)
+        arrange(owner_ref, slot_ref, block_ref, place_ref, count_ref)
         for copy in copies:
             copy.wait()
         echo_ref, ref_ref, first_ref, second_ref, turn_ref = local
@@ -223,31 +200,30 @@
         out_shape=[
             jax.ShapeDtypeStruct((2, outer, pulses, BLK), BF),
             jax.ShapeDtypeStruct((shards, capacity), jnp.int32),
-            jax.ShapeDtypeStruct((capacity,), jnp.int32),
+            jax.ShapeDtypeStruct((shards, capacity), jnp.int32),
         ],
-        in_specs=[smem] * 3 + [pl.BlockSpec(memory_space=pl.ANY)] * len(operands),
-        out_specs=[pl.BlockSpec(memory_space=pltpu.VMEM)] + [smem] * 2,
+        in_specs=[smem] * 2 + [pl.BlockSpec(memory_space=pl.ANY)] * len(operands),
+        out_specs=[pl.BlockSpec(memory_space=pltpu.VMEM), smem, smem],
         scratch_shapes=[pltpu.VMEM(a.shape, a.dtype) for a in operands]
         + [pltpu.VMEM((pulses * outer, BLK), F32)] * 4
         + [
             pltpu.SemaphoreType.DMA((len(operands),)),
             pltpu.SMEM((shards, shards), jnp.int32),
-            pltpu.SMEM((2 * capacity + 2,), jnp.int32),
         ],
         compiler_params=params(K1_MIB),
         cost_estimate=cost(
             pulses * 4 * BLK * outer * (outer + BLK), [echo, echo, echo, reference, turn]
         ),
         name="range_compress",
-    )(owners, slots, place, *operands)
-
-
-def spread_columns(parts, table, place, chunks, plan):
+    )(owners, slots, *operands)
+
+
+def spread_columns(parts, table, place, sizes, plan):
     _, _, pulses, _ = parts[0].shape
     cores = len(parts)
     shards, capacity, most, group, group_columns = plan
     chips = shards // cores
-    each = capacity // chunks
+    chunks = len(sizes)
 
     def kernel(table_ref, place_ref, *rest):
         part_refs = rest[:cores]
@@ -258,20 +234,19 @@
             for k in range(chips):
                 owner = target_of(chip, k, chips) * cores + core
                 out = outs[chunk * chips + k]
-                for s in range(each):
-                    block = jnp.maximum(table_ref[owner, chunk * each + s] // most - 1, 0)
-                    column = block // group * group_columns + block % group % group_columns
+                for s in range(sizes[chunk]):
+                    column = table_ref[owner, sum(sizes[:chunk]) + s]
                     for c in range(cores):
                         at = source_of(core, c, cores) * pulses
                         rows = pl.ds(pl.multiple_of(at, pulses), pulses)
                         out[s, 0, rows, :] = part_refs[c][0, column]
                         out[s, 1, rows, :] = part_refs[c][1, column]
 
-    piece = jax.ShapeDtypeStruct((each, 2, cores * pulses, BLK), BF)
+    pieces = [jax.ShapeDtypeStruct((size, 2, cores * pulses, BLK), BF) for size in sizes]
     smem = pl.BlockSpec(memory_space=pltpu.SMEM)
     outs = pl.pallas_call(
         kernel,
-        out_shape=[piece] * (chunks * chips),
+        out_shape=[piece for piece in pieces for _ in range(chips)],
         in_specs=[smem, smem] + whole(cores),
         out_specs=whole(chunks * chips),
         compiler_params=params(16),
@@ -330,7 +305,7 @@
     )(owners, place, *parts)
 
 
-def focus(pieces, filters, place, table, kinds, start, cores, subs, plan):
+def focus(pieces, filters, place, table, kinds, start, cores, sizes, plan):
     each, _, share, _ = pieces[0].shape
     chips = len(pieces)
     dates = len(filters)
@@ -338,15 +313,15 @@
     rows = filters[0].shape[-2]
     forward = const(dft(pulses, pulses, pulses, -1, 1.0 / math.sqrt(pulses)))
     back = const(resample_table(pulses))
-    per = each // subs
 
     _, _, most, group, group_columns = plan
 
     def kernel(place_ref, table_ref, kind_ref, forward_ref, back_ref, *rest):
         piece_refs = rest[:chips]
         filter_refs = rest[chips : chips + dates]
-        outs = rest[chips + dates : chips + dates + subs]
-        col, fil = rest[chips + dates + subs :]
+        outs = rest[chips + dates : chips + dates + len(sizes)]
+        col, fil = rest[chips + dates + len(sizes) :]
+        homes = [(i, s) for i, size in enumerate(sizes) for s in range(size)]
         chip = place_ref[0] // cores
         entries, table_rows, valid = [], [], []
         for s in range(each):
@@ -381,33 +356,32 @@
                 shaped = jnp.concatenate([re * a - im * b, re * b + im * a], axis=0).astype(BF)
                 image = mm(back_ref[table_rows[s + t]], shaped)
                 image = jnp.where(valid[s + t], image, 0.0).astype(BF)
-                out = outs[(s + t) // per]
-                out[(s + t) % per, 0] = image[:BLK]
-                out[(s + t) % per, 1] = image[BLK:]
+                i, at = homes[s + t]
+                outs[i][at, 0] = image[:BLK]
+                outs[i][at, 1] = image[BLK:]
 
     smem = pl.BlockSpec(memory_space=pltpu.SMEM)
     return pl.pallas_call(
         kernel,
-        out_shape=[jax.ShapeDtypeStruct((per, 2, BLK, BLK), BF)] * subs,
+        out_shape=[jax.ShapeDtypeStruct((size, 2, BLK, BLK), BF) for size in sizes],
         in_specs=[smem] * 3 + whole(2 + chips + dates),
-        out_specs=whole(subs),
+        out_specs=whole(len(sizes)),
         scratch_shapes=[
             pltpu.VMEM((each, 2, pulses, BLK), BF),
             pltpu.VMEM((each, 2, pulses, BLK), BF),
         ],
         compiler_params=params(16),
         cost_estimate=cost(
-            each * 4 * pulses * (pulses + BLK) * BLK, [*pieces, *filters, forward, back]
+            4 * each * 4 * pulses * (pulses + BLK) * BLK, [*pieces, *filters, forward, back] * 4
         ),
         name="focus",
     )(place, table, kinds, forward, back, *pieces, *filters)
 
 
-def goldstein(tiles, follows, seconds, slots, start, result):
+def goldstein(tiles, follows, seconds, start, capacity, result):
     sizes = [tile.shape[0] for tile in tiles]
     count = sum(sizes)
     homes = [(i, s) for i, size in enumerate(sizes) for s in range(size)]
-    capacity = slots.shape[0]
     scale = 1.0 / math.sqrt(BLK)
     ahead = dft(BLK, BLK, BLK, -1, scale)
     behind = dft(BLK, BLK, BLK, 1, scale)
@@ -432,7 +406,7 @@
         power = power + (pltpu.roll(power, 1, 0) + pltpu.roll(power, BLK - 1, 0))
         return power + (pltpu.roll(power, 1, 1) + pltpu.roll(power, BLK - 1, 1))
 
-    def kernel(slot_ref, *rest):
+    def kernel(*rest):
         many = len(tiles)
         tile_refs, follow_refs, second_refs = (rest[i * many : (i + 1) * many] for i in range(3))
         al_ref, ar_ref, bl_ref, br_ref = rest[3 * many : 3 * many + 4]
@@ -471,17 +445,16 @@
                         p * BLK : (p + 1) * BLK, part * BLK : (part + 1) * BLK
                     ]
             for s in batched:
-                pltpu.make_async_copy(buffer.at[s], out_ref.at[slot_ref[start + s]], sems.at[s]).start()
+                pltpu.make_async_copy(buffer.at[s], out_ref.at[start + s], sems.at[s]).start()
         for s in range(count):
-            pltpu.make_async_copy(buffer.at[s], out_ref.at[slot_ref[start + s]], sems.at[s]).wait()
+            pltpu.make_async_copy(buffer.at[s], out_ref.at[start + s], sems.at[s]).wait()
 
     anywhere = pl.BlockSpec(memory_space=pl.ANY)
-    smem = pl.BlockSpec(memory_space=pltpu.SMEM)
-    operands = [slots, *tiles, *follows, *seconds, *tables] + ([result] if have else [])
+    operands = [*tiles, *follows, *seconds, *tables] + ([result] if have else [])
     return pl.pallas_call(
         kernel,
         out_shape=jax.ShapeDtypeStruct((capacity, 2, 2, BLK, BLK), BF),
-        in_specs=[smem] + whole(3 * len(tiles) + 4) + [anywhere] * have,
+        in_specs=whole(3 * len(tiles) + 4) + [anywhere] * have,
         out_specs=anywhere,
         scratch_shapes=[
             pltpu.VMEM((count, 2, 2, BLK, BLK), BF),
@@ -509,9 +482,6 @@
     most = max(2, capacity // shards)
     group_columns = azimuth_reference.shape[2] // BLK
     plan = (shards, capacity, most, group, group_columns)
-    chunks = most if shards * most == capacity else 1
-    each = capacity // chunks
-
     rows = azimuth_reference.shape[1] // dates
     share = lax.dynamic_slice_in_dim(azimuth_reference, date * rows, rows, axis=1)
     shares = [share] + [hop(share, "shard", c, cores) for c in range(1, cores)]
@@ -521,25 +491,20 @@
     got = [sent[0]] + [hop(sent[k], "shard", k * cores) for k in range(1, chips)]
     got = jnp.concatenate(got, axis=0)
     filters = [got] + [hop(got, "date", e) for e in range(1, dates)]
-    compressed, blocks, slot_of = range_compress(
-        echo, range_reference, owners, slots, place, plan
-    )
+    compressed, blocks, columns = range_compress(echo, range_reference, owners, slots, plan)
     parts = [compressed] + [hop(compressed, "shard", c, cores) for c in range(1, cores)]
-    outbox = spread_columns(parts, blocks, place, chunks, plan)
-    splits = (4, 2)
+    splits = ((2, 2, 2, 2), (4, 4)) if capacity == 16 else ((capacity,),)
+    outbox = spread_columns(parts, columns, place, [sum(sizes) for sizes in splits], plan)
     tiles, follows, seconds = [], [], []
-    for chunk in range(chunks):
+    start = 0
+    for chunk, sizes in enumerate(splits):
         pieces = [outbox[chunk][0]] + [
             hop(outbox[chunk][k], "shard", k * cores) for k in range(1, chips)
         ]
-        if chunk > 0 and 1 > 0:
-            pieces, kept = lax.optimization_barrier((pieces, follows[0][:1]))
-            follows[0][:1] = kept
-        subs = splits[chunk] if each % (2 * splits[chunk]) == 0 else 1
-        mine = focus(pieces, filters, place, blocks, kinds, chunk * each, cores, subs, plan)
-        tiles.append(mine)
-        follows.append([])
-        seconds.append([])
+        mine = focus(pieces, filters, place, blocks, kinds, start, cores, sizes, plan)
+        start += sum(sizes)
+        if chunk:
+            mine, follows[:1] = lax.optimization_barrier((mine, follows[:1]))
         for tile in mine:
             if dates == 4:
                 second = hop(tile, "date", 2)
@@ -547,19 +512,18 @@
             else:
                 second = shift(tile, "date", -2)
                 follow = shift(tile, "date", -1)
-            follows[-1].append(follow)
-            seconds[-1].append(second)
+            tiles.append(tile)
+            follows.append(follow)
+            seconds.append(second)
     result = None
     start = 0
-    for chunk in range(chunks):
-        last = chunk == chunks - 1
-        parts = [slice(i, i + 1) for i in range(len(tiles[chunk]))] if last else [slice(None)]
-        for part in parts:
-            mine = tiles[chunk][part]
-            result = goldstein(
-                mine, follows[chunk][part], seconds[chunk][part], slot_of, start, result
-            )
-            start += sum(tile.shape[0] for tile in mine)
+    groups = [4, 1, 1] if len(tiles) == 6 else [len(tiles)]
+    for group in groups:
+        take = slice(0, group)
+        mine = tiles[take], follows[take], seconds[take]
+        result = goldstein(*mine, start, capacity, result)
+        start += sum(tile.shape[0] for tile in mine[0])
+        del tiles[take], follows[take], seconds[take]
     return result[None]
 
 

time: 79.5 us -> 76.9 us (0.967)
  waiting for transfers between devices: 22.2 us -> 18.5 us
  starting transfers between devices: 31.7 us -> 35.1 us
  Pallas kernels: 19.5 us -> 17.3 us
    ppermute x26, waiting for transfers between devices: 22.2 us -> 18.5 us  [hop(): return lax.ppermute(value, axis, pairs)]
    ppermute x26, starting transfers between devices: 31.7 us -> 35.1 us  [hop(): return lax.ppermute(value, axis, pairs)]
    pallas_call x3, Pallas kernels: 8.76 us -> 7.09 us  [goldstein(): pl.pallas_call(kernel, out_shape=jax.ShapeDtypeStruct((capacity, 2, 2, BL...]
    unnamed x37 -> x25, local copies, waits for them, and re-layouts: 4.75 us -> 5.37 us
  transfers between devices with their start and end apart: 26 -> 26, of which waited for: 10 -> 11; matrix products, arithmetic and copies ran while one was open for 0% -> 0% of each run, Pallas kernels for 18% -> 19%
where the time goes in v3:
time: 76.9 us; the launch traced here: 76.6 us
  starting transfers between devices  35.1 us (46%)
  waiting for transfers between devices  18.5 us (24%)
  Pallas kernels  17.3 us (22%)
  local copies, waits for them, and re-layouts  5.39 us (7%)
    ppermute x26, starting transfers between devices, hop(): return lax.ppermute(value, axis, pairs)  35.1 us
    ppermute x26, waiting for transfers between devices, hop(): return lax.ppermute(value, axis, pairs)  18.5 us
    pallas_call x3, Pallas kernels, goldstein(): pl.pallas_call(kernel, out_shape=jax.ShapeDtypeStruct((capacity, 2, 2, BL...  7.09 us
    unnamed x25, local copies, waits for them, and re-layouts  5.37 us
    pallas_call x1, Pallas kernels, range_compress(): pl.pallas_call(kernel, out_shape=[jax.ShapeDtypeStruct((2, outer, pulses,...  5.09 us
    pallas_call x2, Pallas kernels, focus(): pl.pallas_call(kernel, out_shape=[jax.ShapeDtypeStruct((size, 2, BLK, BLK...  3.55 us
  transfers between devices with their start and end apart: 26, of which 11 were waited for; matrix products, arithmetic and copies ran while one was open for 0% of the time, Pallas kernels for 19%

profile of v3, /device:TPU:0, one launch (start us, length us, event | category | flops | bytes accessed | tf_op | source)
XLA Modules:
  0.0 76.6 jit_solution(6965633871402475196)
XLA Ops:
  0.0 1.0 %copy-done = bf16[2,128,1024]{2,1,0:T(8,128)(2,1)S(1)} copy-done((bf16[2,128,1024]{2,1,0:T(8,128)(2,1)S(1)}, bf16[2,128,1024]{2,1,0:T(8,128)(2,1)}, u32[]{:S(2)}) %copy-start) | copy-done | bytes 524312
  1.1 0.5 collective-permute-start
  1.6 0.9 %collective-permute-done.rest_1_ = bf16[2,32,1024]{2,1,0:T(8,128)(2,1)S(1)} collective-permute-done((bf16[2,32,1024]{2,1,0:T(8,128)(2,1)S(1)}, bf16[2,32,1024]{2,1,0:T(8,128)(2,1)S(1)}, u32[]{:S(2)}, u32[]{:S(2)}) %collective-permute-start) | collective-permute-done | bytes 131104 | tf_op jit(solution)/shard_map/ppermute | solution.py:107
  2.6 0.7 copy-done.5
  3.2 0.7 filter_columns.1
  4.0 3.0 %collective-permute-start.5 = (bf16[4,2,32,128]{3,2,1,0:T(8,128)(2,1)S(1)}, bf16[4,2,32,128]{3,2,1,0:T(8,128)(2,1)S(1)}, u32[]{:S(2)}, u32[]{:S(2)}) collective-permute-start(bf16[4,2,32,128]{3,2,1,0:T(8,128)(2,1)S(1)} %get-tuple-element.47), channel_id=1, source_target_pairs={{0,2},{1,3},{2,0},{3,1},{4,6},{5,7},{6,4},{7,5},{8,10},{9,11},{10,... | collective-permute-start | bytes 196616 | tf_op jit(solution)/shard_map/ppermute | solution.py:107
  7.0 2.6 %collective-permute-start.6 = (bf16[4,2,32,128]{3,2,1,0:T(8,128)(2,1)S(1)}, bf16[4,2,32,128]{3,2,1,0:T(8,128)(2,1)S(1)}, u32[]{:S(2)}, u32[]{:S(2)}) collective-permute-start(bf16[4,2,32,128]{3,2,1,0:T(8,128)(2,1)S(1)} %get-tuple-element.48), channel_id=1, source_target_pairs={{0,4},{1,5},{2,6},{3,7},{4,0},{5,1},{6,2},{7,3},{8,12},{9,13},{10,... | collective-permute-start | bytes 196616 | tf_op jit(solution)/shard_map/ppermute | solution.py:107
  9.6 5.1 %range_compress.1 = (bf16[2,64,16,128]{3,2,1,0:T(8,128)(2,1)}, s32[8,16]{1,0:T(8,128)}, s32[8,16]{1,0:T(8,128)}) custom-call(s32[64]{0:T(128)} %bitcast.7, s32[64]{0:T(128)} %bitcast.12, bf16[2,16,8192]{2,1,0:T(8,128)(2,1)} %bitcast.11, f32[2,8192]{1,0:T(2,128)} %refs_1_.1, bf16[128,128]{1,0:T(8,128)(2,1)} %constant.58.refs_2_, ...), custom_call_target="tpu_custom_call" | custom-call | flops 201326592 | bytes 1769472 | tf_op jit(solution)/shard_map/range_compress/pallas_call | solution.py:198
  14.8 0.9 %collective-permute-done.7 = bf16[4,2,32,128]{3,2,1,0:T(8,128)(2,1)S(1)} collective-permute-done((bf16[4,2,32,128]{3,2,1,0:T(8,128)(2,1)S(1)}, bf16[4,2,32,128]{3,2,1,0:T(8,128)(2,1)S(1)}, u32[]{:S(2)}, u32[]{:S(2)}) %collective-permute-start.7) | collective-permute-done | bytes 65568 | tf_op jit(solution)/shard_map/ppermute | solution.py:107
  15.7 2.5 %collective-permute-start.10 = (bf16[16,2,32,128]{3,2,1,0:T(8,128)(2,1)S(1)}, bf16[16,2,32,128]{3,2,1,0:T(8,128)(2,1)S(1)}, u32[]{:S(2)}, u32[]{:S(2)}) collective-permute-start(bf16[16,2,32,128]{3,2,1,0:T(8,128)(2,1)S(1)} %constant_dynamic-update-slice_fusion.rest_4_), channel_id=1, source_target_pairs={{0,24},{8,16},{16,8},{24,0},{1,25},{9,17},{17,9},{25,1},{2,26},{10... | collective-permute-start | bytes 786440 | tf_op jit(solution)/shard_map/ppermute | solution.py:107
  18.2 0.5 collective-permute-start.8
  18.8 0.5 collective-permute-start.9
  19.3 1.0 %copy-done.3 = bf16[2,64,16,128]{3,2,1,0:T(8,128)(2,1)S(1)} copy-done((bf16[2,64,16,128]{3,2,1,0:T(8,128)(2,1)S(1)}, bf16[2,64,16,128]{3,2,1,0:T(8,128)(2,1)}, u32[]{:S(2)}) %copy-start.3) | copy-done | bytes 524312
  20.3 0.7 copy-done.4
  21.0 0.8 %spread_columns.1 = (bf16[8,2,32,128]{3,2,1,0:T(8,128)(2,1)S(1)}, bf16[8,2,32,128]{3,2,1,0:T(8,128)(2,1)S(1)}, bf16[8,2,32,128]{3,2,1,0:T(8,128)(2,1)S(1)}, bf16...) custom-call(s32[8,16]{1,0:T(8,128)S(1)} %copy-done.4, ...), custom_call_target="tpu_custom_call" | custom-call | bytes 2097152 | tf_op jit(solution)/shard_map/spread_columns/pallas_call | solution.py:247
  21.8 0.9 %collective-permute-start.11 = (bf16[8,2,32,128]{3,2,1,0:T(8,128)(2,1)S(1)}, bf16[8,2,32,128]{3,2,1,0:T(8,128)(2,1)S(1)}, u32[]{:S(2)}, u32[]{:S(2)}) collective-permute-start(bf16[8,2,32,128]{3,2,1,0:T(8,128)(2,1)S(1)} %get-tuple-element.53), channel_id=1, source_target_pairs={{0,2},{1,3},{2,0},{3,1},{4,6},{5,7},{6,4},{7,5},{8,10},{9,11},{10,... | collective-permute-start | bytes 393224 | tf_op jit(solution)/shard_map/ppermute | solution.py:107
  22.8 2.6 %collective-permute-start.12 = (bf16[8,2,32,128]{3,2,1,0:T(8,128)(2,1)S(1)}, bf16[8,2,32,128]{3,2,1,0:T(8,128)(2,1)S(1)}, u32[]{:S(2)}, u32[]{:S(2)}) collective-permute-start(bf16[8,2,32,128]{3,2,1,0:T(8,128)(2,1)S(1)} %get-tuple-element.54), channel_id=1, source_target_pairs={{0,4},{1,5},{2,6},{3,7},{4,0},{5,1},{6,2},{7,3},{8,12},{9,13},{10,... | collective-permute-start | bytes 393224 | tf_op jit(solution)/shard_map/ppermute | solution.py:107
  25.4 0.6 collective-permute-done.10.rest_7_
  26.0 2.8 %collective-permute-start.13 = (bf16[8,2,32,128]{3,2,1,0:T(8,128)(2,1)S(1)}, bf16[8,2,32,128]{3,2,1,0:T(8,128)(2,1)S(1)}, u32[]{:S(2)}, u32[]{:S(2)}) collective-permute-start(bf16[8,2,32,128]{3,2,1,0:T(8,128)(2,1)S(1)} %get-tuple-element.55), channel_id=1, source_target_pairs={{0,6},{1,7},{2,4},{3,5},{4,2},{5,3},{6,0},{7,1},{8,14},{9,15},{10,... | collective-permute-start | bytes 393224 | tf_op jit(solution)/shard_map/ppermute | solution.py:107
  28.8 1.7 %collective-permute-done.8.rest_5_ = bf16[16,2,32,128]{3,2,1,0:T(8,128)(2,1)S(1)} collective-permute-done((bf16[16,2,32,128]{3,2,1,0:T(8,128)(2,1)S(1)}, bf16[16,2,32,128]{3,2,1,0:T(8,128)(2,1)S(1)}, u32[]{:S(2)}, u32[]{:S(2)}) %collective-permute-start.8) | collective-permute-done | bytes 262176 | tf_op jit(solution)/shard_map/ppermute | solution.py:107
  30.4 0.7 collective-permute-start.2
  31.1 3.5 %collective-permute-start.3 = (bf16[8,2,32,128]{3,2,1,0:T(8,128)(2,1)S(1)}, bf16[8,2,32,128]{3,2,1,0:T(8,128)(2,1)S(1)}, u32[]{:S(2)}, u32[]{:S(2)}) collective-permute-start(bf16[8,2,32,128]{3,2,1,0:T(8,128)(2,1)S(1)} %get-tuple-element.44), channel_id=1, source_target_pairs={{0,4},{1,5},{2,6},{3,7},{4,0},{5,1},{6,2},{7,3},{8,12},{9,13},{10,... | collective-permute-start | bytes 393224 | tf_op jit(solution)/shard_map/ppermute | solution.py:107
  34.6 0.2 collective-permute-start.4
  34.8 0.6 collective-permute-done.12.rest_2_
  35.5 0.7 copy-done.6
  36.1 1.8 %focus.3 = (bf16[2,2,128,128]{3,2,1,0:T(8,128)(2,1)S(1)}, bf16[2,2,128,128]{3,2,1,0:T(8,128)(2,1)S(1)}, bf16[2,2,128,128]{3,2,1,0:T(8,128)(2,1)S(1)}, bf16[2,2,128,128]{3,2,1,0:T(8,128)(2,1)S(1)}) custom-call(s32[2]{0:T(128)S(1)} %pad_add_fusion.place_ref, s32[8,16]{1,0:T(8,128)S(1)} %copy-done.6, s32[64]{0:T(128)S(1)} %bitcast.9, ...), custom_call_target="tpu_custom_call" | custom-call | flops 1073741824 | bytes 11010048 | tf_op jit(solution)/shard_map/focus/pallas_call | solution.py:364
  37.9 1.6 %collective-permute-start.14 = (bf16[2,2,128,128]{3,2,1,0:T(8,128)(2,1)S(1)}, bf16[2,2,128,128]{3,2,1,0:T(8,128)(2,1)S(1)}, u32[]{:S(2)}, u32[]{:S(2)}) collective-permute-start(bf16[2,2,128,128]{3,2,1,0:T(8,128)(2,1)S(1)} %get-tuple-element.56.rest_0_), channel_id=1, source_target_pairs={{0,16},{8,24},{16,0},{24,8},{1,17},{9,25},{17,1},{25,9},{2,18},{10... | collective-permute-start | bytes 393224 | tf_op jit(solution)/shard_map/ppermute | solution.py:107
  39.5 0.5 collective-permute-start.24
  40.0 1.5 %collective-permute-start.22 = (bf16[2,2,128,128]{3,2,1,0:T(8,128)(2,1)S(1)}, bf16[2,2,128,128]{3,2,1,0:T(8,128)(2,1)S(1)}, u32[]{:S(2)}, u32[]{:S(2)}) collective-permute-start(bf16[2,2,128,128]{3,2,1,0:T(8,128)(2,1)S(1)} %get-tuple-element.60.rest_2_), channel_id=1, source_target_pairs={{0,16},{8,24},{16,0},{24,8},{1,17},{9,25},{17,1},{25,9},{2,18},{10... | collective-permute-start | bytes 393224 | tf_op jit(solution)/shard_map/ppermute | solution.py:107
  41.5 5.1 %collective-permute-done.3.rest_2_ = bf16[8,2,32,128]{3,2,1,0:T(8,128)(2,1)S(1)} collective-permute-done((bf16[8,2,32,128]{3,2,1,0:T(8,128)(2,1)S(1)}, bf16[8,2,32,128]{3,2,1,0:T(8,128)(2,1)S(1)}, u32[]{:S(2)}, u32[]{:S(2)}) %collective-permute-start.3) | collective-permute-done | bytes 131104 | tf_op jit(solution)/shard_map/ppermute | solution.py:107
  46.7 1.5 %collective-permute-start.20 = (bf16[2,2,128,128]{3,2,1,0:T(8,128)(2,1)S(1)}, bf16[2,2,128,128]{3,2,1,0:T(8,128)(2,1)S(1)}, u32[]{:S(2)}, u32[]{:S(2)}) collective-permute-start(bf16[2,2,128,128]{3,2,1,0:T(8,128)(2,1)S(1)} %get-tuple-element.59.rest_1_), channel_id=1, source_target_pairs={{0,16},{8,24},{16,0},{24,8},{1,17},{9,25},{17,1},{25,9},{2,18},{10... | collective-permute-start | bytes 393224 | tf_op jit(solution)/shard_map/ppermute | solution.py:107
  48.2 1.2 %copy-done.10 = bf16[8,256,256]{2,1,0:T(8,128)(2,1)S(1)} copy-done((bf16[8,256,256]{2,1,0:T(8,128)(2,1)S(1)}, bf16[8,256,256]{2,1,0:T(8,128)(2,1)}, u32[]{:S(2)}) %copy-start.10) | copy-done | bytes 1048600
  49.4 1.8 %focus.2 = (bf16[4,2,128,128]{3,2,1,0:T(8,128)(2,1)S(1)}, bf16[4,2,128,128]{3,2,1,0:T(8,128)(2,1)S(1)}) custom-call(s32[2]{0:T(128)S(1)} %pad_add_fusion.place_ref, s32[8,16]{1,0:T(8,128)S(1)} %copy-done.7, s32[64]{0:T(128)S(1)} %bitcast.10, bf16[256,256]{1,0:T(8,128)(2,1)S(1)} %copy-done.1, bf16[8,256,256]{2,1,0:T(8,128)(2,1)S(1)} %copy-done.10, ...), custom_call_target="tpu_custom_call" | custom-call | flops 1073741824 | bytes 11010048 | tf_op jit(solution)/shard_map/focus/pallas_call | solution.py:364
  51.3 1.6 %collective-permute-start.15 = (bf16[2,2,128,128]{3,2,1,0:T(8,128)(2,1)S(1)}, bf16[2,2,128,128]{3,2,1,0:T(8,128)(2,1)S(1)}, u32[]{:S(2)}, u32[]{:S(2)}) collective-permute-start(bf16[2,2,128,128]{3,2,1,0:T(8,128)(2,1)S(1)} %broadcast_select_fusion.5), channel_id=1, source_target_pairs={{0,8},{8,0},{16,24},{24,16},{1,9},{9,1},{17,25},{25,17},{2,10},{10... | collective-permute-start | bytes 393224 | tf_op jit(solution)/shard_map/ppermute | solution.py:107
  52.9 0.6 collective-permute-start.25
  53.5 3.8 %collective-permute-done.15.rest_4_ = bf16[2,2,128,128]{3,2,1,0:T(8,128)(2,1)S(1)} collective-permute-done((bf16[2,2,128,128]{3,2,1,0:T(8,128)(2,1)S(1)}, bf16[2,2,128,128]{3,2,1,0:T(8,128)(2,1)S(1)}, u32[]{:S(2)}, u32[]{:S(2)}) %collective-permute-start.15) | collective-permute-done | bytes 131104 | tf_op jit(solution)/shard_map/ppermute | solution.py:107
  57.3 1.6 %collective-permute-start.23 = (bf16[2,2,128,128]{3,2,1,0:T(8,128)(2,1)S(1)}, bf16[2,2,128,128]{3,2,1,0:T(8,128)(2,1)S(1)}, u32[]{:S(2)}, u32[]{:S(2)}) collective-permute-start(bf16[2,2,128,128]{3,2,1,0:T(8,128)(2,1)S(1)} %broadcast_select_fusion.3), channel_id=1, source_target_pairs={{0,8},{8,0},{16,24},{24,16},{1,9},{9,1},{17,25},{25,17},{2,10},{10... | collective-permute-start | bytes 393224 | tf_op jit(solution)/shard_map/ppermute | solution.py:107
  58.8 2.0 %collective-permute-start.16 = (bf16[4,2,128,128]{3,2,1,0:T(8,128)(2,1)S(1)}, bf16[4,2,128,128]{3,2,1,0:T(8,128)(2,1)S(1)}, u32[]{:S(2)}, u32[]{:S(2)}) collective-permute-start(bf16[4,2,128,128]{3,2,1,0:T(8,128)(2,1)S(1)} %get-tuple-element.57.rest_0_), channel_id=1, source_target_pairs={{0,16},{8,24},{16,0},{24,8},{1,17},{9,25},{17,1},{25,9},{2,18},{10... | collective-permute-start | bytes 786440 | tf_op jit(solution)/shard_map/ppermute | solution.py:107
  60.9 0.6 collective-permute-start.21
  61.5 2.1 %collective-permute-done.18.rest_2_ = bf16[4,2,128,128]{3,2,1,0:T(8,128)(2,1)S(1)} collective-permute-done((bf16[4,2,128,128]{3,2,1,0:T(8,128)(2,1)S(1)}, bf16[4,2,128,128]{3,2,1,0:T(8,128)(2,1)S(1)}, u32[]{:S(2)}, u32[]{:S(2)}) %collective-permute-start.18) | collective-permute-done | bytes 262176 | tf_op jit(solution)/shard_map/ppermute | solution.py:107
  63.6 1.6 %collective-permute-start.19 = (bf16[4,2,128,128]{3,2,1,0:T(8,128)(2,1)S(1)}, bf16[4,2,128,128]{3,2,1,0:T(8,128)(2,1)S(1)}, u32[]{:S(2)}, u32[]{:S(2)}) collective-permute-start(bf16[4,2,128,128]{3,2,1,0:T(8,128)(2,1)S(1)} %broadcast_select_fusion), channel_id=1, source_target_pairs={{0,8},{8,0},{16,24},{24,16},{1,9},{9,1},{17,25},{25,17},{2,10},{10... | collective-permute-start | bytes 786440 | tf_op jit(solution)/shard_map/ppermute | solution.py:107
  65.2 1.2 %collective-permute-done.16.rest_2_ = bf16[4,2,128,128]{3,2,1,0:T(8,128)(2,1)S(1)} collective-permute-done((bf16[4,2,128,128]{3,2,1,0:T(8,128)(2,1)S(1)}, bf16[4,2,128,128]{3,2,1,0:T(8,128)(2,1)S(1)}, u32[]{:S(2)}, u32[]{:S(2)}) %collective-permute-start.16) | collective-permute-done | bytes 262176 | tf_op jit(solution)/shard_map/ppermute | solution.py:107
  66.5 1.6 %collective-permute-start.17 = (bf16[4,2,128,128]{3,2,1,0:T(8,128)(2,1)S(1)}, bf16[4,2,128,128]{3,2,1,0:T(8,128)(2,1)S(1)}, u32[]{:S(2)}, u32[]{:S(2)}) collective-permute-start(bf16[4,2,128,128]{3,2,1,0:T(8,128)(2,1)S(1)} %broadcast_select_fusion.1), channel_id=1, source_target_pairs={{0,8},{8,0},{16,24},{24,16},{1,9},{9,1},{17,25},{25,17},{2,10},{10... | collective-permute-start | bytes 786440 | tf_op jit(solution)/shard_map/ppermute | solution.py:107
  68.0 3.0 %goldstein.3.rest_7_ = bf16[16,2,2,128,128]{4,3,2,1,0:T(8,128)(2,1)} custom-call(bf16[2,2,128,128]{3,2,1,0:T(8,128)(2,1)S(1)} %get-tuple-element.56.rest_0_, bf16[2,2,128,128]{3,2,1,0:T(8,128)(2,1)S(1)} %get-tuple-element.59.rest_1_, bf16[2,2,128,128]{3,2,1,0:T(8,128)(2,1)S(1)} %get-tuple-element.60.rest_2_, ...), custom_call_target="tpu_custom_call" | custom-call | flops 1073741824 | bytes 3145728 | tf_op jit(solution)/shard_map/goldstein/pallas_call | solution.py:454
  71.0 0.7 collective-permute-done.19.rest_1_
  71.8 2.1 %goldstein.4.rest_7_ = bf16[16,2,2,128,128]{4,3,2,1,0:T(8,128)(2,1)} custom-call(bf16[4,2,128,128]{3,2,1,0:T(8,128)(2,1)S(1)} %get-tuple-element.58.rest_0_, bf16[4,2,128,128]{3,2,1,0:T(8,128)(2,1)S(1)} %collective-permute-done.19.rest_1_, bf16[4,2,128,128]{3,2,1,0:T(8,128)(2,1)S(1)} %collective-permute-done.18.rest_2_, ...), custom_call_target="tpu_custom_call", output_to_operand_aliasing={{}: (7, {})} | custom-call | flops 536870912 | bytes 3932160 | tf_op jit(solution)/shard_map/goldstein/pallas_call | solution.py:454
  73.8 0.7 collective-permute-done.17.rest_1_
  74.6 2.1 %goldstein.5 = bf16[16,2,2,128,128]{4,3,2,1,0:T(8,128)(2,1)} custom-call(bf16[4,2,128,128]{3,2,1,0:T(8,128)(2,1)S(1)} %get-tuple-element.57.rest_0_, bf16[4,2,128,128]{3,2,1,0:T(8,128)(2,1)S(1)} %collective-permute-done.17.rest_1_, bf16[4,2,128,128]{3,2,1,0:T(8,128)(2,1)S(1)} %collective-permute-done.16.rest_2_, ...), custom_call_target="tpu_custom_call", output_to_operand_aliasing={{}: (7, {})} | custom-call | flops 536870912 | bytes 3932160 | tf_op jit(solution)/shard_map/goldstein/pallas_call | solution.py:454
  (46 shorter events, 0.4 us)
Async XLA Ops:
  0.0 1.0 %copy-start = (bf16[2,128,1024]{2,1,0:T(8,128)(2,1)S(1)}, bf16[2,128,1024]{2,1,0:T(8,128)(2,1)}, u32[]{:S(2)}) copy-start(bf16[2,128,1024]{2,1,0:T(8,128)(2,1)} %param.27) | copy-start | bytes 1572868
  0.0 35.5 %copy-start.1 = (bf16[256,256]{1,0:T(8,128)(2,1)S(1)}, bf16[256,256]{1,0:T(8,128)(2,1)}, u32[]{:S(2)}) copy-start(bf16[256,256]{1,0:T(8,128)(2,1)} %constant.60.forward_ref.rest_12_.rest_15_.rest_3_.rest_6_) | copy-start | bytes 393220
  0.0 35.5 %copy-start.8 = (s32[1,64]{1,0:T(1,128)S(1)}, s32[1,64]{1,0:T(1,128)}, u32[]{:S(2)}) copy-start(s32[1,64]{1,0:T(1,128)} %param.30) | copy-start | bytes 772
  1.1 1.5 %collective-permute-start = (bf16[2,32,1024]{2,1,0:T(8,128)(2,1)S(1)}, bf16[2,32,1024]{2,1,0:T(8,128)(2,1)S(1)}, u32[]{:S(2)}, u32[]{:S(2)}) collective-permute-start(bf16[2,32,1024]{2,1,0:T(8,128)(2,1)S(1)} %constant_dynamic-slice_fusion.rest_0_), channel_id=1, source_target_pairs={{0,1},{1,0},{2,3},{3,2},{4,5},{5,4},{6,7},{7,6},{8,9},{9,8},{10,11... | collective-permute-start | bytes 393224 | tf_op jit(solution)/shard_map/ppermute | solution.py:107
  2.6 0.7 copy-start.5
  3.2 32.2 %copy-start.9 = (bf16[8,256,256]{2,1,0:T(8,128)(2,1)S(1)}, bf16[8,256,256]{2,1,0:T(8,128)(2,1)}, u32[]{:S(2)}) copy-start(bf16[8,256,256]{2,1,0:T(8,128)(2,1)} %constant.61.back_ref) | copy-start | bytes 3145732
  4.0 10.8 %collective-permute-start.5 = (bf16[4,2,32,128]{3,2,1,0:T(8,128)(2,1)S(1)}, bf16[4,2,32,128]{3,2,1,0:T(8,128)(2,1)S(1)}, u32[]{:S(2)}, u32[]{:S(2)}) collective-permute-start(bf16[4,2,32,128]{3,2,1,0:T(8,128)(2,1)S(1)} %get-tuple-element.47), channel_id=1, source_target_pairs={{0,2},{1,3},{2,0},{3,1},{4,6},{5,7},{6,4},{7,5},{8,10},{9,11},{10,... | collective-permute-start | bytes 196616 | tf_op jit(solution)/shard_map/ppermute | solution.py:107
  7.0 7.8 %collective-permute-start.6 = (bf16[4,2,32,128]{3,2,1,0:T(8,128)(2,1)S(1)}, bf16[4,2,32,128]{3,2,1,0:T(8,128)(2,1)S(1)}, u32[]{:S(2)}, u32[]{:S(2)}) collective-permute-start(bf16[4,2,32,128]{3,2,1,0:T(8,128)(2,1)S(1)} %get-tuple-element.48), channel_id=1, source_target_pairs={{0,4},{1,5},{2,6},{3,7},{4,0},{5,1},{6,2},{7,3},{8,12},{9,13},{10,... | collective-permute-start | bytes 196616 | tf_op jit(solution)/shard_map/ppermute | solution.py:107
  9.6 6.2 %collective-permute-start.7 = (bf16[4,2,32,128]{3,2,1,0:T(8,128)(2,1)S(1)}, bf16[4,2,32,128]{3,2,1,0:T(8,128)(2,1)S(1)}, u32[]{:S(2)}, u32[]{:S(2)}) collective-permute-start(bf16[4,2,32,128]{3,2,1,0:T(8,128)(2,1)S(1)} %get-tuple-element.49), channel_id=1, source_target_pairs={{0,6},{1,7},{2,4},{3,5},{4,2},{5,3},{6,0},{7,1},{8,14},{9,15},{10,... | collective-permute-start | bytes 196616 | tf_op jit(solution)/shard_map/ppermute | solution.py:107
  14.7 4.6 %collective-permute-start.1 = (bf16[2,64,16,128]{3,2,1,0:T(8,128)(2,1)}, bf16[2,64,16,128]{3,2,1,0:T(8,128)(2,1)S(1)}, u32[]{:S(2)}, u32[]{:S(2)}) collective-permute-start(bf16[2,64,16,128]{3,2,1,0:T(8,128)(2,1)} %get-tuple-element.41.rest_0_), channel_id=1, source_target_pairs={{0,1},{1,0},{2,3},{3,2},{4,5},{5,4},{6,7},{7,6},{8,9},{9,8},{10,11... | collective-permute-start | bytes 1572872 | tf_op jit(solution)/shard_map/ppermute | solution.py:107
  15.7 10.2 %collective-permute-start.10 = (bf16[16,2,32,128]{3,2,1,0:T(8,128)(2,1)S(1)}, bf16[16,2,32,128]{3,2,1,0:T(8,128)(2,1)S(1)}, u32[]{:S(2)}, u32[]{:S(2)}) collective-permute-start(bf16[16,2,32,128]{3,2,1,0:T(8,128)(2,1)S(1)} %constant_dynamic-update-slice_fusion.rest_4_), channel_id=1, source_target_pairs={{0,24},{8,16},{16,8},{24,0},{1,25},{9,17},{17,9},{25,1},{2,26},{10... | collective-permute-start | bytes 786440 | tf_op jit(solution)/shard_map/ppermute | solution.py:107
  18.2 12.2 %collective-permute-start.8 = (bf16[16,2,32,128]{3,2,1,0:T(8,128)(2,1)S(1)}, bf16[16,2,32,128]{3,2,1,0:T(8,128)(2,1)S(1)}, u32[]{:S(2)}, u32[]{:S(2)}) collective-permute-start(bf16[16,2,32,128]{3,2,1,0:T(8,128)(2,1)S(1)} %constant_dynamic-update-slice_fusion.rest_4_), channel_id=1, source_target_pairs={{0,8},{8,0},{16,24},{24,16},{1,9},{9,1},{17,25},{25,17},{2,10},{10... | collective-permute-start | bytes 786440 | tf_op jit(solution)/shard_map/ppermute | solution.py:107
  18.8 12.3 %collective-permute-start.9 = (bf16[16,2,32,128]{3,2,1,0:T(8,128)(2,1)S(1)}, bf16[16,2,32,128]{3,2,1,0:T(8,128)(2,1)S(1)}, u32[]{:S(2)}, u32[]{:S(2)}) collective-permute-start(bf16[16,2,32,128]{3,2,1,0:T(8,128)(2,1)S(1)} %constant_dynamic-update-slice_fusion.rest_4_), channel_id=1, source_target_pairs={{0,16},{8,24},{16,0},{24,8},{1,17},{9,25},{17,1},{25,9},{2,18},{10... | collective-permute-start | bytes 786440 | tf_op jit(solution)/shard_map/ppermute | solution.py:107
  19.3 1.0 %copy-start.3 = (bf16[2,64,16,128]{3,2,1,0:T(8,128)(2,1)S(1)}, bf16[2,64,16,128]{3,2,1,0:T(8,128)(2,1)}, u32[]{:S(2)}) copy-start(bf16[2,64,16,128]{3,2,1,0:T(8,128)(2,1)} %get-tuple-element.41.rest_0_) | copy-start | bytes 1572868
  20.3 0.7 copy-start.4
  21.8 26.4 %copy-start.7 = (s32[8,16]{1,0:T(8,128)S(1)}, s32[8,16]{1,0:T(8,128)}, u32[]{:S(2)}) copy-start(s32[8,16]{1,0:T(8,128)} %get-tuple-element.39.table_ref) | copy-start | bytes 1540
  21.8 12.8 %collective-permute-start.11 = (bf16[8,2,32,128]{3,2,1,0:T(8,128)(2,1)S(1)}, bf16[8,2,32,128]{3,2,1,0:T(8,128)(2,1)S(1)}, u32[]{:S(2)}, u32[]{:S(2)}) collective-permute-start(bf16[8,2,32,128]{3,2,1,0:T(8,128)(2,1)S(1)} %get-tuple-element.53), channel_id=1, source_target_pairs={{0,2},{1,3},{2,0},{3,1},{4,6},{5,7},{6,4},{7,5},{8,10},{9,11},{10,... | collective-permute-start | bytes 393224 | tf_op jit(solution)/shard_map/ppermute | solution.py:107
  22.8 12.7 %collective-permute-start.12 = (bf16[8,2,32,128]{3,2,1,0:T(8,128)(2,1)S(1)}, bf16[8,2,32,128]{3,2,1,0:T(8,128)(2,1)S(1)}, u32[]{:S(2)}, u32[]{:S(2)}) collective-permute-start(bf16[8,2,32,128]{3,2,1,0:T(8,128)(2,1)S(1)} %get-tuple-element.54), channel_id=1, source_target_pairs={{0,4},{1,5},{2,6},{3,7},{4,0},{5,1},{6,2},{7,3},{8,12},{9,13},{10,... | collective-permute-start | bytes 393224 | tf_op jit(solution)/shard_map/ppermute | solution.py:107
  26.0 9.5 %collective-permute-start.13 = (bf16[8,2,32,128]{3,2,1,0:T(8,128)(2,1)S(1)}, bf16[8,2,32,128]{3,2,1,0:T(8,128)(2,1)S(1)}, u32[]{:S(2)}, u32[]{:S(2)}) collective-permute-start(bf16[8,2,32,128]{3,2,1,0:T(8,128)(2,1)S(1)} %get-tuple-element.55), channel_id=1, source_target_pairs={{0,6},{1,7},{2,4},{3,5},{4,2},{5,3},{6,0},{7,1},{8,14},{9,15},{10,... | collective-permute-start | bytes 393224 | tf_op jit(solution)/shard_map/ppermute | solution.py:107
  30.4 9.6 %collective-permute-start.2 = (bf16[8,2,32,128]{3,2,1,0:T(8,128)(2,1)S(1)}, bf16[8,2,32,128]{3,2,1,0:T(8,128)(2,1)S(1)}, u32[]{:S(2)}, u32[]{:S(2)}) collective-permute-start(bf16[8,2,32,128]{3,2,1,0:T(8,128)(2,1)S(1)} %get-tuple-element.43), channel_id=1, source_target_pairs={{0,2},{1,3},{2,0},{3,1},{4,6},{5,7},{6,4},{7,5},{8,10},{9,11},{10,... | collective-permute-start | bytes 393224 | tf_op jit(solution)/shard_map/ppermute | solution.py:107
  31.1 15.6 %collective-permute-start.3 = (bf16[8,2,32,128]{3,2,1,0:T(8,128)(2,1)S(1)}, bf16[8,2,32,128]{3,2,1,0:T(8,128)(2,1)S(1)}, u32[]{:S(2)}, u32[]{:S(2)}) collective-permute-start(bf16[8,2,32,128]{3,2,1,0:T(8,128)(2,1)S(1)} %get-tuple-element.44), channel_id=1, source_target_pairs={{0,4},{1,5},{2,6},{3,7},{4,0},{5,1},{6,2},{7,3},{8,12},{9,13},{10,... | collective-permute-start | bytes 393224 | tf_op jit(solution)/shard_map/ppermute | solution.py:107
  34.6 13.6 %collective-permute-start.4 = (bf16[8,2,32,128]{3,2,1,0:T(8,128)(2,1)S(1)}, bf16[8,2,32,128]{3,2,1,0:T(8,128)(2,1)S(1)}, u32[]{:S(2)}, u32[]{:S(2)}) collective-permute-start(bf16[8,2,32,128]{3,2,1,0:T(8,128)(2,1)S(1)} %get-tuple-element.45), channel_id=1, source_target_pairs={{0,6},{1,7},{2,4},{3,5},{4,2},{5,3},{6,0},{7,1},{8,14},{9,15},{10,... | collective-permute-start | bytes 393224 | tf_op jit(solution)/shard_map/ppermute | solution.py:107
  35.5 0.7 copy-start.6
  37.9 13.3 %collective-permute-start.14 = (bf16[2,2,128,128]{3,2,1,0:T(8,128)(2,1)S(1)}, bf16[2,2,128,128]{3,2,1,0:T(8,128)(2,1)S(1)}, u32[]{:S(2)}, u32[]{:S(2)}) collective-permute-start(bf16[2,2,128,128]{3,2,1,0:T(8,128)(2,1)S(1)} %get-tuple-element.56.rest_0_), channel_id=1, source_target_pairs={{0,16},{8,24},{16,0},{24,8},{1,17},{9,25},{17,1},{25,9},{2,18},{10... | collective-permute-start | bytes 393224 | tf_op jit(solution)/shard_map/ppermute | solution.py:107
  39.5 13.3 %collective-permute-start.24 = (bf16[2,2,128,128]{3,2,1,0:T(8,128)(2,1)S(1)}, bf16[2,2,128,128]{3,2,1,0:T(8,128)(2,1)S(1)}, u32[]{:S(2)}, u32[]{:S(2)}) collective-permute-start(bf16[2,2,128,128]{3,2,1,0:T(8,128)(2,1)S(1)} %get-tuple-element.61.rest_3_), channel_id=1, source_target_pairs={{0,16},{8,24},{16,0},{24,8},{1,17},{9,25},{17,1},{25,9},{2,18},{10... | collective-permute-start | bytes 393224 | tf_op jit(solution)/shard_map/ppermute | solution.py:107
  40.0 17.2 %collective-permute-start.22 = (bf16[2,2,128,128]{3,2,1,0:T(8,128)(2,1)S(1)}, bf16[2,2,128,128]{3,2,1,0:T(8,128)(2,1)S(1)}, u32[]{:S(2)}, u32[]{:S(2)}) collective-permute-start(bf16[2,2,128,128]{3,2,1,0:T(8,128)(2,1)S(1)} %get-tuple-element.60.rest_2_), channel_id=1, source_target_pairs={{0,16},{8,24},{16,0},{24,8},{1,17},{9,25},{17,1},{25,9},{2,18},{10... | collective-permute-start | bytes 393224 | tf_op jit(solution)/shard_map/ppermute | solution.py:107
  46.7 14.2 %collective-permute-start.20 = (bf16[2,2,128,128]{3,2,1,0:T(8,128)(2,1)S(1)}, bf16[2,2,128,128]{3,2,1,0:T(8,128)(2,1)S(1)}, u32[]{:S(2)}, u32[]{:S(2)}) collective-permute-start(bf16[2,2,128,128]{3,2,1,0:T(8,128)(2,1)S(1)} %get-tuple-element.59.rest_1_), channel_id=1, source_target_pairs={{0,16},{8,24},{16,0},{24,8},{1,17},{9,25},{17,1},{25,9},{2,18},{10... | collective-permute-start | bytes 393224 | tf_op jit(solution)/shard_map/ppermute | solution.py:107
  48.2 1.2 %copy-start.10 = (bf16[8,256,256]{2,1,0:T(8,128)(2,1)S(1)}, bf16[8,256,256]{2,1,0:T(8,128)(2,1)}, u32[]{:S(2)}) copy-start(bf16[8,256,256]{2,1,0:T(8,128)(2,1)} %constant.61.back_ref) | copy-start | bytes 3145732
  51.2 16.8 %copy-start.2 = (bf16[256,256]{1,0:T(8,128)(2,1)S(1)}, bf16[256,256]{1,0:T(8,128)(2,1)}, u32[]{:S(2)}) copy-start(bf16[256,256]{1,0:T(8,128)(2,1)} %constant.62.rest_13_.rest_14_.rest_4_.rest_5_) | copy-start | bytes 393220
  51.3 6.0 %collective-permute-start.15 = (bf16[2,2,128,128]{3,2,1,0:T(8,128)(2,1)S(1)}, bf16[2,2,128,128]{3,2,1,0:T(8,128)(2,1)S(1)}, u32[]{:S(2)}, u32[]{:S(2)}) collective-permute-start(bf16[2,2,128,128]{3,2,1,0:T(8,128)(2,1)S(1)} %broadcast_select_fusion.5), channel_id=1, source_target_pairs={{0,8},{8,0},{16,24},{24,16},{1,9},{9,1},{17,25},{25,17},{2,10},{10... | collective-permute-start | bytes 393224 | tf_op jit(solution)/shard_map/ppermute | solution.py:107
  52.9 15.2 %collective-permute-start.25 = (bf16[2,2,128,128]{3,2,1,0:T(8,128)(2,1)S(1)}, bf16[2,2,128,128]{3,2,1,0:T(8,128)(2,1)S(1)}, u32[]{:S(2)}, u32[]{:S(2)}) collective-permute-start(bf16[2,2,128,128]{3,2,1,0:T(8,128)(2,1)S(1)} %broadcast_select_fusion.2), channel_id=1, source_target_pairs={{0,8},{8,0},{16,24},{24,16},{1,9},{9,1},{17,25},{25,17},{2,10},{10... | collective-permute-start | bytes 393224 | tf_op jit(solution)/shard_map/ppermute | solution.py:107
  57.2 6.4 %collective-permute-start.18 = (bf16[4,2,128,128]{3,2,1,0:T(8,128)(2,1)S(1)}, bf16[4,2,128,128]{3,2,1,0:T(8,128)(2,1)S(1)}, u32[]{:S(2)}, u32[]{:S(2)}) collective-permute-start(bf16[4,2,128,128]{3,2,1,0:T(8,128)(2,1)S(1)} %get-tuple-element.58.rest_0_), channel_id=1, source_target_pairs={{0,16},{8,24},{16,0},{24,8},{1,17},{9,25},{17,1},{25,9},{2,18},{10... | collective-permute-start | bytes 786440 | tf_op jit(solution)/shard_map/ppermute | solution.py:107
  57.3 10.7 %collective-permute-start.23 = (bf16[2,2,128,128]{3,2,1,0:T(8,128)(2,1)S(1)}, bf16[2,2,128,128]{3,2,1,0:T(8,128)(2,1)S(1)}, u32[]{:S(2)}, u32[]{:S(2)}) collective-permute-start(bf16[2,2,128,128]{3,2,1,0:T(8,128)(2,1)S(1)} %broadcast_select_fusion.3), channel_id=1, source_target_pairs={{0,8},{8,0},{16,24},{24,16},{1,9},{9,1},{17,25},{25,17},{2,10},{10... | collective-permute-start | bytes 393224 | tf_op jit(solution)/shard_map/ppermute | solution.py:107
  58.8 7.6 %collective-permute-start.16 = (bf16[4,2,128,128]{3,2,1,0:T(8,128)(2,1)S(1)}, bf16[4,2,128,128]{3,2,1,0:T(8,128)(2,1)S(1)}, u32[]{:S(2)}, u32[]{:S(2)}) collective-permute-start(bf16[4,2,128,128]{3,2,1,0:T(8,128)(2,1)S(1)} %get-tuple-element.57.rest_0_), channel_id=1, source_target_pairs={{0,16},{8,24},{16,0},{24,8},{1,17},{9,25},{17,1},{25,9},{2,18},{10... | collective-permute-start | bytes 786440 | tf_op jit(solution)/shard_map/ppermute | solution.py:107
  60.9 7.1 %collective-permute-start.21 = (bf16[2,2,128,128]{3,2,1,0:T(8,128)(2,1)S(1)}, bf16[2,2,128,128]{3,2,1,0:T(8,128)(2,1)S(1)}, u32[]{:S(2)}, u32[]{:S(2)}) collective-permute-start(bf16[2,2,128,128]{3,2,1,0:T(8,128)(2,1)S(1)} %broadcast_select_fusion.4), channel_id=1, source_target_pairs={{0,8},{8,0},{16,24},{24,16},{1,9},{9,1},{17,25},{25,17},{2,10},{10... | collective-permute-start | bytes 393224 | tf_op jit(solution)/shard_map/ppermute | solution.py:107
  63.6 8.1 %collective-permute-start.19 = (bf16[4,2,128,128]{3,2,1,0:T(8,128)(2,1)S(1)}, bf16[4,2,128,128]{3,2,1,0:T(8,128)(2,1)S(1)}, u32[]{:S(2)}, u32[]{:S(2)}) collective-permute-start(bf16[4,2,128,128]{3,2,1,0:T(8,128)(2,1)S(1)} %broadcast_select_fusion), channel_id=1, source_target_pairs={{0,8},{8,0},{16,24},{24,16},{1,9},{9,1},{17,25},{25,17},{2,10},{10... | collective-permute-start | bytes 786440 | tf_op jit(solution)/shard_map/ppermute | solution.py:107
  66.5 8.1 %collective-permute-start.17 = (bf16[4,2,128,128]{3,2,1,0:T(8,128)(2,1)S(1)}, bf16[4,2,128,128]{3,2,1,0:T(8,128)(2,1)S(1)}, u32[]{:S(2)}, u32[]{:S(2)}) collective-permute-start(bf16[4,2,128,128]{3,2,1,0:T(8,128)(2,1)S(1)} %broadcast_select_fusion.1), channel_id=1, source_target_pairs={{0,8},{8,0},{16,24},{24,16},{1,9},{9,1},{17,25},{25,17},{2,10},{10... | collective-permute-start | bytes 786440 | tf_op jit(solution)/shard_map/ppermute | solution.py:107

commit v4 on v3

--- a/solution.py
+++ b/solution.py
@@ -13,7 +13,6 @@
 BF = jnp.bfloat16
 F32 = jnp.float32
 MIB = 1024 * 1024
-K1_MIB = 56
 
 
 def dft(rows, cols, size, sign, scale):
@@ -112,21 +111,22 @@
     return lax.ppermute(value, axis, [(i, (i + steps) % count) for i in range(count)])
 
 
-def range_compress(echo, reference, owners, slots, plan):
-    _, pulses, samples = echo.shape
+def range_compress(real, imag, info, plan):
+    pulses, samples = real.shape
     shards, capacity, most, group, group_columns = plan
-    total = owners.shape[0]
+    total = shards * group
     outer = samples // BLK
-    first = const(dft(outer, outer, outer, 1, 1.0 / math.sqrt(outer)))
-    second = const(dft(outer, BLK, outer, 1, 1.0 / math.sqrt(BLK)))
+    first = dft(outer, outer, outer, 1, 1.0 / math.sqrt(outer))
+    second = dft(outer, BLK, outer, 1, 1.0 / math.sqrt(BLK))
     phase = np.outer(np.arange(BLK), np.arange(BLK)) % samples
     angle = 2.0 * np.pi / samples * phase
-    turn = jnp.asarray(np.stack([np.cos(angle), np.sin(angle)]).astype(np.float32))
+    first = np.pad(first, ((0, 0), (0, BLK - 2 * outer)))
+    rows = [np.cos(angle), np.sin(angle), first, second[:, :BLK], second[:, BLK:]]
+    tables = jnp.asarray(np.concatenate(rows).astype(np.float32))
     spread = BLK // outer
-    operands = [echo, reference, first, second, turn]
     smem = pl.BlockSpec(memory_space=pltpu.SMEM)
 
-    def arrange(owner_ref, slot_ref, block_ref, place_ref, count_ref):
+    def arrange(info_ref, block_ref, place_ref, count_ref):
         for o in range(shards):
             for w in range(capacity):
                 block_ref[o, w] = 0
@@ -134,43 +134,35 @@
             for g in range(shards):
                 count_ref[g, o] = 0
         for b in range(total):
-            owner = owner_ref[b]
+            owner = info_ref[b]
             rank = count_ref[b // group, owner]
             count_ref[b // group, owner] = rank + 1
-            slot = slot_ref[b]
+            slot = info_ref[total + b]
             block_ref[owner, slot] = (b + 1) * most + rank
             place_ref[owner, slot] = b // group * group_columns + b % group % group_columns
 
-    def kernel(owner_ref, slot_ref, *refs):
-        count = len(operands)
-        out_ref, block_ref, place_ref = refs[count : count + 3]
-        local = refs[count + 3 : 2 * count + 3]
-        x_re, x_im, y_re, y_im, sems, count_ref = refs[2 * count + 3 :]
-        copies = [
-            pltpu.make_async_copy(refs[i], local[i], sems.at[i]) for i in range(count)
-        ]
-        for copy in copies:
-            copy.start()
-        arrange(owner_ref, slot_ref, block_ref, place_ref, count_ref)
-        for copy in copies:
-            copy.wait()
-        echo_ref, ref_ref, first_ref, second_ref, turn_ref = local
+    def kernel(info_ref, real_ref, imag_ref, tables_ref, *rest):
+        out_ref, block_ref, place_ref, x_re, x_im, y_re, y_im, count_ref = rest
+        arrange(info_ref, block_ref, place_ref, count_ref)
+        at = 2 * BLK
+        first_table = tables_ref[at : at + 2 * outer, : 2 * outer].astype(BF)
+        at += 2 * outer
+        second_table = jnp.concatenate(
+            [tables_ref[at : at + 2 * outer, :], tables_ref[at + 2 * outer : at + 4 * outer, :]],
+            axis=1,
+        ).astype(BF)
         for j in range(outer):
             lanes = slice(j * BLK, (j + 1) * BLK)
-            a = echo_ref[0, :, lanes].astype(F32)
-            b = echo_ref[1, :, lanes].astype(F32)
-            c = ref_ref[0:1, lanes]
-            d = ref_ref[1:2, lanes]
-            x_re[pl.ds(j, pulses, stride=outer), :] = a * c + b * d
-            x_im[pl.ds(j, pulses, stride=outer), :] = b * c - a * d
-        turn_c = turn_ref[0]
-        turn_s = turn_ref[1]
+            x_re[pl.ds(j, pulses, stride=outer), :] = real_ref[:, lanes].astype(F32)
+            x_im[pl.ds(j, pulses, stride=outer), :] = imag_ref[:, lanes].astype(F32)
+        turn_c = tables_ref[:BLK, :]
+        turn_s = tables_ref[BLK : 2 * BLK, :]
         for q in range(pulses // 2):
             pair = []
             for p in (2 * q, 2 * q + 1):
                 rows = slice(p * outer, (p + 1) * outer)
                 pair.append(jnp.concatenate([x_re[rows, :], x_im[rows, :]], axis=0))
-            section = mm(first_ref[...], jnp.concatenate(pair, axis=1).astype(BF))
+            section = mm(first_table, jnp.concatenate(pair, axis=1).astype(BF))
             turned = []
             for p in range(2):
                 lanes = slice(p * BLK, (p + 1) * BLK)
@@ -183,7 +175,7 @@
                 )
             turned = jnp.concatenate(turned, axis=0).astype(BF)
             done = lax.dot_general(
-                second_ref[...], turned, (((1,), (1,)), ((), ())), preferred_element_type=F32
+                second_table, turned, (((1,), (1,)), ((), ())), preferred_element_type=F32
             )
             for p in range(2):
                 lanes = slice(p * BLK, (p + 1) * BLK)
@@ -202,34 +194,32 @@
             jax.ShapeDtypeStruct((shards, capacity), jnp.int32),
             jax.ShapeDtypeStruct((shards, capacity), jnp.int32),
         ],
-        in_specs=[smem] * 2 + [pl.BlockSpec(memory_space=pl.ANY)] * len(operands),
+        in_specs=[smem] + whole(3),
         out_specs=[pl.BlockSpec(memory_space=pltpu.VMEM), smem, smem],
-        scratch_shapes=[pltpu.VMEM(a.shape, a.dtype) for a in operands]
-        + [pltpu.VMEM((pulses * outer, BLK), F32)] * 4
+        scratch_shapes=[pltpu.VMEM((pulses * outer, BLK), F32)] * 4
         + [
-            pltpu.SemaphoreType.DMA((len(operands),)),
             pltpu.SMEM((shards, shards), jnp.int32),
         ],
-        compiler_params=params(K1_MIB),
+        compiler_params=params(16),
         cost_estimate=cost(
-            pulses * 4 * BLK * outer * (outer + BLK), [echo, echo, echo, reference, turn]
+            pulses * 4 * BLK * outer * (outer + BLK), [real] * 6 + [tables]
         ),
         name="range_compress",
-    )(owners, slots, *operands)
-
-
-def spread_columns(parts, table, place, sizes, plan):
+    )(info, real, imag, tables)
+
+
+def spread_columns(parts, table, info, sizes, plan):
     _, _, pulses, _ = parts[0].shape
     cores = len(parts)
     shards, capacity, most, group, group_columns = plan
     chips = shards // cores
     chunks = len(sizes)
 
-    def kernel(table_ref, place_ref, *rest):
+    def kernel(table_ref, info_ref, *rest):
         part_refs = rest[:cores]
         outs = rest[cores:]
-        chip = place_ref[0] // cores
-        core = place_ref[0] % cores
+        chip = info_ref[3 * shards * group] // cores
+        core = info_ref[3 * shards * group] % cores
         for chunk in range(chunks):
             for k in range(chips):
                 owner = target_of(chip, k, chips) * cores + core
@@ -252,29 +242,29 @@
         compiler_params=params(16),
         cost_estimate=cost(0, [*parts] * 2),
         name="spread_columns",
-    )(table, place, *parts)
+    )(table, info, *parts)
     return [outs[chunk * chips : (chunk + 1) * chips] for chunk in range(chunks)]
 
 
-def filter_columns(parts, owners, place, plan):
+def filter_columns(parts, info, plan):
     _, rows, columns = parts[0].shape
     cores = len(parts)
     shards, _, most, group, group_columns = plan
     chips = shards // cores
 
-    def kernel(owner_ref, place_ref, *rest):
+    def kernel(info_ref, *rest):
         part_refs = rest[:cores]
         outs = rest[cores : cores + chips]
         column_ref, count_ref = rest[cores + chips :]
-        chip = place_ref[0] // cores
-        core = place_ref[0] % cores
+        chip = info_ref[3 * shards * group] // cores
+        core = info_ref[3 * shards * group] % cores
         for c in range(cores):
             for o in range(shards):
                 count_ref[c, o] = 0
                 for r in range(most):
                     column_ref[c, o * most + r] = 0
             for b in range(group):
-                owner = owner_ref[(chip * cores + c) * group + b]
+                owner = info_ref[(chip * cores + c) * group + b]
                 rank = count_ref[c, owner]
                 count_ref[c, owner] = rank + 1
                 column_ref[c, owner * most + rank] = b % group_columns
@@ -293,7 +283,7 @@
     return pl.pallas_call(
         kernel,
         out_shape=[piece] * chips,
-        in_specs=[smem, smem] + whole(cores),
+        in_specs=[smem] + whole(cores),
         out_specs=whole(chips),
         scratch_shapes=[
             pltpu.SMEM((cores, shards * most), jnp.int32),
@@ -302,37 +292,41 @@
         compiler_params=params(16),
         cost_estimate=cost(0, [*parts] * 2),
         name="filter_columns",
-    )(owners, place, *parts)
-
-
-def focus(pieces, filters, place, table, kinds, start, cores, sizes, plan):
+    )(info, *parts)
+
+
+def focus(pieces, filters, table, info, start, cores, sizes, plan, flip):
     each, _, share, _ = pieces[0].shape
     chips = len(pieces)
     dates = len(filters)
     pulses = share * chips
     rows = filters[0].shape[-2]
     forward = const(dft(pulses, pulses, pulses, -1, 1.0 / math.sqrt(pulses)))
-    back = const(resample_table(pulses))
-
-    _, _, most, group, group_columns = plan
-
-    def kernel(place_ref, table_ref, kind_ref, forward_ref, back_ref, *rest):
+    back = resample_table(pulses)
+    last = len(back) - 1
+    back = const(back[::-1] if flip else back)
+
+    shards, _, most, group, group_columns = plan
+
+    def kernel(info_ref, table_ref, forward_ref, back_ref, *rest):
         piece_refs = rest[:chips]
         filter_refs = rest[chips : chips + dates]
         outs = rest[chips + dates : chips + dates + len(sizes)]
         col, fil = rest[chips + dates + len(sizes) :]
         homes = [(i, s) for i, size in enumerate(sizes) for s in range(size)]
-        chip = place_ref[0] // cores
+        chip = info_ref[3 * shards * group] // cores
         entries, table_rows, valid = [], [], []
         for s in range(each):
-            code = table_ref[place_ref[0], start + s]
+            code = table_ref[info_ref[3 * shards * group], start + s]
             block = code // most - 1
             valid.append(block >= 0)
             block = jnp.maximum(block, 0)
             sender = block // group
             step = step_from(chip, sender // cores, chips)
             entries.append((step * cores + sender % cores) * most + code % most)
-            table_rows.append(kind_ref[block] * (pulses // BLK) + block % group // group_columns)
+            row = info_ref[2 * shards * group + block] * (pulses // BLK)
+            row = row + block % group // group_columns
+            table_rows.append(last - row if flip else row)
         for k in range(chips):
             source = source_of(chip, k, chips)
             at = pl.multiple_of(source * share, share)
@@ -340,7 +334,7 @@
                 for part in range(2):
                     col[s, part, pl.ds(at, share), :] = piece_refs[k][s, part]
         for e in range(dates):
-            at = pl.multiple_of(source_of(place_ref[1], e, dates) * rows, rows)
+            at = pl.multiple_of(source_of(info_ref[3 * shards * group + 1], e, dates) * rows, rows)
             for s in range(each):
                 for part in range(2):
                     fil[s, part, pl.ds(at, rows), :] = filter_refs[e][entries[s], part]
@@ -364,7 +358,7 @@
     return pl.pallas_call(
         kernel,
         out_shape=[jax.ShapeDtypeStruct((size, 2, BLK, BLK), BF) for size in sizes],
-        in_specs=[smem] * 3 + whole(2 + chips + dates),
+        in_specs=[smem] * 2 + whole(2 + chips + dates),
         out_specs=whole(len(sizes)),
         scratch_shapes=[
             pltpu.VMEM((each, 2, pulses, BLK), BF),
@@ -375,7 +369,7 @@
             4 * each * 4 * pulses * (pulses + BLK) * BLK, [*pieces, *filters, forward, back] * 4
         ),
         name="focus",
-    )(place, table, kinds, forward, back, *pieces, *filters)
+    )(info, table, forward, back, *pieces, *filters)
 
 
 def goldstein(tiles, follows, seconds, start, capacity, result):
@@ -462,7 +456,7 @@
         ],
         input_output_aliases={len(operands) - 1: 0} if have else {},
         compiler_params=params(16),
-        cost_estimate=cost(count * 2 * 4 * 4 * BLK**3, operands + [*seconds] * 2),
+        cost_estimate=cost(4 * count * 2 * 4 * 4 * BLK**3, operands + [*seconds] * 8),
         name="goldstein",
     )(*operands)
 
@@ -472,11 +466,12 @@
     dates = lax.axis_size("date")
     me = lax.axis_index("shard")
     date = lax.axis_index("date")
-    place = jnp.stack([me, date]).astype(jnp.int32)
-    owners, slots, kinds = block_owner[0], block_slot[0], kernel_index[0]
+    info = jnp.concatenate(
+        [block_owner[0], block_slot[0], kernel_index[0], jnp.stack([me, date]).astype(jnp.int32)]
+    )
     cores = 2 if shards % 2 == 0 else 1
     chips = shards // cores
-    total = owners.shape[0]
+    total = block_owner.shape[1]
     group = total // shards
     capacity = 2 * group
     most = max(2, capacity // shards)
@@ -485,23 +480,25 @@
     rows = azimuth_reference.shape[1] // dates
     share = lax.dynamic_slice_in_dim(azimuth_reference, date * rows, rows, axis=1)
     shares = [share] + [hop(share, "shard", c, cores) for c in range(1, cores)]
-    sent = filter_columns(shares, owners, place, plan)
-    echo = echo_spectra[0]
-    echo, sent = lax.optimization_barrier((echo, sent))
+    sent = filter_columns(shares, info, plan)
+    echo = echo_spectra[0].astype(F32)
+    real = (echo[0] * range_reference[0] + echo[1] * range_reference[1]).astype(BF)
+    imag = (echo[1] * range_reference[0] - echo[0] * range_reference[1]).astype(BF)
+    real, imag, sent = lax.optimization_barrier((real, imag, sent))
     got = [sent[0]] + [hop(sent[k], "shard", k * cores) for k in range(1, chips)]
     got = jnp.concatenate(got, axis=0)
     filters = [got] + [hop(got, "date", e) for e in range(1, dates)]
-    compressed, blocks, columns = range_compress(echo, range_reference, owners, slots, plan)
+    compressed, blocks, columns = range_compress(real, imag, info, plan)
     parts = [compressed] + [hop(compressed, "shard", c, cores) for c in range(1, cores)]
     splits = ((2, 2, 2, 2), (4, 4)) if capacity == 16 else ((capacity,),)
-    outbox = spread_columns(parts, columns, place, [sum(sizes) for sizes in splits], plan)
+    outbox = spread_columns(parts, columns, info, [sum(sizes) for sizes in splits], plan)
     tiles, follows, seconds = [], [], []
     start = 0
     for chunk, sizes in enumerate(splits):
         pieces = [outbox[chunk][0]] + [
             hop(outbox[chunk][k], "shard", k * cores) for k in range(1, chips)
         ]
-        mine = focus(pieces, filters, place, blocks, kinds, start, cores, sizes, plan)
+        mine = focus(pieces, filters, blocks, info, start, cores, sizes, plan, 0)
         start += sum(sizes)
         if chunk:
             mine, follows[:1] = lax.optimization_barrier((mine, follows[:1]))

time: 76.9 us -> 75.1 us (0.977)
  starting transfers between devices: 35.1 us -> 33.8 us
  Pallas kernels: 17.3 us -> 16.1 us
  other arithmetic: 0.22 us -> 1.37 us
    unnamed x25 -> x21, local copies, waits for them, and re-layouts: 5.37 us -> 3.57 us
    ppermute x26, starting transfers between devices: 35.1 us -> 33.8 us  [hop(): return lax.ppermute(value, axis, pairs)]
    convert_element_type x0 -> x2, other arithmetic: none -> 1.24 us  [the longest x1 1.11 us: body(): echo = echo_spectra[0].astype(F32)]
    pallas_call x1, Pallas kernels: 5.09 us -> 3.91 us  [range_compress(): pl.pallas_call(kernel, out_shape=[jax.ShapeDtypeStruct((2, outer, pulses,...]
    slice x0 -> x1, local copies, waits for them, and re-layouts: none -> 0.97 us  [body(): range_reference[0]]
  transfers between devices with their start and end apart: 26 -> 26, of which waited for: 11 -> 10; matrix products, arithmetic and copies ran while one was open for 0% -> 3% of each run, Pallas kernels for 19% -> 18%
where the time goes in v4:
time: 75.1 us; the launch traced here: 74.4 us
  starting transfers between devices  33.8 us (45%)
  waiting for transfers between devices  18.3 us (24%)
  Pallas kernels  16.1 us (21%)
  local copies, waits for them, and re-layouts  4.65 us (6%)
  other arithmetic  1.37 us (2%)
    ppermute x26, starting transfers between devices, hop(): return lax.ppermute(value, axis, pairs)  33.8 us
    ppermute x26, waiting for transfers between devices, hop(): return lax.ppermute(value, axis, pairs)  18.3 us
    pallas_call x3, Pallas kernels, goldstein(): pl.pallas_call(kernel, out_shape=jax.ShapeDtypeStruct((capacity, 2, 2, BL...  7.13 us
    pallas_call x1, Pallas kernels, range_compress(): pl.pallas_call(kernel, out_shape=[jax.ShapeDtypeStruct((2, outer, pulses,...  3.91 us
    unnamed x21, local copies, waits for them, and re-layouts  3.57 us
    pallas_call x2, Pallas kernels, focus(): pl.pallas_call(kernel, out_shape=[jax.ShapeDtypeStruct((size, 2, BLK, BLK...  3.56 us
  transfers between devices with their start and end apart: 26, of which 10 were waited for; matrix products, arithmetic and copies ran while one was open for 3% of the time, Pallas kernels for 18%

profile of v4, /device:TPU:0, one launch (start us, length us, event | category | flops | bytes accessed | tf_op | source)
XLA Modules:
  0.0 74.4 jit_solution(13976835887158038667)
XLA Ops:
  0.0 1.1 %copy-done = bf16[2,128,1024]{2,1,0:T(8,128)(2,1)S(1)} copy-done((bf16[2,128,1024]{2,1,0:T(8,128)(2,1)S(1)}, bf16[2,128,1024]{2,1,0:T(8,128)(2,1)}, u32[]{:S(2)}) %copy-start) | copy-done | bytes 524312
  1.1 0.5 collective-permute-start
  1.6 1.0 %fusion = (f32[1,8192]{1,0:T(1,128)S(1)}, f32[1,8192]{1,0:T(1,128)S(1)}) fusion(f32[2,8192]{1,0:T(2,128)} %param.24), kind=kLoop, calls=%fused_computation.15 | loop fusion | bytes 131072 | tf_op jit(solution)/shard_map/slice | solution.py:485
  2.6 1.1 %convert_element_type.58 = f32[1,2,16,8192]{3,2,1,0:T(8,128)S(1)} convert(bf16[1,2,16,8192]{3,2,1,0:T(8,128)(2,1)} %param.23) | non-fusion elementwise | flops 262144 | bytes 1572864 | tf_op jit(solution)/shard_map/convert_element_type | solution.py:484
  3.7 0.1 subtract_convert_fusion
  4.0 0.7 %filter_columns.1 = (bf16[4,2,32,128]{3,2,1,0:T(8,128)(2,1)S(1)}, bf16[4,2,32,128]{3,2,1,0:T(8,128)(2,1)S(1)}, bf16[4,2,32,128]{3,2,1,0:T(8,128)(2,1)S(1)}, bf16[4,2,32,128]{3,2,1,0:T(8,128)(2,1)S(1)}) custom-call(s32[194]{0:T(256)S(1)} %concatenate.6.info_ref, bf16[2,32,1024]{2,1,0:T(8,128)(2,1)S(1)} %constant_dynamic-slice_fusion.rest_0_, ...), custom_call_target="tpu_custom_call" | custom-call | bytes 524288 | tf_op jit(solution)/shard_map/filter_columns/pallas_call | solution.py:283
  4.7 2.7 %collective-permute-start.5 = (bf16[4,2,32,128]{3,2,1,0:T(8,128)(2,1)S(1)}, bf16[4,2,32,128]{3,2,1,0:T(8,128)(2,1)S(1)}, u32[]{:S(2)}, u32[]{:S(2)}) collective-permute-start(bf16[4,2,32,128]{3,2,1,0:T(8,128)(2,1)S(1)} %get-tuple-element.49), channel_id=1, source_target_pairs={{0,2},{1,3},{2,0},{3,1},{4,6},{5,7},{6,4},{7,5},{8,10},{9,11},{10,... | collective-permute-start | bytes 196616 | tf_op jit(solution)/shard_map/ppermute | solution.py:106
  7.4 2.6 %collective-permute-start.6 = (bf16[4,2,32,128]{3,2,1,0:T(8,128)(2,1)S(1)}, bf16[4,2,32,128]{3,2,1,0:T(8,128)(2,1)S(1)}, u32[]{:S(2)}, u32[]{:S(2)}) collective-permute-start(bf16[4,2,32,128]{3,2,1,0:T(8,128)(2,1)S(1)} %get-tuple-element.50), channel_id=1, source_target_pairs={{0,4},{1,5},{2,6},{3,7},{4,0},{5,1},{6,2},{7,3},{8,12},{9,13},{10,... | collective-permute-start | bytes 196616 | tf_op jit(solution)/shard_map/ppermute | solution.py:106
  10.0 3.9 %range_compress.1 = (bf16[2,64,16,128]{3,2,1,0:T(8,128)(2,1)S(1)}, s32[8,16]{1,0:T(8,128)S(1)}, s32[8,16]{1,0:T(8,128)S(1)}) custom-call(s32[194]{0:T(256)S(1)} %concatenate.6.info_ref, bf16[16,8192]{1,0:T(8,128)(2,1)S(1)} %get-tuple-element.39.real_ref, bf16[16,8192]{1,0:T(8,128)(2,1)S(1)} %get-tuple-element.40.imag_ref, f32[640,128]{1,0:T(8,128)S(1)} %copy-done.1), custom_call_target="tpu_custom_call" | custom-call | flops 201326592 | bytes 1900544 | tf_op jit(solution)/shard_map/range_compress/pallas_call | solution.py:190
  14.0 0.3 collective-permute-done.6
  14.4 1.7 %collective-permute-done.7 = bf16[4,2,32,128]{3,2,1,0:T(8,128)(2,1)S(1)} collective-permute-done((bf16[4,2,32,128]{3,2,1,0:T(8,128)(2,1)S(1)}, bf16[4,2,32,128]{3,2,1,0:T(8,128)(2,1)S(1)}, u32[]{:S(2)}, u32[]{:S(2)}) %collective-permute-start.7) | collective-permute-done | bytes 65568 | tf_op jit(solution)/shard_map/ppermute | solution.py:106
  16.1 2.5 %collective-permute-start.10 = (bf16[16,2,32,128]{3,2,1,0:T(8,128)(2,1)S(1)}, bf16[16,2,32,128]{3,2,1,0:T(8,128)(2,1)S(1)}, u32[]{:S(2)}, u32[]{:S(2)}) collective-permute-start(bf16[16,2,32,128]{3,2,1,0:T(8,128)(2,1)S(1)} %constant_dynamic-update-slice_fusion.rest_4_), channel_id=1, source_target_pairs={{0,24},{8,16},{16,8},{24,0},{1,25},{9,17},{17,9},{25,1},{2,26},{10... | collective-permute-start | bytes 786440 | tf_op jit(solution)/shard_map/ppermute | solution.py:106
  18.6 0.5 collective-permute-start.8
  19.2 0.5 collective-permute-start.9
  19.7 0.8 %spread_columns.1 = (bf16[8,2,32,128]{3,2,1,0:T(8,128)(2,1)S(1)}, bf16[8,2,32,128]{3,2,1,0:T(8,128)(2,1)S(1)}, bf16[8,2,32,128]{3,2,1,0:T(8,128)(2,1)S(1)}, bf16...) custom-call(s32[8,16]{1,0:T(8,128)S(1)} %get-tuple-element.42.table_, ...), custom_call_target="tpu_custom_call" | custom-call | bytes 2097152 | tf_op jit(solution)/shard_map/spread_columns/pallas_call | solution.py:237
  20.5 1.3 %collective-permute-start.11 = (bf16[8,2,32,128]{3,2,1,0:T(8,128)(2,1)S(1)}, bf16[8,2,32,128]{3,2,1,0:T(8,128)(2,1)S(1)}, u32[]{:S(2)}, u32[]{:S(2)}) collective-permute-start(bf16[8,2,32,128]{3,2,1,0:T(8,128)(2,1)S(1)} %get-tuple-element.55), channel_id=1, source_target_pairs={{0,2},{1,3},{2,0},{3,1},{4,6},{5,7},{6,4},{7,5},{8,10},{9,11},{10,... | collective-permute-start | bytes 393224 | tf_op jit(solution)/shard_map/ppermute | solution.py:106
  21.8 1.7 %collective-permute-start.12 = (bf16[8,2,32,128]{3,2,1,0:T(8,128)(2,1)S(1)}, bf16[8,2,32,128]{3,2,1,0:T(8,128)(2,1)S(1)}, u32[]{:S(2)}, u32[]{:S(2)}) collective-permute-start(bf16[8,2,32,128]{3,2,1,0:T(8,128)(2,1)S(1)} %get-tuple-element.56), channel_id=1, source_target_pairs={{0,4},{1,5},{2,6},{3,7},{4,0},{5,1},{6,2},{7,3},{8,12},{9,13},{10,... | collective-permute-start | bytes 393224 | tf_op jit(solution)/shard_map/ppermute | solution.py:106
  23.5 2.8 %collective-permute-done.10.rest_7_ = bf16[16,2,32,128]{3,2,1,0:T(8,128)(2,1)S(1)} collective-permute-done((bf16[16,2,32,128]{3,2,1,0:T(8,128)(2,1)S(1)}, bf16[16,2,32,128]{3,2,1,0:T(8,128)(2,1)S(1)}, u32[]{:S(2)}, u32[]{:S(2)}) %collective-permute-start.10) | collective-permute-done | bytes 262176 | tf_op jit(solution)/shard_map/ppermute | solution.py:106
  26.4 2.4 %collective-permute-start.13 = (bf16[8,2,32,128]{3,2,1,0:T(8,128)(2,1)S(1)}, bf16[8,2,32,128]{3,2,1,0:T(8,128)(2,1)S(1)}, u32[]{:S(2)}, u32[]{:S(2)}) collective-permute-start(bf16[8,2,32,128]{3,2,1,0:T(8,128)(2,1)S(1)} %get-tuple-element.57), channel_id=1, source_target_pairs={{0,6},{1,7},{2,4},{3,5},{4,2},{5,3},{6,0},{7,1},{8,14},{9,15},{10,... | collective-permute-start | bytes 393224 | tf_op jit(solution)/shard_map/ppermute | solution.py:106
  28.7 1.1 %collective-permute-done.8.rest_5_ = bf16[16,2,32,128]{3,2,1,0:T(8,128)(2,1)S(1)} collective-permute-done((bf16[16,2,32,128]{3,2,1,0:T(8,128)(2,1)S(1)}, bf16[16,2,32,128]{3,2,1,0:T(8,128)(2,1)S(1)}, u32[]{:S(2)}, u32[]{:S(2)}) %collective-permute-start.8) | collective-permute-done | bytes 262176 | tf_op jit(solution)/shard_map/ppermute | solution.py:106
  29.8 2.1 %collective-permute-start.2 = (bf16[8,2,32,128]{3,2,1,0:T(8,128)(2,1)S(1)}, bf16[8,2,32,128]{3,2,1,0:T(8,128)(2,1)S(1)}, u32[]{:S(2)}, u32[]{:S(2)}) collective-permute-start(bf16[8,2,32,128]{3,2,1,0:T(8,128)(2,1)S(1)} %get-tuple-element.45), channel_id=1, source_target_pairs={{0,2},{1,3},{2,0},{3,1},{4,6},{5,7},{6,4},{7,5},{8,10},{9,11},{10,... | collective-permute-start | bytes 393224 | tf_op jit(solution)/shard_map/ppermute | solution.py:106
  32.0 1.9 %collective-permute-start.3 = (bf16[8,2,32,128]{3,2,1,0:T(8,128)(2,1)S(1)}, bf16[8,2,32,128]{3,2,1,0:T(8,128)(2,1)S(1)}, u32[]{:S(2)}, u32[]{:S(2)}) collective-permute-start(bf16[8,2,32,128]{3,2,1,0:T(8,128)(2,1)S(1)} %get-tuple-element.46), channel_id=1, source_target_pairs={{0,4},{1,5},{2,6},{3,7},{4,0},{5,1},{6,2},{7,3},{8,12},{9,13},{10,... | collective-permute-start | bytes 393224 | tf_op jit(solution)/shard_map/ppermute | solution.py:106
  33.9 0.5 collective-permute-start.4
  34.4 1.2 %copy-done.2 = bf16[8,256,256]{2,1,0:T(8,128)(2,1)S(1)} copy-done((bf16[8,256,256]{2,1,0:T(8,128)(2,1)S(1)}, bf16[8,256,256]{2,1,0:T(8,128)(2,1)}, u32[]{:S(2)}) %copy-start.2) | copy-done | bytes 1048600
  35.6 1.8 %focus.3 = (bf16[2,2,128,128]{3,2,1,0:T(8,128)(2,1)S(1)}, bf16[2,2,128,128]{3,2,1,0:T(8,128)(2,1)S(1)}, bf16[2,2,128,128]{3,2,1,0:T(8,128)(2,1)S(1)}, bf16[2,2,128,128]{3,2,1,0:T(8,128)(2,1)S(1)}) custom-call(s32[194]{0:T(256)S(1)} %concatenate.6.info_ref, s32[8,16]{1,0:T(8,128)S(1)} %get-tuple-element.41.table_ref, bf16[256,256]{1,0:T(8,128)(2,1)S(1)} %copy-done.4, ...), custom_call_target="tpu_custom_call" | custom-call | flops 1073741824 | bytes 11010048 | tf_op jit(solution)/shard_map/focus/pallas_call | solution.py:358
  37.4 1.5 %collective-permute-start.14 = (bf16[2,2,128,128]{3,2,1,0:T(8,128)(2,1)S(1)}, bf16[2,2,128,128]{3,2,1,0:T(8,128)(2,1)S(1)}, u32[]{:S(2)}, u32[]{:S(2)}) collective-permute-start(bf16[2,2,128,128]{3,2,1,0:T(8,128)(2,1)S(1)} %get-tuple-element.58.rest_0_), channel_id=1, source_target_pairs={{0,16},{8,24},{16,0},{24,8},{1,17},{9,25},{17,1},{25,9},{2,18},{10... | collective-permute-start | bytes 393224 | tf_op jit(solution)/shard_map/ppermute | solution.py:106
  38.8 0.6 collective-permute-start.24
  39.5 1.4 %collective-permute-start.22 = (bf16[2,2,128,128]{3,2,1,0:T(8,128)(2,1)S(1)}, bf16[2,2,128,128]{3,2,1,0:T(8,128)(2,1)S(1)}, u32[]{:S(2)}, u32[]{:S(2)}) collective-permute-start(bf16[2,2,128,128]{3,2,1,0:T(8,128)(2,1)S(1)} %get-tuple-element.62.rest_2_), channel_id=1, source_target_pairs={{0,16},{8,24},{16,0},{24,8},{1,17},{9,25},{17,1},{25,9},{2,18},{10... | collective-permute-start | bytes 393224 | tf_op jit(solution)/shard_map/ppermute | solution.py:106
  40.9 3.6 %collective-permute-done.3.rest_2_ = bf16[8,2,32,128]{3,2,1,0:T(8,128)(2,1)S(1)} collective-permute-done((bf16[8,2,32,128]{3,2,1,0:T(8,128)(2,1)S(1)}, bf16[8,2,32,128]{3,2,1,0:T(8,128)(2,1)S(1)}, u32[]{:S(2)}, u32[]{:S(2)}) %collective-permute-start.3) | collective-permute-done | bytes 131104 | tf_op jit(solution)/shard_map/ppermute | solution.py:106
  44.5 1.5 %collective-permute-start.20 = (bf16[2,2,128,128]{3,2,1,0:T(8,128)(2,1)S(1)}, bf16[2,2,128,128]{3,2,1,0:T(8,128)(2,1)S(1)}, u32[]{:S(2)}, u32[]{:S(2)}) collective-permute-start(bf16[2,2,128,128]{3,2,1,0:T(8,128)(2,1)S(1)} %get-tuple-element.61.rest_1_), channel_id=1, source_target_pairs={{0,16},{8,24},{16,0},{24,8},{1,17},{9,25},{17,1},{25,9},{2,18},{10... | collective-permute-start | bytes 393224 | tf_op jit(solution)/shard_map/ppermute | solution.py:106
  46.0 1.2 %copy-done.3 = bf16[8,256,256]{2,1,0:T(8,128)(2,1)S(1)} copy-done((bf16[8,256,256]{2,1,0:T(8,128)(2,1)S(1)}, bf16[8,256,256]{2,1,0:T(8,128)(2,1)}, u32[]{:S(2)}) %copy-start.3) | copy-done | bytes 1048600
  47.2 1.8 %focus.2 = (bf16[4,2,128,128]{3,2,1,0:T(8,128)(2,1)S(1)}, bf16[4,2,128,128]{3,2,1,0:T(8,128)(2,1)S(1)}) custom-call(s32[194]{0:T(256)S(1)} %concatenate.6.info_ref, s32[8,16]{1,0:T(8,128)S(1)} %get-tuple-element.41.table_ref, bf16[256,256]{1,0:T(8,128)(2,1)S(1)} %copy-done.4, bf16[8,256,256]{2,1,0:T(8,128)(2,1)S(1)} %copy-done.3, ...), custom_call_target="tpu_custom_call" | custom-call | flops 1073741824 | bytes 11010048 | tf_op jit(solution)/shard_map/focus/pallas_call | solution.py:358
  49.1 1.6 %collective-permute-start.15 = (bf16[2,2,128,128]{3,2,1,0:T(8,128)(2,1)S(1)}, bf16[2,2,128,128]{3,2,1,0:T(8,128)(2,1)S(1)}, u32[]{:S(2)}, u32[]{:S(2)}) collective-permute-start(bf16[2,2,128,128]{3,2,1,0:T(8,128)(2,1)S(1)} %broadcast_select_fusion.5), channel_id=1, source_target_pairs={{0,8},{8,0},{16,24},{24,16},{1,9},{9,1},{17,25},{25,17},{2,10},{10... | collective-permute-start | bytes 393224 | tf_op jit(solution)/shard_map/ppermute | solution.py:106
  50.6 0.6 collective-permute-start.25
  51.3 2.9 %collective-permute-done.15.rest_4_ = bf16[2,2,128,128]{3,2,1,0:T(8,128)(2,1)S(1)} collective-permute-done((bf16[2,2,128,128]{3,2,1,0:T(8,128)(2,1)S(1)}, bf16[2,2,128,128]{3,2,1,0:T(8,128)(2,1)S(1)}, u32[]{:S(2)}, u32[]{:S(2)}) %collective-permute-start.15) | collective-permute-done | bytes 131104 | tf_op jit(solution)/shard_map/ppermute | solution.py:106
  54.1 0.5 collective-permute-start.18
  54.6 1.6 %collective-permute-start.23 = (bf16[2,2,128,128]{3,2,1,0:T(8,128)(2,1)S(1)}, bf16[2,2,128,128]{3,2,1,0:T(8,128)(2,1)S(1)}, u32[]{:S(2)}, u32[]{:S(2)}) collective-permute-start(bf16[2,2,128,128]{3,2,1,0:T(8,128)(2,1)S(1)} %broadcast_select_fusion.3), channel_id=1, source_target_pairs={{0,8},{8,0},{16,24},{24,16},{1,9},{9,1},{17,25},{25,17},{2,10},{10... | collective-permute-start | bytes 393224 | tf_op jit(solution)/shard_map/ppermute | solution.py:106
  56.2 1.5 %collective-permute-start.16 = (bf16[4,2,128,128]{3,2,1,0:T(8,128)(2,1)S(1)}, bf16[4,2,128,128]{3,2,1,0:T(8,128)(2,1)S(1)}, u32[]{:S(2)}, u32[]{:S(2)}) collective-permute-start(bf16[4,2,128,128]{3,2,1,0:T(8,128)(2,1)S(1)} %get-tuple-element.59.rest_0_), channel_id=1, source_target_pairs={{0,16},{8,24},{16,0},{24,8},{1,17},{9,25},{17,1},{25,9},{2,18},{10... | collective-permute-start | bytes 786440 | tf_op jit(solution)/shard_map/ppermute | solution.py:106
  57.7 0.6 collective-permute-start.21
  58.3 3.6 %collective-permute-done.18.rest_2_ = bf16[4,2,128,128]{3,2,1,0:T(8,128)(2,1)S(1)} collective-permute-done((bf16[4,2,128,128]{3,2,1,0:T(8,128)(2,1)S(1)}, bf16[4,2,128,128]{3,2,1,0:T(8,128)(2,1)S(1)}, u32[]{:S(2)}, u32[]{:S(2)}) %collective-permute-start.18) | collective-permute-done | bytes 262176 | tf_op jit(solution)/shard_map/ppermute | solution.py:106
  61.9 1.6 %collective-permute-start.19 = (bf16[4,2,128,128]{3,2,1,0:T(8,128)(2,1)S(1)}, bf16[4,2,128,128]{3,2,1,0:T(8,128)(2,1)S(1)}, u32[]{:S(2)}, u32[]{:S(2)}) collective-permute-start(bf16[4,2,128,128]{3,2,1,0:T(8,128)(2,1)S(1)} %broadcast_select_fusion), channel_id=1, source_target_pairs={{0,8},{8,0},{16,24},{24,16},{1,9},{9,1},{17,25},{25,17},{2,10},{10... | collective-permute-start | bytes 786440 | tf_op jit(solution)/shard_map/ppermute | solution.py:106
  63.5 1.2 %collective-permute-done.16.rest_2_ = bf16[4,2,128,128]{3,2,1,0:T(8,128)(2,1)S(1)} collective-permute-done((bf16[4,2,128,128]{3,2,1,0:T(8,128)(2,1)S(1)}, bf16[4,2,128,128]{3,2,1,0:T(8,128)(2,1)S(1)}, u32[]{:S(2)}, u32[]{:S(2)}) %collective-permute-start.16) | collective-permute-done | bytes 262176 | tf_op jit(solution)/shard_map/ppermute | solution.py:106
  64.7 1.6 %collective-permute-start.17 = (bf16[4,2,128,128]{3,2,1,0:T(8,128)(2,1)S(1)}, bf16[4,2,128,128]{3,2,1,0:T(8,128)(2,1)S(1)}, u32[]{:S(2)}, u32[]{:S(2)}) collective-permute-start(bf16[4,2,128,128]{3,2,1,0:T(8,128)(2,1)S(1)} %broadcast_select_fusion.1), channel_id=1, source_target_pairs={{0,8},{8,0},{16,24},{24,16},{1,9},{9,1},{17,25},{25,17},{2,10},{10... | collective-permute-start | bytes 786440 | tf_op jit(solution)/shard_map/ppermute | solution.py:106
  66.3 3.0 %goldstein.3.rest_7_ = bf16[16,2,2,128,128]{4,3,2,1,0:T(8,128)(2,1)} custom-call(bf16[2,2,128,128]{3,2,1,0:T(8,128)(2,1)S(1)} %get-tuple-element.58.rest_0_, bf16[2,2,128,128]{3,2,1,0:T(8,128)(2,1)S(1)} %get-tuple-element.61.rest_1_, bf16[2,2,128,128]{3,2,1,0:T(8,128)(2,1)S(1)} %get-tuple-element.62.rest_2_, ...), custom_call_target="tpu_custom_call" | custom-call | flops 4294967296 | bytes 6291456 | tf_op jit(solution)/shard_map/goldstein/pallas_call | solution.py:448
  69.3 0.2 collective-permute-done.19.rest_1_
  69.6 2.1 %goldstein.4.rest_7_ = bf16[16,2,2,128,128]{4,3,2,1,0:T(8,128)(2,1)} custom-call(bf16[4,2,128,128]{3,2,1,0:T(8,128)(2,1)S(1)} %get-tuple-element.60.rest_0_, bf16[4,2,128,128]{3,2,1,0:T(8,128)(2,1)S(1)} %collective-permute-done.19.rest_1_, bf16[4,2,128,128]{3,2,1,0:T(8,128)(2,1)S(1)} %collective-permute-done.18.rest_2_, ...), custom_call_target="tpu_custom_call", output_to_operand_aliasing={{}: (7, {})} | custom-call | flops 2147483648 | bytes 5505024 | tf_op jit(solution)/shard_map/goldstein/pallas_call | solution.py:448
  71.6 0.7 collective-permute-done.17.rest_1_
  72.4 2.1 %goldstein.5 = bf16[16,2,2,128,128]{4,3,2,1,0:T(8,128)(2,1)} custom-call(bf16[4,2,128,128]{3,2,1,0:T(8,128)(2,1)S(1)} %get-tuple-element.59.rest_0_, bf16[4,2,128,128]{3,2,1,0:T(8,128)(2,1)S(1)} %collective-permute-done.17.rest_1_, bf16[4,2,128,128]{3,2,1,0:T(8,128)(2,1)S(1)} %collective-permute-done.16.rest_2_, ...), custom_call_target="tpu_custom_call", output_to_operand_aliasing={{}: (7, {})} | custom-call | flops 2147483648 | bytes 5505024 | tf_op jit(solution)/shard_map/goldstein/pallas_call | solution.py:448
  (45 shorter events, 0.4 us)
Async XLA Ops:
  0.0 1.1 %copy-start = (bf16[2,128,1024]{2,1,0:T(8,128)(2,1)S(1)}, bf16[2,128,1024]{2,1,0:T(8,128)(2,1)}, u32[]{:S(2)}) copy-start(bf16[2,128,1024]{2,1,0:T(8,128)(2,1)} %param.25) | copy-start | bytes 1572868
  0.0 10.0 %copy-start.1 = (f32[640,128]{1,0:T(8,128)S(1)}, f32[640,128]{1,0:T(8,128)}, u32[]{:S(2)}) copy-start(f32[640,128]{1,0:T(8,128)} %constant.44.clone.tables_ref) | copy-start | bytes 983044
  0.0 3.9 %copy-start.6 = (s32[1,64]{1,0:T(1,128)S(1)}, s32[1,64]{1,0:T(1,128)}, u32[]{:S(2)}) copy-start(s32[1,64]{1,0:T(1,128)} %param.26) | copy-start | bytes 772
  0.0 3.9 %copy-start.7 = (s32[1,64]{1,0:T(1,128)S(1)}, s32[1,64]{1,0:T(1,128)}, u32[]{:S(2)}) copy-start(s32[1,64]{1,0:T(1,128)} %param.27) | copy-start | bytes 772
  0.0 3.9 %copy-start.8 = (s32[1,64]{1,0:T(1,128)S(1)}, s32[1,64]{1,0:T(1,128)}, u32[]{:S(2)}) copy-start(s32[1,64]{1,0:T(1,128)} %param.28) | copy-start | bytes 772
  1.1 2.9 %collective-permute-start = (bf16[2,32,1024]{2,1,0:T(8,128)(2,1)S(1)}, bf16[2,32,1024]{2,1,0:T(8,128)(2,1)S(1)}, u32[]{:S(2)}, u32[]{:S(2)}) collective-permute-start(bf16[2,32,1024]{2,1,0:T(8,128)(2,1)S(1)} %constant_dynamic-slice_fusion.rest_0_), channel_id=1, source_target_pairs={{0,1},{1,0},{2,3},{3,2},{4,5},{5,4},{6,7},{7,6},{8,9},{9,8},{10,11... | collective-permute-start | bytes 393224 | tf_op jit(solution)/shard_map/ppermute | solution.py:106
  3.7 30.6 %copy-start.4 = (bf16[256,256]{1,0:T(8,128)(2,1)S(1)}, bf16[256,256]{1,0:T(8,128)(2,1)}, u32[]{:S(2)}) copy-start(bf16[256,256]{1,0:T(8,128)(2,1)} %constant.52.forward_ref.rest_12_.rest_15_.rest_3_.rest_6_) | copy-start | bytes 393220
  4.7 9.3 %collective-permute-start.5 = (bf16[4,2,32,128]{3,2,1,0:T(8,128)(2,1)S(1)}, bf16[4,2,32,128]{3,2,1,0:T(8,128)(2,1)S(1)}, u32[]{:S(2)}, u32[]{:S(2)}) collective-permute-start(bf16[4,2,32,128]{3,2,1,0:T(8,128)(2,1)S(1)} %get-tuple-element.49), channel_id=1, source_target_pairs={{0,2},{1,3},{2,0},{3,1},{4,6},{5,7},{6,4},{7,5},{8,10},{9,11},{10,... | collective-permute-start | bytes 196616 | tf_op jit(solution)/shard_map/ppermute | solution.py:106
  7.4 7.0 %collective-permute-start.6 = (bf16[4,2,32,128]{3,2,1,0:T(8,128)(2,1)S(1)}, bf16[4,2,32,128]{3,2,1,0:T(8,128)(2,1)S(1)}, u32[]{:S(2)}, u32[]{:S(2)}) collective-permute-start(bf16[4,2,32,128]{3,2,1,0:T(8,128)(2,1)S(1)} %get-tuple-element.50), channel_id=1, source_target_pairs={{0,4},{1,5},{2,6},{3,7},{4,0},{5,1},{6,2},{7,3},{8,12},{9,13},{10,... | collective-permute-start | bytes 196616 | tf_op jit(solution)/shard_map/ppermute | solution.py:106
  10.0 6.1 %collective-permute-start.7 = (bf16[4,2,32,128]{3,2,1,0:T(8,128)(2,1)S(1)}, bf16[4,2,32,128]{3,2,1,0:T(8,128)(2,1)S(1)}, u32[]{:S(2)}, u32[]{:S(2)}) collective-permute-start(bf16[4,2,32,128]{3,2,1,0:T(8,128)(2,1)S(1)} %get-tuple-element.51), channel_id=1, source_target_pairs={{0,6},{1,7},{2,4},{3,5},{4,2},{5,3},{6,0},{7,1},{8,14},{9,15},{10,... | collective-permute-start | bytes 196616 | tf_op jit(solution)/shard_map/ppermute | solution.py:106
  13.9 5.8 %collective-permute-start.1 = (bf16[2,64,16,128]{3,2,1,0:T(8,128)(2,1)S(1)}, bf16[2,64,16,128]{3,2,1,0:T(8,128)(2,1)S(1)}, u32[]{:S(2)}, u32[]{:S(2)}) collective-permute-start(bf16[2,64,16,128]{3,2,1,0:T(8,128)(2,1)S(1)} %get-tuple-element.43.rest_0_), channel_id=1, source_target_pairs={{0,1},{1,0},{2,3},{3,2},{4,5},{5,4},{6,7},{7,6},{8,9},{9,8},{10,11... | collective-permute-start | bytes 1572872 | tf_op jit(solution)/shard_map/ppermute | solution.py:106
  16.1 10.3 %collective-permute-start.10 = (bf16[16,2,32,128]{3,2,1,0:T(8,128)(2,1)S(1)}, bf16[16,2,32,128]{3,2,1,0:T(8,128)(2,1)S(1)}, u32[]{:S(2)}, u32[]{:S(2)}) collective-permute-start(bf16[16,2,32,128]{3,2,1,0:T(8,128)(2,1)S(1)} %constant_dynamic-update-slice_fusion.rest_4_), channel_id=1, source_target_pairs={{0,24},{8,16},{16,8},{24,0},{1,25},{9,17},{17,9},{25,1},{2,26},{10... | collective-permute-start | bytes 786440 | tf_op jit(solution)/shard_map/ppermute | solution.py:106
  18.6 11.2 %collective-permute-start.8 = (bf16[16,2,32,128]{3,2,1,0:T(8,128)(2,1)S(1)}, bf16[16,2,32,128]{3,2,1,0:T(8,128)(2,1)S(1)}, u32[]{:S(2)}, u32[]{:S(2)}) collective-permute-start(bf16[16,2,32,128]{3,2,1,0:T(8,128)(2,1)S(1)} %constant_dynamic-update-slice_fusion.rest_4_), channel_id=1, source_target_pairs={{0,8},{8,0},{16,24},{24,16},{1,9},{9,1},{17,25},{25,17},{2,10},{10... | collective-permute-start | bytes 786440 | tf_op jit(solution)/shard_map/ppermute | solution.py:106
  19.2 12.8 %collective-permute-start.9 = (bf16[16,2,32,128]{3,2,1,0:T(8,128)(2,1)S(1)}, bf16[16,2,32,128]{3,2,1,0:T(8,128)(2,1)S(1)}, u32[]{:S(2)}, u32[]{:S(2)}) collective-permute-start(bf16[16,2,32,128]{3,2,1,0:T(8,128)(2,1)S(1)} %constant_dynamic-update-slice_fusion.rest_4_), channel_id=1, source_target_pairs={{0,16},{8,24},{16,0},{24,8},{1,17},{9,25},{17,1},{25,9},{2,18},{10... | collective-permute-start | bytes 786440 | tf_op jit(solution)/shard_map/ppermute | solution.py:106
  20.5 13.4 %collective-permute-start.11 = (bf16[8,2,32,128]{3,2,1,0:T(8,128)(2,1)S(1)}, bf16[8,2,32,128]{3,2,1,0:T(8,128)(2,1)S(1)}, u32[]{:S(2)}, u32[]{:S(2)}) collective-permute-start(bf16[8,2,32,128]{3,2,1,0:T(8,128)(2,1)S(1)} %get-tuple-element.55), channel_id=1, source_target_pairs={{0,2},{1,3},{2,0},{3,1},{4,6},{5,7},{6,4},{7,5},{8,10},{9,11},{10,... | collective-permute-start | bytes 393224 | tf_op jit(solution)/shard_map/ppermute | solution.py:106
  21.8 12.6 %collective-permute-start.12 = (bf16[8,2,32,128]{3,2,1,0:T(8,128)(2,1)S(1)}, bf16[8,2,32,128]{3,2,1,0:T(8,128)(2,1)S(1)}, u32[]{:S(2)}, u32[]{:S(2)}) collective-permute-start(bf16[8,2,32,128]{3,2,1,0:T(8,128)(2,1)S(1)} %get-tuple-element.56), channel_id=1, source_target_pairs={{0,4},{1,5},{2,6},{3,7},{4,0},{5,1},{6,2},{7,3},{8,12},{9,13},{10,... | collective-permute-start | bytes 393224 | tf_op jit(solution)/shard_map/ppermute | solution.py:106
  26.4 8.0 %collective-permute-start.13 = (bf16[8,2,32,128]{3,2,1,0:T(8,128)(2,1)S(1)}, bf16[8,2,32,128]{3,2,1,0:T(8,128)(2,1)S(1)}, u32[]{:S(2)}, u32[]{:S(2)}) collective-permute-start(bf16[8,2,32,128]{3,2,1,0:T(8,128)(2,1)S(1)} %get-tuple-element.57), channel_id=1, source_target_pairs={{0,6},{1,7},{2,4},{3,5},{4,2},{5,3},{6,0},{7,1},{8,14},{9,15},{10,... | collective-permute-start | bytes 393224 | tf_op jit(solution)/shard_map/ppermute | solution.py:106
  29.8 9.6 %collective-permute-start.2 = (bf16[8,2,32,128]{3,2,1,0:T(8,128)(2,1)S(1)}, bf16[8,2,32,128]{3,2,1,0:T(8,128)(2,1)S(1)}, u32[]{:S(2)}, u32[]{:S(2)}) collective-permute-start(bf16[8,2,32,128]{3,2,1,0:T(8,128)(2,1)S(1)} %get-tuple-element.45), channel_id=1, source_target_pairs={{0,2},{1,3},{2,0},{3,1},{4,6},{5,7},{6,4},{7,5},{8,10},{9,11},{10,... | collective-permute-start | bytes 393224 | tf_op jit(solution)/shard_map/ppermute | solution.py:106
  32.0 12.5 %collective-permute-start.3 = (bf16[8,2,32,128]{3,2,1,0:T(8,128)(2,1)S(1)}, bf16[8,2,32,128]{3,2,1,0:T(8,128)(2,1)S(1)}, u32[]{:S(2)}, u32[]{:S(2)}) collective-permute-start(bf16[8,2,32,128]{3,2,1,0:T(8,128)(2,1)S(1)} %get-tuple-element.46), channel_id=1, source_target_pairs={{0,4},{1,5},{2,6},{3,7},{4,0},{5,1},{6,2},{7,3},{8,12},{9,13},{10,... | collective-permute-start | bytes 393224 | tf_op jit(solution)/shard_map/ppermute | solution.py:106
  33.9 12.2 %collective-permute-start.4 = (bf16[8,2,32,128]{3,2,1,0:T(8,128)(2,1)S(1)}, bf16[8,2,32,128]{3,2,1,0:T(8,128)(2,1)S(1)}, u32[]{:S(2)}, u32[]{:S(2)}) collective-permute-start(bf16[8,2,32,128]{3,2,1,0:T(8,128)(2,1)S(1)} %get-tuple-element.47), channel_id=1, source_target_pairs={{0,6},{1,7},{2,4},{3,5},{4,2},{5,3},{6,0},{7,1},{8,14},{9,15},{10,... | collective-permute-start | bytes 393224 | tf_op jit(solution)/shard_map/ppermute | solution.py:106
  34.3 1.2 %copy-start.2 = (bf16[8,256,256]{2,1,0:T(8,128)(2,1)S(1)}, bf16[8,256,256]{2,1,0:T(8,128)(2,1)}, u32[]{:S(2)}) copy-start(bf16[8,256,256]{2,1,0:T(8,128)(2,1)} %constant.53.back_ref) | copy-start | bytes 3145732
  37.4 11.7 %collective-permute-start.14 = (bf16[2,2,128,128]{3,2,1,0:T(8,128)(2,1)S(1)}, bf16[2,2,128,128]{3,2,1,0:T(8,128)(2,1)S(1)}, u32[]{:S(2)}, u32[]{:S(2)}) collective-permute-start(bf16[2,2,128,128]{3,2,1,0:T(8,128)(2,1)S(1)} %get-tuple-element.58.rest_0_), channel_id=1, source_target_pairs={{0,16},{8,24},{16,0},{24,8},{1,17},{9,25},{17,1},{25,9},{2,18},{10... | collective-permute-start | bytes 393224 | tf_op jit(solution)/shard_map/ppermute | solution.py:106
  38.8 11.8 %collective-permute-start.24 = (bf16[2,2,128,128]{3,2,1,0:T(8,128)(2,1)S(1)}, bf16[2,2,128,128]{3,2,1,0:T(8,128)(2,1)S(1)}, u32[]{:S(2)}, u32[]{:S(2)}) collective-permute-start(bf16[2,2,128,128]{3,2,1,0:T(8,128)(2,1)S(1)} %get-tuple-element.63.rest_3_), channel_id=1, source_target_pairs={{0,16},{8,24},{16,0},{24,8},{1,17},{9,25},{17,1},{25,9},{2,18},{10... | collective-permute-start | bytes 393224 | tf_op jit(solution)/shard_map/ppermute | solution.py:106
  39.5 15.2 %collective-permute-start.22 = (bf16[2,2,128,128]{3,2,1,0:T(8,128)(2,1)S(1)}, bf16[2,2,128,128]{3,2,1,0:T(8,128)(2,1)S(1)}, u32[]{:S(2)}, u32[]{:S(2)}) collective-permute-start(bf16[2,2,128,128]{3,2,1,0:T(8,128)(2,1)S(1)} %get-tuple-element.62.rest_2_), channel_id=1, source_target_pairs={{0,16},{8,24},{16,0},{24,8},{1,17},{9,25},{17,1},{25,9},{2,18},{10... | collective-permute-start | bytes 393224 | tf_op jit(solution)/shard_map/ppermute | solution.py:106
  44.5 13.2 %collective-permute-start.20 = (bf16[2,2,128,128]{3,2,1,0:T(8,128)(2,1)S(1)}, bf16[2,2,128,128]{3,2,1,0:T(8,128)(2,1)S(1)}, u32[]{:S(2)}, u32[]{:S(2)}) collective-permute-start(bf16[2,2,128,128]{3,2,1,0:T(8,128)(2,1)S(1)} %get-tuple-element.61.rest_1_), channel_id=1, source_target_pairs={{0,16},{8,24},{16,0},{24,8},{1,17},{9,25},{17,1},{25,9},{2,18},{10... | collective-permute-start | bytes 393224 | tf_op jit(solution)/shard_map/ppermute | solution.py:106
  46.0 1.2 %copy-start.3 = (bf16[8,256,256]{2,1,0:T(8,128)(2,1)S(1)}, bf16[8,256,256]{2,1,0:T(8,128)(2,1)}, u32[]{:S(2)}) copy-start(bf16[8,256,256]{2,1,0:T(8,128)(2,1)} %constant.53.back_ref) | copy-start | bytes 3145732
  49.0 17.3 %copy-start.5 = (bf16[256,256]{1,0:T(8,128)(2,1)S(1)}, bf16[256,256]{1,0:T(8,128)(2,1)}, u32[]{:S(2)}) copy-start(bf16[256,256]{1,0:T(8,128)(2,1)} %constant.54.rest_13_.rest_14_.rest_4_.rest_5_) | copy-start | bytes 393220
  49.1 5.0 %collective-permute-start.15 = (bf16[2,2,128,128]{3,2,1,0:T(8,128)(2,1)S(1)}, bf16[2,2,128,128]{3,2,1,0:T(8,128)(2,1)S(1)}, u32[]{:S(2)}, u32[]{:S(2)}) collective-permute-start(bf16[2,2,128,128]{3,2,1,0:T(8,128)(2,1)S(1)} %broadcast_select_fusion.5), channel_id=1, source_target_pairs={{0,8},{8,0},{16,24},{24,16},{1,9},{9,1},{17,25},{25,17},{2,10},{10... | collective-permute-start | bytes 393224 | tf_op jit(solution)/shard_map/ppermute | solution.py:106
  50.6 15.7 %collective-permute-start.25 = (bf16[2,2,128,128]{3,2,1,0:T(8,128)(2,1)S(1)}, bf16[2,2,128,128]{3,2,1,0:T(8,128)(2,1)S(1)}, u32[]{:S(2)}, u32[]{:S(2)}) collective-permute-start(bf16[2,2,128,128]{3,2,1,0:T(8,128)(2,1)S(1)} %broadcast_select_fusion.2), channel_id=1, source_target_pairs={{0,8},{8,0},{16,24},{24,16},{1,9},{9,1},{17,25},{25,17},{2,10},{10... | collective-permute-start | bytes 393224 | tf_op jit(solution)/shard_map/ppermute | solution.py:106
  54.1 7.8 %collective-permute-start.18 = (bf16[4,2,128,128]{3,2,1,0:T(8,128)(2,1)S(1)}, bf16[4,2,128,128]{3,2,1,0:T(8,128)(2,1)S(1)}, u32[]{:S(2)}, u32[]{:S(2)}) collective-permute-start(bf16[4,2,128,128]{3,2,1,0:T(8,128)(2,1)S(1)} %get-tuple-element.60.rest_0_), channel_id=1, source_target_pairs={{0,16},{8,24},{16,0},{24,8},{1,17},{9,25},{17,1},{25,9},{2,18},{10... | collective-permute-start | bytes 786440 | tf_op jit(solution)/shard_map/ppermute | solution.py:106
  54.6 11.7 %collective-permute-start.23 = (bf16[2,2,128,128]{3,2,1,0:T(8,128)(2,1)S(1)}, bf16[2,2,128,128]{3,2,1,0:T(8,128)(2,1)S(1)}, u32[]{:S(2)}, u32[]{:S(2)}) collective-permute-start(bf16[2,2,128,128]{3,2,1,0:T(8,128)(2,1)S(1)} %broadcast_select_fusion.3), channel_id=1, source_target_pairs={{0,8},{8,0},{16,24},{24,16},{1,9},{9,1},{17,25},{25,17},{2,10},{10... | collective-permute-start | bytes 393224 | tf_op jit(solution)/shard_map/ppermute | solution.py:106
  56.2 8.5 %collective-permute-start.16 = (bf16[4,2,128,128]{3,2,1,0:T(8,128)(2,1)S(1)}, bf16[4,2,128,128]{3,2,1,0:T(8,128)(2,1)S(1)}, u32[]{:S(2)}, u32[]{:S(2)}) collective-permute-start(bf16[4,2,128,128]{3,2,1,0:T(8,128)(2,1)S(1)} %get-tuple-element.59.rest_0_), channel_id=1, source_target_pairs={{0,16},{8,24},{16,0},{24,8},{1,17},{9,25},{17,1},{25,9},{2,18},{10... | collective-permute-start | bytes 786440 | tf_op jit(solution)/shard_map/ppermute | solution.py:106
  57.7 8.6 %collective-permute-start.21 = (bf16[2,2,128,128]{3,2,1,0:T(8,128)(2,1)S(1)}, bf16[2,2,128,128]{3,2,1,0:T(8,128)(2,1)S(1)}, u32[]{:S(2)}, u32[]{:S(2)}) collective-permute-start(bf16[2,2,128,128]{3,2,1,0:T(8,128)(2,1)S(1)} %broadcast_select_fusion.4), channel_id=1, source_target_pairs={{0,8},{8,0},{16,24},{24,16},{1,9},{9,1},{17,25},{25,17},{2,10},{10... | collective-permute-start | bytes 393224 | tf_op jit(solution)/shard_map/ppermute | solution.py:106
  61.9 7.6 %collective-permute-start.19 = (bf16[4,2,128,128]{3,2,1,0:T(8,128)(2,1)S(1)}, bf16[4,2,128,128]{3,2,1,0:T(8,128)(2,1)S(1)}, u32[]{:S(2)}, u32[]{:S(2)}) collective-permute-start(bf16[4,2,128,128]{3,2,1,0:T(8,128)(2,1)S(1)} %broadcast_select_fusion), channel_id=1, source_target_pairs={{0,8},{8,0},{16,24},{24,16},{1,9},{9,1},{17,25},{25,17},{2,10},{10... | collective-permute-start | bytes 786440 | tf_op jit(solution)/shard_map/ppermute | solution.py:106
  64.7 7.6 %collective-permute-start.17 = (bf16[4,2,128,128]{3,2,1,0:T(8,128)(2,1)S(1)}, bf16[4,2,128,128]{3,2,1,0:T(8,128)(2,1)S(1)}, u32[]{:S(2)}, u32[]{:S(2)}) collective-permute-start(bf16[4,2,128,128]{3,2,1,0:T(8,128)(2,1)S(1)} %broadcast_select_fusion.1), channel_id=1, source_target_pairs={{0,8},{8,0},{16,24},{24,16},{1,9},{9,1},{17,25},{25,17},{2,10},{10... | collective-permute-start | bytes 786440 | tf_op jit(solution)/shard_map/ppermute | solution.py:106

commit v5 on v4

--- a/solution.py
+++ b/solution.py
@@ -23,27 +23,11 @@
     return np.block([[cosine, -sine], [sine, cosine]])
 
 
-def kernel_table():
-    offset = (np.arange(NSUB) + 0.5) / NSUB
-    cells = np.arange(BLK)
-    dist = cells[None, None, :] - cells[None, :, None] - offset[:, None, None]
+def kernel_taps():
+    cells = np.arange(-3, 5)
+    dist = cells[None, :] - (np.arange(NSUB)[:, None] + 0.5) / NSUB
     window = np.where(np.abs(dist) < 4.0, 0.5 + 0.5 * np.cos(np.pi * dist / 4.0), 0.0)
-    return np.sinc(dist) * window
-
-
-def resample_table(pulses):
-    inverse = dft(pulses, pulses, pulses, 1, 1.0 / math.sqrt(pulses))
-    rows = pulses // BLK
-    table = np.zeros((NSUB, rows, 2 * BLK, 2 * pulses))
-    kernels = kernel_table()
-    for kind in range(NSUB):
-        for row in range(rows):
-            for part in range(2):
-                start = part * pulses + row * BLK
-                table[kind, row, part * BLK : (part + 1) * BLK] = (
-                    kernels[kind] @ inverse[start : start + BLK]
-                )
-    return table.reshape(NSUB * rows, 2 * BLK, 2 * pulses)
+    return cells, np.sinc(dist) * window
 
 
 def const(table):
@@ -295,17 +279,49 @@
     )(info, *parts)
 
 
-def focus(pieces, filters, table, info, start, cores, sizes, plan, flip):
+def resample_tables(forward):
+    pulses = forward.shape[0] // 2
+    rows = pulses // BLK
+    cells, taps = kernel_taps()
+
+    def kernel(forward_ref, out_ref):
+        low, high = slice(0, pulses), slice(pulses, 2 * pulses)
+        halves = [
+            jnp.concatenate([forward_ref[low, side], forward_ref[high, side]], axis=1)
+            for side in (low, high)
+        ]
+        down = lax.broadcasted_iota(jnp.int32, (BLK, BLK), 0)
+        ahead = lax.broadcasted_iota(jnp.int32, (BLK, BLK), 1) - down
+        for kind in range(NSUB):
+            band = jnp.zeros((BLK, BLK), F32)
+            for cell, tap in zip(cells, taps[kind]):
+                band = jnp.where(ahead == int(cell), float(tap), band)
+            band = band.astype(BF)
+            for row in range(rows):
+                for part in range(2):
+                    mine = halves[part][row * BLK : (row + 1) * BLK]
+                    out_ref[kind * rows + row, part * BLK : (part + 1) * BLK, :] = mm(
+                        band, mine
+                    ).astype(BF)
+
+    shape = (NSUB * rows, 2 * BLK, 2 * pulses)
+    return pl.pallas_call(
+        kernel,
+        out_shape=jax.ShapeDtypeStruct(shape, BF),
+        in_specs=whole(1),
+        out_specs=pl.BlockSpec(memory_space=pltpu.VMEM),
+        compiler_params=params(16),
+        cost_estimate=cost(math.prod(shape) * BLK, [forward] * 16),
+        name="resample_tables",
+    )(forward)
+
+
+def focus(pieces, filters, table, info, start, cores, sizes, plan, forward, back):
     each, _, share, _ = pieces[0].shape
     chips = len(pieces)
     dates = len(filters)
     pulses = share * chips
     rows = filters[0].shape[-2]
-    forward = const(dft(pulses, pulses, pulses, -1, 1.0 / math.sqrt(pulses)))
-    back = resample_table(pulses)
-    last = len(back) - 1
-    back = const(back[::-1] if flip else back)
-
     shards, _, most, group, group_columns = plan
 
     def kernel(info_ref, table_ref, forward_ref, back_ref, *rest):
@@ -326,7 +342,7 @@
             entries.append((step * cores + sender % cores) * most + code % most)
             row = info_ref[2 * shards * group + block] * (pulses // BLK)
             row = row + block % group // group_columns
-            table_rows.append(last - row if flip else row)
+            table_rows.append(row)
         for k in range(chips):
             source = source_of(chip, k, chips)
             at = pl.multiple_of(source * share, share)
@@ -490,37 +506,43 @@
     filters = [got] + [hop(got, "date", e) for e in range(1, dates)]
     compressed, blocks, columns = range_compress(real, imag, info, plan)
     parts = [compressed] + [hop(compressed, "shard", c, cores) for c in range(1, cores)]
-    splits = ((2, 2, 2, 2), (4, 4)) if capacity == 16 else ((capacity,),)
+    splits = ((2, 4, 2), (4, 4)) if capacity == 16 else ((capacity,),)
     outbox = spread_columns(parts, columns, info, [sum(sizes) for sizes in splits], plan)
+    pulses = echo_spectra.shape[2] * shards
+    forward = const(dft(pulses, pulses, pulses, -1, 1.0 / math.sqrt(pulses)))
+    back = resample_tables(forward)
     tiles, follows, seconds = [], [], []
+    result, done = None, 0
     start = 0
     for chunk, sizes in enumerate(splits):
         pieces = [outbox[chunk][0]] + [
             hop(outbox[chunk][k], "shard", k * cores) for k in range(1, chips)
         ]
-        mine = focus(pieces, filters, blocks, info, start, cores, sizes, plan, 0)
+        mine = focus(pieces, filters, blocks, info, start, cores, sizes, plan, forward, back)
         start += sum(sizes)
         if chunk:
-            mine, follows[:1] = lax.optimization_barrier((mine, follows[:1]))
-        for tile in mine:
+            mine, seconds[:1] = lax.optimization_barrier((mine, seconds[:1]))
+        for i, tile in enumerate(mine):
+            held = chunk and i == len(sizes) - 1
             if dates == 4:
                 second = hop(tile, "date", 2)
-                follow = hop(jnp.where(date % 2 == 0, second, tile), "date", 1)
+                sent_on = jnp.where(date % 2 == 0, second, tile)
+                if held:
+                    sent_on, result = lax.optimization_barrier((sent_on, result))
+                follow = hop(sent_on, "date", 1)
             else:
                 second = shift(tile, "date", -2)
                 follow = shift(tile, "date", -1)
             tiles.append(tile)
             follows.append(follow)
             seconds.append(second)
-    result = None
-    start = 0
-    groups = [4, 1, 1] if len(tiles) == 6 else [len(tiles)]
-    for group in groups:
-        take = slice(0, group)
-        mine = tiles[take], follows[take], seconds[take]
-        result = goldstein(*mine, start, capacity, result)
-        start += sum(tile.shape[0] for tile in mine[0])
-        del tiles[take], follows[take], seconds[take]
+        groups = [1] * len(sizes) if chunk else [len(sizes)]
+        for group in groups:
+            take = slice(done, done + group)
+            pieces = tiles[take], follows[take], seconds[take]
+            at = sum(tile.shape[0] for tile in tiles[:done])
+            result = goldstein(*pieces, at, capacity, result)
+            done += group
     return result[None]
 
 

time: 75.1 us -> 74.5 us (level)
  waiting for transfers between devices: 18.3 us -> 22.8 us
  starting transfers between devices: 33.8 us -> 30 us
  local copies, waits for them, and re-layouts: 4.65 us -> 2.21 us
  Pallas kernels: 16.1 us -> 17.7 us
    ppermute x26 -> x24, waiting for transfers between devices: 18.3 us -> 22.8 us  [hop(): return lax.ppermute(value, axis, pairs)]
    ppermute x26 -> x24, starting transfers between devices: 33.8 us -> 30 us  [hop(): return lax.ppermute(value, axis, pairs)]
    unnamed x21 -> x17, local copies, waits for them, and re-layouts: 3.57 us -> 1.13 us
  transfers between devices with their start and end apart: 26 -> 24, of which waited for: 10 -> 10; matrix products, arithmetic and copies ran while one was open for 3% -> 3% of each run, Pallas kernels for 18% -> 20%
where the time goes in v5:
time: 74.5 us; the launch traced here: 74.3 us
  starting transfers between devices  30 us (40%)
  waiting for transfers between devices  22.8 us (31%)
  Pallas kernels  17.7 us (24%)
  local copies, waits for them, and re-layouts  2.21 us (3%)
  other arithmetic  1.37 us (2%)
    ppermute x24, starting transfers between devices, hop(): return lax.ppermute(value, axis, pairs)  30 us
    ppermute x24, waiting for transfers between devices, hop(): return lax.ppermute(value, axis, pairs)  22.8 us
    pallas_call x3, Pallas kernels, goldstein(): pl.pallas_call(kernel, out_shape=jax.ShapeDtypeStruct((capacity, 2, 2, BL...  7.08 us
    pallas_call x2, Pallas kernels, focus(): pl.pallas_call(kernel, out_shape=[jax.ShapeDtypeStruct((size, 2, BLK, BLK...  3.97 us
    pallas_call x1, Pallas kernels, range_compress(): pl.pallas_call(kernel, out_shape=[jax.ShapeDtypeStruct((2, outer, pulses,...  3.91 us
    pallas_call x1, Pallas kernels, spread_columns(): pl.pallas_call(kernel, out_shape=[piece for piece in pieces for _ in rang...  1.53 us
  transfers between devices with their start and end apart: 24, of which 10 were waited for; matrix products, arithmetic and copies ran while one was open for 3% of the time, Pallas kernels for 20%

profile of v5, /device:TPU:0, one launch (start us, length us, event | category | flops | bytes accessed | tf_op | source)
XLA Modules:
  0.0 74.3 jit_solution(3965605061195687214)
XLA Ops:
  0.0 1.1 %copy-done = bf16[2,128,1024]{2,1,0:T(8,128)(2,1)S(1)} copy-done((bf16[2,128,1024]{2,1,0:T(8,128)(2,1)S(1)}, bf16[2,128,1024]{2,1,0:T(8,128)(2,1)}, u32[]{:S(2)}) %copy-start) | copy-done | bytes 524312
  1.1 0.5 collective-permute-start
  1.6 1.0 %fusion = (f32[1,8192]{1,0:T(1,128)S(1)}, f32[1,8192]{1,0:T(1,128)S(1)}) fusion(f32[2,8192]{1,0:T(2,128)} %param.21), kind=kLoop, calls=%fused_computation.14 | loop fusion | bytes 131072 | tf_op jit(solution)/shard_map/slice | solution.py:501
  2.6 1.1 %convert_element_type.49 = f32[1,2,16,8192]{3,2,1,0:T(8,128)S(1)} convert(bf16[1,2,16,8192]{3,2,1,0:T(8,128)(2,1)} %param.20) | non-fusion elementwise | flops 262144 | bytes 1572864 | tf_op jit(solution)/shard_map/convert_element_type | solution.py:500
  3.7 0.0 copy-start.2
  3.7 0.1 subtract_convert_fusion
  3.9 0.1 concatenate.6.info_ref
  4.0 0.7 %filter_columns.1 = (bf16[4,2,32,128]{3,2,1,0:T(8,128)(2,1)S(1)}, bf16[4,2,32,128]{3,2,1,0:T(8,128)(2,1)S(1)}, bf16[4,2,32,128]{3,2,1,0:T(8,128)(2,1)S(1)}, bf16[4,2,32,128]{3,2,1,0:T(8,128)(2,1)S(1)}) custom-call(s32[194]{0:T(256)S(1)} %concatenate.6.info_ref, bf16[2,32,1024]{2,1,0:T(8,128)(2,1)S(1)} %constant_dynamic-slice_fusion.rest_0_, ...), custom_call_target="tpu_custom_call" | custom-call | bytes 524288 | tf_op jit(solution)/shard_map/filter_columns/pallas_call | solution.py:267
  4.7 2.7 %collective-permute-start.5 = (bf16[4,2,32,128]{3,2,1,0:T(8,128)(2,1)S(1)}, bf16[4,2,32,128]{3,2,1,0:T(8,128)(2,1)S(1)}, u32[]{:S(2)}, u32[]{:S(2)}) collective-permute-start(bf16[4,2,32,128]{3,2,1,0:T(8,128)(2,1)S(1)} %get-tuple-element.49), channel_id=1, source_target_pairs={{0,2},{1,3},{2,0},{3,1},{4,6},{5,7},{6,4},{7,5},{8,10},{9,11},{10,... | collective-permute-start | bytes 196616 | tf_op jit(solution)/shard_map/ppermute | solution.py:90
  7.4 2.6 %collective-permute-start.6 = (bf16[4,2,32,128]{3,2,1,0:T(8,128)(2,1)S(1)}, bf16[4,2,32,128]{3,2,1,0:T(8,128)(2,1)S(1)}, u32[]{:S(2)}, u32[]{:S(2)}) collective-permute-start(bf16[4,2,32,128]{3,2,1,0:T(8,128)(2,1)S(1)} %get-tuple-element.50), channel_id=1, source_target_pairs={{0,4},{1,5},{2,6},{3,7},{4,0},{5,1},{6,2},{7,3},{8,12},{9,13},{10,... | collective-permute-start | bytes 196616 | tf_op jit(solution)/shard_map/ppermute | solution.py:90
  10.0 3.9 %range_compress.1 = (bf16[2,64,16,128]{3,2,1,0:T(8,128)(2,1)S(1)}, s32[8,16]{1,0:T(8,128)S(1)}, s32[8,16]{1,0:T(8,128)S(1)}) custom-call(s32[194]{0:T(256)S(1)} %concatenate.6.info_ref, bf16[16,8192]{1,0:T(8,128)(2,1)S(1)} %get-tuple-element.39.real_ref, bf16[16,8192]{1,0:T(8,128)(2,1)S(1)} %get-tuple-element.40.imag_ref, f32[640,128]{1,0:T(8,128)S(1)} %copy-done.1), custom_call_target="tpu_custom_call" | custom-call | flops 201326592 | bytes 1900544 | tf_op jit(solution)/shard_map/range_compress/pallas_call | solution.py:174
  13.9 0.1 collective-permute-start.1
  14.0 0.3 collective-permute-done.6
  14.4 1.7 %collective-permute-done.7 = bf16[4,2,32,128]{3,2,1,0:T(8,128)(2,1)S(1)} collective-permute-done((bf16[4,2,32,128]{3,2,1,0:T(8,128)(2,1)S(1)}, bf16[4,2,32,128]{3,2,1,0:T(8,128)(2,1)S(1)}, u32[]{:S(2)}, u32[]{:S(2)}) %collective-permute-start.7) | collective-permute-done | bytes 65568 | tf_op jit(solution)/shard_map/ppermute | solution.py:90
  16.1 2.5 %collective-permute-start.10 = (bf16[16,2,32,128]{3,2,1,0:T(8,128)(2,1)S(1)}, bf16[16,2,32,128]{3,2,1,0:T(8,128)(2,1)S(1)}, u32[]{:S(2)}, u32[]{:S(2)}) collective-permute-start(bf16[16,2,32,128]{3,2,1,0:T(8,128)(2,1)S(1)} %constant_dynamic-update-slice_fusion.rest_4_), channel_id=1, source_target_pairs={{0,24},{8,16},{16,8},{24,0},{1,25},{9,17},{17,9},{25,1},{2,26},{10... | collective-permute-start | bytes 786440 | tf_op jit(solution)/shard_map/ppermute | solution.py:90
  18.6 0.5 collective-permute-start.9
  19.1 0.5 collective-permute-start.8
  19.7 1.5 %spread_columns.1 = (bf16[8,2,32,128]{3,2,1,0:T(8,128)(2,1)S(1)}, bf16[8,2,32,128]{3,2,1,0:T(8,128)(2,1)S(1)}, bf16[8,2,32,128]{3,2,1,0:T(8,128)(2,1)S(1)}, bf16...) custom-call(s32[8,16]{1,0:T(8,128)S(1)} %get-tuple-element.42.table_, ...), custom_call_target="tpu_custom_call" | custom-call | bytes 2097152 | tf_op jit(solution)/shard_map/spread_columns/pallas_call | solution.py:221
  21.2 1.2 %collective-permute-start.11 = (bf16[8,2,32,128]{3,2,1,0:T(8,128)(2,1)S(1)}, bf16[8,2,32,128]{3,2,1,0:T(8,128)(2,1)S(1)}, u32[]{:S(2)}, u32[]{:S(2)}) collective-permute-start(bf16[8,2,32,128]{3,2,1,0:T(8,128)(2,1)S(1)} %get-tuple-element.55), channel_id=1, source_target_pairs={{0,2},{1,3},{2,0},{3,1},{4,6},{5,7},{6,4},{7,5},{8,10},{9,11},{10,... | collective-permute-start | bytes 393224 | tf_op jit(solution)/shard_map/ppermute | solution.py:90
  22.4 1.7 %collective-permute-start.12 = (bf16[8,2,32,128]{3,2,1,0:T(8,128)(2,1)S(1)}, bf16[8,2,32,128]{3,2,1,0:T(8,128)(2,1)S(1)}, u32[]{:S(2)}, u32[]{:S(2)}) collective-permute-start(bf16[8,2,32,128]{3,2,1,0:T(8,128)(2,1)S(1)} %get-tuple-element.56), channel_id=1, source_target_pairs={{0,4},{1,5},{2,6},{3,7},{4,0},{5,1},{6,2},{7,3},{8,12},{9,13},{10,... | collective-permute-start | bytes 393224 | tf_op jit(solution)/shard_map/ppermute | solution.py:90
  24.2 2.2 %collective-permute-done.10.rest_7_ = bf16[16,2,32,128]{3,2,1,0:T(8,128)(2,1)S(1)} collective-permute-done((bf16[16,2,32,128]{3,2,1,0:T(8,128)(2,1)S(1)}, bf16[16,2,32,128]{3,2,1,0:T(8,128)(2,1)S(1)}, u32[]{:S(2)}, u32[]{:S(2)}) %collective-permute-start.10) | collective-permute-done | bytes 262176 | tf_op jit(solution)/shard_map/ppermute | solution.py:90
  26.4 2.4 %collective-permute-start.13 = (bf16[8,2,32,128]{3,2,1,0:T(8,128)(2,1)S(1)}, bf16[8,2,32,128]{3,2,1,0:T(8,128)(2,1)S(1)}, u32[]{:S(2)}, u32[]{:S(2)}) collective-permute-start(bf16[8,2,32,128]{3,2,1,0:T(8,128)(2,1)S(1)} %get-tuple-element.57), channel_id=1, source_target_pairs={{0,6},{1,7},{2,4},{3,5},{4,2},{5,3},{6,0},{7,1},{8,14},{9,15},{10,... | collective-permute-start | bytes 393224 | tf_op jit(solution)/shard_map/ppermute | solution.py:90
  28.7 0.5 resample_tables.1.back_ref
  29.2 0.5 collective-permute-done.9.rest_6_
  29.7 2.1 %collective-permute-start.2 = (bf16[8,2,32,128]{3,2,1,0:T(8,128)(2,1)}, bf16[8,2,32,128]{3,2,1,0:T(8,128)(2,1)}, u32[]{:S(2)}, u32[]{:S(2)}) collective-permute-start(bf16[8,2,32,128]{3,2,1,0:T(8,128)(2,1)} %get-tuple-element.45), channel_id=1, source_target_pairs={{0,2},{1,3},{2,0},{3,1},{4,6},{5,7},{6,4},{7,5},{8,10},{9,11},{10,... | collective-permute-start | bytes 393224 | tf_op jit(solution)/shard_map/ppermute | solution.py:90
  31.9 1.9 %collective-permute-start.3 = (bf16[8,2,32,128]{3,2,1,0:T(8,128)(2,1)}, bf16[8,2,32,128]{3,2,1,0:T(8,128)(2,1)}, u32[]{:S(2)}, u32[]{:S(2)}) collective-permute-start(bf16[8,2,32,128]{3,2,1,0:T(8,128)(2,1)} %get-tuple-element.46), channel_id=1, source_target_pairs={{0,4},{1,5},{2,6},{3,7},{4,0},{5,1},{6,2},{7,3},{8,12},{9,13},{10,... | collective-permute-start | bytes 393224 | tf_op jit(solution)/shard_map/ppermute | solution.py:90
  33.8 0.6 collective-permute-start.4
  34.3 1.8 %focus.3 = (bf16[2,2,128,128]{3,2,1,0:T(8,128)(2,1)S(1)}, bf16[4,2,128,128]{3,2,1,0:T(8,128)(2,1)S(1)}, bf16[2,2,128,128]{3,2,1,0:T(8,128)(2,1)S(1)}) custom-call(s32[194]{0:T(256)S(1)} %concatenate.6.info_ref, s32[8,16]{1,0:T(8,128)S(1)} %get-tuple-element.41.table_ref, bf16[256,256]{1,0:T(8,128)(2,1)S(1)} %copy-done.2, ...), custom_call_target="tpu_custom_call" | custom-call | flops 1073741824 | bytes 11010048 | tf_op jit(solution)/shard_map/focus/pallas_call | solution.py:374
  36.1 1.5 %collective-permute-start.14 = (bf16[2,2,128,128]{3,2,1,0:T(8,128)(2,1)S(1)}, bf16[2,2,128,128]{3,2,1,0:T(8,128)(2,1)S(1)}, u32[]{:S(2)}, u32[]{:S(2)}) collective-permute-start(bf16[2,2,128,128]{3,2,1,0:T(8,128)(2,1)S(1)} %get-tuple-element.58.rest_0_), channel_id=1, source_target_pairs={{0,16},{8,24},{16,0},{24,8},{1,17},{9,25},{17,1},{25,9},{2,18},{10... | collective-permute-start | bytes 393224 | tf_op jit(solution)/shard_map/ppermute | solution.py:90
  37.6 0.6 collective-permute-start.19
  38.2 1.4 %collective-permute-start.17 = (bf16[4,2,128,128]{3,2,1,0:T(8,128)(2,1)S(1)}, bf16[4,2,128,128]{3,2,1,0:T(8,128)(2,1)S(1)}, u32[]{:S(2)}, u32[]{:S(2)}) collective-permute-start(bf16[4,2,128,128]{3,2,1,0:T(8,128)(2,1)S(1)} %get-tuple-element.60.rest_1_), channel_id=1, source_target_pairs={{0,16},{8,24},{16,0},{24,8},{1,17},{9,25},{17,1},{25,9},{2,18},{10... | collective-permute-start | bytes 786440 | tf_op jit(solution)/shard_map/ppermute | solution.py:90
  39.6 5.4 %collective-permute-done.3.rest_2_ = bf16[8,2,32,128]{3,2,1,0:T(8,128)(2,1)} collective-permute-done((bf16[8,2,32,128]{3,2,1,0:T(8,128)(2,1)}, bf16[8,2,32,128]{3,2,1,0:T(8,128)(2,1)}, u32[]{:S(2)}, u32[]{:S(2)}) %collective-permute-start.3) | collective-permute-done | bytes 131104 | tf_op jit(solution)/shard_map/ppermute | solution.py:90
  45.0 2.2 %focus.2 = (bf16[4,2,128,128]{3,2,1,0:T(8,128)(2,1)S(1)}, bf16[4,2,128,128]{3,2,1,0:T(8,128)(2,1)S(1)}) custom-call(s32[194]{0:T(256)S(1)} %concatenate.6.info_ref, s32[8,16]{1,0:T(8,128)S(1)} %get-tuple-element.41.table_ref, bf16[256,256]{1,0:T(8,128)(2,1)S(1)} %copy-done.2, bf16[8,256,256]{2,1,0:T(8,128)(2,1)S(1)} %resample_tables.1.back_ref, ...), custom_call_target="tpu_custom_call" | custom-call | flops 1073741824 | bytes 11010048 | tf_op jit(solution)/shard_map/focus/pallas_call | solution.py:374
  47.2 1.6 %collective-permute-start.16 = (bf16[2,2,128,128]{3,2,1,0:T(8,128)(2,1)S(1)}, bf16[2,2,128,128]{3,2,1,0:T(8,128)(2,1)S(1)}, u32[]{:S(2)}, u32[]{:S(2)}) collective-permute-start(bf16[2,2,128,128]{3,2,1,0:T(8,128)(2,1)S(1)} %broadcast_select_fusion.4), channel_id=1, source_target_pairs={{0,8},{8,0},{16,24},{24,16},{1,9},{9,1},{17,25},{25,17},{2,10},{10... | collective-permute-start | bytes 393224 | tf_op jit(solution)/shard_map/ppermute | solution.py:90
  48.8 1.9 %collective-permute-start.22 = (bf16[4,2,128,128]{3,2,1,0:T(8,128)(2,1)S(1)}, bf16[4,2,128,128]{3,2,1,0:T(8,128)(2,1)S(1)}, u32[]{:S(2)}, u32[]{:S(2)}) collective-permute-start(bf16[4,2,128,128]{3,2,1,0:T(8,128)(2,1)S(1)} %get-tuple-element.63.rest_0_), channel_id=1, source_target_pairs={{0,16},{8,24},{16,0},{24,8},{1,17},{9,25},{17,1},{25,9},{2,18},{10... | collective-permute-start | bytes 786440 | tf_op jit(solution)/shard_map/ppermute | solution.py:90
  50.7 0.3 collective-permute-start.20
  50.9 0.5 collective-permute-start.15
  51.5 1.5 %collective-permute-start.18 = (bf16[4,2,128,128]{3,2,1,0:T(8,128)(2,1)S(1)}, bf16[4,2,128,128]{3,2,1,0:T(8,128)(2,1)S(1)}, u32[]{:S(2)}, u32[]{:S(2)}) collective-permute-start(bf16[4,2,128,128]{3,2,1,0:T(8,128)(2,1)S(1)} %broadcast_select_fusion.1), channel_id=1, source_target_pairs={{0,8},{8,0},{16,24},{24,16},{1,9},{9,1},{17,25},{25,17},{2,10},{10... | collective-permute-start | bytes 786440 | tf_op jit(solution)/shard_map/ppermute | solution.py:90
  53.0 5.0 %collective-permute-done.22.rest_2_ = bf16[4,2,128,128]{3,2,1,0:T(8,128)(2,1)S(1)} collective-permute-done((bf16[4,2,128,128]{3,2,1,0:T(8,128)(2,1)S(1)}, bf16[4,2,128,128]{3,2,1,0:T(8,128)(2,1)S(1)}, u32[]{:S(2)}, u32[]{:S(2)}) %collective-permute-start.22) | collective-permute-done | bytes 262176 | tf_op jit(solution)/shard_map/ppermute | solution.py:90
  58.1 0.6 collective-permute-start.23
  58.7 2.4 %collective-permute-done.15.rest_2_ = bf16[4,2,128,128]{3,2,1,0:T(8,128)(2,1)S(1)} collective-permute-done((bf16[4,2,128,128]{3,2,1,0:T(8,128)(2,1)S(1)}, bf16[4,2,128,128]{3,2,1,0:T(8,128)(2,1)S(1)}, u32[]{:S(2)}, u32[]{:S(2)}) %collective-permute-start.15) | collective-permute-done | bytes 262176 | tf_op jit(solution)/shard_map/ppermute | solution.py:90
  61.1 1.7 %collective-permute-done.18.rest_4_ = bf16[4,2,128,128]{3,2,1,0:T(8,128)(2,1)S(1)} collective-permute-done((bf16[4,2,128,128]{3,2,1,0:T(8,128)(2,1)S(1)}, bf16[4,2,128,128]{3,2,1,0:T(8,128)(2,1)S(1)}, u32[]{:S(2)}, u32[]{:S(2)}) %collective-permute-start.18) | collective-permute-done | bytes 262176 | tf_op jit(solution)/shard_map/ppermute | solution.py:90
  62.8 3.0 %goldstein.3.rest_7_ = bf16[16,2,2,128,128]{4,3,2,1,0:T(8,128)(2,1)} custom-call(bf16[2,2,128,128]{3,2,1,0:T(8,128)(2,1)S(1)} %get-tuple-element.58.rest_0_, bf16[4,2,128,128]{3,2,1,0:T(8,128)(2,1)S(1)} %get-tuple-element.60.rest_1_, bf16[2,2,128,128]{3,2,1,0:T(8,128)(2,1)S(1)} %get-tuple-element.61.rest_2_, ...), custom_call_target="tpu_custom_call" | custom-call | flops 4294967296 | bytes 6291456 | tf_op jit(solution)/shard_map/goldstein/pallas_call | solution.py:464
  65.8 0.8 %collective-permute-start.21 = (bf16[4,2,128,128]{3,2,1,0:T(8,128)(2,1)S(1)}, bf16[4,2,128,128]{3,2,1,0:T(8,128)(2,1)S(1)}, u32[]{:S(2)}, u32[]{:S(2)}) collective-permute-start(bf16[4,2,128,128]{3,2,1,0:T(8,128)(2,1)S(1)} %broadcast_select_fusion.2), channel_id=1, source_target_pairs={{0,8},{8,0},{16,24},{24,16},{1,9},{9,1},{17,25},{25,17},{2,10},{10... | collective-permute-start | bytes 786440 | tf_op jit(solution)/shard_map/ppermute | solution.py:90
  66.6 1.6 %collective-permute-done.23.rest_1_ = bf16[4,2,128,128]{3,2,1,0:T(8,128)(2,1)S(1)} collective-permute-done((bf16[4,2,128,128]{3,2,1,0:T(8,128)(2,1)S(1)}, bf16[4,2,128,128]{3,2,1,0:T(8,128)(2,1)S(1)}, u32[]{:S(2)}, u32[]{:S(2)}) %collective-permute-start.23) | collective-permute-done | bytes 262176 | tf_op jit(solution)/shard_map/ppermute | solution.py:90
  68.2 2.1 %goldstein.4.rest_7_ = bf16[16,2,2,128,128]{4,3,2,1,0:T(8,128)(2,1)} custom-call(bf16[4,2,128,128]{3,2,1,0:T(8,128)(2,1)S(1)} %get-tuple-element.63.rest_0_, bf16[4,2,128,128]{3,2,1,0:T(8,128)(2,1)S(1)} %collective-permute-done.23.rest_1_, bf16[4,2,128,128]{3,2,1,0:T(8,128)(2,1)S(1)} %collective-permute-done.22.rest_2_, ...), custom_call_target="tpu_custom_call", output_to_operand_aliasing={{}: (7, {})} | custom-call | flops 2147483648 | bytes 5505024 | tf_op jit(solution)/shard_map/goldstein/pallas_call | solution.py:464
  70.2 2.0 %collective-permute-done.21.rest_1_ = bf16[4,2,128,128]{3,2,1,0:T(8,128)(2,1)S(1)} collective-permute-done((bf16[4,2,128,128]{3,2,1,0:T(8,128)(2,1)S(1)}, bf16[4,2,128,128]{3,2,1,0:T(8,128)(2,1)S(1)}, u32[]{:S(2)}, u32[]{:S(2)}) %collective-permute-start.21) | collective-permute-done | bytes 262176 | tf_op jit(solution)/shard_map/ppermute | solution.py:90
  72.2 2.1 %goldstein.5 = bf16[16,2,2,128,128]{4,3,2,1,0:T(8,128)(2,1)} custom-call(bf16[4,2,128,128]{3,2,1,0:T(8,128)(2,1)S(1)} %get-tuple-element.59.rest_0_, bf16[4,2,128,128]{3,2,1,0:T(8,128)(2,1)S(1)} %collective-permute-done.21.rest_1_, bf16[4,2,128,128]{3,2,1,0:T(8,128)(2,1)S(1)} %collective-permute-done.15.rest_2_, ...), custom_call_target="tpu_custom_call", output_to_operand_aliasing={{}: (7, {})} | custom-call | flops 2147483648 | bytes 5505024 | tf_op jit(solution)/shard_map/goldstein/pallas_call | solution.py:464
  (37 shorter events, 0.3 us)
Async XLA Ops:
  0.0 1.1 %copy-start = (bf16[2,128,1024]{2,1,0:T(8,128)(2,1)S(1)}, bf16[2,128,1024]{2,1,0:T(8,128)(2,1)}, u32[]{:S(2)}) copy-start(bf16[2,128,1024]{2,1,0:T(8,128)(2,1)} %param.22) | copy-start | bytes 1572868
  0.0 10.0 %copy-start.1 = (f32[640,128]{1,0:T(8,128)S(1)}, f32[640,128]{1,0:T(8,128)}, u32[]{:S(2)}) copy-start(f32[640,128]{1,0:T(8,128)} %constant.40.clone.tables_ref) | copy-start | bytes 983044
  0.0 3.9 %copy-start.6 = (s32[1,64]{1,0:T(1,128)S(1)}, s32[1,64]{1,0:T(1,128)}, u32[]{:S(2)}) copy-start(s32[1,64]{1,0:T(1,128)} %param.25) | copy-start | bytes 772
  0.0 3.9 %copy-start.5 = (s32[1,64]{1,0:T(1,128)S(1)}, s32[1,64]{1,0:T(1,128)}, u32[]{:S(2)}) copy-start(s32[1,64]{1,0:T(1,128)} %param.24) | copy-start | bytes 772
  0.0 3.9 %copy-start.4 = (s32[1,64]{1,0:T(1,128)S(1)}, s32[1,64]{1,0:T(1,128)}, u32[]{:S(2)}) copy-start(s32[1,64]{1,0:T(1,128)} %param.23) | copy-start | bytes 772
  1.1 2.9 %collective-permute-start = (bf16[2,32,1024]{2,1,0:T(8,128)(2,1)S(1)}, bf16[2,32,1024]{2,1,0:T(8,128)(2,1)S(1)}, u32[]{:S(2)}, u32[]{:S(2)}) collective-permute-start(bf16[2,32,1024]{2,1,0:T(8,128)(2,1)S(1)} %constant_dynamic-slice_fusion.rest_0_), channel_id=1, source_target_pairs={{0,1},{1,0},{2,3},{3,2},{4,5},{5,4},{6,7},{7,6},{8,9},{9,8},{10,11... | collective-permute-start | bytes 393224 | tf_op jit(solution)/shard_map/ppermute | solution.py:90
  3.7 25.0 %copy-start.2 = (bf16[256,256]{1,0:T(8,128)(2,1)S(1)}, bf16[256,256]{1,0:T(8,128)(2,1)}, u32[]{:S(2)}) copy-start(bf16[256,256]{1,0:T(8,128)(2,1)} %constant.47.forward_ref.rest_9_.rest_12_.rest_3_.rest_6_) | copy-start | bytes 393220
  4.7 9.3 %collective-permute-start.5 = (bf16[4,2,32,128]{3,2,1,0:T(8,128)(2,1)S(1)}, bf16[4,2,32,128]{3,2,1,0:T(8,128)(2,1)S(1)}, u32[]{:S(2)}, u32[]{:S(2)}) collective-permute-start(bf16[4,2,32,128]{3,2,1,0:T(8,128)(2,1)S(1)} %get-tuple-element.49), channel_id=1, source_target_pairs={{0,2},{1,3},{2,0},{3,1},{4,6},{5,7},{6,4},{7,5},{8,10},{9,11},{10,... | collective-permute-start | bytes 196616 | tf_op jit(solution)/shard_map/ppermute | solution.py:90
  7.4 7.0 %collective-permute-start.6 = (bf16[4,2,32,128]{3,2,1,0:T(8,128)(2,1)S(1)}, bf16[4,2,32,128]{3,2,1,0:T(8,128)(2,1)S(1)}, u32[]{:S(2)}, u32[]{:S(2)}) collective-permute-start(bf16[4,2,32,128]{3,2,1,0:T(8,128)(2,1)S(1)} %get-tuple-element.50), channel_id=1, source_target_pairs={{0,4},{1,5},{2,6},{3,7},{4,0},{5,1},{6,2},{7,3},{8,12},{9,13},{10,... | collective-permute-start | bytes 196616 | tf_op jit(solution)/shard_map/ppermute | solution.py:90
  10.0 6.1 %collective-permute-start.7 = (bf16[4,2,32,128]{3,2,1,0:T(8,128)(2,1)S(1)}, bf16[4,2,32,128]{3,2,1,0:T(8,128)(2,1)S(1)}, u32[]{:S(2)}, u32[]{:S(2)}) collective-permute-start(bf16[4,2,32,128]{3,2,1,0:T(8,128)(2,1)S(1)} %get-tuple-element.51), channel_id=1, source_target_pairs={{0,6},{1,7},{2,4},{3,5},{4,2},{5,3},{6,0},{7,1},{8,14},{9,15},{10,... | collective-permute-start | bytes 196616 | tf_op jit(solution)/shard_map/ppermute | solution.py:90
  13.9 5.8 %collective-permute-start.1 = (bf16[2,64,16,128]{3,2,1,0:T(8,128)(2,1)S(1)}, bf16[2,64,16,128]{3,2,1,0:T(8,128)(2,1)S(1)}, u32[]{:S(2)}, u32[]{:S(2)}) collective-permute-start(bf16[2,64,16,128]{3,2,1,0:T(8,128)(2,1)S(1)} %get-tuple-element.43.rest_0_), channel_id=1, source_target_pairs={{0,1},{1,0},{2,3},{3,2},{4,5},{5,4},{6,7},{7,6},{8,9},{9,8},{10,11... | collective-permute-start | bytes 1572872 | tf_op jit(solution)/shard_map/ppermute | solution.py:90
  16.1 10.3 %collective-permute-start.10 = (bf16[16,2,32,128]{3,2,1,0:T(8,128)(2,1)S(1)}, bf16[16,2,32,128]{3,2,1,0:T(8,128)(2,1)S(1)}, u32[]{:S(2)}, u32[]{:S(2)}) collective-permute-start(bf16[16,2,32,128]{3,2,1,0:T(8,128)(2,1)S(1)} %constant_dynamic-update-slice_fusion.rest_4_), channel_id=1, source_target_pairs={{0,24},{8,16},{16,8},{24,0},{1,25},{9,17},{17,9},{25,1},{2,26},{10... | collective-permute-start | bytes 786440 | tf_op jit(solution)/shard_map/ppermute | solution.py:90
  18.6 11.1 %collective-permute-start.9 = (bf16[16,2,32,128]{3,2,1,0:T(8,128)(2,1)S(1)}, bf16[16,2,32,128]{3,2,1,0:T(8,128)(2,1)S(1)}, u32[]{:S(2)}, u32[]{:S(2)}) collective-permute-start(bf16[16,2,32,128]{3,2,1,0:T(8,128)(2,1)S(1)} %constant_dynamic-update-slice_fusion.rest_4_), channel_id=1, source_target_pairs={{0,16},{8,24},{16,0},{24,8},{1,17},{9,25},{17,1},{25,9},{2,18},{10... | collective-permute-start | bytes 786440 | tf_op jit(solution)/shard_map/ppermute | solution.py:90
  19.1 12.7 %collective-permute-start.8 = (bf16[16,2,32,128]{3,2,1,0:T(8,128)(2,1)S(1)}, bf16[16,2,32,128]{3,2,1,0:T(8,128)(2,1)S(1)}, u32[]{:S(2)}, u32[]{:S(2)}) collective-permute-start(bf16[16,2,32,128]{3,2,1,0:T(8,128)(2,1)S(1)} %constant_dynamic-update-slice_fusion.rest_4_), channel_id=1, source_target_pairs={{0,8},{8,0},{16,24},{24,16},{1,9},{9,1},{17,25},{25,17},{2,10},{10... | collective-permute-start | bytes 786440 | tf_op jit(solution)/shard_map/ppermute | solution.py:90
  21.2 12.5 %collective-permute-start.11 = (bf16[8,2,32,128]{3,2,1,0:T(8,128)(2,1)S(1)}, bf16[8,2,32,128]{3,2,1,0:T(8,128)(2,1)S(1)}, u32[]{:S(2)}, u32[]{:S(2)}) collective-permute-start(bf16[8,2,32,128]{3,2,1,0:T(8,128)(2,1)S(1)} %get-tuple-element.55), channel_id=1, source_target_pairs={{0,2},{1,3},{2,0},{3,1},{4,6},{5,7},{6,4},{7,5},{8,10},{9,11},{10,... | collective-permute-start | bytes 393224 | tf_op jit(solution)/shard_map/ppermute | solution.py:90
  22.4 11.9 %collective-permute-start.12 = (bf16[8,2,32,128]{3,2,1,0:T(8,128)(2,1)S(1)}, bf16[8,2,32,128]{3,2,1,0:T(8,128)(2,1)S(1)}, u32[]{:S(2)}, u32[]{:S(2)}) collective-permute-start(bf16[8,2,32,128]{3,2,1,0:T(8,128)(2,1)S(1)} %get-tuple-element.56), channel_id=1, source_target_pairs={{0,4},{1,5},{2,6},{3,7},{4,0},{5,1},{6,2},{7,3},{8,12},{9,13},{10,... | collective-permute-start | bytes 393224 | tf_op jit(solution)/shard_map/ppermute | solution.py:90
  26.4 8.0 %collective-permute-start.13 = (bf16[8,2,32,128]{3,2,1,0:T(8,128)(2,1)S(1)}, bf16[8,2,32,128]{3,2,1,0:T(8,128)(2,1)S(1)}, u32[]{:S(2)}, u32[]{:S(2)}) collective-permute-start(bf16[8,2,32,128]{3,2,1,0:T(8,128)(2,1)S(1)} %get-tuple-element.57), channel_id=1, source_target_pairs={{0,6},{1,7},{2,4},{3,5},{4,2},{5,3},{6,0},{7,1},{8,14},{9,15},{10,... | collective-permute-start | bytes 393224 | tf_op jit(solution)/shard_map/ppermute | solution.py:90
  29.7 8.5 %collective-permute-start.2 = (bf16[8,2,32,128]{3,2,1,0:T(8,128)(2,1)}, bf16[8,2,32,128]{3,2,1,0:T(8,128)(2,1)}, u32[]{:S(2)}, u32[]{:S(2)}) collective-permute-start(bf16[8,2,32,128]{3,2,1,0:T(8,128)(2,1)} %get-tuple-element.45), channel_id=1, source_target_pairs={{0,2},{1,3},{2,0},{3,1},{4,6},{5,7},{6,4},{7,5},{8,10},{9,11},{10,... | collective-permute-start | bytes 393224 | tf_op jit(solution)/shard_map/ppermute | solution.py:90
  31.9 13.1 %collective-permute-start.3 = (bf16[8,2,32,128]{3,2,1,0:T(8,128)(2,1)}, bf16[8,2,32,128]{3,2,1,0:T(8,128)(2,1)}, u32[]{:S(2)}, u32[]{:S(2)}) collective-permute-start(bf16[8,2,32,128]{3,2,1,0:T(8,128)(2,1)} %get-tuple-element.46), channel_id=1, source_target_pairs={{0,4},{1,5},{2,6},{3,7},{4,0},{5,1},{6,2},{7,3},{8,12},{9,13},{10,... | collective-permute-start | bytes 393224 | tf_op jit(solution)/shard_map/ppermute | solution.py:90
  33.8 11.2 %collective-permute-start.4 = (bf16[8,2,32,128]{3,2,1,0:T(8,128)(2,1)}, bf16[8,2,32,128]{3,2,1,0:T(8,128)(2,1)}, u32[]{:S(2)}, u32[]{:S(2)}) collective-permute-start(bf16[8,2,32,128]{3,2,1,0:T(8,128)(2,1)} %get-tuple-element.47), channel_id=1, source_target_pairs={{0,6},{1,7},{2,4},{3,5},{4,2},{5,3},{6,0},{7,1},{8,14},{9,15},{10,... | collective-permute-start | bytes 393224 | tf_op jit(solution)/shard_map/ppermute | solution.py:90
  36.1 11.1 %collective-permute-start.14 = (bf16[2,2,128,128]{3,2,1,0:T(8,128)(2,1)S(1)}, bf16[2,2,128,128]{3,2,1,0:T(8,128)(2,1)S(1)}, u32[]{:S(2)}, u32[]{:S(2)}) collective-permute-start(bf16[2,2,128,128]{3,2,1,0:T(8,128)(2,1)S(1)} %get-tuple-element.58.rest_0_), channel_id=1, source_target_pairs={{0,16},{8,24},{16,0},{24,8},{1,17},{9,25},{17,1},{25,9},{2,18},{10... | collective-permute-start | bytes 393224 | tf_op jit(solution)/shard_map/ppermute | solution.py:90
  37.6 13.1 %collective-permute-start.19 = (bf16[2,2,128,128]{3,2,1,0:T(8,128)(2,1)S(1)}, bf16[2,2,128,128]{3,2,1,0:T(8,128)(2,1)S(1)}, u32[]{:S(2)}, u32[]{:S(2)}) collective-permute-start(bf16[2,2,128,128]{3,2,1,0:T(8,128)(2,1)S(1)} %get-tuple-element.61.rest_2_), channel_id=1, source_target_pairs={{0,16},{8,24},{16,0},{24,8},{1,17},{9,25},{17,1},{25,9},{2,18},{10... | collective-permute-start | bytes 393224 | tf_op jit(solution)/shard_map/ppermute | solution.py:90
  38.2 13.3 %collective-permute-start.17 = (bf16[4,2,128,128]{3,2,1,0:T(8,128)(2,1)S(1)}, bf16[4,2,128,128]{3,2,1,0:T(8,128)(2,1)S(1)}, u32[]{:S(2)}, u32[]{:S(2)}) collective-permute-start(bf16[4,2,128,128]{3,2,1,0:T(8,128)(2,1)S(1)} %get-tuple-element.60.rest_1_), channel_id=1, source_target_pairs={{0,16},{8,24},{16,0},{24,8},{1,17},{9,25},{17,1},{25,9},{2,18},{10... | collective-permute-start | bytes 786440 | tf_op jit(solution)/shard_map/ppermute | solution.py:90
  47.2 15.6 %copy-start.3 = (bf16[256,256]{1,0:T(8,128)(2,1)S(1)}, bf16[256,256]{1,0:T(8,128)(2,1)}, u32[]{:S(2)}) copy-start(bf16[256,256]{1,0:T(8,128)(2,1)} %constant.48.rest_10_.rest_11_.rest_4_.rest_5_) | copy-start | bytes 393220
  47.2 13.9 %collective-permute-start.16 = (bf16[2,2,128,128]{3,2,1,0:T(8,128)(2,1)S(1)}, bf16[2,2,128,128]{3,2,1,0:T(8,128)(2,1)S(1)}, u32[]{:S(2)}, u32[]{:S(2)}) collective-permute-start(bf16[2,2,128,128]{3,2,1,0:T(8,128)(2,1)S(1)} %broadcast_select_fusion.4), channel_id=1, source_target_pairs={{0,8},{8,0},{16,24},{24,16},{1,9},{9,1},{17,25},{25,17},{2,10},{10... | collective-permute-start | bytes 393224 | tf_op jit(solution)/shard_map/ppermute | solution.py:90
  48.8 9.2 %collective-permute-start.22 = (bf16[4,2,128,128]{3,2,1,0:T(8,128)(2,1)S(1)}, bf16[4,2,128,128]{3,2,1,0:T(8,128)(2,1)S(1)}, u32[]{:S(2)}, u32[]{:S(2)}) collective-permute-start(bf16[4,2,128,128]{3,2,1,0:T(8,128)(2,1)S(1)} %get-tuple-element.63.rest_0_), channel_id=1, source_target_pairs={{0,16},{8,24},{16,0},{24,8},{1,17},{9,25},{17,1},{25,9},{2,18},{10... | collective-permute-start | bytes 786440 | tf_op jit(solution)/shard_map/ppermute | solution.py:90
  50.7 10.4 %collective-permute-start.20 = (bf16[2,2,128,128]{3,2,1,0:T(8,128)(2,1)S(1)}, bf16[2,2,128,128]{3,2,1,0:T(8,128)(2,1)S(1)}, u32[]{:S(2)}, u32[]{:S(2)}) collective-permute-start(bf16[2,2,128,128]{3,2,1,0:T(8,128)(2,1)S(1)} %broadcast_select_fusion.3), channel_id=1, source_target_pairs={{0,8},{8,0},{16,24},{24,16},{1,9},{9,1},{17,25},{25,17},{2,10},{10... | collective-permute-start | bytes 393224 | tf_op jit(solution)/shard_map/ppermute | solution.py:90
  50.9 10.1 %collective-permute-start.15 = (bf16[4,2,128,128]{3,2,1,0:T(8,128)(2,1)S(1)}, bf16[4,2,128,128]{3,2,1,0:T(8,128)(2,1)S(1)}, u32[]{:S(2)}, u32[]{:S(2)}) collective-permute-start(bf16[4,2,128,128]{3,2,1,0:T(8,128)(2,1)S(1)} %get-tuple-element.59.rest_0_), channel_id=1, source_target_pairs={{0,16},{8,24},{16,0},{24,8},{1,17},{9,25},{17,1},{25,9},{2,18},{10... | collective-permute-start | bytes 786440 | tf_op jit(solution)/shard_map/ppermute | solution.py:90
  51.5 11.3 %collective-permute-start.18 = (bf16[4,2,128,128]{3,2,1,0:T(8,128)(2,1)S(1)}, bf16[4,2,128,128]{3,2,1,0:T(8,128)(2,1)S(1)}, u32[]{:S(2)}, u32[]{:S(2)}) collective-permute-start(bf16[4,2,128,128]{3,2,1,0:T(8,128)(2,1)S(1)} %broadcast_select_fusion.1), channel_id=1, source_target_pairs={{0,8},{8,0},{16,24},{24,16},{1,9},{9,1},{17,25},{25,17},{2,10},{10... | collective-permute-start | bytes 786440 | tf_op jit(solution)/shard_map/ppermute | solution.py:90
  58.1 10.1 %collective-permute-start.23 = (bf16[4,2,128,128]{3,2,1,0:T(8,128)(2,1)S(1)}, bf16[4,2,128,128]{3,2,1,0:T(8,128)(2,1)S(1)}, u32[]{:S(2)}, u32[]{:S(2)}) collective-permute-start(bf16[4,2,128,128]{3,2,1,0:T(8,128)(2,1)S(1)} %broadcast_select_fusion), channel_id=1, source_target_pairs={{0,8},{8,0},{16,24},{24,16},{1,9},{9,1},{17,25},{25,17},{2,10},{10... | collective-permute-start | bytes 786440 | tf_op jit(solution)/shard_map/ppermute | solution.py:90
  65.8 6.4 %collective-permute-start.21 = (bf16[4,2,128,128]{3,2,1,0:T(8,128)(2,1)S(1)}, bf16[4,2,128,128]{3,2,1,0:T(8,128)(2,1)S(1)}, u32[]{:S(2)}, u32[]{:S(2)}) collective-permute-start(bf16[4,2,128,128]{3,2,1,0:T(8,128)(2,1)S(1)} %broadcast_select_fusion.2), channel_id=1, source_target_pairs={{0,8},{8,0},{16,24},{24,16},{1,9},{9,1},{17,25},{25,17},{2,10},{10... | collective-permute-start | bytes 786440 | tf_op jit(solution)/shard_map/ppermute | solution.py:90

commit v6 on v5

--- a/solution.py
+++ b/solution.py
@@ -382,7 +382,7 @@
         ],
         compiler_params=params(16),
         cost_estimate=cost(
-            4 * each * 4 * pulses * (pulses + BLK) * BLK, [*pieces, *filters, forward, back] * 4
+            11 * each * 4 * pulses * (pulses + BLK) * BLK, [*pieces, *filters, forward, back] * 8
         ),
         name="focus",
     )(info, table, forward, back, *pieces, *filters)

time: 74.5 us -> 73.6 us (0.988)
  waiting for transfers between devices: 22.8 us -> 21.7 us
  Pallas kernels: 17.7 us -> 16.6 us
  starting transfers between devices: 30 us -> 30.9 us
    ppermute x24, waiting for transfers between devices: 22.8 us -> 21.7 us  [hop(): return lax.ppermute(value, axis, pairs)]
    ppermute x24, starting transfers between devices: 30 us -> 30.9 us  [hop(): return lax.ppermute(value, axis, pairs)]
  transfers between devices with their start and end apart: 24 -> 24, of which waited for: 10 -> 10; matrix products, arithmetic and copies ran while one was open for 3% -> 3% of each run, Pallas kernels for 20% -> 19%
where the time goes in v6:
time: 73.6 us; the launch traced here: 73 us
  starting transfers between devices  30.9 us (42%)
  waiting for transfers between devices  21.7 us (29%)
  Pallas kernels  16.6 us (23%)
  local copies, waits for them, and re-layouts  2.21 us (3%)
  other arithmetic  1.37 us (2%)
    ppermute x24, starting transfers between devices, hop(): return lax.ppermute(value, axis, pairs)  30.9 us
    ppermute x24, waiting for transfers between devices, hop(): return lax.ppermute(value, axis, pairs)  21.7 us
    pallas_call x3, Pallas kernels, goldstein(): pl.pallas_call(kernel, out_shape=jax.ShapeDtypeStruct((capacity, 2, 2, BL...  7.09 us
    pallas_call x1, Pallas kernels, range_compress(): pl.pallas_call(kernel, out_shape=[jax.ShapeDtypeStruct((2, outer, pulses,...  3.91 us
    pallas_call x2, Pallas kernels, focus(): pl.pallas_call(kernel, out_shape=[jax.ShapeDtypeStruct((size, 2, BLK, BLK...  3.56 us
  transfers between devices with their start and end apart: 24, of which 10 were waited for; matrix products, arithmetic and copies ran while one was open for 3% of the time, Pallas kernels for 19%

profile of v6, /device:TPU:0, one launch (start us, length us, event | category | flops | bytes accessed | tf_op | source)
XLA Modules:
  0.0 73.0 jit_solution(12863398948018572360)
XLA Ops:
  0.0 1.1 %copy-done = bf16[2,128,1024]{2,1,0:T(8,128)(2,1)S(1)} copy-done((bf16[2,128,1024]{2,1,0:T(8,128)(2,1)S(1)}, bf16[2,128,1024]{2,1,0:T(8,128)(2,1)}, u32[]{:S(2)}) %copy-start) | copy-done | bytes 524312
  1.1 0.5 collective-permute-start
  1.6 1.0 %fusion = (f32[1,8192]{1,0:T(1,128)S(1)}, f32[1,8192]{1,0:T(1,128)S(1)}) fusion(f32[2,8192]{1,0:T(2,128)} %param.21), kind=kLoop, calls=%fused_computation.14 | loop fusion | bytes 131072 | tf_op jit(solution)/shard_map/slice | solution.py:501
  2.6 1.1 %convert_element_type.49 = f32[1,2,16,8192]{3,2,1,0:T(8,128)S(1)} convert(bf16[1,2,16,8192]{3,2,1,0:T(8,128)(2,1)} %param.20) | non-fusion elementwise | flops 262144 | bytes 1572864 | tf_op jit(solution)/shard_map/convert_element_type | solution.py:500
  3.7 0.0 copy-start.2
  3.7 0.1 subtract_convert_fusion
  3.9 0.1 concatenate.6.info_ref
  4.0 0.7 %filter_columns.1 = (bf16[4,2,32,128]{3,2,1,0:T(8,128)(2,1)S(1)}, bf16[4,2,32,128]{3,2,1,0:T(8,128)(2,1)S(1)}, bf16[4,2,32,128]{3,2,1,0:T(8,128)(2,1)S(1)}, bf16[4,2,32,128]{3,2,1,0:T(8,128)(2,1)S(1)}) custom-call(s32[194]{0:T(256)S(1)} %concatenate.6.info_ref, bf16[2,32,1024]{2,1,0:T(8,128)(2,1)S(1)} %constant_dynamic-slice_fusion.rest_0_, ...), custom_call_target="tpu_custom_call" | custom-call | bytes 524288 | tf_op jit(solution)/shard_map/filter_columns/pallas_call | solution.py:267
  4.7 2.7 %collective-permute-start.5 = (bf16[4,2,32,128]{3,2,1,0:T(8,128)(2,1)S(1)}, bf16[4,2,32,128]{3,2,1,0:T(8,128)(2,1)S(1)}, u32[]{:S(2)}, u32[]{:S(2)}) collective-permute-start(bf16[4,2,32,128]{3,2,1,0:T(8,128)(2,1)S(1)} %get-tuple-element.49), channel_id=1, source_target_pairs={{0,2},{1,3},{2,0},{3,1},{4,6},{5,7},{6,4},{7,5},{8,10},{9,11},{10,... | collective-permute-start | bytes 196616 | tf_op jit(solution)/shard_map/ppermute | solution.py:90
  7.4 2.6 %collective-permute-start.6 = (bf16[4,2,32,128]{3,2,1,0:T(8,128)(2,1)S(1)}, bf16[4,2,32,128]{3,2,1,0:T(8,128)(2,1)S(1)}, u32[]{:S(2)}, u32[]{:S(2)}) collective-permute-start(bf16[4,2,32,128]{3,2,1,0:T(8,128)(2,1)S(1)} %get-tuple-element.50), channel_id=1, source_target_pairs={{0,4},{1,5},{2,6},{3,7},{4,0},{5,1},{6,2},{7,3},{8,12},{9,13},{10,... | collective-permute-start | bytes 196616 | tf_op jit(solution)/shard_map/ppermute | solution.py:90
  10.0 3.9 %range_compress.1 = (bf16[2,64,16,128]{3,2,1,0:T(8,128)(2,1)S(1)}, s32[8,16]{1,0:T(8,128)S(1)}, s32[8,16]{1,0:T(8,128)S(1)}) custom-call(s32[194]{0:T(256)S(1)} %concatenate.6.info_ref, bf16[16,8192]{1,0:T(8,128)(2,1)S(1)} %get-tuple-element.39.real_ref, bf16[16,8192]{1,0:T(8,128)(2,1)S(1)} %get-tuple-element.40.imag_ref, f32[640,128]{1,0:T(8,128)S(1)} %copy-done.1), custom_call_target="tpu_custom_call" | custom-call | flops 201326592 | bytes 1900544 | tf_op jit(solution)/shard_map/range_compress/pallas_call | solution.py:174
  13.9 0.1 collective-permute-start.1
  14.0 0.3 collective-permute-done.6
  14.4 1.7 %collective-permute-done.7 = bf16[4,2,32,128]{3,2,1,0:T(8,128)(2,1)S(1)} collective-permute-done((bf16[4,2,32,128]{3,2,1,0:T(8,128)(2,1)S(1)}, bf16[4,2,32,128]{3,2,1,0:T(8,128)(2,1)S(1)}, u32[]{:S(2)}, u32[]{:S(2)}) %collective-permute-start.7) | collective-permute-done | bytes 65568 | tf_op jit(solution)/shard_map/ppermute | solution.py:90
  16.1 2.5 %collective-permute-start.10 = (bf16[16,2,32,128]{3,2,1,0:T(8,128)(2,1)S(1)}, bf16[16,2,32,128]{3,2,1,0:T(8,128)(2,1)S(1)}, u32[]{:S(2)}, u32[]{:S(2)}) collective-permute-start(bf16[16,2,32,128]{3,2,1,0:T(8,128)(2,1)S(1)} %constant_dynamic-update-slice_fusion.rest_4_), channel_id=1, source_target_pairs={{0,24},{8,16},{16,8},{24,0},{1,25},{9,17},{17,9},{25,1},{2,26},{10... | collective-permute-start | bytes 786440 | tf_op jit(solution)/shard_map/ppermute | solution.py:90
  18.6 0.5 collective-permute-start.9
  19.1 0.5 collective-permute-start.8
  19.7 0.8 %spread_columns.1 = (bf16[8,2,32,128]{3,2,1,0:T(8,128)(2,1)S(1)}, bf16[8,2,32,128]{3,2,1,0:T(8,128)(2,1)S(1)}, bf16[8,2,32,128]{3,2,1,0:T(8,128)(2,1)S(1)}, bf16...) custom-call(s32[8,16]{1,0:T(8,128)S(1)} %get-tuple-element.42.table_, ...), custom_call_target="tpu_custom_call" | custom-call | bytes 2097152 | tf_op jit(solution)/shard_map/spread_columns/pallas_call | solution.py:221
  20.5 1.3 %collective-permute-start.11 = (bf16[8,2,32,128]{3,2,1,0:T(8,128)(2,1)S(1)}, bf16[8,2,32,128]{3,2,1,0:T(8,128)(2,1)S(1)}, u32[]{:S(2)}, u32[]{:S(2)}) collective-permute-start(bf16[8,2,32,128]{3,2,1,0:T(8,128)(2,1)S(1)} %get-tuple-element.55), channel_id=1, source_target_pairs={{0,2},{1,3},{2,0},{3,1},{4,6},{5,7},{6,4},{7,5},{8,10},{9,11},{10,... | collective-permute-start | bytes 393224 | tf_op jit(solution)/shard_map/ppermute | solution.py:90
  21.8 1.7 %collective-permute-start.12 = (bf16[8,2,32,128]{3,2,1,0:T(8,128)(2,1)S(1)}, bf16[8,2,32,128]{3,2,1,0:T(8,128)(2,1)S(1)}, u32[]{:S(2)}, u32[]{:S(2)}) collective-permute-start(bf16[8,2,32,128]{3,2,1,0:T(8,128)(2,1)S(1)} %get-tuple-element.56), channel_id=1, source_target_pairs={{0,4},{1,5},{2,6},{3,7},{4,0},{5,1},{6,2},{7,3},{8,12},{9,13},{10,... | collective-permute-start | bytes 393224 | tf_op jit(solution)/shard_map/ppermute | solution.py:90
  23.5 2.8 %collective-permute-done.10.rest_7_ = bf16[16,2,32,128]{3,2,1,0:T(8,128)(2,1)S(1)} collective-permute-done((bf16[16,2,32,128]{3,2,1,0:T(8,128)(2,1)S(1)}, bf16[16,2,32,128]{3,2,1,0:T(8,128)(2,1)S(1)}, u32[]{:S(2)}, u32[]{:S(2)}) %collective-permute-start.10) | collective-permute-done | bytes 262176 | tf_op jit(solution)/shard_map/ppermute | solution.py:90
  26.4 2.4 %collective-permute-start.13 = (bf16[8,2,32,128]{3,2,1,0:T(8,128)(2,1)S(1)}, bf16[8,2,32,128]{3,2,1,0:T(8,128)(2,1)S(1)}, u32[]{:S(2)}, u32[]{:S(2)}) collective-permute-start(bf16[8,2,32,128]{3,2,1,0:T(8,128)(2,1)S(1)} %get-tuple-element.57), channel_id=1, source_target_pairs={{0,6},{1,7},{2,4},{3,5},{4,2},{5,3},{6,0},{7,1},{8,14},{9,15},{10,... | collective-permute-start | bytes 393224 | tf_op jit(solution)/shard_map/ppermute | solution.py:90
  28.7 0.5 resample_tables.1.back_ref
  29.2 0.5 collective-permute-done.9.rest_6_
  29.7 2.1 %collective-permute-start.2 = (bf16[8,2,32,128]{3,2,1,0:T(8,128)(2,1)S(1)}, bf16[8,2,32,128]{3,2,1,0:T(8,128)(2,1)S(1)}, u32[]{:S(2)}, u32[]{:S(2)}) collective-permute-start(bf16[8,2,32,128]{3,2,1,0:T(8,128)(2,1)S(1)} %get-tuple-element.45), channel_id=1, source_target_pairs={{0,2},{1,3},{2,0},{3,1},{4,6},{5,7},{6,4},{7,5},{8,10},{9,11},{10,... | collective-permute-start | bytes 393224 | tf_op jit(solution)/shard_map/ppermute | solution.py:90
  31.9 1.9 %collective-permute-start.3 = (bf16[8,2,32,128]{3,2,1,0:T(8,128)(2,1)S(1)}, bf16[8,2,32,128]{3,2,1,0:T(8,128)(2,1)S(1)}, u32[]{:S(2)}, u32[]{:S(2)}) collective-permute-start(bf16[8,2,32,128]{3,2,1,0:T(8,128)(2,1)S(1)} %get-tuple-element.46), channel_id=1, source_target_pairs={{0,4},{1,5},{2,6},{3,7},{4,0},{5,1},{6,2},{7,3},{8,12},{9,13},{10,... | collective-permute-start | bytes 393224 | tf_op jit(solution)/shard_map/ppermute | solution.py:90
  33.8 0.6 collective-permute-start.4
  34.3 1.8 %focus.3 = (bf16[2,2,128,128]{3,2,1,0:T(8,128)(2,1)S(1)}, bf16[4,2,128,128]{3,2,1,0:T(8,128)(2,1)S(1)}, bf16[2,2,128,128]{3,2,1,0:T(8,128)(2,1)S(1)}) custom-call(s32[194]{0:T(256)S(1)} %concatenate.6.info_ref, s32[8,16]{1,0:T(8,128)S(1)} %get-tuple-element.41.table_ref, bf16[256,256]{1,0:T(8,128)(2,1)S(1)} %copy-done.2, ...), custom_call_target="tpu_custom_call" | custom-call | flops 2952790016 | bytes 22020096 | tf_op jit(solution)/shard_map/focus/pallas_call | solution.py:374
  36.1 1.5 %collective-permute-start.14 = (bf16[2,2,128,128]{3,2,1,0:T(8,128)(2,1)S(1)}, bf16[2,2,128,128]{3,2,1,0:T(8,128)(2,1)S(1)}, u32[]{:S(2)}, u32[]{:S(2)}) collective-permute-start(bf16[2,2,128,128]{3,2,1,0:T(8,128)(2,1)S(1)} %get-tuple-element.58.rest_0_), channel_id=1, source_target_pairs={{0,16},{8,24},{16,0},{24,8},{1,17},{9,25},{17,1},{25,9},{2,18},{10... | collective-permute-start | bytes 393224 | tf_op jit(solution)/shard_map/ppermute | solution.py:90
  37.6 0.6 collective-permute-start.19
  38.2 1.4 %collective-permute-start.17 = (bf16[4,2,128,128]{3,2,1,0:T(8,128)(2,1)S(1)}, bf16[4,2,128,128]{3,2,1,0:T(8,128)(2,1)S(1)}, u32[]{:S(2)}, u32[]{:S(2)}) collective-permute-start(bf16[4,2,128,128]{3,2,1,0:T(8,128)(2,1)S(1)} %get-tuple-element.60.rest_1_), channel_id=1, source_target_pairs={{0,16},{8,24},{16,0},{24,8},{1,17},{9,25},{17,1},{25,9},{2,18},{10... | collective-permute-start | bytes 786440 | tf_op jit(solution)/shard_map/ppermute | solution.py:90
  39.6 5.0 %collective-permute-done.3.rest_2_ = bf16[8,2,32,128]{3,2,1,0:T(8,128)(2,1)S(1)} collective-permute-done((bf16[8,2,32,128]{3,2,1,0:T(8,128)(2,1)S(1)}, bf16[8,2,32,128]{3,2,1,0:T(8,128)(2,1)S(1)}, u32[]{:S(2)}, u32[]{:S(2)}) %collective-permute-start.3) | collective-permute-done | bytes 131104 | tf_op jit(solution)/shard_map/ppermute | solution.py:90
  44.7 1.8 %focus.2 = (bf16[4,2,128,128]{3,2,1,0:T(8,128)(2,1)S(1)}, bf16[4,2,128,128]{3,2,1,0:T(8,128)(2,1)S(1)}) custom-call(s32[194]{0:T(256)S(1)} %concatenate.6.info_ref, s32[8,16]{1,0:T(8,128)S(1)} %get-tuple-element.41.table_ref, bf16[256,256]{1,0:T(8,128)(2,1)S(1)} %copy-done.2, bf16[8,256,256]{2,1,0:T(8,128)(2,1)S(1)} %resample_tables.1.back_ref, ...), custom_call_target="tpu_custom_call" | custom-call | flops 2952790016 | bytes 22020096 | tf_op jit(solution)/shard_map/focus/pallas_call | solution.py:374
  46.5 1.6 %collective-permute-start.16 = (bf16[2,2,128,128]{3,2,1,0:T(8,128)(2,1)S(1)}, bf16[2,2,128,128]{3,2,1,0:T(8,128)(2,1)S(1)}, u32[]{:S(2)}, u32[]{:S(2)}) collective-permute-start(bf16[2,2,128,128]{3,2,1,0:T(8,128)(2,1)S(1)} %broadcast_select_fusion.4), channel_id=1, source_target_pairs={{0,8},{8,0},{16,24},{24,16},{1,9},{9,1},{17,25},{25,17},{2,10},{10... | collective-permute-start | bytes 393224 | tf_op jit(solution)/shard_map/ppermute | solution.py:90
  48.1 1.3 %collective-permute-start.22 = (bf16[4,2,128,128]{3,2,1,0:T(8,128)(2,1)S(1)}, bf16[4,2,128,128]{3,2,1,0:T(8,128)(2,1)S(1)}, u32[]{:S(2)}, u32[]{:S(2)}) collective-permute-start(bf16[4,2,128,128]{3,2,1,0:T(8,128)(2,1)S(1)} %get-tuple-element.63.rest_0_), channel_id=1, source_target_pairs={{0,16},{8,24},{16,0},{24,8},{1,17},{9,25},{17,1},{25,9},{2,18},{10... | collective-permute-start | bytes 786440 | tf_op jit(solution)/shard_map/ppermute | solution.py:90
  49.4 0.8 %collective-permute-start.20 = (bf16[2,2,128,128]{3,2,1,0:T(8,128)(2,1)S(1)}, bf16[2,2,128,128]{3,2,1,0:T(8,128)(2,1)S(1)}, u32[]{:S(2)}, u32[]{:S(2)}) collective-permute-start(bf16[2,2,128,128]{3,2,1,0:T(8,128)(2,1)S(1)} %broadcast_select_fusion.3), channel_id=1, source_target_pairs={{0,8},{8,0},{16,24},{24,16},{1,9},{9,1},{17,25},{25,17},{2,10},{10... | collective-permute-start | bytes 393224 | tf_op jit(solution)/shard_map/ppermute | solution.py:90
  50.2 0.5 collective-permute-start.15
  50.8 1.9 %collective-permute-start.18 = (bf16[4,2,128,128]{3,2,1,0:T(8,128)(2,1)S(1)}, bf16[4,2,128,128]{3,2,1,0:T(8,128)(2,1)S(1)}, u32[]{:S(2)}, u32[]{:S(2)}) collective-permute-start(bf16[4,2,128,128]{3,2,1,0:T(8,128)(2,1)S(1)} %broadcast_select_fusion.1), channel_id=1, source_target_pairs={{0,8},{8,0},{16,24},{24,16},{1,9},{9,1},{17,25},{25,17},{2,10},{10... | collective-permute-start | bytes 786440 | tf_op jit(solution)/shard_map/ppermute | solution.py:90
  52.6 4.7 %collective-permute-done.22.rest_2_ = bf16[4,2,128,128]{3,2,1,0:T(8,128)(2,1)S(1)} collective-permute-done((bf16[4,2,128,128]{3,2,1,0:T(8,128)(2,1)S(1)}, bf16[4,2,128,128]{3,2,1,0:T(8,128)(2,1)S(1)}, u32[]{:S(2)}, u32[]{:S(2)}) %collective-permute-start.22) | collective-permute-done | bytes 262176 | tf_op jit(solution)/shard_map/ppermute | solution.py:90
  57.3 0.9 %collective-permute-start.23 = (bf16[4,2,128,128]{3,2,1,0:T(8,128)(2,1)S(1)}, bf16[4,2,128,128]{3,2,1,0:T(8,128)(2,1)S(1)}, u32[]{:S(2)}, u32[]{:S(2)}) collective-permute-start(bf16[4,2,128,128]{3,2,1,0:T(8,128)(2,1)S(1)} %broadcast_select_fusion), channel_id=1, source_target_pairs={{0,8},{8,0},{16,24},{24,16},{1,9},{9,1},{17,25},{25,17},{2,10},{10... | collective-permute-start | bytes 786440 | tf_op jit(solution)/shard_map/ppermute | solution.py:90
  58.3 2.4 %collective-permute-done.15.rest_2_ = bf16[4,2,128,128]{3,2,1,0:T(8,128)(2,1)S(1)} collective-permute-done((bf16[4,2,128,128]{3,2,1,0:T(8,128)(2,1)S(1)}, bf16[4,2,128,128]{3,2,1,0:T(8,128)(2,1)S(1)}, u32[]{:S(2)}, u32[]{:S(2)}) %collective-permute-start.15) | collective-permute-done | bytes 262176 | tf_op jit(solution)/shard_map/ppermute | solution.py:90
  60.7 0.8 %collective-permute-done.18.rest_4_ = bf16[4,2,128,128]{3,2,1,0:T(8,128)(2,1)S(1)} collective-permute-done((bf16[4,2,128,128]{3,2,1,0:T(8,128)(2,1)S(1)}, bf16[4,2,128,128]{3,2,1,0:T(8,128)(2,1)S(1)}, u32[]{:S(2)}, u32[]{:S(2)}) %collective-permute-start.18) | collective-permute-done | bytes 262176 | tf_op jit(solution)/shard_map/ppermute | solution.py:90
  61.5 3.0 %goldstein.3.rest_7_ = bf16[16,2,2,128,128]{4,3,2,1,0:T(8,128)(2,1)} custom-call(bf16[2,2,128,128]{3,2,1,0:T(8,128)(2,1)S(1)} %get-tuple-element.58.rest_0_, bf16[4,2,128,128]{3,2,1,0:T(8,128)(2,1)S(1)} %get-tuple-element.60.rest_1_, bf16[2,2,128,128]{3,2,1,0:T(8,128)(2,1)S(1)} %get-tuple-element.61.rest_2_, ...), custom_call_target="tpu_custom_call" | custom-call | flops 4294967296 | bytes 6291456 | tf_op jit(solution)/shard_map/goldstein/pallas_call | solution.py:464
  64.5 1.0 %collective-permute-start.21 = (bf16[4,2,128,128]{3,2,1,0:T(8,128)(2,1)S(1)}, bf16[4,2,128,128]{3,2,1,0:T(8,128)(2,1)S(1)}, u32[]{:S(2)}, u32[]{:S(2)}) collective-permute-start(bf16[4,2,128,128]{3,2,1,0:T(8,128)(2,1)S(1)} %broadcast_select_fusion.2), channel_id=1, source_target_pairs={{0,8},{8,0},{16,24},{24,16},{1,9},{9,1},{17,25},{25,17},{2,10},{10... | collective-permute-start | bytes 786440 | tf_op jit(solution)/shard_map/ppermute | solution.py:90
  65.5 0.4 collective-permute-done.23.rest_1_
  65.9 2.1 %goldstein.4.rest_7_ = bf16[16,2,2,128,128]{4,3,2,1,0:T(8,128)(2,1)} custom-call(bf16[4,2,128,128]{3,2,1,0:T(8,128)(2,1)S(1)} %get-tuple-element.63.rest_0_, bf16[4,2,128,128]{3,2,1,0:T(8,128)(2,1)S(1)} %collective-permute-done.23.rest_1_, bf16[4,2,128,128]{3,2,1,0:T(8,128)(2,1)S(1)} %collective-permute-done.22.rest_2_, ...), custom_call_target="tpu_custom_call", output_to_operand_aliasing={{}: (7, {})} | custom-call | flops 2147483648 | bytes 5505024 | tf_op jit(solution)/shard_map/goldstein/pallas_call | solution.py:464
  67.9 3.0 %collective-permute-done.21.rest_1_ = bf16[4,2,128,128]{3,2,1,0:T(8,128)(2,1)S(1)} collective-permute-done((bf16[4,2,128,128]{3,2,1,0:T(8,128)(2,1)S(1)}, bf16[4,2,128,128]{3,2,1,0:T(8,128)(2,1)S(1)}, u32[]{:S(2)}, u32[]{:S(2)}) %collective-permute-start.21) | collective-permute-done | bytes 262176 | tf_op jit(solution)/shard_map/ppermute | solution.py:90
  70.9 2.1 %goldstein.5 = bf16[16,2,2,128,128]{4,3,2,1,0:T(8,128)(2,1)} custom-call(bf16[4,2,128,128]{3,2,1,0:T(8,128)(2,1)S(1)} %get-tuple-element.59.rest_0_, bf16[4,2,128,128]{3,2,1,0:T(8,128)(2,1)S(1)} %collective-permute-done.21.rest_1_, bf16[4,2,128,128]{3,2,1,0:T(8,128)(2,1)S(1)} %collective-permute-done.15.rest_2_, ...), custom_call_target="tpu_custom_call", output_to_operand_aliasing={{}: (7, {})} | custom-call | flops 2147483648 | bytes 5505024 | tf_op jit(solution)/shard_map/goldstein/pallas_call | solution.py:464
  (37 shorter events, 0.3 us)
Async XLA Ops:
  0.0 1.1 %copy-start = (bf16[2,128,1024]{2,1,0:T(8,128)(2,1)S(1)}, bf16[2,128,1024]{2,1,0:T(8,128)(2,1)}, u32[]{:S(2)}) copy-start(bf16[2,128,1024]{2,1,0:T(8,128)(2,1)} %param.22) | copy-start | bytes 1572868
  0.0 10.0 %copy-start.1 = (f32[640,128]{1,0:T(8,128)S(1)}, f32[640,128]{1,0:T(8,128)}, u32[]{:S(2)}) copy-start(f32[640,128]{1,0:T(8,128)} %constant.40.clone.tables_ref) | copy-start | bytes 983044
  0.0 3.9 %copy-start.6 = (s32[1,64]{1,0:T(1,128)S(1)}, s32[1,64]{1,0:T(1,128)}, u32[]{:S(2)}) copy-start(s32[1,64]{1,0:T(1,128)} %param.25) | copy-start | bytes 772
  0.0 3.9 %copy-start.5 = (s32[1,64]{1,0:T(1,128)S(1)}, s32[1,64]{1,0:T(1,128)}, u32[]{:S(2)}) copy-start(s32[1,64]{1,0:T(1,128)} %param.24) | copy-start | bytes 772
  0.0 3.9 %copy-start.4 = (s32[1,64]{1,0:T(1,128)S(1)}, s32[1,64]{1,0:T(1,128)}, u32[]{:S(2)}) copy-start(s32[1,64]{1,0:T(1,128)} %param.23) | copy-start | bytes 772
  1.1 2.9 %collective-permute-start = (bf16[2,32,1024]{2,1,0:T(8,128)(2,1)S(1)}, bf16[2,32,1024]{2,1,0:T(8,128)(2,1)S(1)}, u32[]{:S(2)}, u32[]{:S(2)}) collective-permute-start(bf16[2,32,1024]{2,1,0:T(8,128)(2,1)S(1)} %constant_dynamic-slice_fusion.rest_0_), channel_id=1, source_target_pairs={{0,1},{1,0},{2,3},{3,2},{4,5},{5,4},{6,7},{7,6},{8,9},{9,8},{10,11... | collective-permute-start | bytes 393224 | tf_op jit(solution)/shard_map/ppermute | solution.py:90
  3.7 25.0 %copy-start.2 = (bf16[256,256]{1,0:T(8,128)(2,1)S(1)}, bf16[256,256]{1,0:T(8,128)(2,1)}, u32[]{:S(2)}) copy-start(bf16[256,256]{1,0:T(8,128)(2,1)} %constant.47.forward_ref.rest_9_.rest_12_.rest_3_.rest_6_) | copy-start | bytes 393220
  4.7 9.3 %collective-permute-start.5 = (bf16[4,2,32,128]{3,2,1,0:T(8,128)(2,1)S(1)}, bf16[4,2,32,128]{3,2,1,0:T(8,128)(2,1)S(1)}, u32[]{:S(2)}, u32[]{:S(2)}) collective-permute-start(bf16[4,2,32,128]{3,2,1,0:T(8,128)(2,1)S(1)} %get-tuple-element.49), channel_id=1, source_target_pairs={{0,2},{1,3},{2,0},{3,1},{4,6},{5,7},{6,4},{7,5},{8,10},{9,11},{10,... | collective-permute-start | bytes 196616 | tf_op jit(solution)/shard_map/ppermute | solution.py:90
  7.4 7.0 %collective-permute-start.6 = (bf16[4,2,32,128]{3,2,1,0:T(8,128)(2,1)S(1)}, bf16[4,2,32,128]{3,2,1,0:T(8,128)(2,1)S(1)}, u32[]{:S(2)}, u32[]{:S(2)}) collective-permute-start(bf16[4,2,32,128]{3,2,1,0:T(8,128)(2,1)S(1)} %get-tuple-element.50), channel_id=1, source_target_pairs={{0,4},{1,5},{2,6},{3,7},{4,0},{5,1},{6,2},{7,3},{8,12},{9,13},{10,... | collective-permute-start | bytes 196616 | tf_op jit(solution)/shard_map/ppermute | solution.py:90
  10.0 6.1 %collective-permute-start.7 = (bf16[4,2,32,128]{3,2,1,0:T(8,128)(2,1)S(1)}, bf16[4,2,32,128]{3,2,1,0:T(8,128)(2,1)S(1)}, u32[]{:S(2)}, u32[]{:S(2)}) collective-permute-start(bf16[4,2,32,128]{3,2,1,0:T(8,128)(2,1)S(1)} %get-tuple-element.51), channel_id=1, source_target_pairs={{0,6},{1,7},{2,4},{3,5},{4,2},{5,3},{6,0},{7,1},{8,14},{9,15},{10,... | collective-permute-start | bytes 196616 | tf_op jit(solution)/shard_map/ppermute | solution.py:90
  13.9 5.8 %collective-permute-start.1 = (bf16[2,64,16,128]{3,2,1,0:T(8,128)(2,1)S(1)}, bf16[2,64,16,128]{3,2,1,0:T(8,128)(2,1)S(1)}, u32[]{:S(2)}, u32[]{:S(2)}) collective-permute-start(bf16[2,64,16,128]{3,2,1,0:T(8,128)(2,1)S(1)} %get-tuple-element.43.rest_0_), channel_id=1, source_target_pairs={{0,1},{1,0},{2,3},{3,2},{4,5},{5,4},{6,7},{7,6},{8,9},{9,8},{10,11... | collective-permute-start | bytes 1572872 | tf_op jit(solution)/shard_map/ppermute | solution.py:90
  16.1 10.3 %collective-permute-start.10 = (bf16[16,2,32,128]{3,2,1,0:T(8,128)(2,1)S(1)}, bf16[16,2,32,128]{3,2,1,0:T(8,128)(2,1)S(1)}, u32[]{:S(2)}, u32[]{:S(2)}) collective-permute-start(bf16[16,2,32,128]{3,2,1,0:T(8,128)(2,1)S(1)} %constant_dynamic-update-slice_fusion.rest_4_), channel_id=1, source_target_pairs={{0,24},{8,16},{16,8},{24,0},{1,25},{9,17},{17,9},{25,1},{2,26},{10... | collective-permute-start | bytes 786440 | tf_op jit(solution)/shard_map/ppermute | solution.py:90
  18.6 11.1 %collective-permute-start.9 = (bf16[16,2,32,128]{3,2,1,0:T(8,128)(2,1)S(1)}, bf16[16,2,32,128]{3,2,1,0:T(8,128)(2,1)S(1)}, u32[]{:S(2)}, u32[]{:S(2)}) collective-permute-start(bf16[16,2,32,128]{3,2,1,0:T(8,128)(2,1)S(1)} %constant_dynamic-update-slice_fusion.rest_4_), channel_id=1, source_target_pairs={{0,16},{8,24},{16,0},{24,8},{1,17},{9,25},{17,1},{25,9},{2,18},{10... | collective-permute-start | bytes 786440 | tf_op jit(solution)/shard_map/ppermute | solution.py:90
  19.1 12.7 %collective-permute-start.8 = (bf16[16,2,32,128]{3,2,1,0:T(8,128)(2,1)S(1)}, bf16[16,2,32,128]{3,2,1,0:T(8,128)(2,1)S(1)}, u32[]{:S(2)}, u32[]{:S(2)}) collective-permute-start(bf16[16,2,32,128]{3,2,1,0:T(8,128)(2,1)S(1)} %constant_dynamic-update-slice_fusion.rest_4_), channel_id=1, source_target_pairs={{0,8},{8,0},{16,24},{24,16},{1,9},{9,1},{17,25},{25,17},{2,10},{10... | collective-permute-start | bytes 786440 | tf_op jit(solution)/shard_map/ppermute | solution.py:90
  20.5 13.3 %collective-permute-start.11 = (bf16[8,2,32,128]{3,2,1,0:T(8,128)(2,1)S(1)}, bf16[8,2,32,128]{3,2,1,0:T(8,128)(2,1)S(1)}, u32[]{:S(2)}, u32[]{:S(2)}) collective-permute-start(bf16[8,2,32,128]{3,2,1,0:T(8,128)(2,1)S(1)} %get-tuple-element.55), channel_id=1, source_target_pairs={{0,2},{1,3},{2,0},{3,1},{4,6},{5,7},{6,4},{7,5},{8,10},{9,11},{10,... | collective-permute-start | bytes 393224 | tf_op jit(solution)/shard_map/ppermute | solution.py:90
  21.8 12.5 %collective-permute-start.12 = (bf16[8,2,32,128]{3,2,1,0:T(8,128)(2,1)S(1)}, bf16[8,2,32,128]{3,2,1,0:T(8,128)(2,1)S(1)}, u32[]{:S(2)}, u32[]{:S(2)}) collective-permute-start(bf16[8,2,32,128]{3,2,1,0:T(8,128)(2,1)S(1)} %get-tuple-element.56), channel_id=1, source_target_pairs={{0,4},{1,5},{2,6},{3,7},{4,0},{5,1},{6,2},{7,3},{8,12},{9,13},{10,... | collective-permute-start | bytes 393224 | tf_op jit(solution)/shard_map/ppermute | solution.py:90
  26.4 8.0 %collective-permute-start.13 = (bf16[8,2,32,128]{3,2,1,0:T(8,128)(2,1)S(1)}, bf16[8,2,32,128]{3,2,1,0:T(8,128)(2,1)S(1)}, u32[]{:S(2)}, u32[]{:S(2)}) collective-permute-start(bf16[8,2,32,128]{3,2,1,0:T(8,128)(2,1)S(1)} %get-tuple-element.57), channel_id=1, source_target_pairs={{0,6},{1,7},{2,4},{3,5},{4,2},{5,3},{6,0},{7,1},{8,14},{9,15},{10,... | collective-permute-start | bytes 393224 | tf_op jit(solution)/shard_map/ppermute | solution.py:90
  29.7 8.5 %collective-permute-start.2 = (bf16[8,2,32,128]{3,2,1,0:T(8,128)(2,1)S(1)}, bf16[8,2,32,128]{3,2,1,0:T(8,128)(2,1)S(1)}, u32[]{:S(2)}, u32[]{:S(2)}) collective-permute-start(bf16[8,2,32,128]{3,2,1,0:T(8,128)(2,1)S(1)} %get-tuple-element.45), channel_id=1, source_target_pairs={{0,2},{1,3},{2,0},{3,1},{4,6},{5,7},{6,4},{7,5},{8,10},{9,11},{10,... | collective-permute-start | bytes 393224 | tf_op jit(solution)/shard_map/ppermute | solution.py:90
  31.9 12.8 %collective-permute-start.3 = (bf16[8,2,32,128]{3,2,1,0:T(8,128)(2,1)S(1)}, bf16[8,2,32,128]{3,2,1,0:T(8,128)(2,1)S(1)}, u32[]{:S(2)}, u32[]{:S(2)}) collective-permute-start(bf16[8,2,32,128]{3,2,1,0:T(8,128)(2,1)S(1)} %get-tuple-element.46), channel_id=1, source_target_pairs={{0,4},{1,5},{2,6},{3,7},{4,0},{5,1},{6,2},{7,3},{8,12},{9,13},{10,... | collective-permute-start | bytes 393224 | tf_op jit(solution)/shard_map/ppermute | solution.py:90
  33.8 10.9 %collective-permute-start.4 = (bf16[8,2,32,128]{3,2,1,0:T(8,128)(2,1)S(1)}, bf16[8,2,32,128]{3,2,1,0:T(8,128)(2,1)S(1)}, u32[]{:S(2)}, u32[]{:S(2)}) collective-permute-start(bf16[8,2,32,128]{3,2,1,0:T(8,128)(2,1)S(1)} %get-tuple-element.47), channel_id=1, source_target_pairs={{0,6},{1,7},{2,4},{3,5},{4,2},{5,3},{6,0},{7,1},{8,14},{9,15},{10,... | collective-permute-start | bytes 393224 | tf_op jit(solution)/shard_map/ppermute | solution.py:90
  36.1 10.4 %collective-permute-start.14 = (bf16[2,2,128,128]{3,2,1,0:T(8,128)(2,1)S(1)}, bf16[2,2,128,128]{3,2,1,0:T(8,128)(2,1)S(1)}, u32[]{:S(2)}, u32[]{:S(2)}) collective-permute-start(bf16[2,2,128,128]{3,2,1,0:T(8,128)(2,1)S(1)} %get-tuple-element.58.rest_0_), channel_id=1, source_target_pairs={{0,16},{8,24},{16,0},{24,8},{1,17},{9,25},{17,1},{25,9},{2,18},{10... | collective-permute-start | bytes 393224 | tf_op jit(solution)/shard_map/ppermute | solution.py:90
  37.6 11.8 %collective-permute-start.19 = (bf16[2,2,128,128]{3,2,1,0:T(8,128)(2,1)S(1)}, bf16[2,2,128,128]{3,2,1,0:T(8,128)(2,1)S(1)}, u32[]{:S(2)}, u32[]{:S(2)}) collective-permute-start(bf16[2,2,128,128]{3,2,1,0:T(8,128)(2,1)S(1)} %get-tuple-element.61.rest_2_), channel_id=1, source_target_pairs={{0,16},{8,24},{16,0},{24,8},{1,17},{9,25},{17,1},{25,9},{2,18},{10... | collective-permute-start | bytes 393224 | tf_op jit(solution)/shard_map/ppermute | solution.py:90
  38.2 12.5 %collective-permute-start.17 = (bf16[4,2,128,128]{3,2,1,0:T(8,128)(2,1)S(1)}, bf16[4,2,128,128]{3,2,1,0:T(8,128)(2,1)S(1)}, u32[]{:S(2)}, u32[]{:S(2)}) collective-permute-start(bf16[4,2,128,128]{3,2,1,0:T(8,128)(2,1)S(1)} %get-tuple-element.60.rest_1_), channel_id=1, source_target_pairs={{0,16},{8,24},{16,0},{24,8},{1,17},{9,25},{17,1},{25,9},{2,18},{10... | collective-permute-start | bytes 786440 | tf_op jit(solution)/shard_map/ppermute | solution.py:90
  46.5 15.0 %copy-start.3 = (bf16[256,256]{1,0:T(8,128)(2,1)S(1)}, bf16[256,256]{1,0:T(8,128)(2,1)}, u32[]{:S(2)}) copy-start(bf16[256,256]{1,0:T(8,128)(2,1)} %constant.48.rest_10_.rest_11_.rest_4_.rest_5_) | copy-start | bytes 393220
  46.5 14.1 %collective-permute-start.16 = (bf16[2,2,128,128]{3,2,1,0:T(8,128)(2,1)S(1)}, bf16[2,2,128,128]{3,2,1,0:T(8,128)(2,1)S(1)}, u32[]{:S(2)}, u32[]{:S(2)}) collective-permute-start(bf16[2,2,128,128]{3,2,1,0:T(8,128)(2,1)S(1)} %broadcast_select_fusion.4), channel_id=1, source_target_pairs={{0,8},{8,0},{16,24},{24,16},{1,9},{9,1},{17,25},{25,17},{2,10},{10... | collective-permute-start | bytes 393224 | tf_op jit(solution)/shard_map/ppermute | solution.py:90
  48.1 9.2 %collective-permute-start.22 = (bf16[4,2,128,128]{3,2,1,0:T(8,128)(2,1)S(1)}, bf16[4,2,128,128]{3,2,1,0:T(8,128)(2,1)S(1)}, u32[]{:S(2)}, u32[]{:S(2)}) collective-permute-start(bf16[4,2,128,128]{3,2,1,0:T(8,128)(2,1)S(1)} %get-tuple-element.63.rest_0_), channel_id=1, source_target_pairs={{0,16},{8,24},{16,0},{24,8},{1,17},{9,25},{17,1},{25,9},{2,18},{10... | collective-permute-start | bytes 786440 | tf_op jit(solution)/shard_map/ppermute | solution.py:90
  49.4 11.3 %collective-permute-start.20 = (bf16[2,2,128,128]{3,2,1,0:T(8,128)(2,1)S(1)}, bf16[2,2,128,128]{3,2,1,0:T(8,128)(2,1)S(1)}, u32[]{:S(2)}, u32[]{:S(2)}) collective-permute-start(bf16[2,2,128,128]{3,2,1,0:T(8,128)(2,1)S(1)} %broadcast_select_fusion.3), channel_id=1, source_target_pairs={{0,8},{8,0},{16,24},{24,16},{1,9},{9,1},{17,25},{25,17},{2,10},{10... | collective-permute-start | bytes 393224 | tf_op jit(solution)/shard_map/ppermute | solution.py:90
  50.2 10.4 %collective-permute-start.15 = (bf16[4,2,128,128]{3,2,1,0:T(8,128)(2,1)S(1)}, bf16[4,2,128,128]{3,2,1,0:T(8,128)(2,1)S(1)}, u32[]{:S(2)}, u32[]{:S(2)}) collective-permute-start(bf16[4,2,128,128]{3,2,1,0:T(8,128)(2,1)S(1)} %get-tuple-element.59.rest_0_), channel_id=1, source_target_pairs={{0,16},{8,24},{16,0},{24,8},{1,17},{9,25},{17,1},{25,9},{2,18},{10... | collective-permute-start | bytes 786440 | tf_op jit(solution)/shard_map/ppermute | solution.py:90
  50.8 10.7 %collective-permute-start.18 = (bf16[4,2,128,128]{3,2,1,0:T(8,128)(2,1)S(1)}, bf16[4,2,128,128]{3,2,1,0:T(8,128)(2,1)S(1)}, u32[]{:S(2)}, u32[]{:S(2)}) collective-permute-start(bf16[4,2,128,128]{3,2,1,0:T(8,128)(2,1)S(1)} %broadcast_select_fusion.1), channel_id=1, source_target_pairs={{0,8},{8,0},{16,24},{24,16},{1,9},{9,1},{17,25},{25,17},{2,10},{10... | collective-permute-start | bytes 786440 | tf_op jit(solution)/shard_map/ppermute | solution.py:90
  57.3 8.5 %collective-permute-start.23 = (bf16[4,2,128,128]{3,2,1,0:T(8,128)(2,1)S(1)}, bf16[4,2,128,128]{3,2,1,0:T(8,128)(2,1)S(1)}, u32[]{:S(2)}, u32[]{:S(2)}) collective-permute-start(bf16[4,2,128,128]{3,2,1,0:T(8,128)(2,1)S(1)} %broadcast_select_fusion), channel_id=1, source_target_pairs={{0,8},{8,0},{16,24},{24,16},{1,9},{9,1},{17,25},{25,17},{2,10},{10... | collective-permute-start | bytes 786440 | tf_op jit(solution)/shard_map/ppermute | solution.py:90
  64.5 6.4 %collective-permute-start.21 = (bf16[4,2,128,128]{3,2,1,0:T(8,128)(2,1)S(1)}, bf16[4,2,128,128]{3,2,1,0:T(8,128)(2,1)S(1)}, u32[]{:S(2)}, u32[]{:S(2)}) collective-permute-start(bf16[4,2,128,128]{3,2,1,0:T(8,128)(2,1)S(1)} %broadcast_select_fusion.2), channel_id=1, source_target_pairs={{0,8},{8,0},{16,24},{24,16},{1,9},{9,1},{17,25},{25,17},{2,10},{10... | collective-permute-start | bytes 786440 | tf_op jit(solution)/shard_map/ppermute | solution.py:90

commit v7 on v6

--- a/solution.py
+++ b/solution.py
@@ -448,13 +448,14 @@
                     jnp.concatenate([(s_re * weight).astype(BF), (s_im * weight).astype(BF)], axis=0)
                 )
             back = aside(mm(bl_ref[...], jnp.concatenate(weighted, axis=1)).astype(BF))
-            filtered = mm(back, br_ref[...]).astype(BF)
-            for p in range(len(pairs)):
-                for part in range(2):
-                    buffer[base + p // 2, p % 2, part] = filtered[
-                        p * BLK : (p + 1) * BLK, part * BLK : (part + 1) * BLK
-                    ]
-            for s in batched:
+            for n, s in enumerate(batched):
+                mine = back[2 * n * BLK : 2 * (n + 1) * BLK]
+                filtered = mm(mine, br_ref[...]).astype(BF)
+                for p in range(2):
+                    for part in range(2):
+                        buffer[s, p, part] = filtered[
+                            p * BLK : (p + 1) * BLK, part * BLK : (part + 1) * BLK
+                        ]
                 pltpu.make_async_copy(buffer.at[s], out_ref.at[start + s], sems.at[s]).start()
         for s in range(count):
             pltpu.make_async_copy(buffer.at[s], out_ref.at[start + s], sems.at[s]).wait()

time: 73.6 us -> 73.5 us (level)
  no operation moved by 1% of the time
where the time goes in v7:
time: 73.5 us; the launch traced here: 72.8 us
  starting transfers between devices  30.9 us (42%)
  waiting for transfers between devices  21.8 us (30%)
  Pallas kernels  16.3 us (22%)
  local copies, waits for them, and re-layouts  2.21 us (3%)
  other arithmetic  1.37 us (2%)
    ppermute x24, starting transfers between devices, hop(): return lax.ppermute(value, axis, pairs)  30.9 us
    ppermute x24, waiting for transfers between devices, hop(): return lax.ppermute(value, axis, pairs)  21.8 us
    pallas_call x3, Pallas kernels, goldstein(): pl.pallas_call(kernel, out_shape=jax.ShapeDtypeStruct((capacity, 2, 2, BL...  6.81 us
    pallas_call x1, Pallas kernels, range_compress(): pl.pallas_call(kernel, out_shape=[jax.ShapeDtypeStruct((2, outer, pulses,...  3.91 us
    pallas_call x2, Pallas kernels, focus(): pl.pallas_call(kernel, out_shape=[jax.ShapeDtypeStruct((size, 2, BLK, BLK...  3.56 us
  transfers between devices with their start and end apart: 24, of which 10 were waited for; matrix products, arithmetic and copies ran while one was open for 3% of the time, Pallas kernels for 19%

profile of v7, /device:TPU:0, one launch (start us, length us, event | category | flops | bytes accessed | tf_op | source)
XLA Modules:
  0.0 72.8 jit_solution(9568119805692784417)
XLA Ops:
  0.0 1.1 %copy-done = bf16[2,128,1024]{2,1,0:T(8,128)(2,1)S(1)} copy-done((bf16[2,128,1024]{2,1,0:T(8,128)(2,1)S(1)}, bf16[2,128,1024]{2,1,0:T(8,128)(2,1)}, u32[]{:S(2)}) %copy-start) | copy-done | bytes 524312
  1.1 0.5 collective-permute-start
  1.6 1.0 %fusion = (f32[1,8192]{1,0:T(1,128)S(1)}, f32[1,8192]{1,0:T(1,128)S(1)}) fusion(f32[2,8192]{1,0:T(2,128)} %param.21), kind=kLoop, calls=%fused_computation.14 | loop fusion | bytes 131072 | tf_op jit(solution)/shard_map/slice | solution.py:502
  2.6 1.1 %convert_element_type.49 = f32[1,2,16,8192]{3,2,1,0:T(8,128)S(1)} convert(bf16[1,2,16,8192]{3,2,1,0:T(8,128)(2,1)} %param.20) | non-fusion elementwise | flops 262144 | bytes 1572864 | tf_op jit(solution)/shard_map/convert_element_type | solution.py:501
  3.7 0.0 copy-start.2
  3.7 0.1 subtract_convert_fusion
  3.9 0.1 concatenate.6.info_ref
  4.0 0.7 %filter_columns.1 = (bf16[4,2,32,128]{3,2,1,0:T(8,128)(2,1)S(1)}, bf16[4,2,32,128]{3,2,1,0:T(8,128)(2,1)S(1)}, bf16[4,2,32,128]{3,2,1,0:T(8,128)(2,1)S(1)}, bf16[4,2,32,128]{3,2,1,0:T(8,128)(2,1)S(1)}) custom-call(s32[194]{0:T(256)S(1)} %concatenate.6.info_ref, bf16[2,32,1024]{2,1,0:T(8,128)(2,1)S(1)} %constant_dynamic-slice_fusion.rest_0_, ...), custom_call_target="tpu_custom_call" | custom-call | bytes 524288 | tf_op jit(solution)/shard_map/filter_columns/pallas_call | solution.py:267
  4.7 2.7 %collective-permute-start.5 = (bf16[4,2,32,128]{3,2,1,0:T(8,128)(2,1)S(1)}, bf16[4,2,32,128]{3,2,1,0:T(8,128)(2,1)S(1)}, u32[]{:S(2)}, u32[]{:S(2)}) collective-permute-start(bf16[4,2,32,128]{3,2,1,0:T(8,128)(2,1)S(1)} %get-tuple-element.49), channel_id=1, source_target_pairs={{0,2},{1,3},{2,0},{3,1},{4,6},{5,7},{6,4},{7,5},{8,10},{9,11},{10,... | collective-permute-start | bytes 196616 | tf_op jit(solution)/shard_map/ppermute | solution.py:90
  7.4 2.6 %collective-permute-start.6 = (bf16[4,2,32,128]{3,2,1,0:T(8,128)(2,1)S(1)}, bf16[4,2,32,128]{3,2,1,0:T(8,128)(2,1)S(1)}, u32[]{:S(2)}, u32[]{:S(2)}) collective-permute-start(bf16[4,2,32,128]{3,2,1,0:T(8,128)(2,1)S(1)} %get-tuple-element.50), channel_id=1, source_target_pairs={{0,4},{1,5},{2,6},{3,7},{4,0},{5,1},{6,2},{7,3},{8,12},{9,13},{10,... | collective-permute-start | bytes 196616 | tf_op jit(solution)/shard_map/ppermute | solution.py:90
  10.0 3.9 %range_compress.1 = (bf16[2,64,16,128]{3,2,1,0:T(8,128)(2,1)S(1)}, s32[8,16]{1,0:T(8,128)S(1)}, s32[8,16]{1,0:T(8,128)S(1)}) custom-call(s32[194]{0:T(256)S(1)} %concatenate.6.info_ref, bf16[16,8192]{1,0:T(8,128)(2,1)S(1)} %get-tuple-element.39.real_ref, bf16[16,8192]{1,0:T(8,128)(2,1)S(1)} %get-tuple-element.40.imag_ref, f32[640,128]{1,0:T(8,128)S(1)} %copy-done.1), custom_call_target="tpu_custom_call" | custom-call | flops 201326592 | bytes 1900544 | tf_op jit(solution)/shard_map/range_compress/pallas_call | solution.py:174
  13.9 0.1 collective-permute-start.1
  14.0 0.3 collective-permute-done.6
  14.4 1.7 %collective-permute-done.7 = bf16[4,2,32,128]{3,2,1,0:T(8,128)(2,1)S(1)} collective-permute-done((bf16[4,2,32,128]{3,2,1,0:T(8,128)(2,1)S(1)}, bf16[4,2,32,128]{3,2,1,0:T(8,128)(2,1)S(1)}, u32[]{:S(2)}, u32[]{:S(2)}) %collective-permute-start.7) | collective-permute-done | bytes 65568 | tf_op jit(solution)/shard_map/ppermute | solution.py:90
  16.1 2.5 %collective-permute-start.10 = (bf16[16,2,32,128]{3,2,1,0:T(8,128)(2,1)S(1)}, bf16[16,2,32,128]{3,2,1,0:T(8,128)(2,1)S(1)}, u32[]{:S(2)}, u32[]{:S(2)}) collective-permute-start(bf16[16,2,32,128]{3,2,1,0:T(8,128)(2,1)S(1)} %constant_dynamic-update-slice_fusion.rest_4_), channel_id=1, source_target_pairs={{0,24},{8,16},{16,8},{24,0},{1,25},{9,17},{17,9},{25,1},{2,26},{10... | collective-permute-start | bytes 786440 | tf_op jit(solution)/shard_map/ppermute | solution.py:90
  18.6 0.5 collective-permute-start.9
  19.1 0.5 collective-permute-start.8
  19.7 0.8 %spread_columns.1 = (bf16[8,2,32,128]{3,2,1,0:T(8,128)(2,1)S(1)}, bf16[8,2,32,128]{3,2,1,0:T(8,128)(2,1)S(1)}, bf16[8,2,32,128]{3,2,1,0:T(8,128)(2,1)S(1)}, bf16...) custom-call(s32[8,16]{1,0:T(8,128)S(1)} %get-tuple-element.42.table_, ...), custom_call_target="tpu_custom_call" | custom-call | bytes 2097152 | tf_op jit(solution)/shard_map/spread_columns/pallas_call | solution.py:221
  20.5 1.3 %collective-permute-start.11 = (bf16[8,2,32,128]{3,2,1,0:T(8,128)(2,1)S(1)}, bf16[8,2,32,128]{3,2,1,0:T(8,128)(2,1)S(1)}, u32[]{:S(2)}, u32[]{:S(2)}) collective-permute-start(bf16[8,2,32,128]{3,2,1,0:T(8,128)(2,1)S(1)} %get-tuple-element.55), channel_id=1, source_target_pairs={{0,2},{1,3},{2,0},{3,1},{4,6},{5,7},{6,4},{7,5},{8,10},{9,11},{10,... | collective-permute-start | bytes 393224 | tf_op jit(solution)/shard_map/ppermute | solution.py:90
  21.8 1.7 %collective-permute-start.12 = (bf16[8,2,32,128]{3,2,1,0:T(8,128)(2,1)S(1)}, bf16[8,2,32,128]{3,2,1,0:T(8,128)(2,1)S(1)}, u32[]{:S(2)}, u32[]{:S(2)}) collective-permute-start(bf16[8,2,32,128]{3,2,1,0:T(8,128)(2,1)S(1)} %get-tuple-element.56), channel_id=1, source_target_pairs={{0,4},{1,5},{2,6},{3,7},{4,0},{5,1},{6,2},{7,3},{8,12},{9,13},{10,... | collective-permute-start | bytes 393224 | tf_op jit(solution)/shard_map/ppermute | solution.py:90
  23.5 2.8 %collective-permute-done.10.rest_7_ = bf16[16,2,32,128]{3,2,1,0:T(8,128)(2,1)S(1)} collective-permute-done((bf16[16,2,32,128]{3,2,1,0:T(8,128)(2,1)S(1)}, bf16[16,2,32,128]{3,2,1,0:T(8,128)(2,1)S(1)}, u32[]{:S(2)}, u32[]{:S(2)}) %collective-permute-start.10) | collective-permute-done | bytes 262176 | tf_op jit(solution)/shard_map/ppermute | solution.py:90
  26.4 2.4 %collective-permute-start.13 = (bf16[8,2,32,128]{3,2,1,0:T(8,128)(2,1)S(1)}, bf16[8,2,32,128]{3,2,1,0:T(8,128)(2,1)S(1)}, u32[]{:S(2)}, u32[]{:S(2)}) collective-permute-start(bf16[8,2,32,128]{3,2,1,0:T(8,128)(2,1)S(1)} %get-tuple-element.57), channel_id=1, source_target_pairs={{0,6},{1,7},{2,4},{3,5},{4,2},{5,3},{6,0},{7,1},{8,14},{9,15},{10,... | collective-permute-start | bytes 393224 | tf_op jit(solution)/shard_map/ppermute | solution.py:90
  28.7 0.5 resample_tables.1.back_ref
  29.2 0.5 collective-permute-done.9.rest_6_
  29.7 2.1 %collective-permute-start.2 = (bf16[8,2,32,128]{3,2,1,0:T(8,128)(2,1)S(1)}, bf16[8,2,32,128]{3,2,1,0:T(8,128)(2,1)S(1)}, u32[]{:S(2)}, u32[]{:S(2)}) collective-permute-start(bf16[8,2,32,128]{3,2,1,0:T(8,128)(2,1)S(1)} %get-tuple-element.45), channel_id=1, source_target_pairs={{0,2},{1,3},{2,0},{3,1},{4,6},{5,7},{6,4},{7,5},{8,10},{9,11},{10,... | collective-permute-start | bytes 393224 | tf_op jit(solution)/shard_map/ppermute | solution.py:90
  31.9 1.9 %collective-permute-start.3 = (bf16[8,2,32,128]{3,2,1,0:T(8,128)(2,1)S(1)}, bf16[8,2,32,128]{3,2,1,0:T(8,128)(2,1)S(1)}, u32[]{:S(2)}, u32[]{:S(2)}) collective-permute-start(bf16[8,2,32,128]{3,2,1,0:T(8,128)(2,1)S(1)} %get-tuple-element.46), channel_id=1, source_target_pairs={{0,4},{1,5},{2,6},{3,7},{4,0},{5,1},{6,2},{7,3},{8,12},{9,13},{10,... | collective-permute-start | bytes 393224 | tf_op jit(solution)/shard_map/ppermute | solution.py:90
  33.8 0.6 collective-permute-start.4
  34.3 1.8 %focus.3 = (bf16[2,2,128,128]{3,2,1,0:T(8,128)(2,1)S(1)}, bf16[4,2,128,128]{3,2,1,0:T(8,128)(2,1)S(1)}, bf16[2,2,128,128]{3,2,1,0:T(8,128)(2,1)S(1)}) custom-call(s32[194]{0:T(256)S(1)} %concatenate.6.info_ref, s32[8,16]{1,0:T(8,128)S(1)} %get-tuple-element.41.table_ref, bf16[256,256]{1,0:T(8,128)(2,1)S(1)} %copy-done.2, ...), custom_call_target="tpu_custom_call" | custom-call | flops 2952790016 | bytes 22020096 | tf_op jit(solution)/shard_map/focus/pallas_call | solution.py:374
  36.1 1.5 %collective-permute-start.14 = (bf16[2,2,128,128]{3,2,1,0:T(8,128)(2,1)S(1)}, bf16[2,2,128,128]{3,2,1,0:T(8,128)(2,1)S(1)}, u32[]{:S(2)}, u32[]{:S(2)}) collective-permute-start(bf16[2,2,128,128]{3,2,1,0:T(8,128)(2,1)S(1)} %get-tuple-element.58.rest_0_), channel_id=1, source_target_pairs={{0,16},{8,24},{16,0},{24,8},{1,17},{9,25},{17,1},{25,9},{2,18},{10... | collective-permute-start | bytes 393224 | tf_op jit(solution)/shard_map/ppermute | solution.py:90
  37.6 0.6 collective-permute-start.19
  38.2 1.4 %collective-permute-start.17 = (bf16[4,2,128,128]{3,2,1,0:T(8,128)(2,1)S(1)}, bf16[4,2,128,128]{3,2,1,0:T(8,128)(2,1)S(1)}, u32[]{:S(2)}, u32[]{:S(2)}) collective-permute-start(bf16[4,2,128,128]{3,2,1,0:T(8,128)(2,1)S(1)} %get-tuple-element.60.rest_1_), channel_id=1, source_target_pairs={{0,16},{8,24},{16,0},{24,8},{1,17},{9,25},{17,1},{25,9},{2,18},{10... | collective-permute-start | bytes 786440 | tf_op jit(solution)/shard_map/ppermute | solution.py:90
  39.6 5.0 %collective-permute-done.3.rest_2_ = bf16[8,2,32,128]{3,2,1,0:T(8,128)(2,1)S(1)} collective-permute-done((bf16[8,2,32,128]{3,2,1,0:T(8,128)(2,1)S(1)}, bf16[8,2,32,128]{3,2,1,0:T(8,128)(2,1)S(1)}, u32[]{:S(2)}, u32[]{:S(2)}) %collective-permute-start.3) | collective-permute-done | bytes 131104 | tf_op jit(solution)/shard_map/ppermute | solution.py:90
  44.7 1.8 %focus.2 = (bf16[4,2,128,128]{3,2,1,0:T(8,128)(2,1)S(1)}, bf16[4,2,128,128]{3,2,1,0:T(8,128)(2,1)S(1)}) custom-call(s32[194]{0:T(256)S(1)} %concatenate.6.info_ref, s32[8,16]{1,0:T(8,128)S(1)} %get-tuple-element.41.table_ref, bf16[256,256]{1,0:T(8,128)(2,1)S(1)} %copy-done.2, bf16[8,256,256]{2,1,0:T(8,128)(2,1)S(1)} %resample_tables.1.back_ref, ...), custom_call_target="tpu_custom_call" | custom-call | flops 2952790016 | bytes 22020096 | tf_op jit(solution)/shard_map/focus/pallas_call | solution.py:374
  46.5 1.6 %collective-permute-start.16 = (bf16[2,2,128,128]{3,2,1,0:T(8,128)(2,1)S(1)}, bf16[2,2,128,128]{3,2,1,0:T(8,128)(2,1)S(1)}, u32[]{:S(2)}, u32[]{:S(2)}) collective-permute-start(bf16[2,2,128,128]{3,2,1,0:T(8,128)(2,1)S(1)} %broadcast_select_fusion.4), channel_id=1, source_target_pairs={{0,8},{8,0},{16,24},{24,16},{1,9},{9,1},{17,25},{25,17},{2,10},{10... | collective-permute-start | bytes 393224 | tf_op jit(solution)/shard_map/ppermute | solution.py:90
  48.1 1.3 %collective-permute-start.22 = (bf16[4,2,128,128]{3,2,1,0:T(8,128)(2,1)S(1)}, bf16[4,2,128,128]{3,2,1,0:T(8,128)(2,1)S(1)}, u32[]{:S(2)}, u32[]{:S(2)}) collective-permute-start(bf16[4,2,128,128]{3,2,1,0:T(8,128)(2,1)S(1)} %get-tuple-element.63.rest_0_), channel_id=1, source_target_pairs={{0,16},{8,24},{16,0},{24,8},{1,17},{9,25},{17,1},{25,9},{2,18},{10... | collective-permute-start | bytes 786440 | tf_op jit(solution)/shard_map/ppermute | solution.py:90
  49.4 0.8 %collective-permute-start.20 = (bf16[2,2,128,128]{3,2,1,0:T(8,128)(2,1)S(1)}, bf16[2,2,128,128]{3,2,1,0:T(8,128)(2,1)S(1)}, u32[]{:S(2)}, u32[]{:S(2)}) collective-permute-start(bf16[2,2,128,128]{3,2,1,0:T(8,128)(2,1)S(1)} %broadcast_select_fusion.3), channel_id=1, source_target_pairs={{0,8},{8,0},{16,24},{24,16},{1,9},{9,1},{17,25},{25,17},{2,10},{10... | collective-permute-start | bytes 393224 | tf_op jit(solution)/shard_map/ppermute | solution.py:90
  50.2 0.5 collective-permute-start.15
  50.8 1.9 %collective-permute-start.18 = (bf16[4,2,128,128]{3,2,1,0:T(8,128)(2,1)S(1)}, bf16[4,2,128,128]{3,2,1,0:T(8,128)(2,1)S(1)}, u32[]{:S(2)}, u32[]{:S(2)}) collective-permute-start(bf16[4,2,128,128]{3,2,1,0:T(8,128)(2,1)S(1)} %broadcast_select_fusion.1), channel_id=1, source_target_pairs={{0,8},{8,0},{16,24},{24,16},{1,9},{9,1},{17,25},{25,17},{2,10},{10... | collective-permute-start | bytes 786440 | tf_op jit(solution)/shard_map/ppermute | solution.py:90
  52.6 4.7 %collective-permute-done.22.rest_2_ = bf16[4,2,128,128]{3,2,1,0:T(8,128)(2,1)S(1)} collective-permute-done((bf16[4,2,128,128]{3,2,1,0:T(8,128)(2,1)S(1)}, bf16[4,2,128,128]{3,2,1,0:T(8,128)(2,1)S(1)}, u32[]{:S(2)}, u32[]{:S(2)}) %collective-permute-start.22) | collective-permute-done | bytes 262176 | tf_op jit(solution)/shard_map/ppermute | solution.py:90
  57.3 0.9 %collective-permute-start.23 = (bf16[4,2,128,128]{3,2,1,0:T(8,128)(2,1)S(1)}, bf16[4,2,128,128]{3,2,1,0:T(8,128)(2,1)S(1)}, u32[]{:S(2)}, u32[]{:S(2)}) collective-permute-start(bf16[4,2,128,128]{3,2,1,0:T(8,128)(2,1)S(1)} %broadcast_select_fusion), channel_id=1, source_target_pairs={{0,8},{8,0},{16,24},{24,16},{1,9},{9,1},{17,25},{25,17},{2,10},{10... | collective-permute-start | bytes 786440 | tf_op jit(solution)/shard_map/ppermute | solution.py:90
  58.3 2.4 %collective-permute-done.15.rest_2_ = bf16[4,2,128,128]{3,2,1,0:T(8,128)(2,1)S(1)} collective-permute-done((bf16[4,2,128,128]{3,2,1,0:T(8,128)(2,1)S(1)}, bf16[4,2,128,128]{3,2,1,0:T(8,128)(2,1)S(1)}, u32[]{:S(2)}, u32[]{:S(2)}) %collective-permute-start.15) | collective-permute-done | bytes 262176 | tf_op jit(solution)/shard_map/ppermute | solution.py:90
  60.7 0.8 %collective-permute-done.18.rest_4_ = bf16[4,2,128,128]{3,2,1,0:T(8,128)(2,1)S(1)} collective-permute-done((bf16[4,2,128,128]{3,2,1,0:T(8,128)(2,1)S(1)}, bf16[4,2,128,128]{3,2,1,0:T(8,128)(2,1)S(1)}, u32[]{:S(2)}, u32[]{:S(2)}) %collective-permute-start.18) | collective-permute-done | bytes 262176 | tf_op jit(solution)/shard_map/ppermute | solution.py:90
  61.5 3.0 %goldstein.3.rest_7_ = bf16[16,2,2,128,128]{4,3,2,1,0:T(8,128)(2,1)} custom-call(bf16[2,2,128,128]{3,2,1,0:T(8,128)(2,1)S(1)} %get-tuple-element.58.rest_0_, bf16[4,2,128,128]{3,2,1,0:T(8,128)(2,1)S(1)} %get-tuple-element.60.rest_1_, bf16[2,2,128,128]{3,2,1,0:T(8,128)(2,1)S(1)} %get-tuple-element.61.rest_2_, ...), custom_call_target="tpu_custom_call" | custom-call | flops 4294967296 | bytes 6291456 | tf_op jit(solution)/shard_map/goldstein/pallas_call | solution.py:465
  64.5 1.0 %collective-permute-start.21 = (bf16[4,2,128,128]{3,2,1,0:T(8,128)(2,1)S(1)}, bf16[4,2,128,128]{3,2,1,0:T(8,128)(2,1)S(1)}, u32[]{:S(2)}, u32[]{:S(2)}) collective-permute-start(bf16[4,2,128,128]{3,2,1,0:T(8,128)(2,1)S(1)} %broadcast_select_fusion.2), channel_id=1, source_target_pairs={{0,8},{8,0},{16,24},{24,16},{1,9},{9,1},{17,25},{25,17},{2,10},{10... | collective-permute-start | bytes 786440 | tf_op jit(solution)/shard_map/ppermute | solution.py:90
  65.5 0.4 collective-permute-done.23.rest_1_
  65.9 1.9 %goldstein.4.rest_7_ = bf16[16,2,2,128,128]{4,3,2,1,0:T(8,128)(2,1)} custom-call(bf16[4,2,128,128]{3,2,1,0:T(8,128)(2,1)S(1)} %get-tuple-element.63.rest_0_, bf16[4,2,128,128]{3,2,1,0:T(8,128)(2,1)S(1)} %collective-permute-done.23.rest_1_, bf16[4,2,128,128]{3,2,1,0:T(8,128)(2,1)S(1)} %collective-permute-done.22.rest_2_, ...), custom_call_target="tpu_custom_call", output_to_operand_aliasing={{}: (7, {})} | custom-call | flops 2147483648 | bytes 5505024 | tf_op jit(solution)/shard_map/goldstein/pallas_call | solution.py:465
  67.8 3.1 %collective-permute-done.21.rest_1_ = bf16[4,2,128,128]{3,2,1,0:T(8,128)(2,1)S(1)} collective-permute-done((bf16[4,2,128,128]{3,2,1,0:T(8,128)(2,1)S(1)}, bf16[4,2,128,128]{3,2,1,0:T(8,128)(2,1)S(1)}, u32[]{:S(2)}, u32[]{:S(2)}) %collective-permute-start.21) | collective-permute-done | bytes 262176 | tf_op jit(solution)/shard_map/ppermute | solution.py:90
  70.9 1.9 %goldstein.5 = bf16[16,2,2,128,128]{4,3,2,1,0:T(8,128)(2,1)} custom-call(bf16[4,2,128,128]{3,2,1,0:T(8,128)(2,1)S(1)} %get-tuple-element.59.rest_0_, bf16[4,2,128,128]{3,2,1,0:T(8,128)(2,1)S(1)} %collective-permute-done.21.rest_1_, bf16[4,2,128,128]{3,2,1,0:T(8,128)(2,1)S(1)} %collective-permute-done.15.rest_2_, ...), custom_call_target="tpu_custom_call", output_to_operand_aliasing={{}: (7, {})} | custom-call | flops 2147483648 | bytes 5505024 | tf_op jit(solution)/shard_map/goldstein/pallas_call | solution.py:465
  (37 shorter events, 0.3 us)
Async XLA Ops:
  0.0 1.1 %copy-start = (bf16[2,128,1024]{2,1,0:T(8,128)(2,1)S(1)}, bf16[2,128,1024]{2,1,0:T(8,128)(2,1)}, u32[]{:S(2)}) copy-start(bf16[2,128,1024]{2,1,0:T(8,128)(2,1)} %param.22) | copy-start | bytes 1572868
  0.0 10.0 %copy-start.1 = (f32[640,128]{1,0:T(8,128)S(1)}, f32[640,128]{1,0:T(8,128)}, u32[]{:S(2)}) copy-start(f32[640,128]{1,0:T(8,128)} %constant.40.clone.tables_ref) | copy-start | bytes 983044
  0.0 3.9 %copy-start.6 = (s32[1,64]{1,0:T(1,128)S(1)}, s32[1,64]{1,0:T(1,128)}, u32[]{:S(2)}) copy-start(s32[1,64]{1,0:T(1,128)} %param.25) | copy-start | bytes 772
  0.0 3.9 %copy-start.5 = (s32[1,64]{1,0:T(1,128)S(1)}, s32[1,64]{1,0:T(1,128)}, u32[]{:S(2)}) copy-start(s32[1,64]{1,0:T(1,128)} %param.24) | copy-start | bytes 772
  0.0 3.9 %copy-start.4 = (s32[1,64]{1,0:T(1,128)S(1)}, s32[1,64]{1,0:T(1,128)}, u32[]{:S(2)}) copy-start(s32[1,64]{1,0:T(1,128)} %param.23) | copy-start | bytes 772
  1.1 2.9 %collective-permute-start = (bf16[2,32,1024]{2,1,0:T(8,128)(2,1)S(1)}, bf16[2,32,1024]{2,1,0:T(8,128)(2,1)S(1)}, u32[]{:S(2)}, u32[]{:S(2)}) collective-permute-start(bf16[2,32,1024]{2,1,0:T(8,128)(2,1)S(1)} %constant_dynamic-slice_fusion.rest_0_), channel_id=1, source_target_pairs={{0,1},{1,0},{2,3},{3,2},{4,5},{5,4},{6,7},{7,6},{8,9},{9,8},{10,11... | collective-permute-start | bytes 393224 | tf_op jit(solution)/shard_map/ppermute | solution.py:90
  3.7 25.0 %copy-start.2 = (bf16[256,256]{1,0:T(8,128)(2,1)S(1)}, bf16[256,256]{1,0:T(8,128)(2,1)}, u32[]{:S(2)}) copy-start(bf16[256,256]{1,0:T(8,128)(2,1)} %constant.47.forward_ref.rest_9_.rest_12_.rest_3_.rest_6_) | copy-start | bytes 393220
  4.7 9.3 %collective-permute-start.5 = (bf16[4,2,32,128]{3,2,1,0:T(8,128)(2,1)S(1)}, bf16[4,2,32,128]{3,2,1,0:T(8,128)(2,1)S(1)}, u32[]{:S(2)}, u32[]{:S(2)}) collective-permute-start(bf16[4,2,32,128]{3,2,1,0:T(8,128)(2,1)S(1)} %get-tuple-element.49), channel_id=1, source_target_pairs={{0,2},{1,3},{2,0},{3,1},{4,6},{5,7},{6,4},{7,5},{8,10},{9,11},{10,... | collective-permute-start | bytes 196616 | tf_op jit(solution)/shard_map/ppermute | solution.py:90
  7.4 7.0 %collective-permute-start.6 = (bf16[4,2,32,128]{3,2,1,0:T(8,128)(2,1)S(1)}, bf16[4,2,32,128]{3,2,1,0:T(8,128)(2,1)S(1)}, u32[]{:S(2)}, u32[]{:S(2)}) collective-permute-start(bf16[4,2,32,128]{3,2,1,0:T(8,128)(2,1)S(1)} %get-tuple-element.50), channel_id=1, source_target_pairs={{0,4},{1,5},{2,6},{3,7},{4,0},{5,1},{6,2},{7,3},{8,12},{9,13},{10,... | collective-permute-start | bytes 196616 | tf_op jit(solution)/shard_map/ppermute | solution.py:90
  10.0 6.1 %collective-permute-start.7 = (bf16[4,2,32,128]{3,2,1,0:T(8,128)(2,1)S(1)}, bf16[4,2,32,128]{3,2,1,0:T(8,128)(2,1)S(1)}, u32[]{:S(2)}, u32[]{:S(2)}) collective-permute-start(bf16[4,2,32,128]{3,2,1,0:T(8,128)(2,1)S(1)} %get-tuple-element.51), channel_id=1, source_target_pairs={{0,6},{1,7},{2,4},{3,5},{4,2},{5,3},{6,0},{7,1},{8,14},{9,15},{10,... | collective-permute-start | bytes 196616 | tf_op jit(solution)/shard_map/ppermute | solution.py:90
  13.9 5.8 %collective-permute-start.1 = (bf16[2,64,16,128]{3,2,1,0:T(8,128)(2,1)S(1)}, bf16[2,64,16,128]{3,2,1,0:T(8,128)(2,1)S(1)}, u32[]{:S(2)}, u32[]{:S(2)}) collective-permute-start(bf16[2,64,16,128]{3,2,1,0:T(8,128)(2,1)S(1)} %get-tuple-element.43.rest_0_), channel_id=1, source_target_pairs={{0,1},{1,0},{2,3},{3,2},{4,5},{5,4},{6,7},{7,6},{8,9},{9,8},{10,11... | collective-permute-start | bytes 1572872 | tf_op jit(solution)/shard_map/ppermute | solution.py:90
  16.1 10.3 %collective-permute-start.10 = (bf16[16,2,32,128]{3,2,1,0:T(8,128)(2,1)S(1)}, bf16[16,2,32,128]{3,2,1,0:T(8,128)(2,1)S(1)}, u32[]{:S(2)}, u32[]{:S(2)}) collective-permute-start(bf16[16,2,32,128]{3,2,1,0:T(8,128)(2,1)S(1)} %constant_dynamic-update-slice_fusion.rest_4_), channel_id=1, source_target_pairs={{0,24},{8,16},{16,8},{24,0},{1,25},{9,17},{17,9},{25,1},{2,26},{10... | collective-permute-start | bytes 786440 | tf_op jit(solution)/shard_map/ppermute | solution.py:90
  18.6 11.1 %collective-permute-start.9 = (bf16[16,2,32,128]{3,2,1,0:T(8,128)(2,1)S(1)}, bf16[16,2,32,128]{3,2,1,0:T(8,128)(2,1)S(1)}, u32[]{:S(2)}, u32[]{:S(2)}) collective-permute-start(bf16[16,2,32,128]{3,2,1,0:T(8,128)(2,1)S(1)} %constant_dynamic-update-slice_fusion.rest_4_), channel_id=1, source_target_pairs={{0,16},{8,24},{16,0},{24,8},{1,17},{9,25},{17,1},{25,9},{2,18},{10... | collective-permute-start | bytes 786440 | tf_op jit(solution)/shard_map/ppermute | solution.py:90
  19.1 12.7 %collective-permute-start.8 = (bf16[16,2,32,128]{3,2,1,0:T(8,128)(2,1)S(1)}, bf16[16,2,32,128]{3,2,1,0:T(8,128)(2,1)S(1)}, u32[]{:S(2)}, u32[]{:S(2)}) collective-permute-start(bf16[16,2,32,128]{3,2,1,0:T(8,128)(2,1)S(1)} %constant_dynamic-update-slice_fusion.rest_4_), channel_id=1, source_target_pairs={{0,8},{8,0},{16,24},{24,16},{1,9},{9,1},{17,25},{25,17},{2,10},{10... | collective-permute-start | bytes 786440 | tf_op jit(solution)/shard_map/ppermute | solution.py:90
  20.5 13.3 %collective-permute-start.11 = (bf16[8,2,32,128]{3,2,1,0:T(8,128)(2,1)S(1)}, bf16[8,2,32,128]{3,2,1,0:T(8,128)(2,1)S(1)}, u32[]{:S(2)}, u32[]{:S(2)}) collective-permute-start(bf16[8,2,32,128]{3,2,1,0:T(8,128)(2,1)S(1)} %get-tuple-element.55), channel_id=1, source_target_pairs={{0,2},{1,3},{2,0},{3,1},{4,6},{5,7},{6,4},{7,5},{8,10},{9,11},{10,... | collective-permute-start | bytes 393224 | tf_op jit(solution)/shard_map/ppermute | solution.py:90
  21.8 12.5 %collective-permute-start.12 = (bf16[8,2,32,128]{3,2,1,0:T(8,128)(2,1)S(1)}, bf16[8,2,32,128]{3,2,1,0:T(8,128)(2,1)S(1)}, u32[]{:S(2)}, u32[]{:S(2)}) collective-permute-start(bf16[8,2,32,128]{3,2,1,0:T(8,128)(2,1)S(1)} %get-tuple-element.56), channel_id=1, source_target_pairs={{0,4},{1,5},{2,6},{3,7},{4,0},{5,1},{6,2},{7,3},{8,12},{9,13},{10,... | collective-permute-start | bytes 393224 | tf_op jit(solution)/shard_map/ppermute | solution.py:90
  26.4 8.0 %collective-permute-start.13 = (bf16[8,2,32,128]{3,2,1,0:T(8,128)(2,1)S(1)}, bf16[8,2,32,128]{3,2,1,0:T(8,128)(2,1)S(1)}, u32[]{:S(2)}, u32[]{:S(2)}) collective-permute-start(bf16[8,2,32,128]{3,2,1,0:T(8,128)(2,1)S(1)} %get-tuple-element.57), channel_id=1, source_target_pairs={{0,6},{1,7},{2,4},{3,5},{4,2},{5,3},{6,0},{7,1},{8,14},{9,15},{10,... | collective-permute-start | bytes 393224 | tf_op jit(solution)/shard_map/ppermute | solution.py:90
  29.7 8.5 %collective-permute-start.2 = (bf16[8,2,32,128]{3,2,1,0:T(8,128)(2,1)S(1)}, bf16[8,2,32,128]{3,2,1,0:T(8,128)(2,1)S(1)}, u32[]{:S(2)}, u32[]{:S(2)}) collective-permute-start(bf16[8,2,32,128]{3,2,1,0:T(8,128)(2,1)S(1)} %get-tuple-element.45), channel_id=1, source_target_pairs={{0,2},{1,3},{2,0},{3,1},{4,6},{5,7},{6,4},{7,5},{8,10},{9,11},{10,... | collective-permute-start | bytes 393224 | tf_op jit(solution)/shard_map/ppermute | solution.py:90
  31.9 12.8 %collective-permute-start.3 = (bf16[8,2,32,128]{3,2,1,0:T(8,128)(2,1)S(1)}, bf16[8,2,32,128]{3,2,1,0:T(8,128)(2,1)S(1)}, u32[]{:S(2)}, u32[]{:S(2)}) collective-permute-start(bf16[8,2,32,128]{3,2,1,0:T(8,128)(2,1)S(1)} %get-tuple-element.46), channel_id=1, source_target_pairs={{0,4},{1,5},{2,6},{3,7},{4,0},{5,1},{6,2},{7,3},{8,12},{9,13},{10,... | collective-permute-start | bytes 393224 | tf_op jit(solution)/shard_map/ppermute | solution.py:90
  33.8 10.9 %collective-permute-start.4 = (bf16[8,2,32,128]{3,2,1,0:T(8,128)(2,1)S(1)}, bf16[8,2,32,128]{3,2,1,0:T(8,128)(2,1)S(1)}, u32[]{:S(2)}, u32[]{:S(2)}) collective-permute-start(bf16[8,2,32,128]{3,2,1,0:T(8,128)(2,1)S(1)} %get-tuple-element.47), channel_id=1, source_target_pairs={{0,6},{1,7},{2,4},{3,5},{4,2},{5,3},{6,0},{7,1},{8,14},{9,15},{10,... | collective-permute-start | bytes 393224 | tf_op jit(solution)/shard_map/ppermute | solution.py:90
  36.1 10.4 %collective-permute-start.14 = (bf16[2,2,128,128]{3,2,1,0:T(8,128)(2,1)S(1)}, bf16[2,2,128,128]{3,2,1,0:T(8,128)(2,1)S(1)}, u32[]{:S(2)}, u32[]{:S(2)}) collective-permute-start(bf16[2,2,128,128]{3,2,1,0:T(8,128)(2,1)S(1)} %get-tuple-element.58.rest_0_), channel_id=1, source_target_pairs={{0,16},{8,24},{16,0},{24,8},{1,17},{9,25},{17,1},{25,9},{2,18},{10... | collective-permute-start | bytes 393224 | tf_op jit(solution)/shard_map/ppermute | solution.py:90
  37.6 11.8 %collective-permute-start.19 = (bf16[2,2,128,128]{3,2,1,0:T(8,128)(2,1)S(1)}, bf16[2,2,128,128]{3,2,1,0:T(8,128)(2,1)S(1)}, u32[]{:S(2)}, u32[]{:S(2)}) collective-permute-start(bf16[2,2,128,128]{3,2,1,0:T(8,128)(2,1)S(1)} %get-tuple-element.61.rest_2_), channel_id=1, source_target_pairs={{0,16},{8,24},{16,0},{24,8},{1,17},{9,25},{17,1},{25,9},{2,18},{10... | collective-permute-start | bytes 393224 | tf_op jit(solution)/shard_map/ppermute | solution.py:90
  38.2 12.5 %collective-permute-start.17 = (bf16[4,2,128,128]{3,2,1,0:T(8,128)(2,1)S(1)}, bf16[4,2,128,128]{3,2,1,0:T(8,128)(2,1)S(1)}, u32[]{:S(2)}, u32[]{:S(2)}) collective-permute-start(bf16[4,2,128,128]{3,2,1,0:T(8,128)(2,1)S(1)} %get-tuple-element.60.rest_1_), channel_id=1, source_target_pairs={{0,16},{8,24},{16,0},{24,8},{1,17},{9,25},{17,1},{25,9},{2,18},{10... | collective-permute-start | bytes 786440 | tf_op jit(solution)/shard_map/ppermute | solution.py:90
  46.5 15.0 %copy-start.3 = (bf16[256,256]{1,0:T(8,128)(2,1)S(1)}, bf16[256,256]{1,0:T(8,128)(2,1)}, u32[]{:S(2)}) copy-start(bf16[256,256]{1,0:T(8,128)(2,1)} %constant.48.rest_10_.rest_11_.rest_4_.rest_5_) | copy-start | bytes 393220
  46.5 14.1 %collective-permute-start.16 = (bf16[2,2,128,128]{3,2,1,0:T(8,128)(2,1)S(1)}, bf16[2,2,128,128]{3,2,1,0:T(8,128)(2,1)S(1)}, u32[]{:S(2)}, u32[]{:S(2)}) collective-permute-start(bf16[2,2,128,128]{3,2,1,0:T(8,128)(2,1)S(1)} %broadcast_select_fusion.4), channel_id=1, source_target_pairs={{0,8},{8,0},{16,24},{24,16},{1,9},{9,1},{17,25},{25,17},{2,10},{10... | collective-permute-start | bytes 393224 | tf_op jit(solution)/shard_map/ppermute | solution.py:90
  48.1 9.2 %collective-permute-start.22 = (bf16[4,2,128,128]{3,2,1,0:T(8,128)(2,1)S(1)}, bf16[4,2,128,128]{3,2,1,0:T(8,128)(2,1)S(1)}, u32[]{:S(2)}, u32[]{:S(2)}) collective-permute-start(bf16[4,2,128,128]{3,2,1,0:T(8,128)(2,1)S(1)} %get-tuple-element.63.rest_0_), channel_id=1, source_target_pairs={{0,16},{8,24},{16,0},{24,8},{1,17},{9,25},{17,1},{25,9},{2,18},{10... | collective-permute-start | bytes 786440 | tf_op jit(solution)/shard_map/ppermute | solution.py:90
  49.4 11.3 %collective-permute-start.20 = (bf16[2,2,128,128]{3,2,1,0:T(8,128)(2,1)S(1)}, bf16[2,2,128,128]{3,2,1,0:T(8,128)(2,1)S(1)}, u32[]{:S(2)}, u32[]{:S(2)}) collective-permute-start(bf16[2,2,128,128]{3,2,1,0:T(8,128)(2,1)S(1)} %broadcast_select_fusion.3), channel_id=1, source_target_pairs={{0,8},{8,0},{16,24},{24,16},{1,9},{9,1},{17,25},{25,17},{2,10},{10... | collective-permute-start | bytes 393224 | tf_op jit(solution)/shard_map/ppermute | solution.py:90
  50.2 10.4 %collective-permute-start.15 = (bf16[4,2,128,128]{3,2,1,0:T(8,128)(2,1)S(1)}, bf16[4,2,128,128]{3,2,1,0:T(8,128)(2,1)S(1)}, u32[]{:S(2)}, u32[]{:S(2)}) collective-permute-start(bf16[4,2,128,128]{3,2,1,0:T(8,128)(2,1)S(1)} %get-tuple-element.59.rest_0_), channel_id=1, source_target_pairs={{0,16},{8,24},{16,0},{24,8},{1,17},{9,25},{17,1},{25,9},{2,18},{10... | collective-permute-start | bytes 786440 | tf_op jit(solution)/shard_map/ppermute | solution.py:90
  50.8 10.7 %collective-permute-start.18 = (bf16[4,2,128,128]{3,2,1,0:T(8,128)(2,1)S(1)}, bf16[4,2,128,128]{3,2,1,0:T(8,128)(2,1)S(1)}, u32[]{:S(2)}, u32[]{:S(2)}) collective-permute-start(bf16[4,2,128,128]{3,2,1,0:T(8,128)(2,1)S(1)} %broadcast_select_fusion.1), channel_id=1, source_target_pairs={{0,8},{8,0},{16,24},{24,16},{1,9},{9,1},{17,25},{25,17},{2,10},{10... | collective-permute-start | bytes 786440 | tf_op jit(solution)/shard_map/ppermute | solution.py:90
  57.3 8.5 %collective-permute-start.23 = (bf16[4,2,128,128]{3,2,1,0:T(8,128)(2,1)S(1)}, bf16[4,2,128,128]{3,2,1,0:T(8,128)(2,1)S(1)}, u32[]{:S(2)}, u32[]{:S(2)}) collective-permute-start(bf16[4,2,128,128]{3,2,1,0:T(8,128)(2,1)S(1)} %broadcast_select_fusion), channel_id=1, source_target_pairs={{0,8},{8,0},{16,24},{24,16},{1,9},{9,1},{17,25},{25,17},{2,10},{10... | collective-permute-start | bytes 786440 | tf_op jit(solution)/shard_map/ppermute | solution.py:90
  64.5 6.4 %collective-permute-start.21 = (bf16[4,2,128,128]{3,2,1,0:T(8,128)(2,1)S(1)}, bf16[4,2,128,128]{3,2,1,0:T(8,128)(2,1)S(1)}, u32[]{:S(2)}, u32[]{:S(2)}) collective-permute-start(bf16[4,2,128,128]{3,2,1,0:T(8,128)(2,1)S(1)} %broadcast_select_fusion.2), channel_id=1, source_target_pairs={{0,8},{8,0},{16,24},{24,16},{1,9},{9,1},{17,25},{25,17},{2,10},{10... | collective-permute-start | bytes 786440 | tf_op jit(solution)/shard_map/ppermute | solution.py:90
